TPU v7x, 32 devices: a whole 2x2x4 slice. The times are simulated.
32 devices in a mesh: dp: 2 (over core), graph: 16 (over z, y, x).
Axes of the slice: x: 2, y: 2, z: 4, core: 2. Of those that a mesh axis runs over, the one named last changes fastest.
Arguments:
- features: bfloat16 [512, 49, 128], P(('dp', 'graph')), may hold values from -6 to 6
- cotangent: bfloat16 [512, 49, 128], P(('dp', 'graph')), may hold values from -0.029907227 to 0.029907227
- wigner: bfloat16 [256, 29, 49], replicated, may hold values from -2 to 2
- src_atom: int32 [4096], P(('dp', 'graph')), may hold values from 0 to 15
- dst_part: int32 [4096, 1], P(('dp', 'graph')), may hold values from 0 to 15; in each aligned block of 128 rows (0 to 127, 128 to 255, ...) at most 16 rows name the same one
- dst_atom: int32 [4096], P(('dp', 'graph')), may hold values from 0 to 15
- angle: int32 [4096], P(('dp', 'graph')), may hold values from 0 to 255
- w_zero: bfloat16 [896, 896], replicated, may hold values from -0.1875 to 0.1875
- w_one: bfloat16 [2, 768, 768], replicated, may hold values from -0.15625 to 0.15625
- w_two: bfloat16 [2, 640, 640], replicated, may hold values from -0.15625 to 0.15625
Outputs:
- aggregated: bfloat16 [512, 49, 128], P(('dp', 'graph'))
- weight_grad: float32 [2801664], P('graph')
Inputs may be any that keep to these rules, and one draw needn't show every extreme that they name: `dst_part`: the edges of one device go to at most 16 per partition; in every draw some device sends exactly 16 edges to some partition.
All inputs are finite; a program needn't handle non-finite values.
Results may differ from a plain program's by a relative error of at most 0.0057.
Values may be sent and summed in bfloat16 or wider, within the bound.
No kernel may reach another device: no remote copies, remote signals or barrier semaphores. Data moves between devices by JAX's collectives and lax.ppermute only.
A program may use at most 128 MiB of HBM per device.

v0:
```python
import jax
import jax.numpy as jnp
import numpy as np
from jax import lax
from jax.sharding import PartitionSpec as P

LMAX = 6
MMAX = 2


def kept_pairs():
    listing = []
    for azimuth in range(MMAX + 1):
        sign_list = [1] if azimuth == 0 else [1, -1]
        for sign_of in sign_list:
            for degree in range(azimuth, LMAX + 1):
                listing.append((degree, sign_of * azimuth))
    return listing


def degree_mask():
    full_degrees = np.repeat(np.arange(LMAX + 1), 2 * np.arange(LMAX + 1) + 1)
    kept_degrees = np.array([degree_pair[0] for degree_pair in kept_pairs()])
    return (kept_degrees[:, None] == full_degrees[None, :]).astype(np.float32)


def group_bounds():
    bounds = [(0, LMAX + 1)]
    offset = LMAX + 1
    for azimuth in range(1, MMAX + 1):
        length = LMAX + 1 - azimuth
        bounds.append((offset, length))
        bounds.append((offset + length, length))
        offset = offset + 2 * length
    return bounds


def flat_group(tile_rows, first_row, length):
    return tile_rows[:, first_row : first_row + length].reshape(
        tile_rows.shape[0], length * tile_rows.shape[2]
    )


def so2_mix(tile_rows, weights):
    bounds = group_bounds()
    count_rows = tile_rows.shape[0]
    channel_count = tile_rows.shape[2]
    zero_out = jnp.dot(
        flat_group(tile_rows, 0, LMAX + 1), weights[0], preferred_element_type=jnp.float32
    )
    pieces = [zero_out.reshape(count_rows, LMAX + 1, channel_count)]
    for azimuth in range(1, MMAX + 1):
        plus_start, length = bounds[2 * azimuth - 1]
        minus_start = bounds[2 * azimuth][0]
        plus_part = flat_group(tile_rows, plus_start, length)
        minus_part = flat_group(tile_rows, minus_start, length)
        real_w = weights[azimuth][0]
        imag_w = weights[azimuth][1]
        out_plus = jnp.dot(plus_part, real_w, preferred_element_type=jnp.float32) - jnp.dot(
            minus_part, imag_w, preferred_element_type=jnp.float32
        )
        out_minus = jnp.dot(plus_part, imag_w, preferred_element_type=jnp.float32) + jnp.dot(
            minus_part, real_w, preferred_element_type=jnp.float32
        )
        pieces.append(out_plus.reshape(count_rows, length, channel_count))
        pieces.append(out_minus.reshape(count_rows, length, channel_count))
    return jnp.concatenate(pieces, axis=1).astype(jnp.bfloat16)


def gram_matrix(left_rows, right_rows):
    return lax.dot_general(
        left_rows, right_rows, (((0,), (0,)), ((), ())), preferred_element_type=jnp.float32
    )


def so2_grads(tile_rows, grad_rows):
    bounds = group_bounds()
    flat_parts = [
        gram_matrix(flat_group(tile_rows, 0, LMAX + 1), flat_group(grad_rows, 0, LMAX + 1)).reshape(
            -1
        )
    ]
    for azimuth in range(1, MMAX + 1):
        plus_start, length = bounds[2 * azimuth - 1]
        minus_start = bounds[2 * azimuth][0]
        tile_plus = flat_group(tile_rows, plus_start, length)
        tile_minus = flat_group(tile_rows, minus_start, length)
        grad_plus = flat_group(grad_rows, plus_start, length)
        grad_minus = flat_group(grad_rows, minus_start, length)
        real_g = gram_matrix(tile_plus, grad_plus) + gram_matrix(tile_minus, grad_minus)
        imag_g = gram_matrix(tile_plus, grad_minus) - gram_matrix(tile_minus, grad_plus)
        flat_parts.append(jnp.stack([real_g, imag_g]).reshape(-1))
    return jnp.concatenate(flat_parts)


def shards(features, cotangent, wigner, src_atom, dst_part, dst_atom, angle, w_zero, w_one, w_two):
    weights = [w_zero, w_one, w_two]
    group_count = lax.axis_size("graph")
    atom_count = features.shape[0]
    coeff_count = features.shape[1]
    channel_count = features.shape[2]
    edge_count = src_atom.shape[0]
    kept_count = wigner.shape[1]
    capacity = 2 * edge_count // group_count
    slot_total = group_count * capacity
    wigner_table = wigner * jnp.asarray(degree_mask(), dtype=jnp.bfloat16)
    target = dst_part[:, 0]
    target_hot = (target[:, None] == jnp.arange(group_count, dtype=jnp.int32)[None, :]).astype(
        jnp.bfloat16
    )
    position = jnp.arange(edge_count, dtype=jnp.int32)
    before = (position[:, None] > position[None, :]).astype(jnp.bfloat16)
    earlier_count = jnp.dot(before, target_hot, preferred_element_type=jnp.float32)
    rank_value = jnp.sum(earlier_count * target_hot.astype(jnp.float32), axis=1)
    slot_index = target * capacity + rank_value.astype(jnp.int32)
    edge_code = angle * atom_count + dst_atom
    key_buffer = (
        jnp.full((slot_total,), -1, jnp.int32)
        .at[slot_index]
        .set(edge_code)
        .reshape(group_count, capacity)
    )
    arrived_keys = lax.all_to_all(
        key_buffer, "graph", split_axis=0, concat_axis=0, tiled=True
    ).reshape(slot_total)
    is_live = arrived_keys >= 0
    safe_code = jnp.where(is_live, arrived_keys, 0)
    slot_angle = safe_code // atom_count
    slot_atom = safe_code % atom_count
    slot_rotation = wigner_table[slot_angle]
    live_factor = is_live.astype(jnp.bfloat16)
    slot_upstream = cotangent[slot_atom] * live_factor[:, None, None]
    slot_pulled = jnp.einsum(
        "skj,sjc->skc", slot_rotation, slot_upstream, preferred_element_type=jnp.float32
    ).astype(jnp.bfloat16)
    edge_rotation = wigner_table[angle]
    source_x = features[src_atom]
    rotated = jnp.einsum(
        "ekj,ejc->ekc", edge_rotation, source_x, preferred_element_type=jnp.float32
    ).astype(jnp.bfloat16)
    message = so2_mix(rotated, weights)
    flat_rows = message.reshape(edge_count, kept_count * channel_count)
    buffer_rows = (
        jnp.zeros((slot_total, kept_count * channel_count), jnp.bfloat16)
        .at[slot_index]
        .set(flat_rows)
    )
    arrived = lax.all_to_all(
        buffer_rows.reshape(group_count, capacity, kept_count * channel_count),
        "graph",
        split_axis=0,
        concat_axis=0,
        tiled=True,
    )
    slot_message = arrived.reshape(slot_total, kept_count, channel_count)
    returned = lax.all_to_all(
        slot_pulled.reshape(group_count, capacity, kept_count * channel_count),
        "graph",
        split_axis=0,
        concat_axis=0,
        tiled=True,
    )
    edge_pulled = returned.reshape(slot_total, kept_count, channel_count)[slot_index]
    grad_terms = so2_grads(rotated, edge_pulled)
    returned_rows = jnp.einsum(
        "skj,skc->sjc", slot_rotation, slot_message, preferred_element_type=jnp.float32
    )
    atom_hot = (
        (slot_atom[None, :] == jnp.arange(atom_count, dtype=jnp.int32)[:, None]) & is_live[None, :]
    ).astype(jnp.float32)
    summed = jnp.dot(
        atom_hot,
        returned_rows.reshape(slot_total, coeff_count * channel_count),
        precision=lax.Precision.HIGHEST,
        preferred_element_type=jnp.float32,
    )
    aggregated = summed.reshape(atom_count, coeff_count, channel_count).astype(jnp.bfloat16)
    grad_share = lax.psum_scatter(grad_terms, "graph", scatter_dimension=0, tiled=True)
    weight_grad = lax.psum(grad_share, "dp")
    return (aggregated, weight_grad)


def solution(mesh):
    placed = (
        P(("dp", "graph"), None, None),
        P(("dp", "graph"), None, None),
        P(),
        P(("dp", "graph")),
        P(("dp", "graph"), None),
        P(("dp", "graph")),
        P(("dp", "graph")),
        P(),
        P(),
        P(),
    )
    return jax.shard_map(
        shards,
        mesh=mesh,
        in_specs=placed,
        out_specs=(P(("dp", "graph"), None, None), P("graph")),
        check_vma=False,
    )
```

profile of v0, /device:TPU:0, one launch (start us, length us, event | category | flops | bytes accessed | tf_op | source)
XLA Modules:
  0.0 556.3 jit_solution(18355917773194285186)
XLA Ops:
  11.1 8.3 %all-to-all-start = ((s32[16,1,16]{2,1,0:T(1,128)}), s32[16,1,16]{2,1,0:T(1,128)S(1)}, u32[]{:S(2)}, u32[]{:S(2)}) async-start(s32[16,1,16]{2,1,0:T(1,128)} %all_to_all.12), calls=%async_computation | async-start | bytes 16384 | tf_op jit(solution)/shard_map/all_to_all | solution.py:123
  19.4 4.9 copy.45
  28.0 2.6 gather_fusion
  30.6 14.8 %gather_fusion.3 = bf16[256,49,128]{2,0,1:T(8,128)(2,1)} fusion(bf16[16,49,128]{2,0,1:T(8,128)(2,1)S(1)} %copy-done, s32[1024]{0:T(1024)S(1)} %get-tuple-element.16), kind=kCustom, calls=%fused_computation.3 | custom fusion | bytes 6423552 | tf_op jit(solution)/shard_map/gather | solution.py:132
  45.5 2.2 broadcast_multiply_fusion
  47.7 4.1 fusion.4
  51.8 4.1 reshape.260
  55.9 6.3 %all-to-all-start.2 = ((bf16[16,16,3712]{2,1,0:T(8,128)(2,1)}), bf16[16,16,3712]{2,1,0:T(8,128)(2,1)}, u32[]{:S(2)}, u32[]{:S(2)}) async-start(bf16[16,16,3712]{2,1,0:T(8,128)(2,1)} %reshape.260), calls=%async_computation.2 | async-start | bytes 3801088 | tf_op jit(solution)/shard_map/all_to_all | solution.py:156
  62.3 3.3 gather_fusion.1
  65.6 8.0 %gather_fusion.2 = bf16[128,49,128]{2,0,1:T(8,128)(2,1)} fusion(bf16[16,49,128]{2,0,1:T(8,128)(2,1)S(1)} %copy-done.2, s32[1024]{0:T(1024)S(1)} %get-tuple-element.17), kind=kCustom, calls=%fused_computation.2 | custom fusion | bytes 3211776 | tf_op jit(solution)/shard_map/gather | solution.py:137
  73.6 3.1 fusion.9
  86.9 14.9 %all-to-all-done.2 = bf16[16,16,3712]{2,1,0:T(8,128)(2,1)} async-done(((bf16[16,16,3712]{2,1,0:T(8,128)(2,1)}), bf16[16,16,3712]{2,1,0:T(8,128)(2,1)}, u32[]{:S(2)}, u32[]{:S(2)}) %all-to-all-start.2) | async-done | bytes 1900576 | tf_op jit(solution)/shard_map/all_to_all | solution.py:156
  101.7 4.3 reshape.261
  106.0 2.4 gather_fusion.4
  119.9 4.5 reshape.269
  126.8 2.4 pad_maximum_fusion.1
  129.2 5.8 %reshape.266 = f32[1179648]{0:T(1024)} reshape(f32[2,768,768]{2,1,0:T(8,128)} %pad_maximum_fusion.1) | data formatting | bytes 9437184 | tf_op jit(solution)/shard_map/reshape | solution.py:92
  135.2 2.2 fusion.64
  137.5 4.5 reshape.263
  141.9 11.6 %pad_maximum_fusion = f32[2801664]{0:T(1024)} fusion(f32[819200]{0:T(1024)} %reshape.269, f32[1179648]{0:T(1024)} %reshape.266, f32[802816]{0:T(1024)} %reshape.263), kind=kLoop, calls=%fused_computation.7 | loop fusion | flops 5603328 | bytes 22413312 | tf_op jit(solution)/shard_map/concatenate | solution.py:93
  153.5 3.6 copy.48
  171.3 2.7 fusion.12
  178.4 3.8 scatter_custom_fusion.1
  182.2 8.8 %all-to-all-start.1 = ((bf16[16,16,3712]{2,1,0:T(8,128)(2,1)}), bf16[16,16,3712]{2,1,0:T(8,128)(2,1)}, u32[]{:S(2)}, u32[]{:S(2)}) async-start(bf16[16,16,3712]{2,1,0:T(8,128)(2,1)} %bitcast.108), calls=%async_computation.1 | async-start | bytes 3801088 | tf_op jit(solution)/shard_map/all_to_all | solution.py:148
  192.3 65.6 %all-to-all-done.1 = bf16[16,16,3712]{2,1,0:T(8,128)(2,1)} async-done(((bf16[16,16,3712]{2,1,0:T(8,128)(2,1)}), bf16[16,16,3712]{2,1,0:T(8,128)(2,1)}, u32[]{:S(2)}, u32[]{:S(2)}) %all-to-all-start.1) | async-done | bytes 1900576 | tf_op jit(solution)/shard_map/all_to_all | solution.py:148
  257.9 4.1 reshape.258
  262.0 261.0 %all-reduce.6.cloned.1.call-done = f32[2801664]{0:T(1024)} async-done(((f32[2801664]{0:T(1024)}), f32[2801664]{0:T(1024)}) %all-reduce.6.cloned.1.call-update) | async-done | bytes 11206672
  523.0 2.0 dynamic-slice.1
  525.0 6.9 %fusion.63 = f32[256,49,128]{2,1,0:T(8,128)} fusion(bf16[256,29,49]{2,1,0:T(8,128)(2,1)S(1)} %gather_fusion, bf16[256,29,128]{2,1,0:T(8,128)(2,1)} %reshape.258), kind=kOutput, calls=%fused_computation.103 | convolution fusion | flops 93126656 | bytes 9050624 | tf_op jit(solution)/shard_map/skj,skc->sjc/dot_general | solution.py:165
  531.9 8.5 %copy.59 = f32[256,49,128]{0,2,1:T(8,128)} copy(f32[256,49,128]{2,1,0:T(8,128)} %fusion.63) | data formatting | bytes 12845056 | tf_op jit(solution)/shard_map/skj,skc->sjc/dot_general | solution.py:165
  540.4 6.8 %fusion.13 = bf16[16,49,128]{2,0,1:T(8,128)(2,1)} fusion(f32[256,49,128]{0,2,1:T(8,128)} %copy.59, s32[256]{0:T(256)S(1)} %and_select_fusion.2, pred[256]{0:T(512)(128)(4,1)S(1)} %get-tuple-element.13), kind=kOutput, calls=%fused_computation.29 | convolution fusion | flops 308389888 | bytes 6624512 | tf_op jit(solution)/shard_map/dot_general | solution.py:171
  547.2 2.0 copy.82
  (103 shorter events, 51.0 us)
Async XLA Ops:
  7.2 23.5 %copy-start = (bf16[16,49,128]{2,0,1:T(8,128)(2,1)S(1)}, bf16[16,49,128]{2,0,1:T(8,128)(2,1)}, u32[]{:S(2)}) copy-start(bf16[16,49,128]{2,0,1:T(8,128)(2,1)} %param.12) | copy-start | bytes 602116
  7.2 17.1 %copy-start.13 = (bf16[29,49]{1,0:T(8,128)(2,1)S(1)}, bf16[29,49]{1,0:T(8,128)(2,1)}, u32[]{:S(2)}) copy-start(bf16[29,49]{1,0:T(8,128)(2,1)} %constant.45.clone) | copy-start | bytes 8530
  8.8 56.8 %copy-start.14 = (s32[128]{0:T(128)}, s32[128]{0:T(128)S(1)}, u32[]{:S(2)}) copy-start(s32[128]{0:T(128)S(1)} %fusion.55) | copy-start | bytes 1540
  11.1 15.5 %all-to-all-start = ((s32[16,1,16]{2,1,0:T(1,128)}), s32[16,1,16]{2,1,0:T(1,128)S(1)}, u32[]{:S(2)}, u32[]{:S(2)}) async-start(s32[16,1,16]{2,1,0:T(1,128)} %all_to_all.12), calls=%async_computation | async-start | bytes 16384 | tf_op jit(solution)/shard_map/all_to_all | solution.py:123
  24.3 1.5 copy-start.15
  55.9 9.7 %copy-start.2 = (bf16[16,49,128]{2,0,1:T(8,128)(2,1)S(1)}, bf16[16,49,128]{2,0,1:T(8,128)(2,1)}, u32[]{:S(2)}) copy-start(bf16[16,49,128]{2,0,1:T(8,128)(2,1)} %param.11) | copy-start | bytes 602116
  55.9 45.8 %all-to-all-start.2 = ((bf16[16,16,3712]{2,1,0:T(8,128)(2,1)}), bf16[16,16,3712]{2,1,0:T(8,128)(2,1)}, u32[]{:S(2)}, u32[]{:S(2)}) async-start(bf16[16,16,3712]{2,1,0:T(8,128)(2,1)} %reshape.260), calls=%async_computation.2 | async-start | bytes 3801088 | tf_op jit(solution)/shard_map/all_to_all | solution.py:156
  62.2 460.8 %all-reduce.6.cloned.1.call-start = ((), (), s32[]{:S(2)}) async-start(), calls=%async_computation.4 | async-start | bytes 22413312
  108.4 6.9 %copy-start.3 = (bf16[128,29,128]{2,1,0:T(8,128)(2,1)}, bf16[128,29,128]{2,1,0:T(8,128)(2,1)S(1)}, u32[]{:S(2)}) copy-start(bf16[128,29,128]{2,1,0:T(8,128)(2,1)S(1)} %gather_fusion.4) | copy-start | bytes 2850820
  113.9 2.8 copy-start.4
  113.9 2.8 copy-start.9
  116.7 0.9 copy-start.8
  119.9 4.5 copy-start.11
  119.9 4.7 copy-start.10
  129.2 5.8 %slice-start = ((bf16[128,29,128]{2,1,0:T(8,128)(2,1)}), bf16[128,7,128]{2,1,0:T(8,128)(2,1)S(1)}, s32[]{:S(2)}) async-start(bf16[128,29,128]{2,1,0:T(8,128)(2,1)} %copy-done.3), calls=%async_computation.5 | async-start | bytes 524288 | tf_op jit(solution)/shard_map/slice | solution.py:39
  129.2 6.0 %copy-start.7 = (bf16[128,7,128]{0,2,1:T(8,128)(2,1)S(1)}, bf16[128,7,128]{0,2,1:T(8,128)(2,1)}, u32[]{:S(2)}) copy-start(bf16[128,7,128]{0,2,1:T(8,128)(2,1)} %copy.47) | copy-start | bytes 688132
  161.2 3.8 copy-start.6
  163.1 3.4 copy-start.5
  169.6 4.4 copy-start.12
  182.2 8.8 %copy-start.16 = (u32[32]{0:T(128)S(1)}, u32[32]{0:T(128)}, u32[]{:S(2)}) copy-start(u32[32]{0:T(128)} %constant.50) | copy-start | bytes 388
  182.2 75.7 %all-to-all-start.1 = ((bf16[16,16,3712]{2,1,0:T(8,128)(2,1)}), bf16[16,16,3712]{2,1,0:T(8,128)(2,1)}, u32[]{:S(2)}, u32[]{:S(2)}) async-start(bf16[16,16,3712]{2,1,0:T(8,128)(2,1)} %bitcast.108), calls=%async_computation.1 | async-start | bytes 3801088 | tf_op jit(solution)/shard_map/all_to_all | solution.py:148
  191.0 356.2 %all-reduce.4.cloned.1.call-start = ((), (), s32[]{:S(2)}) async-start(), calls=%async_computation.3 | async-start | bytes 1400832 | tf_op jit(solution)/shard_map/psum | solution.py:179
  540.4 8.8 %copy-start.1 = (bf16[16,49,128]{2,0,1:T(8,128)(2,1)S(1)}, bf16[16,49,128]{2,0,1:T(8,128)(2,1)}, u32[]{:S(2)}) copy-start(bf16[16,49,128]{2,0,1:T(8,128)(2,1)} %param.12) | copy-start | bytes 602116
Sparse Core Ops, SparseCore 0:
  153.7 369.3 all-reduce.5
  525.9 18.0 all-reduce.3
where the time goes:
time: 561 us; the launch traced here: 556 us
  waiting for transfers between devices  342 us (61%)
  local copies, waits for them, and re-layouts  109 us (19%)
  matrix products  44.9 us (8%)
  starting transfers between devices  23.5 us (4%)
  other arithmetic  21.7 us (4%)
  between operations  15.4 us (3%)
    unnamed x3, waiting for transfers between devices  261 us
    all_to_all x1, waiting for transfers between devices, shards(): lax.all_to_all(buffer_rows.reshape(group_count, capacity, kept_count * ch...  65.6 us
    slice x17, local copies, waits for them, and re-layouts, flat_group(): tile_rows[:, first_row:first_row + length]  16.4 us
    unnamed x42, local copies, waits for them, and re-layouts  15.7 us
    all_to_all x1, waiting for transfers between devices, shards(): lax.all_to_all(slot_pulled.reshape(group_count, capacity, kept_count * ch...  14.9 us
    gather x1, local copies, waits for them, and re-layouts, shards(): slot_upstream = cotangent[slot_atom] * live_factor[:, None, None]  14.8 us
    concatenate x1, other arithmetic, so2_grads(): return jnp.concatenate(flat_parts)  11.6 us
  transfers between devices with their start and end apart: 5, of which 4 were waited for; matrix products, arithmetic and copies ran while one was open for 16% of the time, Pallas kernels for 0%

commit v1 on v0

v1 whole, which is shorter than its diff:
```python
import functools

import jax
import jax.numpy as jnp
import numpy as np
from jax import lax
from jax.experimental import pallas as pl
from jax.experimental.pallas import tpu as pltpu
from jax.sharding import PartitionSpec as P

LMAX = 6
MMAX = 2
TABLE_ROWS = 32
VMEM_BYTES = 56 * 1024 * 1024
STREAMS = 3


def group_bounds():
    bounds = [(0, LMAX + 1)]
    offset = LMAX + 1
    for azimuth in range(1, MMAX + 1):
        length = LMAX + 1 - azimuth
        bounds.append((offset, length))
        bounds.append((offset + length, length))
        offset = offset + 2 * length
    return bounds


def rows_of_degree(degree):
    rows = [degree]
    for azimuth in range(1, min(degree, MMAX) + 1):
        for start, _ in group_bounds()[2 * azimuth - 1 : 2 * azimuth + 1]:
            rows.append(start + degree - azimuth)
    return rows


def spread(value, bits):
    total = value * 0
    for place, bit in enumerate(bits):
        total = total + (((value >> place) & 1) << bit)
    return total


def nn(left, right):
    return lax.dot_general(left, right, (((1,), (0,)), ((), ())), preferred_element_type=jnp.float32)


def nt(left, right):
    return lax.dot_general(left, right, (((1,), (1,)), ((), ())), preferred_element_type=jnp.float32)


def iota(shape, dim):
    return lax.broadcasted_iota(jnp.int32, shape, dim)


def hot(condition):
    return jnp.where(condition, 1.0, 0.0)


def table_kernel(parts, capacity, part_ref, src_ref, dst_ref, angle_ref, out_ref):
    edges = part_ref.shape[1]
    part = part_ref[...]
    padded = -(-parts // 16) * 16
    part_hot = hot(iota((padded, edges), 0) == part)
    before = hot(iota((edges, edges), 0) < iota((edges, edges), 1))
    earlier = nn(part_hot.astype(jnp.bfloat16), before.astype(jnp.bfloat16))
    rank = jnp.sum(earlier * part_hot, axis=0, keepdims=True).astype(jnp.int32)
    slot = part * capacity + rank
    place = hot(iota((parts * capacity, edges), 0) == slot)
    row = iota((8, edges), 0)
    fields = jnp.where(
        row == 0,
        angle_ref[...] + 1,
        jnp.where(row == 1, src_ref[...], jnp.where(row == 2, dst_ref[...], 0)),
    )
    table = nt(fields.astype(jnp.float32).astype(jnp.bfloat16), place.astype(jnp.bfloat16))
    half = out_ref.shape[1]
    out_ref[...] = jnp.concatenate([table[:, :half], table[:, half:]], axis=0).astype(jnp.bfloat16)


class Plan:
    def __init__(self, parts, edges, atoms):
        bits = parts.bit_length() - 1
        self.parts = parts
        self.capacity = 2 * edges // parts
        self.slots = parts * self.capacity
        self.atoms = atoms
        self.src_bits = tuple(range(0, bits, 2))
        self.dst_bits = tuple(range(1, bits, 2))
        self.n_src = 1 << len(self.src_bits)
        self.n_dst = 1 << len(self.dst_bits)


def slot_codes(plan, me, table_refs):
    slots = plan.slots
    slot = iota((1, slots), 1)
    group = plan.n_dst * plan.capacity
    src_place = slot // group
    dst_place = (slot // plan.capacity) % plan.n_dst
    wanted = (spread(dst_place, plan.dst_bits) ^ me) * plan.capacity + slot % plan.capacity
    codes = jnp.zeros((8, slots), jnp.float32)
    for src in range(plan.n_src):
        both = table_refs[src][...].astype(jnp.float32)
        table = jnp.concatenate([both[0:8], both[8:16]], axis=1).astype(jnp.bfloat16)
        pick = hot(iota((slots, slots), 0) == jnp.where(src_place == src, wanted, -1))
        codes = codes + nn(table, pick.astype(jnp.bfloat16))
    codes = codes.astype(jnp.int32)
    return codes[0:1] - 1, src_place * plan.atoms + codes[1:2], dst_place * plan.atoms + codes[2:3]


def fill_rotation(rot_ref, wigner_ref, angle):
    angles = wigner_ref.shape[1]
    angle_hot = hot(iota((angles, angle.shape[1]), 0) == angle).astype(jnp.bfloat16)
    rot_ref[...] = nn(wigner_ref[...], angle_hot)


def fill_spread(spread_ref, rot_ref, atom_hot, degree, row):
    atoms = atom_hot.shape[0]
    for order in range(2 * degree + 1):
        line = (degree * degree + order) * TABLE_ROWS + row
        spread_ref[order * atoms : (order + 1) * atoms, :] = (
            rot_ref[line : line + 1, :] * atom_hot
        ).astype(jnp.bfloat16)


def fill_nodes(node_ref, block_refs, atoms):
    coeffs = node_ref.shape[0]
    for place, block in enumerate(block_refs):
        node_ref[:, place * atoms : (place + 1) * atoms, :] = block[...].reshape(
            coeffs, atoms, node_ref.shape[2]
        )


def rotate_all(out_ref, node_ref, spread_ref, rot_ref, atom_hot):
    atoms, channels = node_ref.shape[1], node_ref.shape[2]
    for degree in range(LMAX + 1):
        depth = (2 * degree + 1) * atoms
        nodes = node_ref[degree * degree : (degree + 1) * (degree + 1)].reshape(depth, channels).T
        for row in rows_of_degree(degree):
            fill_spread(spread_ref, rot_ref, atom_hot, degree, row)
            out_ref[row * channels : (row + 1) * channels, :] = nn(
                nodes, spread_ref[0:depth, :]
            ).astype(jnp.bfloat16)


def message_kernel(plan, *refs):
    n_src, n_dst = plan.n_src, plan.n_dst
    me_ref, wigner_ref, w_zero, w_one, w_two = refs[:5]
    table_refs = refs[5 : 5 + n_src]
    block_refs = refs[5 + n_src : 5 + 2 * n_src]
    rotated_ref = refs[5 + 2 * n_src]
    part_refs = refs[6 + 2 * n_src : 6 + 2 * n_src + n_dst]
    rot_ref, node_ref, spread_ref, flat_ref, message_ref, sum_ref = refs[6 + 2 * n_src + n_dst :]
    channels = node_ref.shape[2]
    slots = plan.slots
    angle, src, dst = slot_codes(plan, me_ref[0], table_refs)
    fill_rotation(rot_ref, wigner_ref, angle)
    fill_nodes(node_ref, block_refs, plan.atoms)
    src_hot = hot(iota((n_src * plan.atoms, slots), 0) == src)
    rotate_all(rotated_ref, node_ref, spread_ref, rot_ref, src_hot)
    flat_ref[...] = rotated_ref[...].T

    def columns(start, length):
        return slice(start * channels, (start + length) * channels)

    bounds = group_bounds()
    message_ref[:, columns(*bounds[0])] = nn(flat_ref[:, columns(*bounds[0])], w_zero[...]).astype(
        jnp.bfloat16
    )
    for azimuth, weight in ((1, w_one), (2, w_two)):
        plus, minus = columns(*bounds[2 * azimuth - 1]), columns(*bounds[2 * azimuth])
        message_ref[:, plus] = (
            nn(flat_ref[:, plus], weight[0]) - nn(flat_ref[:, minus], weight[1])
        ).astype(jnp.bfloat16)
        message_ref[:, minus] = (
            nn(flat_ref[:, plus], weight[1]) + nn(flat_ref[:, minus], weight[0])
        ).astype(jnp.bfloat16)
    dst_hot = hot(iota((n_dst * plan.atoms, slots), 0) == dst)
    for degree in range(LMAX + 1):
        depth = (2 * degree + 1) * n_dst * plan.atoms
        for number, row in enumerate(rows_of_degree(degree)):
            fill_spread(spread_ref, rot_ref, dst_hot, degree, row)
            term = nn(spread_ref[0:depth, :], message_ref[:, columns(row, 1)])
            if number == 0:
                sum_ref[0:depth, :] = term
            else:
                sum_ref[0:depth, :] += term
        total = sum_ref[0:depth, :].reshape(2 * degree + 1, n_dst * plan.atoms, channels)
        for place in range(n_dst):
            piece = total[:, place * plan.atoms : (place + 1) * plan.atoms, :]
            part_refs[place][
                degree * degree * plan.atoms : (degree + 1) * (degree + 1) * plan.atoms, :
            ] = piece.reshape((2 * degree + 1) * plan.atoms, channels).astype(part_refs[place].dtype)


def gram_kernel(plan, half_rows, sizes, *refs):
    n_src, n_dst = plan.n_src, plan.n_dst
    me_ref, wigner_ref, rotated_ref = refs[:3]
    table_refs = refs[3 : 3 + n_src]
    block_refs = refs[3 + n_src : 3 + n_src + n_dst]
    out_refs = refs[3 + n_src + n_dst :][: 2 * len(sizes)]
    rot_ref, node_ref, spread_ref, pulled_ref, grad_ref = refs[3 + n_src + n_dst + 2 * len(sizes) :]
    channels = node_ref.shape[2]
    me, core = me_ref[0], me_ref[1]
    angle, _, dst = slot_codes(plan, me, table_refs)
    fill_rotation(rot_ref, wigner_ref, angle)
    fill_nodes(node_ref, block_refs, plan.atoms)
    dst_hot = hot(iota((n_dst * plan.atoms, plan.slots), 0) == dst)
    rotate_all(pulled_ref, node_ref, spread_ref, rot_ref, dst_hot)

    def lines(ref, start, length):
        return ref[start * channels : (start + length) * channels, :]

    bounds = group_bounds()
    base = 0
    for azimuth in range(MMAX + 1):
        plus, length = bounds[max(2 * azimuth - 1, 0)]
        minus = bounds[2 * azimuth][0]
        for kind in range(1 if azimuth == 0 else 2):
            for into in range(length):
                p, q = lines(rotated_ref, plus + into, 1), lines(rotated_ref, minus + into, 1)
                for first in range(0, length, 2):
                    width = min(2, length - first)
                    g = lines(pulled_ref, plus + first, width)
                    h = lines(pulled_ref, minus + first, width)
                    if azimuth == 0:
                        block = nt(p, g)
                    elif kind == 0:
                        block = nt(p, g) + nt(q, h)
                    else:
                        block = nt(p, h) - nt(q, g)
                    for step in range(width):
                        grad_ref[
                            pl.ds(base + into * channels * length + first + step, channels, stride=length), :
                        ] = block[:, step * channels : (step + 1) * channels]
            base = base + length * length * channels
    rows = grad_ref.shape[0] // plan.parts
    shift = rows - half_rows

    def emit(part, carry):
        start = part * rows
        if rows % 8 == 0 and shift % 8 == 0:
            own_start = pl.multiple_of(start + core * shift, 8)
            other_start = pl.multiple_of(start + (1 - core) * shift, 8)
        else:
            own_start, other_start = start + core * shift, start + (1 - core) * shift
        place = part ^ me
        skip = 0
        for stream, size in enumerate(sizes):
            out_refs[2 * stream][place] = grad_ref[pl.ds(own_start + skip, size), :]
            out_refs[2 * stream + 1][place] = grad_ref[pl.ds(other_start + skip, size), :].astype(
                jnp.bfloat16
            )
            skip = skip + size
        return carry

    lax.fori_loop(0, plan.parts, emit, 0)


def add_kernel(splits, count, *refs):
    kept, came = refs[:count], refs[count : 2 * count]
    outs = refs[2 * count :]
    for number, lo in enumerate(splits):
        for block in range(kept[number].shape[0]):
            total = kept[number][block] + came[number][block].astype(jnp.float32)
            if lo is None:
                outs[number][...] = total
                continue
            target = outs[2 * number + ((block // lo) % 2)]
            target[(block // (2 * lo)) * lo + block % lo] = total.astype(target.dtype)


def whole_call(kernel, outs, args, scratch=(), smem=0, **cost):
    specs = [pl.BlockSpec(memory_space=pltpu.SMEM)] * smem + [
        pl.BlockSpec(memory_space=pltpu.VMEM)
    ] * (len(args) - smem)
    return pl.pallas_call(
        kernel,
        out_shape=outs,
        in_specs=specs,
        out_specs=[pl.BlockSpec(memory_space=pltpu.VMEM)] * len(outs),
        scratch_shapes=list(scratch),
        compiler_params=pltpu.CompilerParams(vmem_limit_bytes=VMEM_BYTES),
        cost_estimate=pl.CostEstimate(transcendentals=0, **cost),
    )(*args)


def swap(value, flip):
    count = lax.axis_size("graph")
    return lax.ppermute(value, "graph", [(i, i ^ flip) for i in range(count)])


def swap_cores(value):
    return lax.ppermute(value, "dp", [(i, 1 - i) for i in range(2)])


def gather_near(value, bits):
    found = [value]
    for bit in bits:
        found = found + [swap(item, 1 << bit) for item in found]
    return found


def shards(features, cotangent, wigner, src_atom, dst_part, dst_atom, angle, w_zero, w_one, w_two):
    f32, bf16 = jnp.float32, jnp.bfloat16
    parts = lax.axis_size("graph")
    atoms, coeffs, channels = features.shape
    edges = src_atom.shape[0]
    plan = Plan(parts, edges, atoms)
    kept = wigner.shape[1]
    slots = plan.slots
    here = jnp.stack([lax.axis_index("graph"), lax.axis_index("dp")]).astype(jnp.int32)

    def node_rows(value):
        return value.transpose(1, 0, 2).reshape(coeffs * atoms, channels)

    table = whole_call(
        functools.partial(table_kernel, parts, plan.capacity),
        [jax.ShapeDtypeStruct((16, slots // 2), bf16)],
        [x.reshape(1, edges) for x in (dst_part, src_atom, dst_atom, angle)],
        flops=10**7,
        bytes_accessed=10**4,
    )[0]
    tables = [table] + [
        swap(table, sum(1 << bit for place, bit in enumerate(plan.src_bits) if index >> place & 1))
        for index in range(1, plan.n_src)
    ]
    node_blocks = gather_near(node_rows(features), plan.src_bits[::-1])
    pull_blocks = gather_near(node_rows(cotangent), plan.dst_bits[::-1])

    def in_order(blocks, count):
        places = count.bit_length() - 1
        return [blocks[int(format(i, "b").zfill(places)[::-1], 2) if places else 0] for i in range(count)]

    node_blocks = in_order(node_blocks, plan.n_src)
    pull_blocks = in_order(pull_blocks, plan.n_dst)
    rotation = jnp.pad(
        wigner.transpose(2, 1, 0), ((0, 0), (0, TABLE_ROWS - kept), (0, 0))
    ).reshape(coeffs * TABLE_ROWS, wigner.shape[0])

    deepest = (2 * LMAX + 1) * atoms
    outs = [jax.ShapeDtypeStruct((kept * channels, slots), bf16)] + [
        jax.ShapeDtypeStruct((coeffs * atoms, channels), f32 if place == 0 else bf16)
        for place in range(plan.n_dst)
    ]
    rotated, *partial_sums = whole_call(
        functools.partial(message_kernel, plan),
        outs,
        [here, rotation, w_zero, w_one, w_two, *tables, *node_blocks],
        [
            pltpu.VMEM((coeffs * TABLE_ROWS, slots), f32),
            pltpu.VMEM((coeffs, plan.n_src * atoms, channels), bf16),
            pltpu.VMEM((deepest * max(plan.n_src, plan.n_dst), slots), bf16),
            pltpu.VMEM((slots, kept * channels), bf16),
            pltpu.VMEM((slots, kept * channels), bf16),
            pltpu.VMEM((deepest * plan.n_dst, channels), f32),
        ],
        smem=1,
        flops=5 * 10**9,
        bytes_accessed=10**7,
    )
    arrived = [
        swap(
            partial_sums[index],
            sum(1 << bit for place, bit in enumerate(plan.dst_bits) if index >> place & 1),
        )
        for index in range(1, plan.n_dst)
    ]
    total = partial_sums[0]
    for item in arrived:
        total = total + item.astype(f32)
    aggregated = total.astype(bf16).reshape(coeffs, atoms, channels).transpose(1, 0, 2)

    bounds = group_bounds()
    params = (bounds[0][1] ** 2 + 2 * sum(b[1] ** 2 for b in bounds[1::2])) * channels**2
    share = params // parts // channels
    half_rows = -(-(-(-share // 2)) // 16) * 16
    tiles = half_rows // 16
    sizes = [16 * ((tiles + STREAMS - 1 - k) // STREAMS) for k in range(STREAMS)]
    result = whole_call(
        functools.partial(gram_kernel, plan, half_rows, sizes),
        [
            jax.ShapeDtypeStruct((parts, size, channels), kind)
            for size in sizes
            for kind in (f32, bf16)
        ],
        [here, rotation, rotated, *tables, *pull_blocks],
        [
            pltpu.VMEM((coeffs * TABLE_ROWS, slots), f32),
            pltpu.VMEM((coeffs, plan.n_dst * atoms, channels), bf16),
            pltpu.VMEM((deepest * plan.n_dst, slots), bf16),
            pltpu.VMEM((kept * channels, slots), bf16),
            pltpu.VMEM((params // channels, channels), f32),
        ],
        smem=1,
        flops=5 * 10**9,
        bytes_accessed=10**7,
    )
    n_bits = parts.bit_length() - 1
    orders = []
    for k in range(STREAMS):
        front = list(range(n_bits - 1))
        orders.append(front[k:] + front[:k] + [n_bits - 1])
    left = [list(range(n_bits)) for _ in range(STREAMS)]
    keeps, came = result[0::2], [swap_cores(item) for item in result[1::2]]
    for stage in range(n_bits + 1):
        last = stage == n_bits
        splits, outs = [], []
        for k in range(STREAMS):
            if last:
                splits.append(None)
                outs.append(jax.ShapeDtypeStruct((sizes[k], channels), f32))
            else:
                bit = orders[k][stage]
                place = left[k].index(bit)
                splits.append(1 << place)
                left[k].remove(bit)
                blocks = 1 << len(left[k])
                outs.append(jax.ShapeDtypeStruct((blocks, sizes[k], channels), f32))
                outs.append(jax.ShapeDtypeStruct((blocks, sizes[k], channels), bf16))
        result = whole_call(
            functools.partial(add_kernel, splits, STREAMS),
            outs,
            [*keeps, *came],
            flops=10**6,
            bytes_accessed=10**6,
        )
        if last:
            mine = jnp.concatenate(result)
        else:
            keeps = result[0::2]
            came = [swap(result[2 * k + 1], 1 << orders[k][stage]) for k in range(STREAMS)]
    theirs = swap_cores(mine)
    skip = 2 * half_rows - share
    weight_grad = jnp.where(
        lax.axis_index("dp") == 0,
        jnp.concatenate([mine, theirs[skip:]]),
        jnp.concatenate([theirs, mine[skip:]]),
    )
    return (aggregated, weight_grad.reshape(-1))


def solution(mesh):
    placed = (
        P(("dp", "graph"), None, None),
        P(("dp", "graph"), None, None),
        P(),
        P(("dp", "graph")),
        P(("dp", "graph"), None),
        P(("dp", "graph")),
        P(("dp", "graph")),
        P(),
        P(),
        P(),
    )
    return jax.shard_map(
        shards,
        mesh=mesh,
        in_specs=placed,
        out_specs=(P(("dp", "graph"), None, None), P("graph")),
        check_vma=False,
    )
```

time: 561 us -> 133 us (0.24)
  waiting for transfers between devices: 342 us -> 47.8 us
  local copies, waits for them, and re-layouts: 109 us -> 10.7 us
  matrix products: 44.9 us -> 0 us
  Pallas kernels: 0 us -> 41.6 us
  other arithmetic: 21.7 us -> 2.29 us
  between operations: 15.4 us -> 0.85 us
    unnamed x3 -> x0, waiting for transfers between devices: 261 us -> none
    all_to_all x3 -> x0, waiting for transfers between devices: 81.2 us -> none  [the longest x1 65.6 us: shards(): lax.all_to_all(buffer_rows.reshape(group_count, capacity, kept_count * ch...]
    ppermute x0 -> x28, waiting for transfers between devices: none -> 47.8 us  [the longest x24 43 us: swap(): return lax.ppermute(value, 'graph', [(i, i ^ flip) for i in range(count)])]
    dot_general x23 -> x0, matrix products: 44.9 us -> none  [the longest x9 7.65 us: gram_matrix(): lax.dot_general(left_rows, right_rows, (((0,), (0,)), ((), ())), preferre...]
    pallas_call x0 -> x8, Pallas kernels: none -> 41.6 us  [whole_call(): pl.pallas_call(kernel, out_shape=outs, in_specs=specs, out_specs=[pl.Bloc...]
    gather x5 -> x0, local copies, waits for them, and re-layouts: 31.1 us -> none  [the longest x1 14.8 us: shards(): slot_upstream = cotangent[slot_atom] * live_factor[:, None, None]]
    ppermute x0 -> x28, starting transfers between devices: none -> 29.1 us  [the longest x24 28.4 us: swap(): return lax.ppermute(value, 'graph', [(i, i ^ flip) for i in range(count)])]
    reshape x8 -> x0, local copies, waits for them, and re-layouts: 27.5 us -> none  [the longest x2 10.3 us: so2_grads(): flat_parts.append(jnp.stack([real_g, imag_g]).reshape(-1))]
  transfers between devices with their start and end apart: 5 -> 28, of which waited for: 4 -> 14; matrix products, arithmetic and copies ran while one was open for 16% -> 5% of each run, Pallas kernels for 0% -> 11%
where the time goes in v1:
time: 133 us; the launch traced here: 132 us
  waiting for transfers between devices  47.8 us (36%)
  Pallas kernels  41.6 us (31%)
  starting transfers between devices  29.1 us (22%)
  local copies, waits for them, and re-layouts  10.7 us (8%)
  other arithmetic  2.29 us (2%)
    ppermute x24, waiting for transfers between devices, swap(): return lax.ppermute(value, 'graph', [(i, i ^ flip) for i in range(count)])  43 us
    pallas_call x8, Pallas kernels, whole_call(): pl.pallas_call(kernel, out_shape=outs, in_specs=specs, out_specs=[pl.Bloc...  41.6 us
    ppermute x24, starting transfers between devices, swap(): return lax.ppermute(value, 'graph', [(i, i ^ flip) for i in range(count)])  28.4 us
    unnamed x64, local copies, waits for them, and re-layouts  7.67 us
    ppermute x4, waiting for transfers between devices, swap_cores(): return lax.ppermute(value, 'dp', [(i, 1 - i) for i in range(2)])  4.82 us
  transfers between devices with their start and end apart: 28, of which 14 were waited for; matrix products, arithmetic and copies ran while one was open for 5% of the time, Pallas kernels for 11%

profile of v1, /device:TPU:0, one launch (start us, length us, event | category | flops | bytes accessed | tf_op | source)
XLA Modules:
  0.0 132.4 jit_solution(7847043200791637985)
XLA Ops:
  0.6 3.1 %collective-permute-start.4 = (bf16[784,128]{1,0:T(8,128)(2,1)}, bf16[784,128]{1,0:T(8,128)(2,1)S(1)}, u32[]{:S(2)}, u32[]{:S(2)}) collective-permute-start(bf16[784,128]{1,0:T(8,128)(2,1)} %bitcast.23), channel_id=1, source_target_pairs={{0,4},{1,5},{2,6},{3,7},{4,0},{5,1},{6,2},{7,3},{8,12},{9,13},{10,... | collective-permute-start | bytes 602120 | tf_op jit(solution)/shard_map/ppermute | solution.py:290
  3.7 2.6 %collective-permute-start.10 = (bf16[784,128]{1,0:T(8,128)(2,1)}, bf16[784,128]{1,0:T(8,128)(2,1)S(1)}, u32[]{:S(2)}, u32[]{:S(2)}) collective-permute-start(bf16[784,128]{1,0:T(8,128)(2,1)} %bitcast.26), channel_id=1, source_target_pairs={{0,8},{1,9},{2,10},{3,11},{4,12},{5,13},{6,14},{7,15},{8,0},{9,1},... | collective-permute-start | bytes 602120 | tf_op jit(solution)/shard_map/ppermute | solution.py:290
  6.3 1.5 %collective-permute-start.3 = (bf16[784,128]{1,0:T(8,128)(2,1)}, bf16[784,128]{1,0:T(8,128)(2,1)S(1)}, u32[]{:S(2)}, u32[]{:S(2)}) collective-permute-start(bf16[784,128]{1,0:T(8,128)(2,1)} %bitcast.24), channel_id=1, source_target_pairs={{0,1},{1,0},{2,3},{3,2},{4,5},{5,4},{6,7},{7,6},{8,9},{9,8},{10,11... | collective-permute-start | bytes 602120 | tf_op jit(solution)/shard_map/ppermute | solution.py:290
  7.8 5.3 %collective-permute-done.4.refs_11_ = bf16[784,128]{1,0:T(8,128)(2,1)S(1)} collective-permute-done((bf16[784,128]{1,0:T(8,128)(2,1)}, bf16[784,128]{1,0:T(8,128)(2,1)S(1)}, u32[]{:S(2)}, u32[]{:S(2)}) %collective-permute-start.4) | collective-permute-done | bytes 200736 | tf_op jit(solution)/shard_map/ppermute | solution.py:290
  13.1 1.7 %collective-permute-start.5 = (bf16[784,128]{1,0:T(8,128)(2,1)S(1)}, bf16[784,128]{1,0:T(8,128)(2,1)S(1)}, u32[]{:S(2)}, u32[]{:S(2)}) collective-permute-start(bf16[784,128]{1,0:T(8,128)(2,1)S(1)} %collective-permute-done.4.refs_11_), channel_id=1, source_target_pairs={{0,1},{1,0},{2,3},{3,2},{4,5},{5,4},{6,7},{7,6},{8,9},{9,8},{10,11... | collective-permute-start | bytes 602120 | tf_op jit(solution)/shard_map/ppermute | solution.py:290
  14.8 1.6 %shard_map.113.refs_5_.refs_3_ = bf16[16,128]{1,0:T(8,128)(2,1)} custom-call(s32[1,128]{1,0:T(1,128)} %bitcast.29, s32[1,128]{1,0:T(1,128)} %bitcast.30, s32[1,128]{1,0:T(1,128)} %bitcast.31, s32[1,128]{1,0:T(1,128)} %bitcast.32), custom_call_target="tpu_custom_call" | custom-call | flops 10000000 | bytes 10000 | tf_op jit(solution)/shard_map/pallas_call | solution.py:277
  16.4 1.8 %collective-permute-start.1 = (bf16[16,128]{1,0:T(8,128)(2,1)}, bf16[16,128]{1,0:T(8,128)(2,1)S(1)}, u32[]{:S(2)}, u32[]{:S(2)}) collective-permute-start(bf16[16,128]{1,0:T(8,128)(2,1)} %shard_map.113.refs_5_.refs_3_), channel_id=1, source_target_pairs={{0,4},{1,5},{2,6},{3,7},{4,0},{5,1},{6,2},{7,3},{8,12},{9,13},{10,... | collective-permute-start | bytes 12296 | tf_op jit(solution)/shard_map/ppermute | solution.py:290
  18.2 2.9 %collective-permute-done.2.refs_8_.refs_6_ = bf16[16,128]{1,0:T(8,128)(2,1)S(1)} collective-permute-done((bf16[16,128]{1,0:T(8,128)(2,1)}, bf16[16,128]{1,0:T(8,128)(2,1)S(1)}, u32[]{:S(2)}, u32[]{:S(2)}) %collective-permute-start.2) | collective-permute-done | bytes 4128 | tf_op jit(solution)/shard_map/ppermute | solution.py:290
  22.0 2.1 %pad.4 = bf16[49,32,256]{2,1,0:T(8,128)(2,1)} pad(bf16[49,29,256]{2,1,0:T(8,128)(2,1)} %bitcast.19, bf16[]{:T(256)} %constant.11.clone.1), padding=0_0x0_3x0_0 | pad | bytes 1530370 | tf_op jit(solution)/shard_map/jit(_pad)/pad | solution.py:337
  24.1 1.7 %collective-permute-start.9 = (bf16[784,128]{1,0:T(8,128)(2,1)}, bf16[784,128]{1,0:T(8,128)(2,1)S(1)}, u32[]{:S(2)}, u32[]{:S(2)}) collective-permute-start(bf16[784,128]{1,0:T(8,128)(2,1)} %bitcast.27), channel_id=1, source_target_pairs={{0,2},{1,3},{2,0},{3,1},{4,6},{5,7},{6,4},{7,5},{8,10},{9,11},{10,... | collective-permute-start | bytes 602120 | tf_op jit(solution)/shard_map/ppermute | solution.py:290
  26.9 10.9 %shard_map.114 = (bf16[3712,256]{1,0:T(8,128)(2,1)}, f32[784,128]{1,0:T(8,128)}, bf16[784,128]{1,0:T(8,128)(2,1)}, bf16[784,128]{1,0:T(8,128)(2,1)}, bf16[784,128]{1,0:T(8,128)(2,1)}) custom-call(s32[2]{0:T(128)} %pad_add_fusion.refs_0_, bf16[1568,256]{1,0:T(8,128)(2,1)} %bitcast.20, bf16[896,896]{1,0:T(8,128)(2,1)} %refs_2_.1, ...), custom_call_target="tpu_custom_call" | custom-call | flops 5000000000 | bytes 10000000 | tf_op jit(solution)/shard_map/pallas_call | solution.py:277
  38.6 13.5 %shard_map.115 = (f32[16,240,128]{2,1,0:T(8,128)}, bf16[16,240,128]{2,1,0:T(8,128)(2,1)}, f32[16,224,128]{2,1,0:T(8,128)}, bf16[16,224,128]{2,1,0:T(8,128)(2,1)}...) custom-call(s32[2]{0:T(128)} %pad_add_fusion.refs_0_, bf16[1568,256]{1,0:T(8,128)(2,1)} %bitcast.21, ...), custom_call_target="tpu_custom_call" | custom-call | flops 5000000000 | bytes 10000000 | tf_op jit(solution)/shard_map/pallas_call | solution.py:277
  52.7 3.5 %collective-permute-done.13.refs_4_ = bf16[16,224,128]{2,1,0:T(8,128)(2,1)S(1)} collective-permute-done((bf16[16,224,128]{2,1,0:T(8,128)(2,1)}, bf16[16,224,128]{2,1,0:T(8,128)(2,1)S(1)}, u32[]{:S(2)}, u32[]{:S(2)}) %collective-permute-start.13) | collective-permute-done | bytes 917536 | tf_op jit(solution)/shard_map/ppermute | solution.py:294
  56.2 1.3 collective-permute-done.14.refs_5_
  58.9 5.5 %shard_map.116 = (f32[8,240,128]{2,1,0:T(8,128)}, bf16[8,240,128]{2,1,0:T(8,128)(2,1)}, f32[8,224,128]{2,1,0:T(8,128)}, bf16[8,224,128]{2,1,0:T(8,128)(2,1)}, f3...) custom-call(f32[16,240,128]{2,1,0:T(8,128)} %get-tuple-element.45.refs_0_, f32[16,224,128]{2,1,0:T(8,128)} %get-tuple-element.46.refs_1_, ...), custom_call_target="tpu_custom_call" | custom-call | flops 1000000 | bytes 1000000 | tf_op jit(solution)/shard_map/pallas_call | solution.py:277
  64.4 1.7 %collective-permute-start.15 = (bf16[8,240,128]{2,1,0:T(8,128)(2,1)}, bf16[8,240,128]{2,1,0:T(8,128)(2,1)S(1)}, u32[]{:S(2)}, u32[]{:S(2)}) collective-permute-start(bf16[8,240,128]{2,1,0:T(8,128)(2,1)} %get-tuple-element.54), channel_id=1, source_target_pairs={{0,1},{1,0},{2,3},{3,2},{4,5},{5,4},{6,7},{7,6},{8,9},{9,8},{10,11... | collective-permute-start | bytes 1474568 | tf_op jit(solution)/shard_map/ppermute | solution.py:290
  66.0 1.5 %collective-permute-start.16 = (bf16[8,224,128]{2,1,0:T(8,128)(2,1)}, bf16[8,224,128]{2,1,0:T(8,128)(2,1)S(1)}, u32[]{:S(2)}, u32[]{:S(2)}) collective-permute-start(bf16[8,224,128]{2,1,0:T(8,128)(2,1)} %get-tuple-element.55), channel_id=1, source_target_pairs={{0,2},{1,3},{2,0},{3,1},{4,6},{5,7},{6,4},{7,5},{8,10},{9,11},{10,... | collective-permute-start | bytes 1376264 | tf_op jit(solution)/shard_map/ppermute | solution.py:290
  67.5 11.0 %collective-permute-done.16.refs_4_ = bf16[8,224,128]{2,1,0:T(8,128)(2,1)S(1)} collective-permute-done((bf16[8,224,128]{2,1,0:T(8,128)(2,1)}, bf16[8,224,128]{2,1,0:T(8,128)(2,1)S(1)}, u32[]{:S(2)}, u32[]{:S(2)}) %collective-permute-start.16) | collective-permute-done | bytes 458784 | tf_op jit(solution)/shard_map/ppermute | solution.py:290
  80.6 3.6 %shard_map.117 = (f32[4,240,128]{2,1,0:T(8,128)}, bf16[4,240,128]{2,1,0:T(8,128)(2,1)}, f32[4,224,128]{2,1,0:T(8,128)}, bf16[4,224,128]{2,1,0:T(8,128)(2,1)}, f3...) custom-call(f32[8,240,128]{2,1,0:T(8,128)} %get-tuple-element.51.refs_0_, f32[8,224,128]{2,1,0:T(8,128)} %get-tuple-element.52.refs_1_, ...), custom_call_target="tpu_custom_call" | custom-call | flops 1000000 | bytes 1000000 | tf_op jit(solution)/shard_map/pallas_call | solution.py:277
  85.5 5.7 %collective-permute-done.19.refs_4_ = bf16[4,224,128]{2,1,0:T(8,128)(2,1)S(1)} collective-permute-done((bf16[4,224,128]{2,1,0:T(8,128)(2,1)}, bf16[4,224,128]{2,1,0:T(8,128)(2,1)S(1)}, u32[]{:S(2)}, u32[]{:S(2)}) %collective-permute-start.19) | collective-permute-done | bytes 229408 | tf_op jit(solution)/shard_map/ppermute | solution.py:290
  92.1 2.6 %shard_map.118 = (f32[2,240,128]{2,1,0:T(8,128)}, bf16[2,240,128]{2,1,0:T(8,128)(2,1)}, f32[2,224,128]{2,1,0:T(8,128)}, bf16[2,224,128]{2,1,0:T(8,128)(2,1)}, f3...) custom-call(f32[4,240,128]{2,1,0:T(8,128)} %get-tuple-element.57.refs_0_, f32[4,224,128]{2,1,0:T(8,128)} %get-tuple-element.58.refs_1_, ...), custom_call_target="tpu_custom_call" | custom-call | flops 1000000 | bytes 1000000 | tf_op jit(solution)/shard_map/pallas_call | solution.py:277
  94.7 1.7 %collective-permute-start.21 = (bf16[2,240,128]{2,1,0:T(8,128)(2,1)}, bf16[2,240,128]{2,1,0:T(8,128)(2,1)S(1)}, u32[]{:S(2)}, u32[]{:S(2)}) collective-permute-start(bf16[2,240,128]{2,1,0:T(8,128)(2,1)} %get-tuple-element.66), channel_id=1, source_target_pairs={{0,4},{1,5},{2,6},{3,7},{4,0},{5,1},{6,2},{7,3},{8,12},{9,13},{10,... | collective-permute-start | bytes 368648 | tf_op jit(solution)/shard_map/ppermute | solution.py:290
  97.2 1.2 collective-permute-start.23
  98.4 3.0 %collective-permute-done.22.refs_4_ = bf16[2,224,128]{2,1,0:T(8,128)(2,1)S(1)} collective-permute-done((bf16[2,224,128]{2,1,0:T(8,128)(2,1)}, bf16[2,224,128]{2,1,0:T(8,128)(2,1)S(1)}, u32[]{:S(2)}, u32[]{:S(2)}) %collective-permute-start.22) | collective-permute-done | bytes 114720 | tf_op jit(solution)/shard_map/ppermute | solution.py:290
  102.9 2.1 %shard_map.119 = (f32[1,240,128]{2,1,0:T(8,128)}, bf16[1,240,128]{2,1,0:T(8,128)(2,1)}, f32[1,224,128]{2,1,0:T(8,128)}, bf16[1,224,128]{2,1,0:T(8,128)(2,1)}, f3...) custom-call(f32[2,240,128]{2,1,0:T(8,128)} %get-tuple-element.63.refs_0_, f32[2,224,128]{2,1,0:T(8,128)} %get-tuple-element.64.refs_1_, ...), custom_call_target="tpu_custom_call" | custom-call | flops 1000000 | bytes 1000000 | tf_op jit(solution)/shard_map/pallas_call | solution.py:277
  105.0 1.4 %collective-permute-start.24 = (bf16[1,240,128]{2,1,0:T(8,128)(2,1)}, bf16[1,240,128]{2,1,0:T(8,128)(2,1)S(1)}, u32[]{:S(2)}, u32[]{:S(2)}) collective-permute-start(bf16[1,240,128]{2,1,0:T(8,128)(2,1)} %get-tuple-element.72), channel_id=1, source_target_pairs={{0,8},{1,9},{2,10},{3,11},{4,12},{5,13},{6,14},{7,15},{8,0},{9,1},... | collective-permute-start | bytes 184328 | tf_op jit(solution)/shard_map/ppermute | solution.py:290
  106.4 1.6 %collective-permute-start.25 = (bf16[1,224,128]{2,1,0:T(8,128)(2,1)}, bf16[1,224,128]{2,1,0:T(8,128)(2,1)S(1)}, u32[]{:S(2)}, u32[]{:S(2)}) collective-permute-start(bf16[1,224,128]{2,1,0:T(8,128)(2,1)} %get-tuple-element.73), channel_id=1, source_target_pairs={{0,8},{1,9},{2,10},{3,11},{4,12},{5,13},{6,14},{7,15},{8,0},{9,1},... | collective-permute-start | bytes 172040 | tf_op jit(solution)/shard_map/ppermute | solution.py:290
  107.9 1.4 %collective-permute-start.26 = (bf16[1,224,128]{2,1,0:T(8,128)(2,1)}, bf16[1,224,128]{2,1,0:T(8,128)(2,1)S(1)}, u32[]{:S(2)}, u32[]{:S(2)}) collective-permute-start(bf16[1,224,128]{2,1,0:T(8,128)(2,1)} %get-tuple-element.74), channel_id=1, source_target_pairs={{0,8},{1,9},{2,10},{3,11},{4,12},{5,13},{6,14},{7,15},{8,0},{9,1},... | collective-permute-start | bytes 172040 | tf_op jit(solution)/shard_map/ppermute | solution.py:290
  110.4 1.7 %collective-permute-start.7 = (bf16[784,128]{1,0:T(8,128)(2,1)S(1)}, bf16[784,128]{1,0:T(8,128)(2,1)S(1)}, u32[]{:S(2)}, u32[]{:S(2)}) collective-permute-start(bf16[784,128]{1,0:T(8,128)(2,1)S(1)} %copy-done.20), channel_id=1, source_target_pairs={{0,8},{1,9},{2,10},{3,11},{4,12},{5,13},{6,14},{7,15},{8,0},{9,1},... | collective-permute-start | bytes 602120 | tf_op jit(solution)/shard_map/ppermute | solution.py:290
  112.1 8.4 %collective-permute-done.25.refs_4_ = bf16[1,224,128]{2,1,0:T(8,128)(2,1)S(1)} collective-permute-done((bf16[1,224,128]{2,1,0:T(8,128)(2,1)}, bf16[1,224,128]{2,1,0:T(8,128)(2,1)S(1)}, u32[]{:S(2)}, u32[]{:S(2)}) %collective-permute-start.25) | collective-permute-done | bytes 57376 | tf_op jit(solution)/shard_map/ppermute | solution.py:290
  122.4 1.8 %shard_map.120 = (f32[240,128]{1,0:T(8,128)}, f32[224,128]{1,0:T(8,128)}, f32[224,128]{1,0:T(8,128)}) custom-call(f32[1,240,128]{2,1,0:T(8,128)} %get-tuple-element.69.refs_0_, f32[1,224,128]{2,1,0:T(8,128)} %get-tuple-element.70.refs_1_, f32[1,224,128]{2,1,0:T(8,128)} %get-tuple-element.71.refs_2_, bf16[1,240,128]{2,1,0:T(8,128)(2,1)} %copy-done.16, ...), custom_call_target="tpu_custom_call" | custom-call | flops 1000000 | bytes 1000000 | tf_op jit(solution)/shard_map/pallas_call | solution.py:277
  128.0 2.5 %collective-permute-done.8 = bf16[784,128]{1,0:T(8,128)(2,1)S(1)} collective-permute-done((bf16[784,128]{1,0:T(8,128)(2,1)S(1)}, bf16[784,128]{1,0:T(8,128)(2,1)S(1)}, u32[]{:S(2)}, u32[]{:S(2)}) %collective-permute-start.8) | collective-permute-done | bytes 200736 | tf_op jit(solution)/shard_map/ppermute | solution.py:290
  (103 shorter events, 19.9 us)
Async XLA Ops:
  0.6 12.5 %collective-permute-start.4 = (bf16[784,128]{1,0:T(8,128)(2,1)}, bf16[784,128]{1,0:T(8,128)(2,1)S(1)}, u32[]{:S(2)}, u32[]{:S(2)}) collective-permute-start(bf16[784,128]{1,0:T(8,128)(2,1)} %bitcast.23), channel_id=1, source_target_pairs={{0,4},{1,5},{2,6},{3,7},{4,0},{5,1},{6,2},{7,3},{8,12},{9,13},{10,... | collective-permute-start | bytes 602120 | tf_op jit(solution)/shard_map/ppermute | solution.py:290
  3.7 22.1 %collective-permute-start.10 = (bf16[784,128]{1,0:T(8,128)(2,1)}, bf16[784,128]{1,0:T(8,128)(2,1)S(1)}, u32[]{:S(2)}, u32[]{:S(2)}) collective-permute-start(bf16[784,128]{1,0:T(8,128)(2,1)} %bitcast.26), channel_id=1, source_target_pairs={{0,8},{1,9},{2,10},{3,11},{4,12},{5,13},{6,14},{7,15},{8,0},{9,1},... | collective-permute-start | bytes 602120 | tf_op jit(solution)/shard_map/ppermute | solution.py:290
  6.3 19.8 %collective-permute-start.3 = (bf16[784,128]{1,0:T(8,128)(2,1)}, bf16[784,128]{1,0:T(8,128)(2,1)S(1)}, u32[]{:S(2)}, u32[]{:S(2)}) collective-permute-start(bf16[784,128]{1,0:T(8,128)(2,1)} %bitcast.24), channel_id=1, source_target_pairs={{0,1},{1,0},{2,3},{3,2},{4,5},{5,4},{6,7},{7,6},{8,9},{9,8},{10,11... | collective-permute-start | bytes 602120 | tf_op jit(solution)/shard_map/ppermute | solution.py:290
  13.1 13.1 %collective-permute-start.5 = (bf16[784,128]{1,0:T(8,128)(2,1)S(1)}, bf16[784,128]{1,0:T(8,128)(2,1)S(1)}, u32[]{:S(2)}, u32[]{:S(2)}) collective-permute-start(bf16[784,128]{1,0:T(8,128)(2,1)S(1)} %collective-permute-done.4.refs_11_), channel_id=1, source_target_pairs={{0,1},{1,0},{2,3},{3,2},{4,5},{5,4},{6,7},{7,6},{8,9},{9,8},{10,11... | collective-permute-start | bytes 602120 | tf_op jit(solution)/shard_map/ppermute | solution.py:290
  16.4 4.7 %collective-permute-start.2 = (bf16[16,128]{1,0:T(8,128)(2,1)}, bf16[16,128]{1,0:T(8,128)(2,1)S(1)}, u32[]{:S(2)}, u32[]{:S(2)}) collective-permute-start(bf16[16,128]{1,0:T(8,128)(2,1)} %shard_map.113.refs_5_.refs_3_), channel_id=1, source_target_pairs={{0,5},{1,4},{2,7},{3,6},{4,1},{5,0},{6,3},{7,2},{8,13},{9,12},{10,... | collective-permute-start | bytes 12296 | tf_op jit(solution)/shard_map/ppermute | solution.py:290
  16.4 7.7 %collective-permute-start.1 = (bf16[16,128]{1,0:T(8,128)(2,1)}, bf16[16,128]{1,0:T(8,128)(2,1)S(1)}, u32[]{:S(2)}, u32[]{:S(2)}) collective-permute-start(bf16[16,128]{1,0:T(8,128)(2,1)} %shard_map.113.refs_5_.refs_3_), channel_id=1, source_target_pairs={{0,4},{1,5},{2,6},{3,7},{4,0},{5,1},{6,2},{7,3},{8,12},{9,13},{10,... | collective-permute-start | bytes 12296 | tf_op jit(solution)/shard_map/ppermute | solution.py:290
  21.1 5.1 %collective-permute-start = (bf16[16,128]{1,0:T(8,128)(2,1)}, bf16[16,128]{1,0:T(8,128)(2,1)S(1)}, u32[]{:S(2)}, u32[]{:S(2)}) collective-permute-start(bf16[16,128]{1,0:T(8,128)(2,1)} %shard_map.113.refs_5_.refs_3_), channel_id=1, source_target_pairs={{0,1},{1,0},{2,3},{3,2},{4,5},{5,4},{6,7},{7,6},{8,9},{9,8},{10,11... | collective-permute-start | bytes 12296 | tf_op jit(solution)/shard_map/ppermute | solution.py:290
  24.1 13.8 %collective-permute-start.9 = (bf16[784,128]{1,0:T(8,128)(2,1)}, bf16[784,128]{1,0:T(8,128)(2,1)S(1)}, u32[]{:S(2)}, u32[]{:S(2)}) collective-permute-start(bf16[784,128]{1,0:T(8,128)(2,1)} %bitcast.27), channel_id=1, source_target_pairs={{0,2},{1,3},{2,0},{3,1},{4,6},{5,7},{6,4},{7,5},{8,10},{9,11},{10,... | collective-permute-start | bytes 602120 | tf_op jit(solution)/shard_map/ppermute | solution.py:290
  25.8 12.1 %collective-permute-start.11 = (bf16[784,128]{1,0:T(8,128)(2,1)S(1)}, bf16[784,128]{1,0:T(8,128)(2,1)S(1)}, u32[]{:S(2)}, u32[]{:S(2)}) collective-permute-start(bf16[784,128]{1,0:T(8,128)(2,1)S(1)} %collective-permute-done.10.refs_9_), channel_id=1, source_target_pairs={{0,2},{1,3},{2,0},{3,1},{4,6},{5,7},{6,4},{7,5},{8,10},{9,11},{10,... | collective-permute-start | bytes 602120 | tf_op jit(solution)/shard_map/ppermute | solution.py:290
  52.1 5.4 %collective-permute-start.12 = (bf16[16,240,128]{2,1,0:T(8,128)(2,1)}, bf16[16,240,128]{2,1,0:T(8,128)(2,1)S(1)}, u32[]{:S(2)}, u32[]{:S(2)}) collective-permute-start(bf16[16,240,128]{2,1,0:T(8,128)(2,1)} %get-tuple-element.48), channel_id=1, source_target_pairs={{0,16},{16,0},{1,17},{17,1},{2,18},{18,2},{3,19},{19,3},{4,20},{20... | collective-permute-start | bytes 2949128 | tf_op jit(solution)/shard_map/ppermute | solution.py:294
  52.2 4.1 %collective-permute-start.13 = (bf16[16,224,128]{2,1,0:T(8,128)(2,1)}, bf16[16,224,128]{2,1,0:T(8,128)(2,1)S(1)}, u32[]{:S(2)}, u32[]{:S(2)}) collective-permute-start(bf16[16,224,128]{2,1,0:T(8,128)(2,1)} %get-tuple-element.49), channel_id=1, source_target_pairs={{0,16},{16,0},{1,17},{17,1},{2,18},{18,2},{3,19},{19,3},{4,20},{20... | collective-permute-start | bytes 2752520 | tf_op jit(solution)/shard_map/ppermute | solution.py:294
  52.7 4.9 %collective-permute-start.14 = (bf16[16,224,128]{2,1,0:T(8,128)(2,1)}, bf16[16,224,128]{2,1,0:T(8,128)(2,1)S(1)}, u32[]{:S(2)}, u32[]{:S(2)}) collective-permute-start(bf16[16,224,128]{2,1,0:T(8,128)(2,1)} %get-tuple-element.50), channel_id=1, source_target_pairs={{0,16},{16,0},{1,17},{17,1},{2,18},{18,2},{3,19},{19,3},{4,20},{20... | collective-permute-start | bytes 2752520 | tf_op jit(solution)/shard_map/ppermute | solution.py:294
  64.4 15.4 %collective-permute-start.15 = (bf16[8,240,128]{2,1,0:T(8,128)(2,1)}, bf16[8,240,128]{2,1,0:T(8,128)(2,1)S(1)}, u32[]{:S(2)}, u32[]{:S(2)}) collective-permute-start(bf16[8,240,128]{2,1,0:T(8,128)(2,1)} %get-tuple-element.54), channel_id=1, source_target_pairs={{0,1},{1,0},{2,3},{3,2},{4,5},{5,4},{6,7},{7,6},{8,9},{9,8},{10,11... | collective-permute-start | bytes 1474568 | tf_op jit(solution)/shard_map/ppermute | solution.py:290
  66.0 12.5 %collective-permute-start.16 = (bf16[8,224,128]{2,1,0:T(8,128)(2,1)}, bf16[8,224,128]{2,1,0:T(8,128)(2,1)S(1)}, u32[]{:S(2)}, u32[]{:S(2)}) collective-permute-start(bf16[8,224,128]{2,1,0:T(8,128)(2,1)} %get-tuple-element.55), channel_id=1, source_target_pairs={{0,2},{1,3},{2,0},{3,1},{4,6},{5,7},{6,4},{7,5},{8,10},{9,11},{10,... | collective-permute-start | bytes 1376264 | tf_op jit(solution)/shard_map/ppermute | solution.py:290
  67.5 12.2 %collective-permute-start.17 = (bf16[8,224,128]{2,1,0:T(8,128)(2,1)}, bf16[8,224,128]{2,1,0:T(8,128)(2,1)S(1)}, u32[]{:S(2)}, u32[]{:S(2)}) collective-permute-start(bf16[8,224,128]{2,1,0:T(8,128)(2,1)} %get-tuple-element.56), channel_id=1, source_target_pairs={{0,4},{1,5},{2,6},{3,7},{4,0},{5,1},{6,2},{7,3},{8,12},{9,13},{10,... | collective-permute-start | bytes 1376264 | tf_op jit(solution)/shard_map/ppermute | solution.py:290
  84.2 25.1 %copy-start.21 = (bf16[784,128]{1,0:T(8,128)(2,1)S(1)}, bf16[784,128]{1,0:T(8,128)(2,1)}, u32[]{:S(2)}) copy-start(bf16[784,128]{1,0:T(8,128)(2,1)} %get-tuple-element.41) | copy-start | bytes 602116
  84.2 26.2 %copy-start.20 = (bf16[784,128]{1,0:T(8,128)(2,1)S(1)}, bf16[784,128]{1,0:T(8,128)(2,1)}, u32[]{:S(2)}) copy-start(bf16[784,128]{1,0:T(8,128)(2,1)} %get-tuple-element.42) | copy-start | bytes 602116
  84.2 36.3 %copy-start.19 = (bf16[784,128]{1,0:T(8,128)(2,1)S(1)}, bf16[784,128]{1,0:T(8,128)(2,1)}, u32[]{:S(2)}) copy-start(bf16[784,128]{1,0:T(8,128)(2,1)} %get-tuple-element.43) | copy-start | bytes 602116
  84.2 7.1 %collective-permute-start.18 = (bf16[4,240,128]{2,1,0:T(8,128)(2,1)}, bf16[4,240,128]{2,1,0:T(8,128)(2,1)S(1)}, u32[]{:S(2)}, u32[]{:S(2)}) collective-permute-start(bf16[4,240,128]{2,1,0:T(8,128)(2,1)} %get-tuple-element.60), channel_id=1, source_target_pairs={{0,2},{1,3},{2,0},{3,1},{4,6},{5,7},{6,4},{7,5},{8,10},{9,11},{10,... | collective-permute-start | bytes 737288 | tf_op jit(solution)/shard_map/ppermute | solution.py:290
  84.8 6.3 %collective-permute-start.19 = (bf16[4,224,128]{2,1,0:T(8,128)(2,1)}, bf16[4,224,128]{2,1,0:T(8,128)(2,1)S(1)}, u32[]{:S(2)}, u32[]{:S(2)}) collective-permute-start(bf16[4,224,128]{2,1,0:T(8,128)(2,1)} %get-tuple-element.61), channel_id=1, source_target_pairs={{0,4},{1,5},{2,6},{3,7},{4,0},{5,1},{6,2},{7,3},{8,12},{9,13},{10,... | collective-permute-start | bytes 688136 | tf_op jit(solution)/shard_map/ppermute | solution.py:290
  85.1 6.2 %collective-permute-start.20 = (bf16[4,224,128]{2,1,0:T(8,128)(2,1)}, bf16[4,224,128]{2,1,0:T(8,128)(2,1)S(1)}, u32[]{:S(2)}, u32[]{:S(2)}) collective-permute-start(bf16[4,224,128]{2,1,0:T(8,128)(2,1)} %get-tuple-element.62), channel_id=1, source_target_pairs={{0,1},{1,0},{2,3},{3,2},{4,5},{5,4},{6,7},{7,6},{8,9},{9,8},{10,11... | collective-permute-start | bytes 688136 | tf_op jit(solution)/shard_map/ppermute | solution.py:290
  92.1 38.4 %copy-start.9 = (f32[784,128]{1,0:T(8,128)S(1)}, f32[784,128]{1,0:T(8,128)}, u32[]{:S(2)}) copy-start(f32[784,128]{1,0:T(8,128)} %get-tuple-element.40) | copy-start | bytes 1204228
  94.7 7.5 %collective-permute-start.21 = (bf16[2,240,128]{2,1,0:T(8,128)(2,1)}, bf16[2,240,128]{2,1,0:T(8,128)(2,1)S(1)}, u32[]{:S(2)}, u32[]{:S(2)}) collective-permute-start(bf16[2,240,128]{2,1,0:T(8,128)(2,1)} %get-tuple-element.66), channel_id=1, source_target_pairs={{0,4},{1,5},{2,6},{3,7},{4,0},{5,1},{6,2},{7,3},{8,12},{9,13},{10,... | collective-permute-start | bytes 368648 | tf_op jit(solution)/shard_map/ppermute | solution.py:290
  96.4 5.0 %collective-permute-start.22 = (bf16[2,224,128]{2,1,0:T(8,128)(2,1)}, bf16[2,224,128]{2,1,0:T(8,128)(2,1)S(1)}, u32[]{:S(2)}, u32[]{:S(2)}) collective-permute-start(bf16[2,224,128]{2,1,0:T(8,128)(2,1)} %get-tuple-element.67), channel_id=1, source_target_pairs={{0,1},{1,0},{2,3},{3,2},{4,5},{5,4},{6,7},{7,6},{8,9},{9,8},{10,11... | collective-permute-start | bytes 344072 | tf_op jit(solution)/shard_map/ppermute | solution.py:290
  97.2 5.0 %collective-permute-start.23 = (bf16[2,224,128]{2,1,0:T(8,128)(2,1)}, bf16[2,224,128]{2,1,0:T(8,128)(2,1)S(1)}, u32[]{:S(2)}, u32[]{:S(2)}) collective-permute-start(bf16[2,224,128]{2,1,0:T(8,128)(2,1)} %get-tuple-element.68), channel_id=1, source_target_pairs={{0,2},{1,3},{2,0},{3,1},{4,6},{5,7},{6,4},{7,5},{8,10},{9,11},{10,... | collective-permute-start | bytes 344072 | tf_op jit(solution)/shard_map/ppermute | solution.py:290
  105.0 16.7 %collective-permute-start.24 = (bf16[1,240,128]{2,1,0:T(8,128)(2,1)}, bf16[1,240,128]{2,1,0:T(8,128)(2,1)S(1)}, u32[]{:S(2)}, u32[]{:S(2)}) collective-permute-start(bf16[1,240,128]{2,1,0:T(8,128)(2,1)} %get-tuple-element.72), channel_id=1, source_target_pairs={{0,8},{1,9},{2,10},{3,11},{4,12},{5,13},{6,14},{7,15},{8,0},{9,1},... | collective-permute-start | bytes 184328 | tf_op jit(solution)/shard_map/ppermute | solution.py:290
  106.4 14.1 %collective-permute-start.25 = (bf16[1,224,128]{2,1,0:T(8,128)(2,1)}, bf16[1,224,128]{2,1,0:T(8,128)(2,1)S(1)}, u32[]{:S(2)}, u32[]{:S(2)}) collective-permute-start(bf16[1,224,128]{2,1,0:T(8,128)(2,1)} %get-tuple-element.73), channel_id=1, source_target_pairs={{0,8},{1,9},{2,10},{3,11},{4,12},{5,13},{6,14},{7,15},{8,0},{9,1},... | collective-permute-start | bytes 172040 | tf_op jit(solution)/shard_map/ppermute | solution.py:290
  107.9 13.8 %collective-permute-start.26 = (bf16[1,224,128]{2,1,0:T(8,128)(2,1)}, bf16[1,224,128]{2,1,0:T(8,128)(2,1)S(1)}, u32[]{:S(2)}, u32[]{:S(2)}) collective-permute-start(bf16[1,224,128]{2,1,0:T(8,128)(2,1)} %get-tuple-element.74), channel_id=1, source_target_pairs={{0,8},{1,9},{2,10},{3,11},{4,12},{5,13},{6,14},{7,15},{8,0},{9,1},... | collective-permute-start | bytes 172040 | tf_op jit(solution)/shard_map/ppermute | solution.py:290
  109.3 17.8 %collective-permute-start.6 = (bf16[784,128]{1,0:T(8,128)(2,1)S(1)}, bf16[784,128]{1,0:T(8,128)(2,1)S(1)}, u32[]{:S(2)}, u32[]{:S(2)}) collective-permute-start(bf16[784,128]{1,0:T(8,128)(2,1)S(1)} %copy-done.21), channel_id=1, source_target_pairs={{0,2},{1,3},{2,0},{3,1},{4,6},{5,7},{6,4},{7,5},{8,10},{9,11},{10,... | collective-permute-start | bytes 602120 | tf_op jit(solution)/shard_map/ppermute | solution.py:290
  110.4 17.5 %collective-permute-start.7 = (bf16[784,128]{1,0:T(8,128)(2,1)S(1)}, bf16[784,128]{1,0:T(8,128)(2,1)S(1)}, u32[]{:S(2)}, u32[]{:S(2)}) collective-permute-start(bf16[784,128]{1,0:T(8,128)(2,1)S(1)} %copy-done.20), channel_id=1, source_target_pairs={{0,8},{1,9},{2,10},{3,11},{4,12},{5,13},{6,14},{7,15},{8,0},{9,1},... | collective-permute-start | bytes 602120 | tf_op jit(solution)/shard_map/ppermute | solution.py:290
  120.5 10.0 %collective-permute-start.8 = (bf16[784,128]{1,0:T(8,128)(2,1)S(1)}, bf16[784,128]{1,0:T(8,128)(2,1)S(1)}, u32[]{:S(2)}, u32[]{:S(2)}) collective-permute-start(bf16[784,128]{1,0:T(8,128)(2,1)S(1)} %copy-done.19), channel_id=1, source_target_pairs={{0,10},{1,11},{2,8},{3,9},{4,14},{5,15},{6,12},{7,13},{8,2},{9,3},... | collective-permute-start | bytes 602120 | tf_op jit(solution)/shard_map/ppermute | solution.py:290
  127.0 4.4 %collective-permute-start.27 = (f32[688,128]{1,0:T(8,128)S(1)}, f32[688,128]{1,0:T(8,128)S(1)}, u32[]{:S(2)}, u32[]{:S(2)}) collective-permute-start(f32[688,128]{1,0:T(8,128)S(1)} %constant_dynamic-update-slice_fusion), channel_id=1, source_target_pairs={{0,16},{16,0},{1,17},{17,1},{2,18},{18,2},{3,19},{19,3},{4,20},{20... | collective-permute-start | bytes 1056776 | tf_op jit(solution)/shard_map/ppermute | solution.py:294
  (27 other events, 70.7 us)

commit v2 on v1

v2 whole, which is shorter than its diff:
```python
import functools

import jax
import jax.numpy as jnp
import numpy as np
from jax import lax
from jax.experimental import pallas as pl
from jax.experimental.pallas import tpu as pltpu
from jax.sharding import PartitionSpec as P

LMAX = 6
MMAX = 2
TABLE_ROWS = 32
MIB = 1024 * 1024
STREAMS = 3


def group_bounds():
    bounds = [(0, LMAX + 1)]
    offset = LMAX + 1
    for azimuth in range(1, MMAX + 1):
        length = LMAX + 1 - azimuth
        bounds.append((offset, length))
        bounds.append((offset + length, length))
        offset = offset + 2 * length
    return bounds


def rows_of_degree(degree):
    rows = [degree]
    for azimuth in range(1, min(degree, MMAX) + 1):
        for start, _ in group_bounds()[2 * azimuth - 1 : 2 * azimuth + 1]:
            rows.append(start + degree - azimuth)
    return rows


def spread(value, bits):
    total = value * 0
    for place, bit in enumerate(bits):
        total = total + (((value >> place) & 1) << bit)
    return total


def nn(left, right):
    return lax.dot_general(left, right, (((1,), (0,)), ((), ())), preferred_element_type=jnp.float32)


def nt(left, right):
    return lax.dot_general(left, right, (((1,), (1,)), ((), ())), preferred_element_type=jnp.float32)


def iota(shape, dim):
    return lax.broadcasted_iota(jnp.int32, shape, dim)


def hot(condition):
    return jnp.where(condition, 1.0, 0.0)


def payload_kernel(parts, capacity, edge_ref, node_ref, out_ref):
    edges = edge_ref.shape[1]
    part, src, dst, angle = (edge_ref[i : i + 1, :] for i in range(4))
    padded = -(-parts // 16) * 16
    part_hot = hot(iota((padded, edges), 0) == part)
    before = hot(iota((edges, edges), 0) < iota((edges, edges), 1))
    earlier = nn(part_hot.astype(jnp.bfloat16), before.astype(jnp.bfloat16))
    rank = jnp.sum(earlier * part_hot, axis=0, keepdims=True).astype(jnp.int32)
    slot = part * capacity + rank
    place = hot(iota((parts * capacity, edges), 0) == slot)
    row = iota((8, edges), 0)
    fields = jnp.where(row == 0, angle + 1, jnp.where(row == 1, src, jnp.where(row == 2, dst, 0)))
    table = nt(fields.astype(jnp.float32).astype(jnp.bfloat16), place.astype(jnp.bfloat16))
    half = out_ref.shape[1]
    rows = node_ref.shape[0]
    out_ref[0:rows, :] = node_ref[...]
    out_ref[rows : rows + 16, :] = jnp.concatenate([table[:, :half], table[:, half:]], axis=0).astype(
        jnp.bfloat16
    )


class Plan:
    def __init__(self, parts, edges, atoms):
        bits = parts.bit_length() - 1
        self.parts = parts
        self.capacity = 2 * edges // parts
        self.slots = parts * self.capacity
        self.atoms = atoms
        self.src_bits = tuple(range(1, bits, 2))
        self.dst_bits = tuple(range(0, bits, 2))
        self.n_src = 1 << len(self.src_bits)
        self.n_dst = 1 << len(self.dst_bits)


def slot_codes(plan, me, block_refs):
    slots = plan.slots
    slot = iota((1, slots), 1)
    group = plan.n_dst * plan.capacity
    src_place = slot // group
    dst_place = (slot // plan.capacity) % plan.n_dst
    wanted = (spread(dst_place, plan.dst_bits) ^ me) * plan.capacity + slot % plan.capacity
    codes = jnp.zeros((8, slots), jnp.float32)
    for src in range(plan.n_src):
        rows = block_refs[src].shape[0]
        both = block_refs[src][rows - 16 : rows, :].astype(jnp.float32)
        table = jnp.concatenate([both[0:8], both[8:16]], axis=1).astype(jnp.bfloat16)
        pick = hot(iota((slots, slots), 0) == jnp.where(src_place == src, wanted, -1))
        codes = codes + nn(table, pick.astype(jnp.bfloat16))
    codes = codes.astype(jnp.int32)
    return codes[0:1] - 1, src_place * plan.atoms + codes[1:2], dst_place * plan.atoms + codes[2:3]


def fill_rotation(rot_ref, wide_ref, wigner_ref, angle):
    coeffs, kept, angles = wigner_ref.shape
    angle_hot = hot(iota((angles, angle.shape[1]), 0) == angle).astype(jnp.bfloat16)
    wide_ref[...] = jnp.zeros(wide_ref.shape, wide_ref.dtype)
    wide_ref[:, 0:kept, :] = wigner_ref[...]
    rot_ref[...] = nn(wide_ref[...].reshape(coeffs * TABLE_ROWS, angles), angle_hot)


def fill_spread(spread_ref, rot_ref, atom_hot, degree, row):
    atoms, slots = atom_hot.shape
    layers = atom_hot.reshape(atoms // 16, 16, slots)
    for order in range(2 * degree + 1):
        line = (degree * degree + order) * TABLE_ROWS + row
        entry = jnp.broadcast_to(rot_ref[line : line + 1, :], (16, slots)).astype(jnp.bfloat16)
        spread_ref[order * atoms : (order + 1) * atoms, :] = (layers * entry[None]).reshape(
            atoms, slots
        )


def atom_hots(count, atom):
    return hot(iota((count, atom.shape[1]), 0) == atom).astype(jnp.bfloat16)


def fill_nodes(node_ref, block_refs, atoms):
    coeffs = node_ref.shape[0]
    for place, block in enumerate(block_refs):
        node_ref[:, place * atoms : (place + 1) * atoms, :] = block[0 : coeffs * atoms, :].reshape(
            coeffs, atoms, node_ref.shape[2]
        )


def rotate_all(out_ref, node_ref, spread_ref, rot_ref, atom_hot):
    atoms, channels = node_ref.shape[1], node_ref.shape[2]
    for degree in range(LMAX + 1):
        depth = (2 * degree + 1) * atoms
        nodes = node_ref[degree * degree : (degree + 1) * (degree + 1)].reshape(depth, channels).T
        for row in rows_of_degree(degree):
            fill_spread(spread_ref, rot_ref, atom_hot, degree, row)
            out_ref[row * channels : (row + 1) * channels, :] = nn(
                nodes, spread_ref[0:depth, :]
            ).astype(jnp.bfloat16)


def message_kernel(plan, *refs):
    n_dst = plan.n_dst
    rot_ref, atom_ref, rotated_ref, w_zero, w_one, w_two = refs[:6]
    part_refs = refs[6 : 6 + n_dst]
    spread_ref, flat_ref, message_ref, sum_ref = refs[6 + n_dst :]
    channels = sum_ref.shape[1]
    flat_ref[...] = rotated_ref[...].T

    def columns(start, length):
        return slice(start * channels, (start + length) * channels)

    bounds = group_bounds()
    message_ref[:, columns(*bounds[0])] = nn(flat_ref[:, columns(*bounds[0])], w_zero[...]).astype(
        jnp.bfloat16
    )
    for azimuth, weight in ((1, w_one), (2, w_two)):
        plus, minus = columns(*bounds[2 * azimuth - 1]), columns(*bounds[2 * azimuth])
        message_ref[:, plus] = (
            nn(flat_ref[:, plus], weight[0]) - nn(flat_ref[:, minus], weight[1])
        ).astype(jnp.bfloat16)
        message_ref[:, minus] = (
            nn(flat_ref[:, plus], weight[1]) + nn(flat_ref[:, minus], weight[0])
        ).astype(jnp.bfloat16)
    dst_hot = atom_hots(n_dst * plan.atoms, atom_ref[0:1, :])
    for degree in range(LMAX + 1):
        depth = (2 * degree + 1) * n_dst * plan.atoms
        for number, row in enumerate(rows_of_degree(degree)):
            fill_spread(spread_ref, rot_ref, dst_hot, degree, row)
            term = nn(spread_ref[0:depth, :], message_ref[:, columns(row, 1)])
            if number == 0:
                sum_ref[0:depth, :] = term
            else:
                sum_ref[0:depth, :] += term
        total = sum_ref[0:depth, :].reshape(2 * degree + 1, n_dst * plan.atoms, channels)
        for place in range(n_dst):
            piece = total[:, place * plan.atoms : (place + 1) * plan.atoms, :]
            part_refs[place][
                degree * degree * plan.atoms : (degree + 1) * (degree + 1) * plan.atoms, :
            ] = piece.reshape((2 * degree + 1) * plan.atoms, channels).astype(part_refs[place].dtype)


def gram_kernel(plan, half_rows, sizes, *refs):
    n_src, n_dst = plan.n_src, plan.n_dst
    me_ref, wigner_ref, refs = refs[0], refs[1], refs[2:]
    node_blocks, refs = refs[:n_src], refs[n_src:]
    pull_blocks, refs = refs[:n_dst], refs[n_dst:]
    rot_ref, atom_ref, rotated_ref, refs = refs[0], refs[1], refs[2], refs[3:]
    out_refs, refs = refs[: 2 * len(sizes)], refs[2 * len(sizes) :]
    wide_ref, node_ref, pull_ref, spread_ref, pulled_ref, grad_ref = refs
    channels = node_ref.shape[2]
    me, core = me_ref[0], me_ref[1]
    angle, src, dst = slot_codes(plan, me, node_blocks)
    atom_ref[...] = jnp.broadcast_to(dst, atom_ref.shape)
    fill_rotation(rot_ref, wide_ref, wigner_ref, angle)
    fill_nodes(node_ref, node_blocks, plan.atoms)
    fill_nodes(pull_ref, pull_blocks, plan.atoms)
    rotate_all(rotated_ref, node_ref, spread_ref, rot_ref, atom_hots(n_src * plan.atoms, src))
    rotate_all(pulled_ref, pull_ref, spread_ref, rot_ref, atom_hots(n_dst * plan.atoms, dst))

    def lines(ref, start, length):
        return ref[start * channels : (start + length) * channels, :]

    bounds = group_bounds()
    base = 0
    for azimuth in range(MMAX + 1):
        plus, length = bounds[max(2 * azimuth - 1, 0)]
        minus = bounds[2 * azimuth][0]
        for kind in range(1 if azimuth == 0 else 2):
            for into in range(length):
                p, q = lines(rotated_ref, plus + into, 1), lines(rotated_ref, minus + into, 1)
                for first in range(0, length, 2):
                    width = min(2, length - first)
                    g = lines(pulled_ref, plus + first, width)
                    h = lines(pulled_ref, minus + first, width)
                    if azimuth == 0:
                        block = nt(p, g)
                    elif kind == 0:
                        block = nt(p, g) + nt(q, h)
                    else:
                        block = nt(p, h) - nt(q, g)
                    for step in range(width):
                        grad_ref[
                            pl.ds(base + into * channels * length + first + step, channels, stride=length), :
                        ] = block[:, step * channels : (step + 1) * channels]
            base = base + length * length * channels
    rows = grad_ref.shape[0] // plan.parts
    shift = rows - half_rows

    def emit(part, carry):
        start = part * rows
        if rows % 8 == 0 and shift % 8 == 0:
            own_start = pl.multiple_of(start + core * shift, 8)
            other_start = pl.multiple_of(start + (1 - core) * shift, 8)
        else:
            own_start, other_start = start + core * shift, start + (1 - core) * shift
        place = part ^ me
        skip = 0
        for stream, size in enumerate(sizes):
            out_refs[2 * stream][place] = grad_ref[pl.ds(own_start + skip, size), :]
            out_refs[2 * stream + 1][place] = grad_ref[pl.ds(other_start + skip, size), :].astype(
                jnp.bfloat16
            )
            skip = skip + size
        return carry

    lax.fori_loop(0, plan.parts, emit, 0)


def add_kernel(lo, kept_ref, came_ref, *outs):
    outs = outs[-2:] if lo is not None else outs[-1:]
    for block in range(kept_ref.shape[0]):
        total = kept_ref[block] + came_ref[block].astype(jnp.float32)
        if lo is None:
            outs[0][...] = total
            continue
        target = outs[(block // lo) % 2]
        target[(block // (2 * lo)) * lo + block % lo] = total.astype(target.dtype)


def join_kernel(shift, sizes, me_ref, *refs):
    count = len(sizes)
    mine, theirs, out_ref = refs[:count], refs[count : 2 * count], refs[2 * count]
    for core in (1, 0):
        start = core * shift
        for stream, size in enumerate(sizes):
            out_ref[start : start + size, :] = jnp.where(
                me_ref[1] == core, mine[stream][...], theirs[stream][...]
            )
            start = start + size


def padded_bytes(shape, dtype):
    rows = -(-shape[-2] // 16) * 16 if len(shape) > 1 else 16
    lanes = -(-shape[-1] // 128) * 128
    return int(np.prod(shape[:-2], initial=1)) * rows * lanes * jnp.dtype(dtype).itemsize


def whole_call(kernel, outs, args, scratch=(), smem=0, flops=10**6):
    specs = [pl.BlockSpec(memory_space=pltpu.SMEM)] * smem + [
        pl.BlockSpec(memory_space=pltpu.VMEM)
    ] * (len(args) - smem)
    held = sum(padded_bytes(x.shape, x.dtype) for x in [*args[smem:], *outs])
    held = held + sum(padded_bytes(*item) for item in scratch)
    return pl.pallas_call(
        kernel,
        out_shape=outs,
        in_specs=specs,
        out_specs=[pl.BlockSpec(memory_space=pltpu.VMEM)] * len(outs),
        scratch_shapes=[pltpu.VMEM(*item) for item in scratch],
        compiler_params=pltpu.CompilerParams(vmem_limit_bytes=held * 9 // 8 + 4 * MIB),
        cost_estimate=pl.CostEstimate(flops=flops, bytes_accessed=10**5, transcendentals=0),
    )(*args)


def swap(value, flip):
    count = lax.axis_size("graph")
    return lax.ppermute(value, "graph", [(i, i ^ flip) for i in range(count)])


def swap_cores(value):
    return lax.ppermute(value, "dp", [(i, 1 - i) for i in range(2)])


def flips(bits):
    return [spread(index, bits) for index in range(1 << len(bits))]


def shards(features, cotangent, wigner, src_atom, dst_part, dst_atom, angle, w_zero, w_one, w_two):
    f32, bf16 = jnp.float32, jnp.bfloat16
    parts = lax.axis_size("graph")
    atoms, coeffs, channels = features.shape
    edges = src_atom.shape[0]
    plan = Plan(parts, edges, atoms)
    kept = wigner.shape[1]
    slots = plan.slots
    here = jnp.stack([lax.axis_index("graph"), lax.axis_index("dp")]).astype(jnp.int32)

    def node_rows(value):
        return value.transpose(1, 0, 2).reshape(coeffs * atoms, channels)

    payload = whole_call(
        functools.partial(payload_kernel, parts, plan.capacity),
        [jax.ShapeDtypeStruct((coeffs * atoms + 16, channels), bf16)],
        [jnp.stack([dst_part[:, 0], src_atom, dst_atom, angle]), node_rows(features)],
    )[0]
    rotation = wigner.transpose(2, 1, 0)

    blocks = [{0: payload}, {0: node_rows(cotangent)}]
    for held, bits in zip(blocks, (plan.src_bits, plan.dst_bits)):
        for bit in bits[::-1]:
            held.update({flip | 1 << bit: swap(item, 1 << bit) for flip, item in list(held.items())})
    node_blocks = [blocks[0][flip] for flip in flips(plan.src_bits)]
    pull_blocks = [blocks[1][flip] for flip in flips(plan.dst_bits)]

    bounds = group_bounds()
    params = (bounds[0][1] ** 2 + 2 * sum(b[1] ** 2 for b in bounds[1::2])) * channels**2
    share = params // parts // channels
    half_rows = -(-(-(-share // 2)) // 16) * 16
    tiles = half_rows // 16
    sizes = [16 * ((tiles + STREAMS - 1 - k) // STREAMS) for k in range(STREAMS)]
    deepest = (2 * LMAX + 1) * atoms
    most = max(plan.n_src, plan.n_dst)
    rot, dst_slot, rotated, *result = whole_call(
        functools.partial(gram_kernel, plan, half_rows, sizes),
        [
            jax.ShapeDtypeStruct((coeffs * TABLE_ROWS, slots), f32),
            jax.ShapeDtypeStruct((8, slots), jnp.int32),
            jax.ShapeDtypeStruct((kept * channels, slots), bf16),
        ]
        + [
            jax.ShapeDtypeStruct((parts, size, channels), kind)
            for size in sizes
            for kind in (f32, bf16)
        ],
        [here, rotation, *node_blocks, *pull_blocks],
        [
            ((coeffs, TABLE_ROWS, wigner.shape[0]), bf16),
            ((coeffs, plan.n_src * atoms, channels), bf16),
            ((coeffs, plan.n_dst * atoms, channels), bf16),
            ((deepest * most, slots), bf16),
            ((kept * channels, slots), bf16),
            ((params // channels, channels), f32),
        ],
        smem=1,
        flops=8 * 10**9,
    )
    partial_sums = whole_call(
        functools.partial(message_kernel, plan),
        [
            jax.ShapeDtypeStruct((coeffs * atoms, channels), f32 if place == 0 else bf16)
            for place in range(plan.n_dst)
        ],
        [rot, dst_slot, rotated, w_zero, w_one, w_two],
        [
            ((deepest * plan.n_dst, slots), bf16),
            ((slots, kept * channels), bf16),
            ((slots, kept * channels), bf16),
            ((deepest * plan.n_dst, channels), f32),
        ],
        flops=8 * 10**9,
    )
    total = partial_sums[0]
    for place, flip in enumerate(flips(plan.dst_bits)):
        if place > 0:
            total = total + swap(partial_sums[place], flip).astype(f32)
    aggregated = total.astype(bf16).reshape(coeffs, atoms, channels).transpose(1, 0, 2)

    n_bits = parts.bit_length() - 1
    mine = []
    for stream, size in enumerate(sizes):
        front = list(range(n_bits - 1))
        turn = stream % max(1, len(front))
        left = list(range(n_bits))
        kept_part, came = result[2 * stream], swap_cores(result[2 * stream + 1])
        for stage, bit in enumerate(front[turn:] + front[:turn] + [n_bits - 1]):
            place = left.index(bit)
            left.remove(bit)
            shape = (1 << len(left), size, channels)
            kept_part, sent = whole_call(
                functools.partial(add_kernel, 1 << place),
                [jax.ShapeDtypeStruct(shape, f32), jax.ShapeDtypeStruct(shape, bf16)],
                [kept_part, came] + ([partial_sums[1]] if stage == 1 and stream == 0 else []),
            )
            came = swap(sent, 1 << bit)
        mine += whole_call(
            functools.partial(add_kernel, None),
            [jax.ShapeDtypeStruct((size, channels), f32)],
            [kept_part, came],
        )
    theirs = [swap_cores(item) for item in mine]
    weight_grad = whole_call(
        functools.partial(join_kernel, share - half_rows, sizes),
        [jax.ShapeDtypeStruct((share, channels), f32)],
        [here, *mine, *theirs],
        smem=1,
    )[0]
    return (aggregated, weight_grad.reshape(-1))


def solution(mesh):
    placed = (
        P(("dp", "graph"), None, None),
        P(("dp", "graph"), None, None),
        P(),
        P(("dp", "graph")),
        P(("dp", "graph"), None),
        P(("dp", "graph")),
        P(("dp", "graph")),
        P(),
        P(),
        P(),
    )
    return jax.shard_map(
        shards,
        mesh=mesh,
        in_specs=placed,
        out_specs=(P(("dp", "graph"), None, None), P("graph")),
        check_vma=False,
    )
```

time: 133 us -> 92.9 us (0.70)
  Pallas kernels: 41.6 us -> 18.1 us
  waiting for transfers between devices: 47.8 us -> 33.8 us
  local copies, waits for them, and re-layouts: 10.7 us -> 3.01 us
  starting transfers between devices: 29.1 us -> 34.3 us
    pallas_call x8 -> x19, Pallas kernels: 41.6 us -> 18.1 us  [whole_call(): pl.pallas_call(kernel, out_shape=outs, in_specs=specs, out_specs=[pl.Bloc...]
    ppermute x24 -> x21, waiting for transfers between devices: 43 us -> 29.7 us  [swap(): return lax.ppermute(value, 'graph', [(i, i ^ flip) for i in range(count)])]
    unnamed x64 -> x12, local copies, waits for them, and re-layouts: 7.67 us -> 3.01 us
    ppermute x24 -> x21, starting transfers between devices: 28.4 us -> 33 us  [swap(): return lax.ppermute(value, 'graph', [(i, i ^ flip) for i in range(count)])]
    pad x1 -> x0, local copies, waits for them, and re-layouts: 2.1 us -> none  [shards(): jnp.pad(wigner.transpose(2, 1, 0), ((0, 0), (0, TABLE_ROWS - kept), (0, 0)))]
    ppermute x4 -> x6, waiting for transfers between devices: 4.82 us -> 4.12 us  [swap_cores(): return lax.ppermute(value, 'dp', [(i, 1 - i) for i in range(2)])]
  transfers between devices with their start and end apart: 28 -> 27, of which waited for: 14 -> 11; matrix products, arithmetic and copies ran while one was open for 5% -> 1% of each run, Pallas kernels for 11% -> 7%
where the time goes in v2:
time: 92.9 us; the launch traced here: 91.7 us
  starting transfers between devices  34.3 us (37%)
  waiting for transfers between devices  33.8 us (36%)
  Pallas kernels  18.1 us (19%)
  local copies, waits for them, and re-layouts  3.01 us (3%)
  other arithmetic  1.57 us (2%)
    ppermute x21, starting transfers between devices, swap(): return lax.ppermute(value, 'graph', [(i, i ^ flip) for i in range(count)])  33 us
    ppermute x21, waiting for transfers between devices, swap(): return lax.ppermute(value, 'graph', [(i, i ^ flip) for i in range(count)])  29.7 us
    pallas_call x19, Pallas kernels, whole_call(): pl.pallas_call(kernel, out_shape=outs, in_specs=specs, out_specs=[pl.Bloc...  18.1 us
    ppermute x6, waiting for transfers between devices, swap_cores(): return lax.ppermute(value, 'dp', [(i, 1 - i) for i in range(2)])  4.12 us
    unnamed x12, local copies, waits for them, and re-layouts  3.01 us
  transfers between devices with their start and end apart: 27, of which 11 were waited for; matrix products, arithmetic and copies ran while one was open for 1% of the time, Pallas kernels for 7%

profile of v2, /device:TPU:0, one launch (start us, length us, event | category | flops | bytes accessed | tf_op | source)
XLA Modules:
  0.0 91.7 jit_solution(8598194259185333754)
XLA Ops:
  1.3 0.9 %copy-done = bf16[16,49,128]{2,0,1:T(8,128)(2,1)S(1)} copy-done((bf16[16,49,128]{2,0,1:T(8,128)(2,1)S(1)}, bf16[16,49,128]{2,0,1:T(8,128)(2,1)}, u32[]{:S(2)}) %copy-start) | copy-done | bytes 200728
  2.6 4.1 %collective-permute-start.1 = (bf16[800,128]{1,0:T(8,128)(2,1)S(1)}, bf16[800,128]{1,0:T(8,128)(2,1)S(1)}, u32[]{:S(2)}, u32[]{:S(2)}) collective-permute-start(bf16[800,128]{1,0:T(8,128)(2,1)S(1)} %shard_map.113.refs_2_), channel_id=1, source_target_pairs={{0,8},{1,9},{2,10},{3,11},{4,12},{5,13},{6,14},{7,15},{8,0},{9,1},... | collective-permute-start | bytes 614408 | tf_op jit(solution)/shard_map/ppermute | solution.py:311
  6.6 1.6 %collective-permute-start.4 = (bf16[784,128]{1,0:T(8,128)(2,1)}, bf16[784,128]{1,0:T(8,128)(2,1)S(1)}, u32[]{:S(2)}, u32[]{:S(2)}) collective-permute-start(bf16[784,128]{1,0:T(8,128)(2,1)} %bitcast.19), channel_id=1, source_target_pairs={{0,4},{1,5},{2,6},{3,7},{4,0},{5,1},{6,2},{7,3},{8,12},{9,13},{10,... | collective-permute-start | bytes 602120 | tf_op jit(solution)/shard_map/ppermute | solution.py:311
  8.2 1.5 %collective-permute-start = (bf16[800,128]{1,0:T(8,128)(2,1)S(1)}, bf16[800,128]{1,0:T(8,128)(2,1)S(1)}, u32[]{:S(2)}, u32[]{:S(2)}) collective-permute-start(bf16[800,128]{1,0:T(8,128)(2,1)S(1)} %shard_map.113.refs_2_), channel_id=1, source_target_pairs={{0,2},{1,3},{2,0},{3,1},{4,6},{5,7},{6,4},{7,5},{8,10},{9,11},{10,... | collective-permute-start | bytes 614408 | tf_op jit(solution)/shard_map/ppermute | solution.py:311
  9.7 6.5 %collective-permute-done.1.refs_4_ = bf16[800,128]{1,0:T(8,128)(2,1)S(1)} collective-permute-done((bf16[800,128]{1,0:T(8,128)(2,1)S(1)}, bf16[800,128]{1,0:T(8,128)(2,1)S(1)}, u32[]{:S(2)}, u32[]{:S(2)}) %collective-permute-start.1) | collective-permute-done | bytes 204832 | tf_op jit(solution)/shard_map/ppermute | solution.py:311
  16.2 1.6 %collective-permute-start.2 = (bf16[800,128]{1,0:T(8,128)(2,1)S(1)}, bf16[800,128]{1,0:T(8,128)(2,1)S(1)}, u32[]{:S(2)}, u32[]{:S(2)}) collective-permute-start(bf16[800,128]{1,0:T(8,128)(2,1)S(1)} %collective-permute-done.1.refs_4_), channel_id=1, source_target_pairs={{0,2},{1,3},{2,0},{3,1},{4,6},{5,7},{6,4},{7,5},{8,10},{9,11},{10,... | collective-permute-start | bytes 614408 | tf_op jit(solution)/shard_map/ppermute | solution.py:311
  17.8 1.5 %collective-permute-start.3 = (bf16[784,128]{1,0:T(8,128)(2,1)}, bf16[784,128]{1,0:T(8,128)(2,1)S(1)}, u32[]{:S(2)}, u32[]{:S(2)}) collective-permute-start(bf16[784,128]{1,0:T(8,128)(2,1)} %bitcast.20), channel_id=1, source_target_pairs={{0,1},{1,0},{2,3},{3,2},{4,5},{5,4},{6,7},{7,6},{8,9},{9,8},{10,11... | collective-permute-start | bytes 602120 | tf_op jit(solution)/shard_map/ppermute | solution.py:311
  19.9 5.8 %collective-permute-done.3.refs_7_ = bf16[784,128]{1,0:T(8,128)(2,1)S(1)} collective-permute-done((bf16[784,128]{1,0:T(8,128)(2,1)}, bf16[784,128]{1,0:T(8,128)(2,1)S(1)}, u32[]{:S(2)}, u32[]{:S(2)}) %collective-permute-start.3) | collective-permute-done | bytes 200736 | tf_op jit(solution)/shard_map/ppermute | solution.py:311
  25.7 2.1 %collective-permute-done.5.refs_9_ = bf16[784,128]{1,0:T(8,128)(2,1)S(1)} collective-permute-done((bf16[784,128]{1,0:T(8,128)(2,1)S(1)}, bf16[784,128]{1,0:T(8,128)(2,1)S(1)}, u32[]{:S(2)}, u32[]{:S(2)}) %collective-permute-start.5) | collective-permute-done | bytes 200736 | tf_op jit(solution)/shard_map/ppermute | solution.py:311
  27.8 1.1 %copy-done.4 = bf16[256,29,49]{0,1,2:T(8,128)(2,1)S(1)} copy-done((bf16[256,29,49]{0,1,2:T(8,128)(2,1)S(1)}, bf16[256,29,49]{0,1,2:T(8,128)(2,1)}, u32[]{:S(2)}) %copy-start.4) | copy-done | bytes 727576
  28.9 0.9 %copy-done.5 = bf16[16,49,128]{2,0,1:T(8,128)(2,1)S(1)} copy-done((bf16[16,49,128]{2,0,1:T(8,128)(2,1)S(1)}, bf16[16,49,128]{2,0,1:T(8,128)(2,1)}, u32[]{:S(2)}) %copy-start.5) | copy-done | bytes 200728
  29.9 10.2 %shard_map.114 = (f32[1568,256]{1,0:T(8,128)S(1)}, s32[8,256]{1,0:T(8,128)S(1)}, bf16[3712,256]{1,0:T(8,128)(2,1)S(1)}, f32[16,240,128]{2,1,0:T(8,128)S(1)}, bf1...) custom-call(s32[2]{0:T(128)S(1)} %pad_add_fusion.1.refs_0_.me_ref, ...), custom_call_target="tpu_custom_call" | custom-call | flops 8000000000 | bytes 100000 | tf_op jit(solution)/shard_map/pallas_call | solution.py:298
  40.7 1.9 %collective-permute-done.14.came_ref = bf16[16,224,128]{2,1,0:T(8,128)(2,1)S(1)} collective-permute-done((bf16[16,224,128]{2,1,0:T(8,128)(2,1)S(1)}, bf16[16,224,128]{2,1,0:T(8,128)(2,1)S(1)}, u32[]{:S(2)}, u32[]{:S(2)}) %collective-permute-start.14) | collective-permute-done | bytes 917536 | tf_op jit(solution)/shard_map/ppermute | solution.py:315
  42.8 0.8 collective-permute-start.15
  43.6 1.7 %collective-permute-done.19.came_ref = bf16[16,224,128]{2,1,0:T(8,128)(2,1)S(1)} collective-permute-done((bf16[16,224,128]{2,1,0:T(8,128)(2,1)S(1)}, bf16[16,224,128]{2,1,0:T(8,128)(2,1)S(1)}, u32[]{:S(2)}, u32[]{:S(2)}) %collective-permute-start.19) | collective-permute-done | bytes 917536 | tf_op jit(solution)/shard_map/ppermute | solution.py:315
  45.5 1.7 %collective-permute-start.20 = (bf16[8,224,128]{2,1,0:T(8,128)(2,1)S(1)}, bf16[8,224,128]{2,1,0:T(8,128)(2,1)S(1)}, u32[]{:S(2)}, u32[]{:S(2)}) collective-permute-start(bf16[8,224,128]{2,1,0:T(8,128)(2,1)S(1)} %get-tuple-element.69), channel_id=1, source_target_pairs={{0,4},{1,5},{2,6},{3,7},{4,0},{5,1},{6,2},{7,3},{8,12},{9,13},{10,... | collective-permute-start | bytes 1376264 | tf_op jit(solution)/shard_map/ppermute | solution.py:311
  47.4 1.6 %collective-permute-start.10 = (bf16[8,240,128]{2,1,0:T(8,128)(2,1)S(1)}, bf16[8,240,128]{2,1,0:T(8,128)(2,1)S(1)}, u32[]{:S(2)}, u32[]{:S(2)}) collective-permute-start(bf16[8,240,128]{2,1,0:T(8,128)(2,1)S(1)} %get-tuple-element.49), channel_id=1, source_target_pairs={{0,1},{1,0},{2,3},{3,2},{4,5},{5,4},{6,7},{7,6},{8,9},{9,8},{10,11... | collective-permute-start | bytes 1474568 | tf_op jit(solution)/shard_map/ppermute | solution.py:311
  48.9 6.5 %collective-permute-done.15.came_ref = bf16[8,224,128]{2,1,0:T(8,128)(2,1)S(1)} collective-permute-done((bf16[8,224,128]{2,1,0:T(8,128)(2,1)S(1)}, bf16[8,224,128]{2,1,0:T(8,128)(2,1)S(1)}, u32[]{:S(2)}, u32[]{:S(2)}) %collective-permute-start.15) | collective-permute-done | bytes 458784 | tf_op jit(solution)/shard_map/ppermute | solution.py:311
  55.5 1.7 %collective-permute-start.16 = (bf16[4,224,128]{2,1,0:T(8,128)(2,1)S(1)}, bf16[4,224,128]{2,1,0:T(8,128)(2,1)S(1)}, u32[]{:S(2)}, u32[]{:S(2)}) collective-permute-start(bf16[4,224,128]{2,1,0:T(8,128)(2,1)S(1)} %get-tuple-element.61), channel_id=1, source_target_pairs={{0,4},{1,5},{2,6},{3,7},{4,0},{5,1},{6,2},{7,3},{8,12},{9,13},{10,... | collective-permute-start | bytes 688136 | tf_op jit(solution)/shard_map/ppermute | solution.py:311
  57.3 5.2 %shard_map.115 = (f32[784,128]{1,0:T(8,128)S(1)}, bf16[784,128]{1,0:T(8,128)(2,1)S(1)}, bf16[784,128]{1,0:T(8,128)(2,1)S(1)}, bf16[784,128]{1,0:T(8,128)(2,1)S(1)}) custom-call(f32[1568,256]{1,0:T(8,128)S(1)} %get-tuple-element.39.refs_0_, s32[8,256]{1,0:T(8,128)S(1)} %get-tuple-element.40.refs_1_, bf16[3712,256]{1,0:T(8,128)(2,1)S(1)} %get-tuple-element.41.refs_2_, ...), custom_call_target="tpu_custom_call" | custom-call | flops 8000000000 | bytes 100000 | tf_op jit(solution)/shard_map/pallas_call | solution.py:298
  63.2 1.6 %collective-permute-start.21 = (bf16[4,224,128]{2,1,0:T(8,128)(2,1)S(1)}, bf16[4,224,128]{2,1,0:T(8,128)(2,1)S(1)}, u32[]{:S(2)}, u32[]{:S(2)}) collective-permute-start(bf16[4,224,128]{2,1,0:T(8,128)(2,1)S(1)} %get-tuple-element.71), channel_id=1, source_target_pairs={{0,1},{1,0},{2,3},{3,2},{4,5},{5,4},{6,7},{7,6},{8,9},{9,8},{10,11... | collective-permute-start | bytes 688136 | tf_op jit(solution)/shard_map/ppermute | solution.py:311
  65.4 4.1 %collective-permute-done.11.came_ref = bf16[4,240,128]{2,1,0:T(8,128)(2,1)S(1)} collective-permute-done((bf16[4,240,128]{2,1,0:T(8,128)(2,1)S(1)}, bf16[4,240,128]{2,1,0:T(8,128)(2,1)S(1)}, u32[]{:S(2)}, u32[]{:S(2)}) %collective-permute-start.11) | collective-permute-done | bytes 245792 | tf_op jit(solution)/shard_map/ppermute | solution.py:311
  70.0 1.7 %collective-permute-start.7 = (bf16[784,128]{1,0:T(8,128)(2,1)S(1)}, bf16[784,128]{1,0:T(8,128)(2,1)S(1)}, u32[]{:S(2)}, u32[]{:S(2)}) collective-permute-start(bf16[784,128]{1,0:T(8,128)(2,1)S(1)} %get-tuple-element.44), channel_id=1, source_target_pairs={{0,4},{1,5},{2,6},{3,7},{4,0},{5,1},{6,2},{7,3},{8,12},{9,13},{10,... | collective-permute-start | bytes 602120 | tf_op jit(solution)/shard_map/ppermute | solution.py:311
  71.7 1.3 %collective-permute-start.8 = (bf16[784,128]{1,0:T(8,128)(2,1)S(1)}, bf16[784,128]{1,0:T(8,128)(2,1)S(1)}, u32[]{:S(2)}, u32[]{:S(2)}) collective-permute-start(bf16[784,128]{1,0:T(8,128)(2,1)S(1)} %get-tuple-element.45), channel_id=1, source_target_pairs={{0,5},{1,4},{2,7},{3,6},{4,1},{5,0},{6,3},{7,2},{8,13},{9,12},{10,... | collective-permute-start | bytes 602120 | tf_op jit(solution)/shard_map/ppermute | solution.py:311
  73.6 0.8 collective-permute-start.22
  74.4 1.5 %collective-permute-done.12.came_ref = bf16[2,240,128]{2,1,0:T(8,128)(2,1)S(1)} collective-permute-done((bf16[2,240,128]{2,1,0:T(8,128)(2,1)S(1)}, bf16[2,240,128]{2,1,0:T(8,128)(2,1)S(1)}, u32[]{:S(2)}, u32[]{:S(2)}) %collective-permute-start.12) | collective-permute-done | bytes 122912 | tf_op jit(solution)/shard_map/ppermute | solution.py:311
  75.9 3.4 %collective-permute-start.18 = (bf16[1,224,128]{2,1,0:T(8,128)(2,1)S(1)}, bf16[1,224,128]{2,1,0:T(8,128)(2,1)S(1)}, u32[]{:S(2)}, u32[]{:S(2)}) collective-permute-start(bf16[1,224,128]{2,1,0:T(8,128)(2,1)S(1)} %get-tuple-element.65), channel_id=1, source_target_pairs={{0,8},{1,9},{2,10},{3,11},{4,12},{5,13},{6,14},{7,15},{8,0},{9,1},... | collective-permute-start | bytes 172040 | tf_op jit(solution)/shard_map/ppermute | solution.py:311
  79.3 2.4 %collective-permute-start.13 = (bf16[1,240,128]{2,1,0:T(8,128)(2,1)S(1)}, bf16[1,240,128]{2,1,0:T(8,128)(2,1)S(1)}, u32[]{:S(2)}, u32[]{:S(2)}) collective-permute-start(bf16[1,240,128]{2,1,0:T(8,128)(2,1)S(1)} %get-tuple-element.55), channel_id=1, source_target_pairs={{0,8},{1,9},{2,10},{3,11},{4,12},{5,13},{6,14},{7,15},{8,0},{9,1},... | collective-permute-start | bytes 184328 | tf_op jit(solution)/shard_map/ppermute | solution.py:311
  81.8 3.1 %collective-permute-start.23 = (bf16[1,224,128]{2,1,0:T(8,128)(2,1)S(1)}, bf16[1,224,128]{2,1,0:T(8,128)(2,1)S(1)}, u32[]{:S(2)}, u32[]{:S(2)}) collective-permute-start(bf16[1,224,128]{2,1,0:T(8,128)(2,1)S(1)} %get-tuple-element.75), channel_id=1, source_target_pairs={{0,8},{1,9},{2,10},{3,11},{4,12},{5,13},{6,14},{7,15},{8,0},{9,1},... | collective-permute-start | bytes 172040 | tf_op jit(solution)/shard_map/ppermute | solution.py:311
  85.0 3.2 %collective-permute-done.23.came_ref = bf16[1,224,128]{2,1,0:T(8,128)(2,1)S(1)} collective-permute-done((bf16[1,224,128]{2,1,0:T(8,128)(2,1)S(1)}, bf16[1,224,128]{2,1,0:T(8,128)(2,1)S(1)}, u32[]{:S(2)}, u32[]{:S(2)}) %collective-permute-start.23) | collective-permute-done | bytes 57376 | tf_op jit(solution)/shard_map/ppermute | solution.py:311
  88.9 0.8 add_convert_fusion
  90.2 1.4 %shard_map.131 = f32[1368,128]{1,0:T(8,128)} custom-call(s32[2]{0:T(128)S(1)} %pad_add_fusion.1.refs_0_.me_ref, f32[240,128]{1,0:T(8,128)S(1)} %shard_map.120.refs_0_, f32[224,128]{1,0:T(8,128)S(1)} %shard_map.125.refs_1_, f32[224,128]{1,0:T(8,128)S(1)} %shard_map.130.refs_2_, f32[240,128]{1,0:T(8,128)S(1)} %collective-permute-done.24.refs_3_, ...), custom_call_target="tpu_custom_call" | custom-call | flops 1000000 | bytes 100000 | tf_op jit(solution)/shard_map/pallas_call | solution.py:298
  (56 shorter events, 6.6 us)
Async XLA Ops:
  1.3 0.9 %copy-start = (bf16[16,49,128]{2,0,1:T(8,128)(2,1)S(1)}, bf16[16,49,128]{2,0,1:T(8,128)(2,1)}, u32[]{:S(2)}) copy-start(bf16[16,49,128]{2,0,1:T(8,128)(2,1)} %param.10) | copy-start | bytes 602116
  2.6 13.6 %collective-permute-start.1 = (bf16[800,128]{1,0:T(8,128)(2,1)S(1)}, bf16[800,128]{1,0:T(8,128)(2,1)S(1)}, u32[]{:S(2)}, u32[]{:S(2)}) collective-permute-start(bf16[800,128]{1,0:T(8,128)(2,1)S(1)} %shard_map.113.refs_2_), channel_id=1, source_target_pairs={{0,8},{1,9},{2,10},{3,11},{4,12},{5,13},{6,14},{7,15},{8,0},{9,1},... | collective-permute-start | bytes 614408 | tf_op jit(solution)/shard_map/ppermute | solution.py:311
  6.6 12.6 %collective-permute-start.4 = (bf16[784,128]{1,0:T(8,128)(2,1)}, bf16[784,128]{1,0:T(8,128)(2,1)S(1)}, u32[]{:S(2)}, u32[]{:S(2)}) collective-permute-start(bf16[784,128]{1,0:T(8,128)(2,1)} %bitcast.19), channel_id=1, source_target_pairs={{0,4},{1,5},{2,6},{3,7},{4,0},{5,1},{6,2},{7,3},{8,12},{9,13},{10,... | collective-permute-start | bytes 602120 | tf_op jit(solution)/shard_map/ppermute | solution.py:311
  8.2 17.5 %collective-permute-start = (bf16[800,128]{1,0:T(8,128)(2,1)S(1)}, bf16[800,128]{1,0:T(8,128)(2,1)S(1)}, u32[]{:S(2)}, u32[]{:S(2)}) collective-permute-start(bf16[800,128]{1,0:T(8,128)(2,1)S(1)} %shard_map.113.refs_2_), channel_id=1, source_target_pairs={{0,2},{1,3},{2,0},{3,1},{4,6},{5,7},{6,4},{7,5},{8,10},{9,11},{10,... | collective-permute-start | bytes 614408 | tf_op jit(solution)/shard_map/ppermute | solution.py:311
  16.2 11.6 %collective-permute-start.2 = (bf16[800,128]{1,0:T(8,128)(2,1)S(1)}, bf16[800,128]{1,0:T(8,128)(2,1)S(1)}, u32[]{:S(2)}, u32[]{:S(2)}) collective-permute-start(bf16[800,128]{1,0:T(8,128)(2,1)S(1)} %collective-permute-done.1.refs_4_), channel_id=1, source_target_pairs={{0,2},{1,3},{2,0},{3,1},{4,6},{5,7},{6,4},{7,5},{8,10},{9,11},{10,... | collective-permute-start | bytes 614408 | tf_op jit(solution)/shard_map/ppermute | solution.py:311
  17.8 7.9 %collective-permute-start.3 = (bf16[784,128]{1,0:T(8,128)(2,1)}, bf16[784,128]{1,0:T(8,128)(2,1)S(1)}, u32[]{:S(2)}, u32[]{:S(2)}) collective-permute-start(bf16[784,128]{1,0:T(8,128)(2,1)} %bitcast.20), channel_id=1, source_target_pairs={{0,1},{1,0},{2,3},{3,2},{4,5},{5,4},{6,7},{7,6},{8,9},{9,8},{10,11... | collective-permute-start | bytes 602120 | tf_op jit(solution)/shard_map/ppermute | solution.py:311
  19.2 8.6 %collective-permute-start.5 = (bf16[784,128]{1,0:T(8,128)(2,1)S(1)}, bf16[784,128]{1,0:T(8,128)(2,1)S(1)}, u32[]{:S(2)}, u32[]{:S(2)}) collective-permute-start(bf16[784,128]{1,0:T(8,128)(2,1)S(1)} %collective-permute-done.4.refs_8_), channel_id=1, source_target_pairs={{0,1},{1,0},{2,3},{3,2},{4,5},{5,4},{6,7},{7,6},{8,9},{9,8},{10,11... | collective-permute-start | bytes 602120 | tf_op jit(solution)/shard_map/ppermute | solution.py:311
  27.8 1.1 %copy-start.4 = (bf16[256,29,49]{0,1,2:T(8,128)(2,1)S(1)}, bf16[256,29,49]{0,1,2:T(8,128)(2,1)}, u32[]{:S(2)}) copy-start(bf16[256,29,49]{0,1,2:T(8,128)(2,1)} %param.12) | copy-start | bytes 2182660
  40.1 2.5 %collective-permute-start.14 = (bf16[16,224,128]{2,1,0:T(8,128)(2,1)S(1)}, bf16[16,224,128]{2,1,0:T(8,128)(2,1)S(1)}, u32[]{:S(2)}, u32[]{:S(2)}) collective-permute-start(bf16[16,224,128]{2,1,0:T(8,128)(2,1)S(1)} %get-tuple-element.57), channel_id=1, source_target_pairs={{0,16},{16,0},{1,17},{17,1},{2,18},{18,2},{3,19},{19,3},{4,20},{20... | collective-permute-start | bytes 2752520 | tf_op jit(solution)/shard_map/ppermute | solution.py:315
  40.2 7.1 %collective-permute-start.9 = (bf16[16,240,128]{2,1,0:T(8,128)(2,1)S(1)}, bf16[16,240,128]{2,1,0:T(8,128)(2,1)S(1)}, u32[]{:S(2)}, u32[]{:S(2)}) collective-permute-start(bf16[16,240,128]{2,1,0:T(8,128)(2,1)S(1)} %get-tuple-element.47), channel_id=1, source_target_pairs={{0,16},{16,0},{1,17},{17,1},{2,18},{18,2},{3,19},{19,3},{4,20},{20... | collective-permute-start | bytes 2949128 | tf_op jit(solution)/shard_map/ppermute | solution.py:315
  40.7 4.7 %collective-permute-start.19 = (bf16[16,224,128]{2,1,0:T(8,128)(2,1)S(1)}, bf16[16,224,128]{2,1,0:T(8,128)(2,1)S(1)}, u32[]{:S(2)}, u32[]{:S(2)}) collective-permute-start(bf16[16,224,128]{2,1,0:T(8,128)(2,1)S(1)} %get-tuple-element.67), channel_id=1, source_target_pairs={{0,16},{16,0},{1,17},{17,1},{2,18},{18,2},{3,19},{19,3},{4,20},{20... | collective-permute-start | bytes 2752520 | tf_op jit(solution)/shard_map/ppermute | solution.py:315
  42.8 12.6 %collective-permute-start.15 = (bf16[8,224,128]{2,1,0:T(8,128)(2,1)S(1)}, bf16[8,224,128]{2,1,0:T(8,128)(2,1)S(1)}, u32[]{:S(2)}, u32[]{:S(2)}) collective-permute-start(bf16[8,224,128]{2,1,0:T(8,128)(2,1)S(1)} %get-tuple-element.59), channel_id=1, source_target_pairs={{0,2},{1,3},{2,0},{3,1},{4,6},{5,7},{6,4},{7,5},{8,10},{9,11},{10,... | collective-permute-start | bytes 1376264 | tf_op jit(solution)/shard_map/ppermute | solution.py:311
  45.3 11.9 %copy-start.3 = (bf16[896,896]{1,0:T(8,128)(2,1)S(1)}, bf16[896,896]{1,0:T(8,128)(2,1)}, u32[]{:S(2)}) copy-start(bf16[896,896]{1,0:T(8,128)(2,1)} %refs_3_.1) | copy-start | bytes 4816900
  45.5 17.7 %collective-permute-start.20 = (bf16[8,224,128]{2,1,0:T(8,128)(2,1)S(1)}, bf16[8,224,128]{2,1,0:T(8,128)(2,1)S(1)}, u32[]{:S(2)}, u32[]{:S(2)}) collective-permute-start(bf16[8,224,128]{2,1,0:T(8,128)(2,1)S(1)} %get-tuple-element.69), channel_id=1, source_target_pairs={{0,4},{1,5},{2,6},{3,7},{4,0},{5,1},{6,2},{7,3},{8,12},{9,13},{10,... | collective-permute-start | bytes 1376264 | tf_op jit(solution)/shard_map/ppermute | solution.py:311
  47.2 10.0 %copy-start.1 = (bf16[2,768,768]{2,1,0:T(8,128)(2,1)S(1)}, bf16[2,768,768]{2,1,0:T(8,128)(2,1)}, u32[]{:S(2)}) copy-start(bf16[2,768,768]{2,1,0:T(8,128)(2,1)} %refs_4_.1) | copy-start | bytes 7077892
  47.2 10.0 %copy-start.2 = (bf16[2,640,640]{2,1,0:T(8,128)(2,1)S(1)}, bf16[2,640,640]{2,1,0:T(8,128)(2,1)}, u32[]{:S(2)}) copy-start(bf16[2,640,640]{2,1,0:T(8,128)(2,1)} %refs_5_.1) | copy-start | bytes 4915204
  47.4 15.1 %collective-permute-start.10 = (bf16[8,240,128]{2,1,0:T(8,128)(2,1)S(1)}, bf16[8,240,128]{2,1,0:T(8,128)(2,1)S(1)}, u32[]{:S(2)}, u32[]{:S(2)}) collective-permute-start(bf16[8,240,128]{2,1,0:T(8,128)(2,1)S(1)} %get-tuple-element.49), channel_id=1, source_target_pairs={{0,1},{1,0},{2,3},{3,2},{4,5},{5,4},{6,7},{7,6},{8,9},{9,8},{10,11... | collective-permute-start | bytes 1474568 | tf_op jit(solution)/shard_map/ppermute | solution.py:311
  55.5 9.3 %collective-permute-start.16 = (bf16[4,224,128]{2,1,0:T(8,128)(2,1)S(1)}, bf16[4,224,128]{2,1,0:T(8,128)(2,1)S(1)}, u32[]{:S(2)}, u32[]{:S(2)}) collective-permute-start(bf16[4,224,128]{2,1,0:T(8,128)(2,1)S(1)} %get-tuple-element.61), channel_id=1, source_target_pairs={{0,4},{1,5},{2,6},{3,7},{4,0},{5,1},{6,2},{7,3},{8,12},{9,13},{10,... | collective-permute-start | bytes 688136 | tf_op jit(solution)/shard_map/ppermute | solution.py:311
  62.6 7.0 %collective-permute-start.11 = (bf16[4,240,128]{2,1,0:T(8,128)(2,1)S(1)}, bf16[4,240,128]{2,1,0:T(8,128)(2,1)S(1)}, u32[]{:S(2)}, u32[]{:S(2)}) collective-permute-start(bf16[4,240,128]{2,1,0:T(8,128)(2,1)S(1)} %get-tuple-element.51), channel_id=1, source_target_pairs={{0,2},{1,3},{2,0},{3,1},{4,6},{5,7},{6,4},{7,5},{8,10},{9,11},{10,... | collective-permute-start | bytes 737288 | tf_op jit(solution)/shard_map/ppermute | solution.py:311
  63.2 9.7 %collective-permute-start.21 = (bf16[4,224,128]{2,1,0:T(8,128)(2,1)S(1)}, bf16[4,224,128]{2,1,0:T(8,128)(2,1)S(1)}, u32[]{:S(2)}, u32[]{:S(2)}) collective-permute-start(bf16[4,224,128]{2,1,0:T(8,128)(2,1)S(1)} %get-tuple-element.71), channel_id=1, source_target_pairs={{0,1},{1,0},{2,3},{3,2},{4,5},{5,4},{6,7},{7,6},{8,9},{9,8},{10,11... | collective-permute-start | bytes 688136 | tf_op jit(solution)/shard_map/ppermute | solution.py:311
  64.8 8.7 %collective-permute-start.17 = (bf16[2,224,128]{2,1,0:T(8,128)(2,1)S(1)}, bf16[2,224,128]{2,1,0:T(8,128)(2,1)S(1)}, u32[]{:S(2)}, u32[]{:S(2)}) collective-permute-start(bf16[2,224,128]{2,1,0:T(8,128)(2,1)S(1)} %get-tuple-element.63), channel_id=1, source_target_pairs={{0,1},{1,0},{2,3},{3,2},{4,5},{5,4},{6,7},{7,6},{8,9},{9,8},{10,11... | collective-permute-start | bytes 344072 | tf_op jit(solution)/shard_map/ppermute | solution.py:311
  69.6 6.3 %collective-permute-start.12 = (bf16[2,240,128]{2,1,0:T(8,128)(2,1)S(1)}, bf16[2,240,128]{2,1,0:T(8,128)(2,1)S(1)}, u32[]{:S(2)}, u32[]{:S(2)}) collective-permute-start(bf16[2,240,128]{2,1,0:T(8,128)(2,1)S(1)} %get-tuple-element.53), channel_id=1, source_target_pairs={{0,4},{1,5},{2,6},{3,7},{4,0},{5,1},{6,2},{7,3},{8,12},{9,13},{10,... | collective-permute-start | bytes 368648 | tf_op jit(solution)/shard_map/ppermute | solution.py:311
  70.0 18.8 %collective-permute-start.7 = (bf16[784,128]{1,0:T(8,128)(2,1)S(1)}, bf16[784,128]{1,0:T(8,128)(2,1)S(1)}, u32[]{:S(2)}, u32[]{:S(2)}) collective-permute-start(bf16[784,128]{1,0:T(8,128)(2,1)S(1)} %get-tuple-element.44), channel_id=1, source_target_pairs={{0,4},{1,5},{2,6},{3,7},{4,0},{5,1},{6,2},{7,3},{8,12},{9,13},{10,... | collective-permute-start | bytes 602120 | tf_op jit(solution)/shard_map/ppermute | solution.py:311
  71.7 17.2 %collective-permute-start.8 = (bf16[784,128]{1,0:T(8,128)(2,1)S(1)}, bf16[784,128]{1,0:T(8,128)(2,1)S(1)}, u32[]{:S(2)}, u32[]{:S(2)}) collective-permute-start(bf16[784,128]{1,0:T(8,128)(2,1)S(1)} %get-tuple-element.45), channel_id=1, source_target_pairs={{0,5},{1,4},{2,7},{3,6},{4,1},{5,0},{6,3},{7,2},{8,13},{9,12},{10,... | collective-permute-start | bytes 602120 | tf_op jit(solution)/shard_map/ppermute | solution.py:311
  73.0 15.9 %collective-permute-start.6 = (bf16[784,128]{1,0:T(8,128)(2,1)S(1)}, bf16[784,128]{1,0:T(8,128)(2,1)S(1)}, u32[]{:S(2)}, u32[]{:S(2)}) collective-permute-start(bf16[784,128]{1,0:T(8,128)(2,1)S(1)} %get-tuple-element.43.outs_0_), channel_id=1, source_target_pairs={{0,1},{1,0},{2,3},{3,2},{4,5},{5,4},{6,7},{7,6},{8,9},{9,8},{10,11... | collective-permute-start | bytes 602120 | tf_op jit(solution)/shard_map/ppermute | solution.py:311
  73.6 5.7 %collective-permute-start.22 = (bf16[2,224,128]{2,1,0:T(8,128)(2,1)S(1)}, bf16[2,224,128]{2,1,0:T(8,128)(2,1)S(1)}, u32[]{:S(2)}, u32[]{:S(2)}) collective-permute-start(bf16[2,224,128]{2,1,0:T(8,128)(2,1)S(1)} %get-tuple-element.73), channel_id=1, source_target_pairs={{0,2},{1,3},{2,0},{3,1},{4,6},{5,7},{6,4},{7,5},{8,10},{9,11},{10,... | collective-permute-start | bytes 344072 | tf_op jit(solution)/shard_map/ppermute | solution.py:311
  75.9 5.9 %collective-permute-start.18 = (bf16[1,224,128]{2,1,0:T(8,128)(2,1)S(1)}, bf16[1,224,128]{2,1,0:T(8,128)(2,1)S(1)}, u32[]{:S(2)}, u32[]{:S(2)}) collective-permute-start(bf16[1,224,128]{2,1,0:T(8,128)(2,1)S(1)} %get-tuple-element.65), channel_id=1, source_target_pairs={{0,8},{1,9},{2,10},{3,11},{4,12},{5,13},{6,14},{7,15},{8,0},{9,1},... | collective-permute-start | bytes 172040 | tf_op jit(solution)/shard_map/ppermute | solution.py:311
  79.3 8.9 %collective-permute-start.13 = (bf16[1,240,128]{2,1,0:T(8,128)(2,1)S(1)}, bf16[1,240,128]{2,1,0:T(8,128)(2,1)S(1)}, u32[]{:S(2)}, u32[]{:S(2)}) collective-permute-start(bf16[1,240,128]{2,1,0:T(8,128)(2,1)S(1)} %get-tuple-element.55), channel_id=1, source_target_pairs={{0,8},{1,9},{2,10},{3,11},{4,12},{5,13},{6,14},{7,15},{8,0},{9,1},... | collective-permute-start | bytes 184328 | tf_op jit(solution)/shard_map/ppermute | solution.py:311
  81.8 6.4 %collective-permute-start.23 = (bf16[1,224,128]{2,1,0:T(8,128)(2,1)S(1)}, bf16[1,224,128]{2,1,0:T(8,128)(2,1)S(1)}, u32[]{:S(2)}, u32[]{:S(2)}) collective-permute-start(bf16[1,224,128]{2,1,0:T(8,128)(2,1)S(1)} %get-tuple-element.75), channel_id=1, source_target_pairs={{0,8},{1,9},{2,10},{3,11},{4,12},{5,13},{6,14},{7,15},{8,0},{9,1},... | collective-permute-start | bytes 172040 | tf_op jit(solution)/shard_map/ppermute | solution.py:311
  88.2 1.5 %collective-permute-start.25 = (f32[224,128]{1,0:T(8,128)S(1)}, f32[224,128]{1,0:T(8,128)S(1)}, u32[]{:S(2)}, u32[]{:S(2)}) collective-permute-start(f32[224,128]{1,0:T(8,128)S(1)} %shard_map.125.refs_1_), channel_id=1, source_target_pairs={{0,16},{16,0},{1,17},{17,1},{2,18},{18,2},{3,19},{19,3},{4,20},{20... | collective-permute-start | bytes 344072 | tf_op jit(solution)/shard_map/ppermute | solution.py:315
  88.2 1.5 %collective-permute-start.26 = (f32[224,128]{1,0:T(8,128)S(1)}, f32[224,128]{1,0:T(8,128)S(1)}, u32[]{:S(2)}, u32[]{:S(2)}) collective-permute-start(f32[224,128]{1,0:T(8,128)S(1)} %shard_map.130.refs_2_), channel_id=1, source_target_pairs={{0,16},{16,0},{1,17},{17,1},{2,18},{18,2},{3,19},{19,3},{4,20},{20... | collective-permute-start | bytes 344072 | tf_op jit(solution)/shard_map/ppermute | solution.py:315
  88.8 1.4 %collective-permute-start.24 = (f32[240,128]{1,0:T(8,128)S(1)}, f32[240,128]{1,0:T(8,128)S(1)}, u32[]{:S(2)}, u32[]{:S(2)}) collective-permute-start(f32[240,128]{1,0:T(8,128)S(1)} %shard_map.120.refs_0_), channel_id=1, source_target_pairs={{0,16},{16,0},{1,17},{17,1},{2,18},{18,2},{3,19},{19,3},{4,20},{20... | collective-permute-start | bytes 368648 | tf_op jit(solution)/shard_map/ppermute | solution.py:315
  (1 other events, 0.9 us)

commit v3 on v2

--- a/solution.py
+++ b/solution.py
@@ -109,12 +109,19 @@
     return codes[0:1] - 1, src_place * plan.atoms + codes[1:2], dst_place * plan.atoms + codes[2:3]
 
 
-def fill_rotation(rot_ref, wide_ref, wigner_ref, angle):
-    coeffs, kept, angles = wigner_ref.shape
+def fill_rotation(rot_ref, wide_ref, angle):
+    coeffs, rows, angles = wide_ref.shape
     angle_hot = hot(iota((angles, angle.shape[1]), 0) == angle).astype(jnp.bfloat16)
-    wide_ref[...] = jnp.zeros(wide_ref.shape, wide_ref.dtype)
+    rot_ref[...] = nn(wide_ref[...].reshape(coeffs * rows, angles), angle_hot)
+
+
+def middle_kernel(far, near, *refs):
+    wigner_ref, own_ref = refs[far + near : far + near + 2]
+    wide_ref, copy_ref = refs[-2:]
+    kept = wigner_ref.shape[1]
+    wide_ref[:, kept:, :] = jnp.zeros((wide_ref.shape[0], wide_ref.shape[1] - kept, wide_ref.shape[2]), wide_ref.dtype)
     wide_ref[:, 0:kept, :] = wigner_ref[...]
-    rot_ref[...] = nn(wide_ref[...].reshape(coeffs * TABLE_ROWS, angles), angle_hot)
+    copy_ref[...] = own_ref[...]
 
 
 def fill_spread(spread_ref, rot_ref, atom_hot, degree, row):
@@ -140,16 +147,21 @@
         )
 
 
-def rotate_all(out_ref, node_ref, spread_ref, rot_ref, atom_hot):
+def rotate_all(put, node_ref, spread_ref, rot_ref, atom_hot):
     atoms, channels = node_ref.shape[1], node_ref.shape[2]
     for degree in range(LMAX + 1):
         depth = (2 * degree + 1) * atoms
         nodes = node_ref[degree * degree : (degree + 1) * (degree + 1)].reshape(depth, channels).T
         for row in rows_of_degree(degree):
             fill_spread(spread_ref, rot_ref, atom_hot, degree, row)
-            out_ref[row * channels : (row + 1) * channels, :] = nn(
-                nodes, spread_ref[0:depth, :]
-            ).astype(jnp.bfloat16)
+            put(row, nn(nodes, spread_ref[0:depth, :]).astype(jnp.bfloat16))
+
+
+def place_of(row):
+    bounds = group_bounds()
+    for number, (start, length) in enumerate(bounds):
+        if start <= row < start + length:
+            return (number + 1) // 2, (number + 1) % 2 if number else 0, row - start
 
 
 def message_kernel(plan, *refs):
@@ -195,47 +207,54 @@
 
 def gram_kernel(plan, half_rows, sizes, *refs):
     n_src, n_dst = plan.n_src, plan.n_dst
-    me_ref, wigner_ref, refs = refs[0], refs[1], refs[2:]
+    me_ref, wide_ref, refs = refs[0], refs[1], refs[2:]
     node_blocks, refs = refs[:n_src], refs[n_src:]
     pull_blocks, refs = refs[:n_dst], refs[n_dst:]
     rot_ref, atom_ref, rotated_ref, refs = refs[0], refs[1], refs[2], refs[3:]
     out_refs, refs = refs[: 2 * len(sizes)], refs[2 * len(sizes) :]
-    wide_ref, node_ref, pull_ref, spread_ref, pulled_ref, grad_ref = refs
-    channels = node_ref.shape[2]
+    node_ref, pull_ref, spread_ref = refs[:3]
+    left_refs, right_refs, refs = refs[3 : 4 + MMAX], refs[4 + MMAX : 5 + 2 * MMAX], refs[5 + 2 * MMAX :]
+    turned_refs, grad_ref = refs[:MMAX], refs[MMAX]
+    channels, slots = node_ref.shape[2], plan.slots
     me, core = me_ref[0], me_ref[1]
     angle, src, dst = slot_codes(plan, me, node_blocks)
     atom_ref[...] = jnp.broadcast_to(dst, atom_ref.shape)
-    fill_rotation(rot_ref, wide_ref, wigner_ref, angle)
+    fill_rotation(rot_ref, wide_ref, angle)
     fill_nodes(node_ref, node_blocks, plan.atoms)
     fill_nodes(pull_ref, pull_blocks, plan.atoms)
-    rotate_all(rotated_ref, node_ref, spread_ref, rot_ref, atom_hots(n_src * plan.atoms, src))
-    rotate_all(pulled_ref, pull_ref, spread_ref, rot_ref, atom_hots(n_dst * plan.atoms, dst))
-
-    def lines(ref, start, length):
-        return ref[start * channels : (start + length) * channels, :]
-
-    bounds = group_bounds()
+
+    def put_rotated(row, value):
+        azimuth, side, place = place_of(row)
+        rotated_ref[row * channels : (row + 1) * channels, :] = value
+        left_refs[azimuth][
+            place * channels : (place + 1) * channels, side * slots : (side + 1) * slots
+        ] = value
+
+    def put_pulled(row, value):
+        azimuth, side, place = place_of(row)
+        lines = slice(place * channels, (place + 1) * channels)
+        right_refs[azimuth][lines, side * slots : (side + 1) * slots] = value
+        if azimuth > 0:
+            turned_refs[azimuth - 1][lines, (1 - side) * slots : (2 - side) * slots] = (
+                value if side == 1 else -value
+            )
+
+    rotate_all(put_rotated, node_ref, spread_ref, rot_ref, atom_hots(n_src * plan.atoms, src))
+    rotate_all(put_pulled, pull_ref, spread_ref, rot_ref, atom_hots(n_dst * plan.atoms, dst))
+
     base = 0
     for azimuth in range(MMAX + 1):
-        plus, length = bounds[max(2 * azimuth - 1, 0)]
-        minus = bounds[2 * azimuth][0]
-        for kind in range(1 if azimuth == 0 else 2):
-            for into in range(length):
-                p, q = lines(rotated_ref, plus + into, 1), lines(rotated_ref, minus + into, 1)
-                for first in range(0, length, 2):
-                    width = min(2, length - first)
-                    g = lines(pulled_ref, plus + first, width)
-                    h = lines(pulled_ref, minus + first, width)
-                    if azimuth == 0:
-                        block = nt(p, g)
-                    elif kind == 0:
-                        block = nt(p, g) + nt(q, h)
-                    else:
-                        block = nt(p, h) - nt(q, g)
-                    for step in range(width):
-                        grad_ref[
-                            pl.ds(base + into * channels * length + first + step, channels, stride=length), :
-                        ] = block[:, step * channels : (step + 1) * channels]
+        length = LMAX + 1 - azimuth
+        for right in [right_refs[azimuth], *turned_refs[azimuth - 1 : azimuth]] if azimuth else right_refs[:1]:
+            for first in range(0, length, 2):
+                width = min(2, length - first)
+                block = nt(
+                    left_refs[azimuth][...], right[first * channels : (first + width) * channels, :]
+                )
+                for step in range(width):
+                    grad_ref[pl.ds(base + first + step, length * channels, stride=length), :] = block[
+                        :, step * channels : (step + 1) * channels
+                    ]
             base = base + length * length * channels
     rows = grad_ref.shape[0] // plan.parts
     shift = rows - half_rows
@@ -289,7 +308,7 @@
     return int(np.prod(shape[:-2], initial=1)) * rows * lanes * jnp.dtype(dtype).itemsize
 
 
-def whole_call(kernel, outs, args, scratch=(), smem=0, flops=10**6):
+def whole_call(kernel, outs, args, scratch=(), smem=0, flops=10**6, passed=0):
     specs = [pl.BlockSpec(memory_space=pltpu.SMEM)] * smem + [
         pl.BlockSpec(memory_space=pltpu.VMEM)
     ] * (len(args) - smem)
@@ -301,6 +320,7 @@
         in_specs=specs,
         out_specs=[pl.BlockSpec(memory_space=pltpu.VMEM)] * len(outs),
         scratch_shapes=[pltpu.VMEM(*item) for item in scratch],
+        input_output_aliases={i: i for i in range(passed)},
         compiler_params=pltpu.CompilerParams(vmem_limit_bytes=held * 9 // 8 + 4 * MIB),
         cost_estimate=pl.CostEstimate(flops=flops, bytes_accessed=10**5, transcendentals=0),
     )(*args)
@@ -337,12 +357,28 @@
         [jax.ShapeDtypeStruct((coeffs * atoms + 16, channels), bf16)],
         [jnp.stack([dst_part[:, 0], src_atom, dst_atom, angle]), node_rows(features)],
     )[0]
-    rotation = wigner.transpose(2, 1, 0)
-
-    blocks = [{0: payload}, {0: node_rows(cotangent)}]
-    for held, bits in zip(blocks, (plan.src_bits, plan.dst_bits)):
-        for bit in bits[::-1]:
-            held.update({flip | 1 << bit: swap(item, 1 << bit) for flip, item in list(held.items())})
+    own = node_rows(cotangent)
+    blocks = [{0: payload}, {0: own}]
+    bit_lists = (plan.src_bits[::-1], plan.dst_bits[::-1])
+    for held, bits in zip(blocks, bit_lists):
+        held.update({1 << bit: swap(held[0], 1 << bit) for bit in bits})
+    far = [held[1 << bits[0]] for held, bits in zip(blocks, bit_lists)]
+    near = [held[1 << bit] for held, bits in zip(blocks, bit_lists) for bit in bits[1:]]
+    *far, wide, blocks[1][0] = whole_call(
+        functools.partial(middle_kernel, len(far), len(near)),
+        [jax.ShapeDtypeStruct(x.shape, bf16) for x in far]
+        + [
+            jax.ShapeDtypeStruct((coeffs, TABLE_ROWS, wigner.shape[0]), bf16),
+            jax.ShapeDtypeStruct(own.shape, bf16),
+        ],
+        [*far, *near, wigner.transpose(2, 1, 0), own],
+        passed=len(far),
+    )
+    for held, bits, item in zip(blocks, bit_lists, far):
+        held[1 << bits[0]] = item
+        for number, bit in enumerate(bits[1:], 1):
+            for flip in flips(bits[:number])[1:]:
+                held[flip | 1 << bit] = swap(held[flip], 1 << bit)
     node_blocks = [blocks[0][flip] for flip in flips(plan.src_bits)]
     pull_blocks = [blocks[1][flip] for flip in flips(plan.dst_bits)]
 
@@ -354,6 +390,10 @@
     sizes = [16 * ((tiles + STREAMS - 1 - k) // STREAMS) for k in range(STREAMS)]
     deepest = (2 * LMAX + 1) * atoms
     most = max(plan.n_src, plan.n_dst)
+    grouped = [
+        (((LMAX + 1 - azimuth) * channels, min(2, 1 + azimuth) * slots), bf16)
+        for azimuth in range(MMAX + 1)
+    ]
     rot, dst_slot, rotated, *result = whole_call(
         functools.partial(gram_kernel, plan, half_rows, sizes),
         [
@@ -366,13 +406,14 @@
             for size in sizes
             for kind in (f32, bf16)
         ],
-        [here, rotation, *node_blocks, *pull_blocks],
+        [here, wide, *node_blocks, *pull_blocks],
         [
-            ((coeffs, TABLE_ROWS, wigner.shape[0]), bf16),
             ((coeffs, plan.n_src * atoms, channels), bf16),
             ((coeffs, plan.n_dst * atoms, channels), bf16),
             ((deepest * most, slots), bf16),
-            ((kept * channels, slots), bf16),
+            *grouped,
+            *grouped,
+            *grouped[1:],
             ((params // channels, channels), f32),
         ],
         smem=1,
@@ -413,7 +454,7 @@
             kept_part, sent = whole_call(
                 functools.partial(add_kernel, 1 << place),
                 [jax.ShapeDtypeStruct(shape, f32), jax.ShapeDtypeStruct(shape, bf16)],
-                [kept_part, came] + ([partial_sums[1]] if stage == 1 and stream == 0 else []),
+                [kept_part, came] + ([partial_sums[1]] if stage == 1 else []),
             )
             came = swap(sent, 1 << bit)
         mine += whole_call(

time: 92.9 us -> 84.1 us (0.905)
  waiting for transfers between devices: 33.8 us -> 29.6 us
  Pallas kernels: 18.1 us -> 15.6 us
  starting transfers between devices: 34.3 us -> 32.1 us
    ppermute x21, waiting for transfers between devices: 29.7 us -> 25.8 us  [swap(): return lax.ppermute(value, 'graph', [(i, i ^ flip) for i in range(count)])]
    pallas_call x19 -> x20, Pallas kernels: 18.1 us -> 15.6 us  [whole_call(): pl.pallas_call(kernel, out_shape=outs, in_specs=specs, out_specs=[pl.Bloc...]
    ppermute x21, starting transfers between devices: 33 us -> 30.8 us  [swap(): return lax.ppermute(value, 'graph', [(i, i ^ flip) for i in range(count)])]
  transfers between devices with their start and end apart: 27 -> 27, of which waited for: 11 -> 12; matrix products, arithmetic and copies ran while one was open for 1% -> 1% of each run, Pallas kernels for 7% -> 8%
where the time goes in v3:
time: 84.1 us; the launch traced here: 83.4 us
  starting transfers between devices  32.1 us (38%)
  waiting for transfers between devices  29.6 us (35%)
  Pallas kernels  15.6 us (19%)
  local copies, waits for them, and re-layouts  3.69 us (4%)
  other arithmetic  1.58 us (2%)
    ppermute x21, starting transfers between devices, swap(): return lax.ppermute(value, 'graph', [(i, i ^ flip) for i in range(count)])  30.8 us
    ppermute x21, waiting for transfers between devices, swap(): return lax.ppermute(value, 'graph', [(i, i ^ flip) for i in range(count)])  25.8 us
    pallas_call x20, Pallas kernels, whole_call(): pl.pallas_call(kernel, out_shape=outs, in_specs=specs, out_specs=[pl.Bloc...  15.6 us
    ppermute x6, waiting for transfers between devices, swap_cores(): return lax.ppermute(value, 'dp', [(i, 1 - i) for i in range(2)])  3.81 us
    unnamed x12, local copies, waits for them, and re-layouts  3.69 us
  transfers between devices with their start and end apart: 27, of which 12 were waited for; matrix products, arithmetic and copies ran while one was open for 1% of the time, Pallas kernels for 8%

profile of v3, /device:TPU:0, one launch (start us, length us, event | category | flops | bytes accessed | tf_op | source)
XLA Modules:
  0.0 83.4 jit_solution(5251216623225970797)
XLA Ops:
  1.3 0.9 %copy-done.2 = bf16[16,49,128]{2,0,1:T(8,128)(2,1)S(1)} copy-done((bf16[16,49,128]{2,0,1:T(8,128)(2,1)S(1)}, bf16[16,49,128]{2,0,1:T(8,128)(2,1)}, u32[]{:S(2)}) %copy-start.2) | copy-done | bytes 200728
  2.6 3.0 %collective-permute-start.2 = (bf16[800,128]{1,0:T(8,128)(2,1)S(1)}, bf16[800,128]{1,0:T(8,128)(2,1)S(1)}, u32[]{:S(2)}, u32[]{:S(2)}) collective-permute-start(bf16[800,128]{1,0:T(8,128)(2,1)S(1)} %shard_map.113.refs_2_), channel_id=1, source_target_pairs={{0,2},{1,3},{2,0},{3,1},{4,6},{5,7},{6,4},{7,5},{8,10},{9,11},{10,... | collective-permute-start | bytes 614408 | tf_op jit(solution)/shard_map/ppermute | solution.py:331
  5.5 2.6 %collective-permute-start = (bf16[800,128]{1,0:T(8,128)(2,1)S(1)}, bf16[800,128]{1,0:T(8,128)(2,1)S(1)}, u32[]{:S(2)}, u32[]{:S(2)}) collective-permute-start(bf16[800,128]{1,0:T(8,128)(2,1)S(1)} %shard_map.113.refs_2_), channel_id=1, source_target_pairs={{0,8},{1,9},{2,10},{3,11},{4,12},{5,13},{6,14},{7,15},{8,0},{9,1},... | collective-permute-start | bytes 614408 | tf_op jit(solution)/shard_map/ppermute | solution.py:331
  8.1 1.5 %collective-permute-start.3 = (bf16[784,128]{1,0:T(8,128)(2,1)}, bf16[784,128]{1,0:T(8,128)(2,1)S(1)}, u32[]{:S(2)}, u32[]{:S(2)}) collective-permute-start(bf16[784,128]{1,0:T(8,128)(2,1)} %bitcast.18), channel_id=1, source_target_pairs={{0,1},{1,0},{2,3},{3,2},{4,5},{5,4},{6,7},{7,6},{8,9},{9,8},{10,11... | collective-permute-start | bytes 602120 | tf_op jit(solution)/shard_map/ppermute | solution.py:331
  9.6 1.6 %collective-permute-start.1 = (bf16[784,128]{1,0:T(8,128)(2,1)}, bf16[784,128]{1,0:T(8,128)(2,1)S(1)}, u32[]{:S(2)}, u32[]{:S(2)}) collective-permute-start(bf16[784,128]{1,0:T(8,128)(2,1)} %bitcast.19), channel_id=1, source_target_pairs={{0,4},{1,5},{2,6},{3,7},{4,0},{5,1},{6,2},{7,3},{8,12},{9,13},{10,... | collective-permute-start | bytes 602120 | tf_op jit(solution)/shard_map/ppermute | solution.py:331
  11.2 3.3 %collective-permute-done.3.refs_3_.refs_7_ = bf16[784,128]{1,0:T(8,128)(2,1)S(1)} collective-permute-done((bf16[784,128]{1,0:T(8,128)(2,1)}, bf16[784,128]{1,0:T(8,128)(2,1)S(1)}, u32[]{:S(2)}, u32[]{:S(2)}) %collective-permute-start.3) | collective-permute-done | bytes 200736 | tf_op jit(solution)/shard_map/ppermute | solution.py:331
  14.5 4.5 %collective-permute-done.1.refs_1_ = bf16[784,128]{1,0:T(8,128)(2,1)S(1)} collective-permute-done((bf16[784,128]{1,0:T(8,128)(2,1)}, bf16[784,128]{1,0:T(8,128)(2,1)S(1)}, u32[]{:S(2)}, u32[]{:S(2)}) %collective-permute-start.1) | collective-permute-done | bytes 200736 | tf_op jit(solution)/shard_map/ppermute | solution.py:331
  19.0 1.1 %copy-done = bf16[256,29,49]{0,1,2:T(8,128)(2,1)S(1)} copy-done((bf16[256,29,49]{0,1,2:T(8,128)(2,1)S(1)}, bf16[256,29,49]{0,1,2:T(8,128)(2,1)}, u32[]{:S(2)}) %copy-start) | copy-done | bytes 727576
  20.1 0.9 %copy-done.1 = bf16[16,49,128]{2,0,1:T(8,128)(2,1)S(1)} copy-done((bf16[16,49,128]{2,0,1:T(8,128)(2,1)S(1)}, bf16[16,49,128]{2,0,1:T(8,128)(2,1)}, u32[]{:S(2)}) %copy-start.1) | copy-done | bytes 200728
  22.4 5.0 %collective-permute-done.5.refs_9_ = bf16[784,128]{1,0:T(8,128)(2,1)S(1)} collective-permute-done((bf16[784,128]{1,0:T(8,128)(2,1)S(1)}, bf16[784,128]{1,0:T(8,128)(2,1)S(1)}, u32[]{:S(2)}, u32[]{:S(2)}) %collective-permute-start.5) | collective-permute-done | bytes 200736 | tf_op jit(solution)/shard_map/ppermute | solution.py:331
  27.4 7.5 %shard_map.115 = (f32[1568,256]{1,0:T(8,128)S(1)}, s32[8,256]{1,0:T(8,128)S(1)}, bf16[3712,256]{1,0:T(8,128)(2,1)S(1)}, f32[16,240,128]{2,1,0:T(8,128)S(1)}, bf1...) custom-call(s32[2]{0:T(128)S(1)} %pad_add_fusion.1.refs_0_.me_ref, ...), custom_call_target="tpu_custom_call" | custom-call | flops 8000000000 | bytes 100000 | tf_op jit(solution)/shard_map/pallas_call | solution.py:317
  35.6 3.3 %collective-permute-done.14.came_ref = bf16[16,224,128]{2,1,0:T(8,128)(2,1)S(1)} collective-permute-done((bf16[16,224,128]{2,1,0:T(8,128)(2,1)S(1)}, bf16[16,224,128]{2,1,0:T(8,128)(2,1)S(1)}, u32[]{:S(2)}, u32[]{:S(2)}) %collective-permute-start.14) | collective-permute-done | bytes 917536 | tf_op jit(solution)/shard_map/ppermute | solution.py:335
  39.1 1.6 %collective-permute-start.15 = (bf16[8,224,128]{2,1,0:T(8,128)(2,1)S(1)}, bf16[8,224,128]{2,1,0:T(8,128)(2,1)S(1)}, u32[]{:S(2)}, u32[]{:S(2)}) collective-permute-start(bf16[8,224,128]{2,1,0:T(8,128)(2,1)S(1)} %get-tuple-element.67), channel_id=1, source_target_pairs={{0,2},{1,3},{2,0},{3,1},{4,6},{5,7},{6,4},{7,5},{8,10},{9,11},{10,... | collective-permute-start | bytes 1376264 | tf_op jit(solution)/shard_map/ppermute | solution.py:331
  41.2 1.5 %collective-permute-start.10 = (bf16[8,240,128]{2,1,0:T(8,128)(2,1)S(1)}, bf16[8,240,128]{2,1,0:T(8,128)(2,1)S(1)}, u32[]{:S(2)}, u32[]{:S(2)}) collective-permute-start(bf16[8,240,128]{2,1,0:T(8,128)(2,1)S(1)} %get-tuple-element.57), channel_id=1, source_target_pairs={{0,1},{1,0},{2,3},{3,2},{4,5},{5,4},{6,7},{7,6},{8,9},{9,8},{10,11... | collective-permute-start | bytes 1474568 | tf_op jit(solution)/shard_map/ppermute | solution.py:331
  43.4 5.2 %shard_map.116 = (f32[784,128]{1,0:T(8,128)S(1)}, bf16[784,128]{1,0:T(8,128)(2,1)S(1)}, bf16[784,128]{1,0:T(8,128)(2,1)S(1)}, bf16[784,128]{1,0:T(8,128)(2,1)S(1)}) custom-call(f32[1568,256]{1,0:T(8,128)S(1)} %get-tuple-element.47.refs_0_, s32[8,256]{1,0:T(8,128)S(1)} %get-tuple-element.48.refs_1_, bf16[3712,256]{1,0:T(8,128)(2,1)S(1)} %get-tuple-element.49.refs_2_, ...), custom_call_target="tpu_custom_call" | custom-call | flops 8000000000 | bytes 100000 | tf_op jit(solution)/shard_map/pallas_call | solution.py:317
  48.6 3.1 %collective-permute-done.15.came_ref = bf16[8,224,128]{2,1,0:T(8,128)(2,1)S(1)} collective-permute-done((bf16[8,224,128]{2,1,0:T(8,128)(2,1)S(1)}, bf16[8,224,128]{2,1,0:T(8,128)(2,1)S(1)}, u32[]{:S(2)}, u32[]{:S(2)}) %collective-permute-start.15) | collective-permute-done | bytes 458784 | tf_op jit(solution)/shard_map/ppermute | solution.py:331
  51.9 2.3 %collective-permute-done.10.came_ref = bf16[8,240,128]{2,1,0:T(8,128)(2,1)S(1)} collective-permute-done((bf16[8,240,128]{2,1,0:T(8,128)(2,1)S(1)}, bf16[8,240,128]{2,1,0:T(8,128)(2,1)S(1)}, u32[]{:S(2)}, u32[]{:S(2)}) %collective-permute-start.10) | collective-permute-done | bytes 491552 | tf_op jit(solution)/shard_map/ppermute | solution.py:331
  54.4 1.4 %collective-permute-start.11 = (bf16[4,240,128]{2,1,0:T(8,128)(2,1)S(1)}, bf16[4,240,128]{2,1,0:T(8,128)(2,1)S(1)}, u32[]{:S(2)}, u32[]{:S(2)}) collective-permute-start(bf16[4,240,128]{2,1,0:T(8,128)(2,1)S(1)} %get-tuple-element.59), channel_id=1, source_target_pairs={{0,2},{1,3},{2,0},{3,1},{4,6},{5,7},{6,4},{7,5},{8,10},{9,11},{10,... | collective-permute-start | bytes 737288 | tf_op jit(solution)/shard_map/ppermute | solution.py:331
  55.9 1.3 %collective-permute-start.21 = (bf16[4,224,128]{2,1,0:T(8,128)(2,1)S(1)}, bf16[4,224,128]{2,1,0:T(8,128)(2,1)S(1)}, u32[]{:S(2)}, u32[]{:S(2)}) collective-permute-start(bf16[4,224,128]{2,1,0:T(8,128)(2,1)S(1)} %get-tuple-element.79), channel_id=1, source_target_pairs={{0,1},{1,0},{2,3},{3,2},{4,5},{5,4},{6,7},{7,6},{8,9},{9,8},{10,11... | collective-permute-start | bytes 688136 | tf_op jit(solution)/shard_map/ppermute | solution.py:331
  57.1 1.6 %collective-permute-done.16.came_ref = bf16[4,224,128]{2,1,0:T(8,128)(2,1)S(1)} collective-permute-done((bf16[4,224,128]{2,1,0:T(8,128)(2,1)S(1)}, bf16[4,224,128]{2,1,0:T(8,128)(2,1)S(1)}, u32[]{:S(2)}, u32[]{:S(2)}) %collective-permute-start.16) | collective-permute-done | bytes 229408 | tf_op jit(solution)/shard_map/ppermute | solution.py:331
  59.4 1.9 %collective-permute-done.11.came_ref = bf16[4,240,128]{2,1,0:T(8,128)(2,1)S(1)} collective-permute-done((bf16[4,240,128]{2,1,0:T(8,128)(2,1)S(1)}, bf16[4,240,128]{2,1,0:T(8,128)(2,1)S(1)}, u32[]{:S(2)}, u32[]{:S(2)}) %collective-permute-start.11) | collective-permute-done | bytes 245792 | tf_op jit(solution)/shard_map/ppermute | solution.py:331
  61.3 1.5 %collective-permute-start.12 = (bf16[2,240,128]{2,1,0:T(8,128)(2,1)S(1)}, bf16[2,240,128]{2,1,0:T(8,128)(2,1)S(1)}, u32[]{:S(2)}, u32[]{:S(2)}) collective-permute-start(bf16[2,240,128]{2,1,0:T(8,128)(2,1)S(1)} %get-tuple-element.61), channel_id=1, source_target_pairs={{0,4},{1,5},{2,6},{3,7},{4,0},{5,1},{6,2},{7,3},{8,12},{9,13},{10,... | collective-permute-start | bytes 368648 | tf_op jit(solution)/shard_map/ppermute | solution.py:331
  63.4 1.4 %collective-permute-start.8 = (bf16[784,128]{1,0:T(8,128)(2,1)S(1)}, bf16[784,128]{1,0:T(8,128)(2,1)S(1)}, u32[]{:S(2)}, u32[]{:S(2)}) collective-permute-start(bf16[784,128]{1,0:T(8,128)(2,1)S(1)} %get-tuple-element.53), channel_id=1, source_target_pairs={{0,5},{1,4},{2,7},{3,6},{4,1},{5,0},{6,3},{7,2},{8,13},{9,12},{10,... | collective-permute-start | bytes 602120 | tf_op jit(solution)/shard_map/ppermute | solution.py:331
  64.8 1.5 %collective-permute-start.6 = (bf16[784,128]{1,0:T(8,128)(2,1)S(1)}, bf16[784,128]{1,0:T(8,128)(2,1)S(1)}, u32[]{:S(2)}, u32[]{:S(2)}) collective-permute-start(bf16[784,128]{1,0:T(8,128)(2,1)S(1)} %get-tuple-element.51.outs_0_), channel_id=1, source_target_pairs={{0,1},{1,0},{2,3},{3,2},{4,5},{5,4},{6,7},{7,6},{8,9},{9,8},{10,11... | collective-permute-start | bytes 602120 | tf_op jit(solution)/shard_map/ppermute | solution.py:331
  66.3 1.7 %collective-permute-start.22 = (bf16[2,224,128]{2,1,0:T(8,128)(2,1)S(1)}, bf16[2,224,128]{2,1,0:T(8,128)(2,1)S(1)}, u32[]{:S(2)}, u32[]{:S(2)}) collective-permute-start(bf16[2,224,128]{2,1,0:T(8,128)(2,1)S(1)} %get-tuple-element.81), channel_id=1, source_target_pairs={{0,2},{1,3},{2,0},{3,1},{4,6},{5,7},{6,4},{7,5},{8,10},{9,11},{10,... | collective-permute-start | bytes 344072 | tf_op jit(solution)/shard_map/ppermute | solution.py:331
  68.1 2.3 %collective-permute-start.18 = (bf16[1,224,128]{2,1,0:T(8,128)(2,1)S(1)}, bf16[1,224,128]{2,1,0:T(8,128)(2,1)S(1)}, u32[]{:S(2)}, u32[]{:S(2)}) collective-permute-start(bf16[1,224,128]{2,1,0:T(8,128)(2,1)S(1)} %get-tuple-element.73), channel_id=1, source_target_pairs={{0,8},{1,9},{2,10},{3,11},{4,12},{5,13},{6,14},{7,15},{8,0},{9,1},... | collective-permute-start | bytes 172040 | tf_op jit(solution)/shard_map/ppermute | solution.py:331
  71.2 2.0 %collective-permute-start.13 = (bf16[1,240,128]{2,1,0:T(8,128)(2,1)S(1)}, bf16[1,240,128]{2,1,0:T(8,128)(2,1)S(1)}, u32[]{:S(2)}, u32[]{:S(2)}) collective-permute-start(bf16[1,240,128]{2,1,0:T(8,128)(2,1)S(1)} %get-tuple-element.63), channel_id=1, source_target_pairs={{0,8},{1,9},{2,10},{3,11},{4,12},{5,13},{6,14},{7,15},{8,0},{9,1},... | collective-permute-start | bytes 184328 | tf_op jit(solution)/shard_map/ppermute | solution.py:331
  73.2 1.2 %collective-permute-done.18.came_ref = bf16[1,224,128]{2,1,0:T(8,128)(2,1)S(1)} collective-permute-done((bf16[1,224,128]{2,1,0:T(8,128)(2,1)S(1)}, bf16[1,224,128]{2,1,0:T(8,128)(2,1)S(1)}, u32[]{:S(2)}, u32[]{:S(2)}) %collective-permute-start.18) | collective-permute-done | bytes 57376 | tf_op jit(solution)/shard_map/ppermute | solution.py:331
  74.4 3.4 %collective-permute-start.23 = (bf16[1,224,128]{2,1,0:T(8,128)(2,1)S(1)}, bf16[1,224,128]{2,1,0:T(8,128)(2,1)S(1)}, u32[]{:S(2)}, u32[]{:S(2)}) collective-permute-start(bf16[1,224,128]{2,1,0:T(8,128)(2,1)S(1)} %get-tuple-element.83), channel_id=1, source_target_pairs={{0,8},{1,9},{2,10},{3,11},{4,12},{5,13},{6,14},{7,15},{8,0},{9,1},... | collective-permute-start | bytes 172040 | tf_op jit(solution)/shard_map/ppermute | solution.py:331
  77.8 2.1 %collective-permute-done.23.came_ref = bf16[1,224,128]{2,1,0:T(8,128)(2,1)S(1)} collective-permute-done((bf16[1,224,128]{2,1,0:T(8,128)(2,1)S(1)}, bf16[1,224,128]{2,1,0:T(8,128)(2,1)S(1)}, u32[]{:S(2)}, u32[]{:S(2)}) %collective-permute-start.23) | collective-permute-done | bytes 57376 | tf_op jit(solution)/shard_map/ppermute | solution.py:331
  80.7 0.8 add_convert_fusion
  82.0 1.4 %shard_map.132 = f32[1368,128]{1,0:T(8,128)} custom-call(s32[2]{0:T(128)S(1)} %pad_add_fusion.1.refs_0_.me_ref, f32[240,128]{1,0:T(8,128)S(1)} %shard_map.121.refs_0_, f32[224,128]{1,0:T(8,128)S(1)} %shard_map.126.refs_1_, f32[224,128]{1,0:T(8,128)S(1)} %shard_map.131.refs_2_, f32[240,128]{1,0:T(8,128)S(1)} %collective-permute-done.24.refs_3_, ...), custom_call_target="tpu_custom_call" | custom-call | flops 1000000 | bytes 100000 | tf_op jit(solution)/shard_map/pallas_call | solution.py:317
  (57 shorter events, 8.2 us)
Async XLA Ops:
  1.3 0.9 %copy-start.2 = (bf16[16,49,128]{2,0,1:T(8,128)(2,1)S(1)}, bf16[16,49,128]{2,0,1:T(8,128)(2,1)}, u32[]{:S(2)}) copy-start(bf16[16,49,128]{2,0,1:T(8,128)(2,1)} %param.10) | copy-start | bytes 602116
  2.6 16.4 %collective-permute-start.2 = (bf16[800,128]{1,0:T(8,128)(2,1)S(1)}, bf16[800,128]{1,0:T(8,128)(2,1)S(1)}, u32[]{:S(2)}, u32[]{:S(2)}) collective-permute-start(bf16[800,128]{1,0:T(8,128)(2,1)S(1)} %shard_map.113.refs_2_), channel_id=1, source_target_pairs={{0,2},{1,3},{2,0},{3,1},{4,6},{5,7},{6,4},{7,5},{8,10},{9,11},{10,... | collective-permute-start | bytes 614408 | tf_op jit(solution)/shard_map/ppermute | solution.py:331
  5.5 13.5 %collective-permute-start = (bf16[800,128]{1,0:T(8,128)(2,1)S(1)}, bf16[800,128]{1,0:T(8,128)(2,1)S(1)}, u32[]{:S(2)}, u32[]{:S(2)}) collective-permute-start(bf16[800,128]{1,0:T(8,128)(2,1)S(1)} %shard_map.113.refs_2_), channel_id=1, source_target_pairs={{0,8},{1,9},{2,10},{3,11},{4,12},{5,13},{6,14},{7,15},{8,0},{9,1},... | collective-permute-start | bytes 614408 | tf_op jit(solution)/shard_map/ppermute | solution.py:331
  8.1 6.4 %collective-permute-start.3 = (bf16[784,128]{1,0:T(8,128)(2,1)}, bf16[784,128]{1,0:T(8,128)(2,1)S(1)}, u32[]{:S(2)}, u32[]{:S(2)}) collective-permute-start(bf16[784,128]{1,0:T(8,128)(2,1)} %bitcast.18), channel_id=1, source_target_pairs={{0,1},{1,0},{2,3},{3,2},{4,5},{5,4},{6,7},{7,6},{8,9},{9,8},{10,11... | collective-permute-start | bytes 602120 | tf_op jit(solution)/shard_map/ppermute | solution.py:331
  9.6 9.4 %collective-permute-start.1 = (bf16[784,128]{1,0:T(8,128)(2,1)}, bf16[784,128]{1,0:T(8,128)(2,1)S(1)}, u32[]{:S(2)}, u32[]{:S(2)}) collective-permute-start(bf16[784,128]{1,0:T(8,128)(2,1)} %bitcast.19), channel_id=1, source_target_pairs={{0,4},{1,5},{2,6},{3,7},{4,0},{5,1},{6,2},{7,3},{8,12},{9,13},{10,... | collective-permute-start | bytes 602120 | tf_op jit(solution)/shard_map/ppermute | solution.py:331
  19.0 1.1 %copy-start = (bf16[256,29,49]{0,1,2:T(8,128)(2,1)S(1)}, bf16[256,29,49]{0,1,2:T(8,128)(2,1)}, u32[]{:S(2)}) copy-start(bf16[256,29,49]{0,1,2:T(8,128)(2,1)} %param.12) | copy-start | bytes 2182660
  21.2 6.2 %collective-permute-start.4 = (bf16[800,128]{1,0:T(8,128)(2,1)S(1)}, bf16[800,128]{1,0:T(8,128)(2,1)S(1)}, u32[]{:S(2)}, u32[]{:S(2)}) collective-permute-start(bf16[800,128]{1,0:T(8,128)(2,1)S(1)} %get-tuple-element.44.refs_4_), channel_id=1, source_target_pairs={{0,2},{1,3},{2,0},{3,1},{4,6},{5,7},{6,4},{7,5},{8,10},{9,11},{10,... | collective-permute-start | bytes 614408 | tf_op jit(solution)/shard_map/ppermute | solution.py:331
  21.7 5.7 %collective-permute-start.5 = (bf16[784,128]{1,0:T(8,128)(2,1)S(1)}, bf16[784,128]{1,0:T(8,128)(2,1)S(1)}, u32[]{:S(2)}, u32[]{:S(2)}) collective-permute-start(bf16[784,128]{1,0:T(8,128)(2,1)S(1)} %get-tuple-element.46.refs_8_), channel_id=1, source_target_pairs={{0,1},{1,0},{2,3},{3,2},{4,5},{5,4},{6,7},{7,6},{8,9},{9,8},{10,11... | collective-permute-start | bytes 602120 | tf_op jit(solution)/shard_map/ppermute | solution.py:331
  35.0 6.1 %collective-permute-start.9 = (bf16[16,240,128]{2,1,0:T(8,128)(2,1)S(1)}, bf16[16,240,128]{2,1,0:T(8,128)(2,1)S(1)}, u32[]{:S(2)}, u32[]{:S(2)}) collective-permute-start(bf16[16,240,128]{2,1,0:T(8,128)(2,1)S(1)} %get-tuple-element.55), channel_id=1, source_target_pairs={{0,16},{16,0},{1,17},{17,1},{2,18},{18,2},{3,19},{19,3},{4,20},{20... | collective-permute-start | bytes 2949128 | tf_op jit(solution)/shard_map/ppermute | solution.py:335
  35.0 3.9 %collective-permute-start.14 = (bf16[16,224,128]{2,1,0:T(8,128)(2,1)S(1)}, bf16[16,224,128]{2,1,0:T(8,128)(2,1)S(1)}, u32[]{:S(2)}, u32[]{:S(2)}) collective-permute-start(bf16[16,224,128]{2,1,0:T(8,128)(2,1)S(1)} %get-tuple-element.65), channel_id=1, source_target_pairs={{0,16},{16,0},{1,17},{17,1},{2,18},{18,2},{3,19},{19,3},{4,20},{20... | collective-permute-start | bytes 2752520 | tf_op jit(solution)/shard_map/ppermute | solution.py:335
  35.5 5.2 %collective-permute-start.19 = (bf16[16,224,128]{2,1,0:T(8,128)(2,1)S(1)}, bf16[16,224,128]{2,1,0:T(8,128)(2,1)S(1)}, u32[]{:S(2)}, u32[]{:S(2)}) collective-permute-start(bf16[16,224,128]{2,1,0:T(8,128)(2,1)S(1)} %get-tuple-element.75), channel_id=1, source_target_pairs={{0,16},{16,0},{1,17},{17,1},{2,18},{18,2},{3,19},{19,3},{4,20},{20... | collective-permute-start | bytes 2752520 | tf_op jit(solution)/shard_map/ppermute | solution.py:335
  39.1 12.6 %collective-permute-start.15 = (bf16[8,224,128]{2,1,0:T(8,128)(2,1)S(1)}, bf16[8,224,128]{2,1,0:T(8,128)(2,1)S(1)}, u32[]{:S(2)}, u32[]{:S(2)}) collective-permute-start(bf16[8,224,128]{2,1,0:T(8,128)(2,1)S(1)} %get-tuple-element.67), channel_id=1, source_target_pairs={{0,2},{1,3},{2,0},{3,1},{4,6},{5,7},{6,4},{7,5},{8,10},{9,11},{10,... | collective-permute-start | bytes 1376264 | tf_op jit(solution)/shard_map/ppermute | solution.py:331
  40.7 2.0 %copy-start.4 = (bf16[2,640,640]{2,1,0:T(8,128)(2,1)S(1)}, bf16[2,640,640]{2,1,0:T(8,128)(2,1)}, u32[]{:S(2)}) copy-start(bf16[2,640,640]{2,1,0:T(8,128)(2,1)} %refs_5_.1) | copy-start | bytes 4915204
  40.7 2.0 %copy-start.5 = (bf16[896,896]{1,0:T(8,128)(2,1)S(1)}, bf16[896,896]{1,0:T(8,128)(2,1)}, u32[]{:S(2)}) copy-start(bf16[896,896]{1,0:T(8,128)(2,1)} %refs_3_.1) | copy-start | bytes 4816900
  40.9 2.5 %copy-start.3 = (bf16[2,768,768]{2,1,0:T(8,128)(2,1)S(1)}, bf16[2,768,768]{2,1,0:T(8,128)(2,1)}, u32[]{:S(2)}) copy-start(bf16[2,768,768]{2,1,0:T(8,128)(2,1)} %refs_4_.1) | copy-start | bytes 7077892
  41.0 14.8 %collective-permute-start.20 = (bf16[8,224,128]{2,1,0:T(8,128)(2,1)S(1)}, bf16[8,224,128]{2,1,0:T(8,128)(2,1)S(1)}, u32[]{:S(2)}, u32[]{:S(2)}) collective-permute-start(bf16[8,224,128]{2,1,0:T(8,128)(2,1)S(1)} %get-tuple-element.77), channel_id=1, source_target_pairs={{0,4},{1,5},{2,6},{3,7},{4,0},{5,1},{6,2},{7,3},{8,12},{9,13},{10,... | collective-permute-start | bytes 1376264 | tf_op jit(solution)/shard_map/ppermute | solution.py:331
  41.2 13.0 %collective-permute-start.10 = (bf16[8,240,128]{2,1,0:T(8,128)(2,1)S(1)}, bf16[8,240,128]{2,1,0:T(8,128)(2,1)S(1)}, u32[]{:S(2)}, u32[]{:S(2)}) collective-permute-start(bf16[8,240,128]{2,1,0:T(8,128)(2,1)S(1)} %get-tuple-element.57), channel_id=1, source_target_pairs={{0,1},{1,0},{2,3},{3,2},{4,5},{5,4},{6,7},{7,6},{8,9},{9,8},{10,11... | collective-permute-start | bytes 1474568 | tf_op jit(solution)/shard_map/ppermute | solution.py:331
  51.8 6.9 %collective-permute-start.16 = (bf16[4,224,128]{2,1,0:T(8,128)(2,1)S(1)}, bf16[4,224,128]{2,1,0:T(8,128)(2,1)S(1)}, u32[]{:S(2)}, u32[]{:S(2)}) collective-permute-start(bf16[4,224,128]{2,1,0:T(8,128)(2,1)S(1)} %get-tuple-element.69), channel_id=1, source_target_pairs={{0,4},{1,5},{2,6},{3,7},{4,0},{5,1},{6,2},{7,3},{8,12},{9,13},{10,... | collective-permute-start | bytes 688136 | tf_op jit(solution)/shard_map/ppermute | solution.py:331
  54.4 6.9 %collective-permute-start.11 = (bf16[4,240,128]{2,1,0:T(8,128)(2,1)S(1)}, bf16[4,240,128]{2,1,0:T(8,128)(2,1)S(1)}, u32[]{:S(2)}, u32[]{:S(2)}) collective-permute-start(bf16[4,240,128]{2,1,0:T(8,128)(2,1)S(1)} %get-tuple-element.59), channel_id=1, source_target_pairs={{0,2},{1,3},{2,0},{3,1},{4,6},{5,7},{6,4},{7,5},{8,10},{9,11},{10,... | collective-permute-start | bytes 737288 | tf_op jit(solution)/shard_map/ppermute | solution.py:331
  55.9 8.9 %collective-permute-start.21 = (bf16[4,224,128]{2,1,0:T(8,128)(2,1)S(1)}, bf16[4,224,128]{2,1,0:T(8,128)(2,1)S(1)}, u32[]{:S(2)}, u32[]{:S(2)}) collective-permute-start(bf16[4,224,128]{2,1,0:T(8,128)(2,1)S(1)} %get-tuple-element.79), channel_id=1, source_target_pairs={{0,1},{1,0},{2,3},{3,2},{4,5},{5,4},{6,7},{7,6},{8,9},{9,8},{10,11... | collective-permute-start | bytes 688136 | tf_op jit(solution)/shard_map/ppermute | solution.py:331
  58.8 7.6 %collective-permute-start.17 = (bf16[2,224,128]{2,1,0:T(8,128)(2,1)S(1)}, bf16[2,224,128]{2,1,0:T(8,128)(2,1)S(1)}, u32[]{:S(2)}, u32[]{:S(2)}) collective-permute-start(bf16[2,224,128]{2,1,0:T(8,128)(2,1)S(1)} %get-tuple-element.71), channel_id=1, source_target_pairs={{0,1},{1,0},{2,3},{3,2},{4,5},{5,4},{6,7},{7,6},{8,9},{9,8},{10,11... | collective-permute-start | bytes 344072 | tf_op jit(solution)/shard_map/ppermute | solution.py:331
  61.3 6.8 %collective-permute-start.12 = (bf16[2,240,128]{2,1,0:T(8,128)(2,1)S(1)}, bf16[2,240,128]{2,1,0:T(8,128)(2,1)S(1)}, u32[]{:S(2)}, u32[]{:S(2)}) collective-permute-start(bf16[2,240,128]{2,1,0:T(8,128)(2,1)S(1)} %get-tuple-element.61), channel_id=1, source_target_pairs={{0,4},{1,5},{2,6},{3,7},{4,0},{5,1},{6,2},{7,3},{8,12},{9,13},{10,... | collective-permute-start | bytes 368648 | tf_op jit(solution)/shard_map/ppermute | solution.py:331
  62.8 17.8 %collective-permute-start.7 = (bf16[784,128]{1,0:T(8,128)(2,1)S(1)}, bf16[784,128]{1,0:T(8,128)(2,1)S(1)}, u32[]{:S(2)}, u32[]{:S(2)}) collective-permute-start(bf16[784,128]{1,0:T(8,128)(2,1)S(1)} %get-tuple-element.52), channel_id=1, source_target_pairs={{0,4},{1,5},{2,6},{3,7},{4,0},{5,1},{6,2},{7,3},{8,12},{9,13},{10,... | collective-permute-start | bytes 602120 | tf_op jit(solution)/shard_map/ppermute | solution.py:331
  63.4 17.3 %collective-permute-start.8 = (bf16[784,128]{1,0:T(8,128)(2,1)S(1)}, bf16[784,128]{1,0:T(8,128)(2,1)S(1)}, u32[]{:S(2)}, u32[]{:S(2)}) collective-permute-start(bf16[784,128]{1,0:T(8,128)(2,1)S(1)} %get-tuple-element.53), channel_id=1, source_target_pairs={{0,5},{1,4},{2,7},{3,6},{4,1},{5,0},{6,3},{7,2},{8,13},{9,12},{10,... | collective-permute-start | bytes 602120 | tf_op jit(solution)/shard_map/ppermute | solution.py:331
  64.8 15.9 %collective-permute-start.6 = (bf16[784,128]{1,0:T(8,128)(2,1)S(1)}, bf16[784,128]{1,0:T(8,128)(2,1)S(1)}, u32[]{:S(2)}, u32[]{:S(2)}) collective-permute-start(bf16[784,128]{1,0:T(8,128)(2,1)S(1)} %get-tuple-element.51.outs_0_), channel_id=1, source_target_pairs={{0,1},{1,0},{2,3},{3,2},{4,5},{5,4},{6,7},{7,6},{8,9},{9,8},{10,11... | collective-permute-start | bytes 602120 | tf_op jit(solution)/shard_map/ppermute | solution.py:331
  66.3 4.9 %collective-permute-start.22 = (bf16[2,224,128]{2,1,0:T(8,128)(2,1)S(1)}, bf16[2,224,128]{2,1,0:T(8,128)(2,1)S(1)}, u32[]{:S(2)}, u32[]{:S(2)}) collective-permute-start(bf16[2,224,128]{2,1,0:T(8,128)(2,1)S(1)} %get-tuple-element.81), channel_id=1, source_target_pairs={{0,2},{1,3},{2,0},{3,1},{4,6},{5,7},{6,4},{7,5},{8,10},{9,11},{10,... | collective-permute-start | bytes 344072 | tf_op jit(solution)/shard_map/ppermute | solution.py:331
  68.1 6.3 %collective-permute-start.18 = (bf16[1,224,128]{2,1,0:T(8,128)(2,1)S(1)}, bf16[1,224,128]{2,1,0:T(8,128)(2,1)S(1)}, u32[]{:S(2)}, u32[]{:S(2)}) collective-permute-start(bf16[1,224,128]{2,1,0:T(8,128)(2,1)S(1)} %get-tuple-element.73), channel_id=1, source_target_pairs={{0,8},{1,9},{2,10},{3,11},{4,12},{5,13},{6,14},{7,15},{8,0},{9,1},... | collective-permute-start | bytes 172040 | tf_op jit(solution)/shard_map/ppermute | solution.py:331
  71.2 8.8 %collective-permute-start.13 = (bf16[1,240,128]{2,1,0:T(8,128)(2,1)S(1)}, bf16[1,240,128]{2,1,0:T(8,128)(2,1)S(1)}, u32[]{:S(2)}, u32[]{:S(2)}) collective-permute-start(bf16[1,240,128]{2,1,0:T(8,128)(2,1)S(1)} %get-tuple-element.63), channel_id=1, source_target_pairs={{0,8},{1,9},{2,10},{3,11},{4,12},{5,13},{6,14},{7,15},{8,0},{9,1},... | collective-permute-start | bytes 184328 | tf_op jit(solution)/shard_map/ppermute | solution.py:331
  74.4 5.6 %collective-permute-start.23 = (bf16[1,224,128]{2,1,0:T(8,128)(2,1)S(1)}, bf16[1,224,128]{2,1,0:T(8,128)(2,1)S(1)}, u32[]{:S(2)}, u32[]{:S(2)}) collective-permute-start(bf16[1,224,128]{2,1,0:T(8,128)(2,1)S(1)} %get-tuple-element.83), channel_id=1, source_target_pairs={{0,8},{1,9},{2,10},{3,11},{4,12},{5,13},{6,14},{7,15},{8,0},{9,1},... | collective-permute-start | bytes 172040 | tf_op jit(solution)/shard_map/ppermute | solution.py:331
  80.0 1.5 %collective-permute-start.25 = (f32[224,128]{1,0:T(8,128)S(1)}, f32[224,128]{1,0:T(8,128)S(1)}, u32[]{:S(2)}, u32[]{:S(2)}) collective-permute-start(f32[224,128]{1,0:T(8,128)S(1)} %shard_map.126.refs_1_), channel_id=1, source_target_pairs={{0,16},{16,0},{1,17},{17,1},{2,18},{18,2},{3,19},{19,3},{4,20},{20... | collective-permute-start | bytes 344072 | tf_op jit(solution)/shard_map/ppermute | solution.py:335
  80.0 1.5 %collective-permute-start.26 = (f32[224,128]{1,0:T(8,128)S(1)}, f32[224,128]{1,0:T(8,128)S(1)}, u32[]{:S(2)}, u32[]{:S(2)}) collective-permute-start(f32[224,128]{1,0:T(8,128)S(1)} %shard_map.131.refs_2_), channel_id=1, source_target_pairs={{0,16},{16,0},{1,17},{17,1},{2,18},{18,2},{3,19},{19,3},{4,20},{20... | collective-permute-start | bytes 344072 | tf_op jit(solution)/shard_map/ppermute | solution.py:335
  80.6 1.4 %collective-permute-start.24 = (f32[240,128]{1,0:T(8,128)S(1)}, f32[240,128]{1,0:T(8,128)S(1)}, u32[]{:S(2)}, u32[]{:S(2)}) collective-permute-start(f32[240,128]{1,0:T(8,128)S(1)} %shard_map.121.refs_0_), channel_id=1, source_target_pairs={{0,16},{16,0},{1,17},{17,1},{2,18},{18,2},{3,19},{19,3},{4,20},{20... | collective-permute-start | bytes 368648 | tf_op jit(solution)/shard_map/ppermute | solution.py:335
  (1 other events, 0.9 us)

commit v4 on v3

--- a/solution.py
+++ b/solution.py
@@ -58,8 +58,9 @@
 
 
 def payload_kernel(parts, capacity, edge_ref, node_ref, out_ref):
-    edges = edge_ref.shape[1]
+    rows, edges = node_ref.shape[0], edge_ref.shape[1]
     part, src, dst, angle = (edge_ref[i : i + 1, :] for i in range(4))
+    out_ref[0:rows, :] = node_ref[...]
     padded = -(-parts // 16) * 16
     part_hot = hot(iota((padded, edges), 0) == part)
     before = hot(iota((edges, edges), 0) < iota((edges, edges), 1))
@@ -71,8 +72,6 @@
     fields = jnp.where(row == 0, angle + 1, jnp.where(row == 1, src, jnp.where(row == 2, dst, 0)))
     table = nt(fields.astype(jnp.float32).astype(jnp.bfloat16), place.astype(jnp.bfloat16))
     half = out_ref.shape[1]
-    rows = node_ref.shape[0]
-    out_ref[0:rows, :] = node_ref[...]
     out_ref[rows : rows + 16, :] = jnp.concatenate([table[:, :half], table[:, half:]], axis=0).astype(
         jnp.bfloat16
     )
@@ -115,13 +114,17 @@
     rot_ref[...] = nn(wide_ref[...].reshape(coeffs * rows, angles), angle_hot)
 
 
-def middle_kernel(far, near, *refs):
-    wigner_ref, own_ref = refs[far + near : far + near + 2]
-    wide_ref, copy_ref = refs[-2:]
+def widen_kernel(wigner_ref, own_ref, wide_ref, copy_ref):
     kept = wigner_ref.shape[1]
-    wide_ref[:, kept:, :] = jnp.zeros((wide_ref.shape[0], wide_ref.shape[1] - kept, wide_ref.shape[2]), wide_ref.dtype)
+    wide_ref[:, kept:, :] = jnp.zeros(
+        (wide_ref.shape[0], wide_ref.shape[1] - kept, wide_ref.shape[2]), wide_ref.dtype
+    )
     wide_ref[:, 0:kept, :] = wigner_ref[...]
     copy_ref[...] = own_ref[...]
+
+
+def pass_kernel(*refs):
+    pass
 
 
 def fill_spread(spread_ref, rot_ref, atom_hot, degree, row):
@@ -166,16 +169,21 @@
 
 def message_kernel(plan, *refs):
     n_dst = plan.n_dst
-    rot_ref, atom_ref, rotated_ref, w_zero, w_one, w_two = refs[:6]
-    part_refs = refs[6 : 6 + n_dst]
-    spread_ref, flat_ref, message_ref, sum_ref = refs[6 + n_dst :]
-    channels = sum_ref.shape[1]
-    flat_ref[...] = rotated_ref[...].T
+    rot_ref, atom_ref, refs = refs[0], refs[1], refs[2:]
+    left_refs, (w_zero, w_one, w_two), refs = refs[: MMAX + 1], refs[MMAX + 1 : MMAX + 4], refs[MMAX + 4 :]
+    part_refs = refs[:n_dst]
+    spread_ref, flat_ref, message_ref, sum_ref = refs[n_dst:]
+    channels, slots = sum_ref.shape[1], plan.slots
 
     def columns(start, length):
         return slice(start * channels, (start + length) * channels)
 
     bounds = group_bounds()
+    for number, bound in enumerate(bounds):
+        side = (number + 1) % 2 if number else 0
+        flat_ref[:, columns(*bound)] = left_refs[(number + 1) // 2][
+            :, side * slots : (side + 1) * slots
+        ].T
     message_ref[:, columns(*bounds[0])] = nn(flat_ref[:, columns(*bounds[0])], w_zero[...]).astype(
         jnp.bfloat16
     )
@@ -205,19 +213,17 @@
             ] = piece.reshape((2 * degree + 1) * plan.atoms, channels).astype(part_refs[place].dtype)
 
 
-def gram_kernel(plan, half_rows, sizes, *refs):
+def rotate_kernel(plan, lay, *refs):
     n_src, n_dst = plan.n_src, plan.n_dst
-    me_ref, wide_ref, refs = refs[0], refs[1], refs[2:]
+    wide_ref, refs = refs[0], refs[1:]
     node_blocks, refs = refs[:n_src], refs[n_src:]
     pull_blocks, refs = refs[:n_dst], refs[n_dst:]
-    rot_ref, atom_ref, rotated_ref, refs = refs[0], refs[1], refs[2], refs[3:]
-    out_refs, refs = refs[: 2 * len(sizes)], refs[2 * len(sizes) :]
-    node_ref, pull_ref, spread_ref = refs[:3]
-    left_refs, right_refs, refs = refs[3 : 4 + MMAX], refs[4 + MMAX : 5 + 2 * MMAX], refs[5 + 2 * MMAX :]
-    turned_refs, grad_ref = refs[:MMAX], refs[MMAX]
+    rot_ref, atom_ref, refs = refs[0], refs[1], refs[2:]
+    left_refs, right_refs = refs[: MMAX + 1], refs[MMAX + 1 : 3 * MMAX + 2]
+    out_refs, refs = refs[3 * MMAX + 2 :][: 2 * len(lay.sizes)], refs[3 * MMAX + 2 + 2 * len(lay.sizes) :]
+    node_ref, pull_ref, spread_ref, grad_ref = refs
     channels, slots = node_ref.shape[2], plan.slots
-    me, core = me_ref[0], me_ref[1]
-    angle, src, dst = slot_codes(plan, me, node_blocks)
+    angle, src, dst = slot_codes(plan, lax.axis_index("graph"), node_blocks)
     atom_ref[...] = jnp.broadcast_to(dst, atom_ref.shape)
     fill_rotation(rot_ref, wide_ref, angle)
     fill_nodes(node_ref, node_blocks, plan.atoms)
@@ -225,7 +231,6 @@
 
     def put_rotated(row, value):
         azimuth, side, place = place_of(row)
-        rotated_ref[row * channels : (row + 1) * channels, :] = value
         left_refs[azimuth][
             place * channels : (place + 1) * channels, side * slots : (side + 1) * slots
         ] = value
@@ -235,40 +240,63 @@
         lines = slice(place * channels, (place + 1) * channels)
         right_refs[azimuth][lines, side * slots : (side + 1) * slots] = value
         if azimuth > 0:
-            turned_refs[azimuth - 1][lines, (1 - side) * slots : (2 - side) * slots] = (
+            right_refs[MMAX + azimuth][lines, (1 - side) * slots : (2 - side) * slots] = (
                 value if side == 1 else -value
             )
 
     rotate_all(put_rotated, node_ref, spread_ref, rot_ref, atom_hots(n_src * plan.atoms, src))
     rotate_all(put_pulled, pull_ref, spread_ref, rot_ref, atom_hots(n_dst * plan.atoms, dst))
-
+    gram(plan, lay, 0, left_refs, right_refs, out_refs, grad_ref)
+
+
+def gram_kernel(plan, lay, *refs):
+    left_refs, right_refs, refs = refs[: MMAX + 1], refs[MMAX + 1 : 3 * MMAX + 2], refs[3 * MMAX + 2 :]
+    gram(plan, lay, 1, left_refs, right_refs, refs[:-1], refs[-1])
+
+
+class Layout:
+    margin = 128
+
+    def __init__(self, plan, share):
+        self.share = share
+        self.half_rows = -(-(-(-share // 2)) // 16) * 16
+        tiles = self.half_rows // 16
+        self.sizes = [16 * ((tiles + STREAMS - 1 - k) // STREAMS) for k in range(STREAMS)]
+        self.parts = plan.parts // 2
+        self.rows = self.parts * share
+
+
+def gram(plan, lay, number, left_refs, right_refs, out_refs, grad_ref):
+    channels = grad_ref.shape[1]
+    low, high = number * lay.rows, (number + 1) * lay.rows
     base = 0
     for azimuth in range(MMAX + 1):
         length = LMAX + 1 - azimuth
-        for right in [right_refs[azimuth], *turned_refs[azimuth - 1 : azimuth]] if azimuth else right_refs[:1]:
-            for first in range(0, length, 2):
-                width = min(2, length - first)
-                block = nt(
-                    left_refs[azimuth][...], right[first * channels : (first + width) * channels, :]
-                )
-                for step in range(width):
-                    grad_ref[pl.ds(base + first + step, length * channels, stride=length), :] = block[
-                        :, step * channels : (step + 1) * channels
-                    ]
+        for right in [right_refs[azimuth]] + ([right_refs[MMAX + azimuth]] if azimuth else []):
+            top = min(length * channels, -(-(high - base) // length // 16) * 16)
+            begin = max(0, (low - base) // length // 16 * 16)
+            if begin < top:
+                left = left_refs[azimuth][begin:top, :]
+                for first in range(0, length, 2):
+                    width = min(2, length - first)
+                    block = nt(left, right[first * channels : (first + width) * channels, :])
+                    for step in range(width):
+                        start = base - low + lay.margin + begin * length + first + step
+                        grad_ref[pl.ds(start, top - begin, stride=length), :] = block[
+                            :, step * channels : (step + 1) * channels
+                        ]
             base = base + length * length * channels
-    rows = grad_ref.shape[0] // plan.parts
-    shift = rows - half_rows
-
-    def emit(part, carry):
-        start = part * rows
-        if rows % 8 == 0 and shift % 8 == 0:
-            own_start = pl.multiple_of(start + core * shift, 8)
-            other_start = pl.multiple_of(start + (1 - core) * shift, 8)
-        else:
-            own_start, other_start = start + core * shift, start + (1 - core) * shift
-        place = part ^ me
+    me, core = lax.axis_index("graph"), lax.axis_index("dp")
+    shift = lay.share - lay.half_rows
+
+    def emit(index, carry):
+        start = lay.margin + index * lay.share
+        own_start, other_start = start + core * shift, start + (1 - core) * shift
+        if lay.share % 8 == 0 and shift % 8 == 0:
+            own_start, other_start = pl.multiple_of(own_start, 8), pl.multiple_of(other_start, 8)
+        place = (index ^ me) & (lay.parts - 1)
         skip = 0
-        for stream, size in enumerate(sizes):
+        for stream, size in enumerate(lay.sizes):
             out_refs[2 * stream][place] = grad_ref[pl.ds(own_start + skip, size), :]
             out_refs[2 * stream + 1][place] = grad_ref[pl.ds(other_start + skip, size), :].astype(
                 jnp.bfloat16
@@ -276,7 +304,17 @@
             skip = skip + size
         return carry
 
-    lax.fori_loop(0, plan.parts, emit, 0)
+    lax.fori_loop(0, lay.parts, emit, 0)
+
+
+def join_halves_kernel(lo, parts, *refs):
+    kept, came, outs = refs[0:4:2], refs[1:4:2], refs[-2:]
+    for half in range(2):
+        top = (lax.axis_index("graph") // parts) ^ half
+        for index in range(parts):
+            total = kept[half][index] + came[half][index].astype(jnp.float32)
+            target = outs[(index // lo) % 2]
+            target[top * (parts // 2) + (index // (2 * lo)) * lo + index % lo] = total.astype(target.dtype)
 
 
 def add_kernel(lo, kept_ref, came_ref, *outs):
@@ -290,14 +328,14 @@
         target[(block // (2 * lo)) * lo + block % lo] = total.astype(target.dtype)
 
 
-def join_kernel(shift, sizes, me_ref, *refs):
+def join_kernel(shift, sizes, *refs):
     count = len(sizes)
     mine, theirs, out_ref = refs[:count], refs[count : 2 * count], refs[2 * count]
     for core in (1, 0):
         start = core * shift
         for stream, size in enumerate(sizes):
             out_ref[start : start + size, :] = jnp.where(
-                me_ref[1] == core, mine[stream][...], theirs[stream][...]
+                lax.axis_index("dp") == core, mine[stream][...], theirs[stream][...]
             )
             start = start + size
 
@@ -308,11 +346,9 @@
     return int(np.prod(shape[:-2], initial=1)) * rows * lanes * jnp.dtype(dtype).itemsize
 
 
-def whole_call(kernel, outs, args, scratch=(), smem=0, flops=10**6, passed=0):
-    specs = [pl.BlockSpec(memory_space=pltpu.SMEM)] * smem + [
-        pl.BlockSpec(memory_space=pltpu.VMEM)
-    ] * (len(args) - smem)
-    held = sum(padded_bytes(x.shape, x.dtype) for x in [*args[smem:], *outs])
+def whole_call(kernel, outs, args, scratch=(), flops=10**6, passed=0):
+    specs = [pl.BlockSpec(memory_space=pltpu.VMEM)] * len(args)
+    held = sum(padded_bytes(x.shape, x.dtype) for x in [*args, *outs])
     held = held + sum(padded_bytes(*item) for item in scratch)
     return pl.pallas_call(
         kernel,
@@ -347,7 +383,6 @@
     plan = Plan(parts, edges, atoms)
     kept = wigner.shape[1]
     slots = plan.slots
-    here = jnp.stack([lax.axis_index("graph"), lax.axis_index("dp")]).astype(jnp.int32)
 
     def node_rows(value):
         return value.transpose(1, 0, 2).reshape(coeffs * atoms, channels)
@@ -362,16 +397,20 @@
     bit_lists = (plan.src_bits[::-1], plan.dst_bits[::-1])
     for held, bits in zip(blocks, bit_lists):
         held.update({1 << bit: swap(held[0], 1 << bit) for bit in bits})
-    far = [held[1 << bits[0]] for held, bits in zip(blocks, bit_lists)]
-    near = [held[1 << bit] for held, bits in zip(blocks, bit_lists) for bit in bits[1:]]
-    *far, wide, blocks[1][0] = whole_call(
-        functools.partial(middle_kernel, len(far), len(near)),
-        [jax.ShapeDtypeStruct(x.shape, bf16) for x in far]
-        + [
+    wide, blocks[1][0] = whole_call(
+        widen_kernel,
+        [
             jax.ShapeDtypeStruct((coeffs, TABLE_ROWS, wigner.shape[0]), bf16),
             jax.ShapeDtypeStruct(own.shape, bf16),
         ],
-        [*far, *near, wigner.transpose(2, 1, 0), own],
+        [wigner.transpose(2, 1, 0), own],
+    )
+    far = [held[1 << bits[0]] for held, bits in zip(blocks, bit_lists)]
+    near = [held[1 << bit] for held, bits in zip(blocks, bit_lists) for bit in bits[1:]]
+    far = whole_call(
+        pass_kernel,
+        [jax.ShapeDtypeStruct(x.shape, bf16) for x in far],
+        [*far, *near, wide, blocks[1][0]],
         passed=len(far),
     )
     for held, bits, item in zip(blocks, bit_lists, far):
@@ -385,47 +424,48 @@
     bounds = group_bounds()
     params = (bounds[0][1] ** 2 + 2 * sum(b[1] ** 2 for b in bounds[1::2])) * channels**2
     share = params // parts // channels
-    half_rows = -(-(-(-share // 2)) // 16) * 16
-    tiles = half_rows // 16
-    sizes = [16 * ((tiles + STREAMS - 1 - k) // STREAMS) for k in range(STREAMS)]
+    lay = Layout(plan, share)
+    sizes = lay.sizes
     deepest = (2 * LMAX + 1) * atoms
     most = max(plan.n_src, plan.n_dst)
     grouped = [
-        (((LMAX + 1 - azimuth) * channels, min(2, 1 + azimuth) * slots), bf16)
+        jax.ShapeDtypeStruct(((LMAX + 1 - azimuth) * channels, min(2, 1 + azimuth) * slots), bf16)
         for azimuth in range(MMAX + 1)
     ]
-    rot, dst_slot, rotated, *result = whole_call(
-        functools.partial(gram_kernel, plan, half_rows, sizes),
+    halves = [
+        jax.ShapeDtypeStruct((lay.parts, size, channels), kind) for size in sizes for kind in (f32, bf16)
+    ]
+    flat = ((lay.rows + 2 * lay.margin, channels), f32)
+    rot, dst_slot, *result = whole_call(
+        functools.partial(rotate_kernel, plan, lay),
         [
             jax.ShapeDtypeStruct((coeffs * TABLE_ROWS, slots), f32),
             jax.ShapeDtypeStruct((8, slots), jnp.int32),
-            jax.ShapeDtypeStruct((kept * channels, slots), bf16),
-        ]
-        + [
-            jax.ShapeDtypeStruct((parts, size, channels), kind)
-            for size in sizes
-            for kind in (f32, bf16)
+            *grouped,
+            *grouped,
+            *grouped[1:],
+            *halves,
         ],
-        [here, wide, *node_blocks, *pull_blocks],
+        [wide, *node_blocks, *pull_blocks],
         [
             ((coeffs, plan.n_src * atoms, channels), bf16),
             ((coeffs, plan.n_dst * atoms, channels), bf16),
             ((deepest * most, slots), bf16),
-            *grouped,
-            *grouped,
-            *grouped[1:],
-            ((params // channels, channels), f32),
+            flat,
         ],
-        smem=1,
-        flops=8 * 10**9,
-    )
-    partial_sums = whole_call(
+        flops=5 * 10**9,
+    )
+    sides, first_half = result[: 3 * MMAX + 2], result[3 * MMAX + 2 :]
+    second_half = whole_call(
+        functools.partial(gram_kernel, plan, lay), halves, [*sides], [flat], flops=3 * 10**9
+    )
+    partial_sums = list(whole_call(
         functools.partial(message_kernel, plan),
         [
             jax.ShapeDtypeStruct((coeffs * atoms, channels), f32 if place == 0 else bf16)
             for place in range(plan.n_dst)
         ],
-        [rot, dst_slot, rotated, w_zero, w_one, w_two],
+        [rot, dst_slot, *sides[: MMAX + 1], w_zero, w_one, w_two],
         [
             ((deepest * plan.n_dst, slots), bf16),
             ((slots, kept * channels), bf16),
@@ -433,41 +473,56 @@
             ((deepest * plan.n_dst, channels), f32),
         ],
         flops=8 * 10**9,
-    )
+    ))
+    n_bits = parts.bit_length() - 1
+    came = [[swap_cores(half[2 * k + 1]) for half in (first_half, second_half)] for k in range(STREAMS)]
+    kept_part = [None] * STREAMS
+    mine = [None] * STREAMS
+    orders = [list(range(n_bits)) for _ in range(STREAMS)]
+    orders[1] = orders[1][1:-1] + orders[1][:1] + orders[1][-1:]
+    orders[2] = orders[2][2:-1] + orders[2][:2] + orders[2][-1:]
+    left = [list(range(n_bits)) for _ in range(STREAMS)]
+    for stage in range(n_bits + 1):
+        for k in (1, 2, 0):
+            if stage == n_bits:
+                mine[k] = whole_call(
+                    functools.partial(add_kernel, None),
+                    [jax.ShapeDtypeStruct((sizes[k], channels), f32)],
+                    [kept_part[k], came[k]],
+                )[0]
+                continue
+            bit = orders[k][stage]
+            place = left[k].index(bit)
+            left[k].remove(bit)
+            shape = (1 << len(left[k]), sizes[k], channels)
+            outs = [jax.ShapeDtypeStruct(shape, f32), jax.ShapeDtypeStruct(shape, bf16)]
+            if stage == 0:
+                both = [
+                    first_half[2 * k], came[k][0], second_half[2 * k], came[k][1]
+                ]
+                kept_part[k], sent = whole_call(
+                    functools.partial(join_halves_kernel, 1 << place, lay.parts),
+                    outs,
+                    [*both],
+                            )
+            else:
+                kept_part[k], sent = whole_call(
+                    functools.partial(add_kernel, 1 << place),
+                    outs,
+                    [kept_part[k], came[k]] + ([partial_sums[1]] if stage == 1 else []),
+                )
+            came[k] = swap(sent, 1 << bit)
     total = partial_sums[0]
     for place, flip in enumerate(flips(plan.dst_bits)):
         if place > 0:
             total = total + swap(partial_sums[place], flip).astype(f32)
     aggregated = total.astype(bf16).reshape(coeffs, atoms, channels).transpose(1, 0, 2)
 
-    n_bits = parts.bit_length() - 1
-    mine = []
-    for stream, size in enumerate(sizes):
-        front = list(range(n_bits - 1))
-        turn = stream % max(1, len(front))
-        left = list(range(n_bits))
-        kept_part, came = result[2 * stream], swap_cores(result[2 * stream + 1])
-        for stage, bit in enumerate(front[turn:] + front[:turn] + [n_bits - 1]):
-            place = left.index(bit)
-            left.remove(bit)
-            shape = (1 << len(left), size, channels)
-            kept_part, sent = whole_call(
-                functools.partial(add_kernel, 1 << place),
-                [jax.ShapeDtypeStruct(shape, f32), jax.ShapeDtypeStruct(shape, bf16)],
-                [kept_part, came] + ([partial_sums[1]] if stage == 1 else []),
-            )
-            came = swap(sent, 1 << bit)
-        mine += whole_call(
-            functools.partial(add_kernel, None),
-            [jax.ShapeDtypeStruct((size, channels), f32)],
-            [kept_part, came],
-        )
     theirs = [swap_cores(item) for item in mine]
     weight_grad = whole_call(
-        functools.partial(join_kernel, share - half_rows, sizes),
+        functools.partial(join_kernel, share - lay.half_rows, sizes),
         [jax.ShapeDtypeStruct((share, channels), f32)],
-        [here, *mine, *theirs],
-        smem=1,
+        [*mine, *theirs],
     )[0]
     return (aggregated, weight_grad.reshape(-1))
 

time: 84.1 us -> 80.8 us (0.961)
  waiting for transfers between devices: 29.6 us -> 22.8 us
  starting transfers between devices: 32.1 us -> 37.3 us
    ppermute x21, waiting for transfers between devices: 25.8 us -> 20.8 us  [swap(): return lax.ppermute(value, 'graph', [(i, i ^ flip) for i in range(count)])]
    ppermute x21, starting transfers between devices: 30.8 us -> 35 us  [swap(): return lax.ppermute(value, 'graph', [(i, i ^ flip) for i in range(count)])]
    ppermute x6 -> x9, waiting for transfers between devices: 3.81 us -> 2.03 us  [swap_cores(): return lax.ppermute(value, 'dp', [(i, 1 - i) for i in range(2)])]
    ppermute x6 -> x9, starting transfers between devices: 1.3 us -> 2.31 us  [swap_cores(): return lax.ppermute(value, 'dp', [(i, 1 - i) for i in range(2)])]
    pallas_call x20 -> x22, Pallas kernels: 15.6 us -> 14.8 us  [whole_call(): pl.pallas_call(kernel, out_shape=outs, in_specs=specs, out_specs=[pl.Bloc...]
  transfers between devices with their start and end apart: 27 -> 30, of which waited for: 12 -> 12; matrix products, arithmetic and copies ran while one was open for 1% -> 1% of each run, Pallas kernels for 8% -> 10%
where the time goes in v4:
time: 80.8 us; the launch traced here: 80.2 us
  starting transfers between devices  37.3 us (46%)
  waiting for transfers between devices  22.8 us (28%)
  Pallas kernels  14.8 us (18%)
  local copies, waits for them, and re-layouts  3.01 us (4%)
  other arithmetic  1.5 us (2%)
  between operations  0.81 us (1%)
    ppermute x21, starting transfers between devices, swap(): return lax.ppermute(value, 'graph', [(i, i ^ flip) for i in range(count)])  35 us
    ppermute x21, waiting for transfers between devices, swap(): return lax.ppermute(value, 'graph', [(i, i ^ flip) for i in range(count)])  20.8 us
    pallas_call x22, Pallas kernels, whole_call(): pl.pallas_call(kernel, out_shape=outs, in_specs=specs, out_specs=[pl.Bloc...  14.8 us
    unnamed x12, local copies, waits for them, and re-layouts  3.01 us
    ppermute x9, starting transfers between devices, swap_cores(): return lax.ppermute(value, 'dp', [(i, 1 - i) for i in range(2)])  2.31 us
    ppermute x9, waiting for transfers between devices, swap_cores(): return lax.ppermute(value, 'dp', [(i, 1 - i) for i in range(2)])  2.03 us
  transfers between devices with their start and end apart: 30, of which 12 were waited for; matrix products, arithmetic and copies ran while one was open for 1% of the time, Pallas kernels for 10%

profile of v4, /device:TPU:0, one launch (start us, length us, event | category | flops | bytes accessed | tf_op | source)
XLA Modules:
  0.0 80.2 jit_solution(5808961994903126692)
XLA Ops:
  1.3 0.9 %copy-done.1 = bf16[16,49,128]{2,0,1:T(8,128)(2,1)S(1)} copy-done((bf16[16,49,128]{2,0,1:T(8,128)(2,1)S(1)}, bf16[16,49,128]{2,0,1:T(8,128)(2,1)}, u32[]{:S(2)}) %copy-start.1) | copy-done | bytes 200728
  2.6 3.0 %collective-permute-start = (bf16[800,128]{1,0:T(8,128)(2,1)S(1)}, bf16[800,128]{1,0:T(8,128)(2,1)S(1)}, u32[]{:S(2)}, u32[]{:S(2)}) collective-permute-start(bf16[800,128]{1,0:T(8,128)(2,1)S(1)} %shard_map.114.refs_1_), channel_id=1, source_target_pairs={{0,2},{1,3},{2,0},{3,1},{4,6},{5,7},{6,4},{7,5},{8,10},{9,11},{10,... | collective-permute-start | bytes 614408 | tf_op jit(solution)/shard_map/ppermute | solution.py:367
  5.5 2.6 %collective-permute-start.1 = (bf16[800,128]{1,0:T(8,128)(2,1)S(1)}, bf16[800,128]{1,0:T(8,128)(2,1)S(1)}, u32[]{:S(2)}, u32[]{:S(2)}) collective-permute-start(bf16[800,128]{1,0:T(8,128)(2,1)S(1)} %shard_map.114.refs_1_), channel_id=1, source_target_pairs={{0,8},{1,9},{2,10},{3,11},{4,12},{5,13},{6,14},{7,15},{8,0},{9,1},... | collective-permute-start | bytes 614408 | tf_op jit(solution)/shard_map/ppermute | solution.py:367
  8.1 1.6 %collective-permute-start.2 = (bf16[784,128]{1,0:T(8,128)(2,1)}, bf16[784,128]{1,0:T(8,128)(2,1)S(1)}, u32[]{:S(2)}, u32[]{:S(2)}) collective-permute-start(bf16[784,128]{1,0:T(8,128)(2,1)} %bitcast.17), channel_id=1, source_target_pairs={{0,4},{1,5},{2,6},{3,7},{4,0},{5,1},{6,2},{7,3},{8,12},{9,13},{10,... | collective-permute-start | bytes 602120 | tf_op jit(solution)/shard_map/ppermute | solution.py:367
  9.7 1.5 %collective-permute-start.3 = (bf16[784,128]{1,0:T(8,128)(2,1)}, bf16[784,128]{1,0:T(8,128)(2,1)S(1)}, u32[]{:S(2)}, u32[]{:S(2)}) collective-permute-start(bf16[784,128]{1,0:T(8,128)(2,1)} %bitcast.18), channel_id=1, source_target_pairs={{0,1},{1,0},{2,3},{3,2},{4,5},{5,4},{6,7},{7,6},{8,9},{9,8},{10,11... | collective-permute-start | bytes 602120 | tf_op jit(solution)/shard_map/ppermute | solution.py:367
  11.2 1.1 %copy-done = bf16[256,29,49]{0,1,2:T(8,128)(2,1)S(1)} copy-done((bf16[256,29,49]{0,1,2:T(8,128)(2,1)S(1)}, bf16[256,29,49]{0,1,2:T(8,128)(2,1)}, u32[]{:S(2)}) %copy-start) | copy-done | bytes 727576
  12.3 0.9 %copy-done.2 = bf16[16,49,128]{2,0,1:T(8,128)(2,1)S(1)} copy-done((bf16[16,49,128]{2,0,1:T(8,128)(2,1)S(1)}, bf16[16,49,128]{2,0,1:T(8,128)(2,1)}, u32[]{:S(2)}) %copy-start.2) | copy-done | bytes 200728
  13.4 4.4 %collective-permute-done.2.refs_1_ = bf16[784,128]{1,0:T(8,128)(2,1)S(1)} collective-permute-done((bf16[784,128]{1,0:T(8,128)(2,1)}, bf16[784,128]{1,0:T(8,128)(2,1)S(1)}, u32[]{:S(2)}, u32[]{:S(2)}) %collective-permute-start.2) | collective-permute-done | bytes 200736 | tf_op jit(solution)/shard_map/ppermute | solution.py:367
  18.3 1.5 %collective-permute-start.5 = (bf16[784,128]{1,0:T(8,128)(2,1)S(1)}, bf16[784,128]{1,0:T(8,128)(2,1)S(1)}, u32[]{:S(2)}, u32[]{:S(2)}) collective-permute-start(bf16[784,128]{1,0:T(8,128)(2,1)S(1)} %get-tuple-element.59.refs_7_), channel_id=1, source_target_pairs={{0,1},{1,0},{2,3},{3,2},{4,5},{5,4},{6,7},{7,6},{8,9},{9,8},{10,11... | collective-permute-start | bytes 602120 | tf_op jit(solution)/shard_map/ppermute | solution.py:367
  19.9 4.2 %collective-permute-done.5.refs_8_ = bf16[784,128]{1,0:T(8,128)(2,1)S(1)} collective-permute-done((bf16[784,128]{1,0:T(8,128)(2,1)S(1)}, bf16[784,128]{1,0:T(8,128)(2,1)S(1)}, u32[]{:S(2)}, u32[]{:S(2)}) %collective-permute-start.5) | collective-permute-done | bytes 200736 | tf_op jit(solution)/shard_map/ppermute | solution.py:367
  24.0 5.1 %shard_map.116 = (f32[1568,256]{1,0:T(8,128)S(1)}, s32[8,256]{1,0:T(8,128)S(1)}, bf16[896,256]{1,0:T(8,128)(2,1)S(1)}, bf16[768,512]{1,0:T(8,128)(2,1)S(1)}, bf1...) custom-call(bf16[49,32,256]{2,1,0:T(8,128)(2,1)S(1)} %get-tuple-elem, ...), custom_call_target="tpu_custom_call" | custom-call | flops 5000000000 | bytes 100000 | tf_op jit(solution)/shard_map/pallas_call | solution.py:353
  29.8 2.2 %shard_map.118 = (f32[8,240,128]{2,1,0:T(8,128)S(1)}, bf16[8,240,128]{2,1,0:T(8,128)(2,1)S(1)}, f32[8,224,128]{2,1,0:T(8,128)S(1)}, bf16[8,224,128]{2,1,0:T(8,12...) custom-call(bf16[896,256]{1,0:T(8,128)(2,1)S(1)} %get-tuple-element.62.refs_2_.refs_0_, ...), custom_call_target="tpu_custom_call" | custom-call | flops 3000000000 | bytes 100000 | tf_op jit(solution)/shard_map/pallas_call | solution.py:353
  33.0 1.5 %collective-permute-done.16.refs_3_ = bf16[8,224,128]{2,1,0:T(8,128)(2,1)S(1)} collective-permute-done((bf16[8,224,128]{2,1,0:T(8,128)(2,1)S(1)}, bf16[8,224,128]{2,1,0:T(8,128)(2,1)S(1)}, u32[]{:S(2)}, u32[]{:S(2)}) %collective-permute-start.16) | collective-permute-done | bytes 458784 | tf_op jit(solution)/shard_map/ppermute | solution.py:371
  34.7 1.6 %collective-permute-start.17 = (bf16[8,224,128]{2,1,0:T(8,128)(2,1)S(1)}, bf16[8,224,128]{2,1,0:T(8,128)(2,1)S(1)}, u32[]{:S(2)}, u32[]{:S(2)}) collective-permute-start(bf16[8,224,128]{2,1,0:T(8,128)(2,1)S(1)} %get-tuple-element.91), channel_id=1, source_target_pairs={{0,2},{1,3},{2,0},{3,1},{4,6},{5,7},{6,4},{7,5},{8,10},{9,11},{10,... | collective-permute-start | bytes 1376264 | tf_op jit(solution)/shard_map/ppermute | solution.py:367
  36.6 1.3 %collective-permute-start.23 = (bf16[8,224,128]{2,1,0:T(8,128)(2,1)S(1)}, bf16[8,224,128]{2,1,0:T(8,128)(2,1)S(1)}, u32[]{:S(2)}, u32[]{:S(2)}) collective-permute-start(bf16[8,224,128]{2,1,0:T(8,128)(2,1)S(1)} %get-tuple-element.103), channel_id=1, source_target_pairs={{0,4},{1,5},{2,6},{3,7},{4,0},{5,1},{6,2},{7,3},{8,12},{9,13},{10,... | collective-permute-start | bytes 1376264 | tf_op jit(solution)/shard_map/ppermute | solution.py:367
  38.0 1.6 %collective-permute-start.11 = (bf16[8,240,128]{2,1,0:T(8,128)(2,1)S(1)}, bf16[8,240,128]{2,1,0:T(8,128)(2,1)S(1)}, u32[]{:S(2)}, u32[]{:S(2)}) collective-permute-start(bf16[8,240,128]{2,1,0:T(8,128)(2,1)S(1)} %get-tuple-element.79), channel_id=1, source_target_pairs={{0,1},{1,0},{2,3},{3,2},{4,5},{5,4},{6,7},{7,6},{8,9},{9,8},{10,11... | collective-permute-start | bytes 1474568 | tf_op jit(solution)/shard_map/ppermute | solution.py:367
  39.6 5.1 %shard_map.117 = (f32[784,128]{1,0:T(8,128)S(1)}, bf16[784,128]{1,0:T(8,128)(2,1)S(1)}, bf16[784,128]{1,0:T(8,128)(2,1)S(1)}, bf16[784,128]{1,0:T(8,128)(2,1)S(1)}) custom-call(f32[1568,256]{1,0:T(8,128)S(1)} %get-tuple-element.60.refs_0_, s32[8,256]{1,0:T(8,128)S(1)} %get-tuple-element.61.refs_1_, bf16[896,256]{1,0:T(8,128)(2,1)S(1)} %get-tuple-element.62.refs_2_.refs_0_, ...), custom_call_target="tpu_custom_call" | custom-call | flops 8000000000 | bytes 100000 | tf_op jit(solution)/shard_map/pallas_call | solution.py:353
  44.7 2.6 %collective-permute-done.17.came_ref = bf16[8,224,128]{2,1,0:T(8,128)(2,1)S(1)} collective-permute-done((bf16[8,224,128]{2,1,0:T(8,128)(2,1)S(1)}, bf16[8,224,128]{2,1,0:T(8,128)(2,1)S(1)}, u32[]{:S(2)}, u32[]{:S(2)}) %collective-permute-start.17) | collective-permute-done | bytes 458784 | tf_op jit(solution)/shard_map/ppermute | solution.py:367
  47.4 1.3 %collective-permute-start.18 = (bf16[4,224,128]{2,1,0:T(8,128)(2,1)S(1)}, bf16[4,224,128]{2,1,0:T(8,128)(2,1)S(1)}, u32[]{:S(2)}, u32[]{:S(2)}) collective-permute-start(bf16[4,224,128]{2,1,0:T(8,128)(2,1)S(1)} %get-tuple-element.93), channel_id=1, source_target_pairs={{0,4},{1,5},{2,6},{3,7},{4,0},{5,1},{6,2},{7,3},{8,12},{9,13},{10,... | collective-permute-start | bytes 688136 | tf_op jit(solution)/shard_map/ppermute | solution.py:367
  48.8 2.0 %collective-permute-done.11.came_ref = bf16[8,240,128]{2,1,0:T(8,128)(2,1)S(1)} collective-permute-done((bf16[8,240,128]{2,1,0:T(8,128)(2,1)S(1)}, bf16[8,240,128]{2,1,0:T(8,128)(2,1)S(1)}, u32[]{:S(2)}, u32[]{:S(2)}) %collective-permute-start.11) | collective-permute-done | bytes 491552 | tf_op jit(solution)/shard_map/ppermute | solution.py:367
  50.9 1.4 %collective-permute-start.12 = (bf16[4,240,128]{2,1,0:T(8,128)(2,1)S(1)}, bf16[4,240,128]{2,1,0:T(8,128)(2,1)S(1)}, u32[]{:S(2)}, u32[]{:S(2)}) collective-permute-start(bf16[4,240,128]{2,1,0:T(8,128)(2,1)S(1)} %get-tuple-element.81), channel_id=1, source_target_pairs={{0,2},{1,3},{2,0},{3,1},{4,6},{5,7},{6,4},{7,5},{8,10},{9,11},{10,... | collective-permute-start | bytes 737288 | tf_op jit(solution)/shard_map/ppermute | solution.py:367
  52.4 1.6 %collective-permute-start.24 = (bf16[4,224,128]{2,1,0:T(8,128)(2,1)S(1)}, bf16[4,224,128]{2,1,0:T(8,128)(2,1)S(1)}, u32[]{:S(2)}, u32[]{:S(2)}) collective-permute-start(bf16[4,224,128]{2,1,0:T(8,128)(2,1)S(1)} %get-tuple-element.105), channel_id=1, source_target_pairs={{0,1},{1,0},{2,3},{3,2},{4,5},{5,4},{6,7},{7,6},{8,9},{9,8},{10,11... | collective-permute-start | bytes 688136 | tf_op jit(solution)/shard_map/ppermute | solution.py:367
  54.4 1.6 %collective-permute-start.19 = (bf16[2,224,128]{2,1,0:T(8,128)(2,1)S(1)}, bf16[2,224,128]{2,1,0:T(8,128)(2,1)S(1)}, u32[]{:S(2)}, u32[]{:S(2)}) collective-permute-start(bf16[2,224,128]{2,1,0:T(8,128)(2,1)S(1)} %get-tuple-element.95), channel_id=1, source_target_pairs={{0,1},{1,0},{2,3},{3,2},{4,5},{5,4},{6,7},{7,6},{8,9},{9,8},{10,11... | collective-permute-start | bytes 344072 | tf_op jit(solution)/shard_map/ppermute | solution.py:367
  56.0 1.5 %collective-permute-done.12.came_ref = bf16[4,240,128]{2,1,0:T(8,128)(2,1)S(1)} collective-permute-done((bf16[4,240,128]{2,1,0:T(8,128)(2,1)S(1)}, bf16[4,240,128]{2,1,0:T(8,128)(2,1)S(1)}, u32[]{:S(2)}, u32[]{:S(2)}) %collective-permute-start.12) | collective-permute-done | bytes 245792 | tf_op jit(solution)/shard_map/ppermute | solution.py:367
  58.4 2.2 %collective-permute-start.8 = (bf16[784,128]{1,0:T(8,128)(2,1)S(1)}, bf16[784,128]{1,0:T(8,128)(2,1)S(1)}, u32[]{:S(2)}, u32[]{:S(2)}) collective-permute-start(bf16[784,128]{1,0:T(8,128)(2,1)S(1)} %get-tuple-element.68), channel_id=1, source_target_pairs={{0,5},{1,4},{2,7},{3,6},{4,1},{5,0},{6,3},{7,2},{8,13},{9,12},{10,... | collective-permute-start | bytes 602120 | tf_op jit(solution)/shard_map/ppermute | solution.py:367
  61.3 2.5 %collective-permute-start.6 = (bf16[784,128]{1,0:T(8,128)(2,1)S(1)}, bf16[784,128]{1,0:T(8,128)(2,1)S(1)}, u32[]{:S(2)}, u32[]{:S(2)}) collective-permute-start(bf16[784,128]{1,0:T(8,128)(2,1)S(1)} %get-tuple-element.66.outs_0_), channel_id=1, source_target_pairs={{0,1},{1,0},{2,3},{3,2},{4,5},{5,4},{6,7},{7,6},{8,9},{9,8},{10,11... | collective-permute-start | bytes 602120 | tf_op jit(solution)/shard_map/ppermute | solution.py:367
  64.2 3.2 %collective-permute-start.20 = (bf16[1,224,128]{2,1,0:T(8,128)(2,1)S(1)}, bf16[1,224,128]{2,1,0:T(8,128)(2,1)S(1)}, u32[]{:S(2)}, u32[]{:S(2)}) collective-permute-start(bf16[1,224,128]{2,1,0:T(8,128)(2,1)S(1)} %get-tuple-element.97), channel_id=1, source_target_pairs={{0,8},{1,9},{2,10},{3,11},{4,12},{5,13},{6,14},{7,15},{8,0},{9,1},... | collective-permute-start | bytes 172040 | tf_op jit(solution)/shard_map/ppermute | solution.py:367
  67.4 1.5 %collective-permute-done.25.came_ref = bf16[2,224,128]{2,1,0:T(8,128)(2,1)S(1)} collective-permute-done((bf16[2,224,128]{2,1,0:T(8,128)(2,1)S(1)}, bf16[2,224,128]{2,1,0:T(8,128)(2,1)S(1)}, u32[]{:S(2)}, u32[]{:S(2)}) %collective-permute-start.25) | collective-permute-done | bytes 114720 | tf_op jit(solution)/shard_map/ppermute | solution.py:367
  69.0 3.1 %collective-permute-start.14 = (bf16[1,240,128]{2,1,0:T(8,128)(2,1)S(1)}, bf16[1,240,128]{2,1,0:T(8,128)(2,1)S(1)}, u32[]{:S(2)}, u32[]{:S(2)}) collective-permute-start(bf16[1,240,128]{2,1,0:T(8,128)(2,1)S(1)} %get-tuple-element.85), channel_id=1, source_target_pairs={{0,8},{1,9},{2,10},{3,11},{4,12},{5,13},{6,14},{7,15},{8,0},{9,1},... | collective-permute-start | bytes 184328 | tf_op jit(solution)/shard_map/ppermute | solution.py:367
  72.1 1.2 %collective-permute-start.26 = (bf16[1,224,128]{2,1,0:T(8,128)(2,1)S(1)}, bf16[1,224,128]{2,1,0:T(8,128)(2,1)S(1)}, u32[]{:S(2)}, u32[]{:S(2)}) collective-permute-start(bf16[1,224,128]{2,1,0:T(8,128)(2,1)S(1)} %get-tuple-element.109), channel_id=1, source_target_pairs={{0,8},{1,9},{2,10},{3,11},{4,12},{5,13},{6,14},{7,15},{8,0},{9,1},... | collective-permute-start | bytes 172040 | tf_op jit(solution)/shard_map/ppermute | solution.py:367
  73.4 3.9 %collective-permute-done.26.came_ref = bf16[1,224,128]{2,1,0:T(8,128)(2,1)S(1)} collective-permute-done((bf16[1,224,128]{2,1,0:T(8,128)(2,1)S(1)}, bf16[1,224,128]{2,1,0:T(8,128)(2,1)S(1)}, u32[]{:S(2)}, u32[]{:S(2)}) %collective-permute-start.26) | collective-permute-done | bytes 57376 | tf_op jit(solution)/shard_map/ppermute | solution.py:367
  79.3 0.9 %shard_map.134 = f32[1368,128]{1,0:T(8,128)} custom-call(f32[240,128]{1,0:T(8,128)S(1)} %shard_map.123.refs_0_, f32[224,128]{1,0:T(8,128)S(1)} %shard_map.128.refs_1_, f32[224,128]{1,0:T(8,128)S(1)} %shard_map.133.refs_2_, f32[240,128]{1,0:T(8,128)S(1)} %collective-permute-done.27.refs_3_, f32[224,128]{1,0:T(8,128)S(1)} %collective-permute-done.28.refs_4_, ...), custom_call_target="tpu_custom_call" | custom-call | flops 1000000 | bytes 100000 | tf_op jit(solution)/shard_map/pallas_call | solution.py:353
  (64 shorter events, 8.6 us)
Async XLA Ops:
  2.6 15.2 %collective-permute-start = (bf16[800,128]{1,0:T(8,128)(2,1)S(1)}, bf16[800,128]{1,0:T(8,128)(2,1)S(1)}, u32[]{:S(2)}, u32[]{:S(2)}) collective-permute-start(bf16[800,128]{1,0:T(8,128)(2,1)S(1)} %shard_map.114.refs_1_), channel_id=1, source_target_pairs={{0,2},{1,3},{2,0},{3,1},{4,6},{5,7},{6,4},{7,5},{8,10},{9,11},{10,... | collective-permute-start | bytes 614408 | tf_op jit(solution)/shard_map/ppermute | solution.py:367
  5.5 12.3 %collective-permute-start.1 = (bf16[800,128]{1,0:T(8,128)(2,1)S(1)}, bf16[800,128]{1,0:T(8,128)(2,1)S(1)}, u32[]{:S(2)}, u32[]{:S(2)}) collective-permute-start(bf16[800,128]{1,0:T(8,128)(2,1)S(1)} %shard_map.114.refs_1_), channel_id=1, source_target_pairs={{0,8},{1,9},{2,10},{3,11},{4,12},{5,13},{6,14},{7,15},{8,0},{9,1},... | collective-permute-start | bytes 614408 | tf_op jit(solution)/shard_map/ppermute | solution.py:367
  8.1 9.7 %collective-permute-start.2 = (bf16[784,128]{1,0:T(8,128)(2,1)}, bf16[784,128]{1,0:T(8,128)(2,1)S(1)}, u32[]{:S(2)}, u32[]{:S(2)}) collective-permute-start(bf16[784,128]{1,0:T(8,128)(2,1)} %bitcast.17), channel_id=1, source_target_pairs={{0,4},{1,5},{2,6},{3,7},{4,0},{5,1},{6,2},{7,3},{8,12},{9,13},{10,... | collective-permute-start | bytes 602120 | tf_op jit(solution)/shard_map/ppermute | solution.py:367
  9.7 8.1 %collective-permute-start.3 = (bf16[784,128]{1,0:T(8,128)(2,1)}, bf16[784,128]{1,0:T(8,128)(2,1)S(1)}, u32[]{:S(2)}, u32[]{:S(2)}) collective-permute-start(bf16[784,128]{1,0:T(8,128)(2,1)} %bitcast.18), channel_id=1, source_target_pairs={{0,1},{1,0},{2,3},{3,2},{4,5},{5,4},{6,7},{7,6},{8,9},{9,8},{10,11... | collective-permute-start | bytes 602120 | tf_op jit(solution)/shard_map/ppermute | solution.py:367
  17.8 6.2 %collective-permute-start.4 = (bf16[800,128]{1,0:T(8,128)(2,1)S(1)}, bf16[800,128]{1,0:T(8,128)(2,1)S(1)}, u32[]{:S(2)}, u32[]{:S(2)}) collective-permute-start(bf16[800,128]{1,0:T(8,128)(2,1)S(1)} %get-tuple-element.58.refs_3_), channel_id=1, source_target_pairs={{0,2},{1,3},{2,0},{3,1},{4,6},{5,7},{6,4},{7,5},{8,10},{9,11},{10,... | collective-permute-start | bytes 614408 | tf_op jit(solution)/shard_map/ppermute | solution.py:367
  18.3 5.7 %collective-permute-start.5 = (bf16[784,128]{1,0:T(8,128)(2,1)S(1)}, bf16[784,128]{1,0:T(8,128)(2,1)S(1)}, u32[]{:S(2)}, u32[]{:S(2)}) collective-permute-start(bf16[784,128]{1,0:T(8,128)(2,1)S(1)} %get-tuple-element.59.refs_7_), channel_id=1, source_target_pairs={{0,1},{1,0},{2,3},{3,2},{4,5},{5,4},{6,7},{7,6},{8,9},{9,8},{10,11... | collective-permute-start | bytes 602120 | tf_op jit(solution)/shard_map/ppermute | solution.py:367
  29.2 3.4 %collective-permute-start.15 = (bf16[8,224,128]{2,1,0:T(8,128)(2,1)S(1)}, bf16[8,224,128]{2,1,0:T(8,128)(2,1)S(1)}, u32[]{:S(2)}, u32[]{:S(2)}) collective-permute-start(bf16[8,224,128]{2,1,0:T(8,128)(2,1)S(1)} %get-tuple-element.87), channel_id=1, source_target_pairs={{0,16},{16,0},{1,17},{17,1},{2,18},{18,2},{3,19},{19,3},{4,20},{20... | collective-permute-start | bytes 1376264 | tf_op jit(solution)/shard_map/ppermute | solution.py:371
  29.3 8.6 %collective-permute-start.9 = (bf16[8,240,128]{2,1,0:T(8,128)(2,1)S(1)}, bf16[8,240,128]{2,1,0:T(8,128)(2,1)S(1)}, u32[]{:S(2)}, u32[]{:S(2)}) collective-permute-start(bf16[8,240,128]{2,1,0:T(8,128)(2,1)S(1)} %get-tuple-element.70), channel_id=1, source_target_pairs={{0,16},{16,0},{1,17},{17,1},{2,18},{18,2},{3,19},{19,3},{4,20},{20... | collective-permute-start | bytes 1474568 | tf_op jit(solution)/shard_map/ppermute | solution.py:371
  31.9 5.9 %collective-permute-start.10 = (bf16[8,240,128]{2,1,0:T(8,128)(2,1)S(1)}, bf16[8,240,128]{2,1,0:T(8,128)(2,1)S(1)}, u32[]{:S(2)}, u32[]{:S(2)}) collective-permute-start(bf16[8,240,128]{2,1,0:T(8,128)(2,1)S(1)} %get-tuple-element.77), channel_id=1, source_target_pairs={{0,16},{16,0},{1,17},{17,1},{2,18},{18,2},{3,19},{19,3},{4,20},{20... | collective-permute-start | bytes 1474568 | tf_op jit(solution)/shard_map/ppermute | solution.py:371
  32.1 2.4 %collective-permute-start.16 = (bf16[8,224,128]{2,1,0:T(8,128)(2,1)S(1)}, bf16[8,224,128]{2,1,0:T(8,128)(2,1)S(1)}, u32[]{:S(2)}, u32[]{:S(2)}) collective-permute-start(bf16[8,224,128]{2,1,0:T(8,128)(2,1)S(1)} %get-tuple-element.89), channel_id=1, source_target_pairs={{0,16},{16,0},{1,17},{17,1},{2,18},{18,2},{3,19},{19,3},{4,20},{20... | collective-permute-start | bytes 1376264 | tf_op jit(solution)/shard_map/ppermute | solution.py:371
  32.5 3.8 %collective-permute-start.21 = (bf16[8,224,128]{2,1,0:T(8,128)(2,1)S(1)}, bf16[8,224,128]{2,1,0:T(8,128)(2,1)S(1)}, u32[]{:S(2)}, u32[]{:S(2)}) collective-permute-start(bf16[8,224,128]{2,1,0:T(8,128)(2,1)S(1)} %get-tuple-element.99), channel_id=1, source_target_pairs={{0,16},{16,0},{1,17},{17,1},{2,18},{18,2},{3,19},{19,3},{4,20},{20... | collective-permute-start | bytes 1376264 | tf_op jit(solution)/shard_map/ppermute | solution.py:371
  32.6 3.8 %collective-permute-start.22 = (bf16[8,224,128]{2,1,0:T(8,128)(2,1)S(1)}, bf16[8,224,128]{2,1,0:T(8,128)(2,1)S(1)}, u32[]{:S(2)}, u32[]{:S(2)}) collective-permute-start(bf16[8,224,128]{2,1,0:T(8,128)(2,1)S(1)} %get-tuple-element.101), channel_id=1, source_target_pairs={{0,16},{16,0},{1,17},{17,1},{2,18},{18,2},{3,19},{19,3},{4,20},{20... | collective-permute-start | bytes 1376264 | tf_op jit(solution)/shard_map/ppermute | solution.py:371
  34.7 12.6 %collective-permute-start.17 = (bf16[8,224,128]{2,1,0:T(8,128)(2,1)S(1)}, bf16[8,224,128]{2,1,0:T(8,128)(2,1)S(1)}, u32[]{:S(2)}, u32[]{:S(2)}) collective-permute-start(bf16[8,224,128]{2,1,0:T(8,128)(2,1)S(1)} %get-tuple-element.91), channel_id=1, source_target_pairs={{0,2},{1,3},{2,0},{3,1},{4,6},{5,7},{6,4},{7,5},{8,10},{9,11},{10,... | collective-permute-start | bytes 1376264 | tf_op jit(solution)/shard_map/ppermute | solution.py:367
  36.4 3.2 %copy-start.4 = (bf16[2,640,640]{2,1,0:T(8,128)(2,1)S(1)}, bf16[2,640,640]{2,1,0:T(8,128)(2,1)}, u32[]{:S(2)}) copy-start(bf16[2,640,640]{2,1,0:T(8,128)(2,1)} %refs_7_.1) | copy-start | bytes 4915204
  36.4 3.2 %copy-start.5 = (bf16[896,896]{1,0:T(8,128)(2,1)S(1)}, bf16[896,896]{1,0:T(8,128)(2,1)}, u32[]{:S(2)}) copy-start(bf16[896,896]{1,0:T(8,128)(2,1)} %refs_5_.1) | copy-start | bytes 4816900
  36.6 15.7 %collective-permute-start.23 = (bf16[8,224,128]{2,1,0:T(8,128)(2,1)S(1)}, bf16[8,224,128]{2,1,0:T(8,128)(2,1)S(1)}, u32[]{:S(2)}, u32[]{:S(2)}) collective-permute-start(bf16[8,224,128]{2,1,0:T(8,128)(2,1)S(1)} %get-tuple-element.103), channel_id=1, source_target_pairs={{0,4},{1,5},{2,6},{3,7},{4,0},{5,1},{6,2},{7,3},{8,12},{9,13},{10,... | collective-permute-start | bytes 1376264 | tf_op jit(solution)/shard_map/ppermute | solution.py:367
  38.0 12.8 %collective-permute-start.11 = (bf16[8,240,128]{2,1,0:T(8,128)(2,1)S(1)}, bf16[8,240,128]{2,1,0:T(8,128)(2,1)S(1)}, u32[]{:S(2)}, u32[]{:S(2)}) collective-permute-start(bf16[8,240,128]{2,1,0:T(8,128)(2,1)S(1)} %get-tuple-element.79), channel_id=1, source_target_pairs={{0,1},{1,0},{2,3},{3,2},{4,5},{5,4},{6,7},{7,6},{8,9},{9,8},{10,11... | collective-permute-start | bytes 1474568 | tf_op jit(solution)/shard_map/ppermute | solution.py:367
  47.4 6.9 %collective-permute-start.18 = (bf16[4,224,128]{2,1,0:T(8,128)(2,1)S(1)}, bf16[4,224,128]{2,1,0:T(8,128)(2,1)S(1)}, u32[]{:S(2)}, u32[]{:S(2)}) collective-permute-start(bf16[4,224,128]{2,1,0:T(8,128)(2,1)S(1)} %get-tuple-element.93), channel_id=1, source_target_pairs={{0,4},{1,5},{2,6},{3,7},{4,0},{5,1},{6,2},{7,3},{8,12},{9,13},{10,... | collective-permute-start | bytes 688136 | tf_op jit(solution)/shard_map/ppermute | solution.py:367
  50.9 6.6 %collective-permute-start.12 = (bf16[4,240,128]{2,1,0:T(8,128)(2,1)S(1)}, bf16[4,240,128]{2,1,0:T(8,128)(2,1)S(1)}, u32[]{:S(2)}, u32[]{:S(2)}) collective-permute-start(bf16[4,240,128]{2,1,0:T(8,128)(2,1)S(1)} %get-tuple-element.81), channel_id=1, source_target_pairs={{0,2},{1,3},{2,0},{3,1},{4,6},{5,7},{6,4},{7,5},{8,10},{9,11},{10,... | collective-permute-start | bytes 737288 | tf_op jit(solution)/shard_map/ppermute | solution.py:367
  52.4 9.0 %collective-permute-start.24 = (bf16[4,224,128]{2,1,0:T(8,128)(2,1)S(1)}, bf16[4,224,128]{2,1,0:T(8,128)(2,1)S(1)}, u32[]{:S(2)}, u32[]{:S(2)}) collective-permute-start(bf16[4,224,128]{2,1,0:T(8,128)(2,1)S(1)} %get-tuple-element.105), channel_id=1, source_target_pairs={{0,1},{1,0},{2,3},{3,2},{4,5},{5,4},{6,7},{7,6},{8,9},{9,8},{10,11... | collective-permute-start | bytes 688136 | tf_op jit(solution)/shard_map/ppermute | solution.py:367
  54.4 9.8 %collective-permute-start.19 = (bf16[2,224,128]{2,1,0:T(8,128)(2,1)S(1)}, bf16[2,224,128]{2,1,0:T(8,128)(2,1)S(1)}, u32[]{:S(2)}, u32[]{:S(2)}) collective-permute-start(bf16[2,224,128]{2,1,0:T(8,128)(2,1)S(1)} %get-tuple-element.95), channel_id=1, source_target_pairs={{0,1},{1,0},{2,3},{3,2},{4,5},{5,4},{6,7},{7,6},{8,9},{9,8},{10,11... | collective-permute-start | bytes 344072 | tf_op jit(solution)/shard_map/ppermute | solution.py:367
  57.5 6.7 %collective-permute-start.13 = (bf16[2,240,128]{2,1,0:T(8,128)(2,1)S(1)}, bf16[2,240,128]{2,1,0:T(8,128)(2,1)S(1)}, u32[]{:S(2)}, u32[]{:S(2)}) collective-permute-start(bf16[2,240,128]{2,1,0:T(8,128)(2,1)S(1)} %get-tuple-element.83), channel_id=1, source_target_pairs={{0,4},{1,5},{2,6},{3,7},{4,0},{5,1},{6,2},{7,3},{8,12},{9,13},{10,... | collective-permute-start | bytes 368648 | tf_op jit(solution)/shard_map/ppermute | solution.py:367
  58.4 19.5 %collective-permute-start.8 = (bf16[784,128]{1,0:T(8,128)(2,1)S(1)}, bf16[784,128]{1,0:T(8,128)(2,1)S(1)}, u32[]{:S(2)}, u32[]{:S(2)}) collective-permute-start(bf16[784,128]{1,0:T(8,128)(2,1)S(1)} %get-tuple-element.68), channel_id=1, source_target_pairs={{0,5},{1,4},{2,7},{3,6},{4,1},{5,0},{6,3},{7,2},{8,13},{9,12},{10,... | collective-permute-start | bytes 602120 | tf_op jit(solution)/shard_map/ppermute | solution.py:367
  60.5 17.4 %collective-permute-start.7 = (bf16[784,128]{1,0:T(8,128)(2,1)S(1)}, bf16[784,128]{1,0:T(8,128)(2,1)S(1)}, u32[]{:S(2)}, u32[]{:S(2)}) collective-permute-start(bf16[784,128]{1,0:T(8,128)(2,1)S(1)} %get-tuple-element.67), channel_id=1, source_target_pairs={{0,4},{1,5},{2,6},{3,7},{4,0},{5,1},{6,2},{7,3},{8,12},{9,13},{10,... | collective-permute-start | bytes 602120 | tf_op jit(solution)/shard_map/ppermute | solution.py:367
  61.3 16.6 %collective-permute-start.6 = (bf16[784,128]{1,0:T(8,128)(2,1)S(1)}, bf16[784,128]{1,0:T(8,128)(2,1)S(1)}, u32[]{:S(2)}, u32[]{:S(2)}) collective-permute-start(bf16[784,128]{1,0:T(8,128)(2,1)S(1)} %get-tuple-element.66.outs_0_), channel_id=1, source_target_pairs={{0,1},{1,0},{2,3},{3,2},{4,5},{5,4},{6,7},{7,6},{8,9},{9,8},{10,11... | collective-permute-start | bytes 602120 | tf_op jit(solution)/shard_map/ppermute | solution.py:367
  64.2 4.8 %collective-permute-start.25 = (bf16[2,224,128]{2,1,0:T(8,128)(2,1)S(1)}, bf16[2,224,128]{2,1,0:T(8,128)(2,1)S(1)}, u32[]{:S(2)}, u32[]{:S(2)}) collective-permute-start(bf16[2,224,128]{2,1,0:T(8,128)(2,1)S(1)} %get-tuple-element.107), channel_id=1, source_target_pairs={{0,2},{1,3},{2,0},{3,1},{4,6},{5,7},{6,4},{7,5},{8,10},{9,11},{10,... | collective-permute-start | bytes 344072 | tf_op jit(solution)/shard_map/ppermute | solution.py:367
  64.2 7.9 %collective-permute-start.20 = (bf16[1,224,128]{2,1,0:T(8,128)(2,1)S(1)}, bf16[1,224,128]{2,1,0:T(8,128)(2,1)S(1)}, u32[]{:S(2)}, u32[]{:S(2)}) collective-permute-start(bf16[1,224,128]{2,1,0:T(8,128)(2,1)S(1)} %get-tuple-element.97), channel_id=1, source_target_pairs={{0,8},{1,9},{2,10},{3,11},{4,12},{5,13},{6,14},{7,15},{8,0},{9,1},... | collective-permute-start | bytes 172040 | tf_op jit(solution)/shard_map/ppermute | solution.py:367
  69.0 8.3 %collective-permute-start.14 = (bf16[1,240,128]{2,1,0:T(8,128)(2,1)S(1)}, bf16[1,240,128]{2,1,0:T(8,128)(2,1)S(1)}, u32[]{:S(2)}, u32[]{:S(2)}) collective-permute-start(bf16[1,240,128]{2,1,0:T(8,128)(2,1)S(1)} %get-tuple-element.85), channel_id=1, source_target_pairs={{0,8},{1,9},{2,10},{3,11},{4,12},{5,13},{6,14},{7,15},{8,0},{9,1},... | collective-permute-start | bytes 184328 | tf_op jit(solution)/shard_map/ppermute | solution.py:367
  72.1 5.1 %collective-permute-start.26 = (bf16[1,224,128]{2,1,0:T(8,128)(2,1)S(1)}, bf16[1,224,128]{2,1,0:T(8,128)(2,1)S(1)}, u32[]{:S(2)}, u32[]{:S(2)}) collective-permute-start(bf16[1,224,128]{2,1,0:T(8,128)(2,1)S(1)} %get-tuple-element.109), channel_id=1, source_target_pairs={{0,8},{1,9},{2,10},{3,11},{4,12},{5,13},{6,14},{7,15},{8,0},{9,1},... | collective-permute-start | bytes 172040 | tf_op jit(solution)/shard_map/ppermute | solution.py:367
  77.3 1.5 %collective-permute-start.28 = (f32[224,128]{1,0:T(8,128)S(1)}, f32[224,128]{1,0:T(8,128)S(1)}, u32[]{:S(2)}, u32[]{:S(2)}) collective-permute-start(f32[224,128]{1,0:T(8,128)S(1)} %shard_map.128.refs_1_), channel_id=1, source_target_pairs={{0,16},{16,0},{1,17},{17,1},{2,18},{18,2},{3,19},{19,3},{4,20},{20... | collective-permute-start | bytes 344072 | tf_op jit(solution)/shard_map/ppermute | solution.py:371
  77.3 1.5 %collective-permute-start.29 = (f32[224,128]{1,0:T(8,128)S(1)}, f32[224,128]{1,0:T(8,128)S(1)}, u32[]{:S(2)}, u32[]{:S(2)}) collective-permute-start(f32[224,128]{1,0:T(8,128)S(1)} %shard_map.133.refs_2_), channel_id=1, source_target_pairs={{0,16},{16,0},{1,17},{17,1},{2,18},{18,2},{3,19},{19,3},{4,20},{20... | collective-permute-start | bytes 344072 | tf_op jit(solution)/shard_map/ppermute | solution.py:371
  77.9 1.4 %collective-permute-start.27 = (f32[240,128]{1,0:T(8,128)S(1)}, f32[240,128]{1,0:T(8,128)S(1)}, u32[]{:S(2)}, u32[]{:S(2)}) collective-permute-start(f32[240,128]{1,0:T(8,128)S(1)} %shard_map.123.refs_0_), channel_id=1, source_target_pairs={{0,16},{16,0},{1,17},{17,1},{2,18},{18,2},{3,19},{19,3},{4,20},{20... | collective-permute-start | bytes 368648 | tf_op jit(solution)/shard_map/ppermute | solution.py:371
  (4 other events, 6.0 us)

commit v5 on v4

--- a/solution.py
+++ b/solution.py
@@ -13,6 +13,7 @@
 TABLE_ROWS = 32
 MIB = 1024 * 1024
 STREAMS = 3
+MIDDLE = 15
 
 
 def group_bounds():
@@ -171,9 +172,10 @@
     n_dst = plan.n_dst
     rot_ref, atom_ref, refs = refs[0], refs[1], refs[2:]
     left_refs, (w_zero, w_one, w_two), refs = refs[: MMAX + 1], refs[MMAX + 1 : MMAX + 4], refs[MMAX + 4 :]
-    part_refs = refs[:n_dst]
-    spread_ref, flat_ref, message_ref, sum_ref = refs[n_dst:]
+    part_refs = refs[:2]
+    spread_ref, flat_ref, message_ref, sum_ref = refs[2:]
     channels, slots = sum_ref.shape[1], plan.slots
+    rows = part_refs[0].shape[0] // (n_dst // 2)
 
     def columns(start, length):
         return slice(start * channels, (start + length) * channels)
@@ -208,9 +210,10 @@
         total = sum_ref[0:depth, :].reshape(2 * degree + 1, n_dst * plan.atoms, channels)
         for place in range(n_dst):
             piece = total[:, place * plan.atoms : (place + 1) * plan.atoms, :]
-            part_refs[place][
-                degree * degree * plan.atoms : (degree + 1) * (degree + 1) * plan.atoms, :
-            ] = piece.reshape((2 * degree + 1) * plan.atoms, channels).astype(part_refs[place].dtype)
+            target, start = part_refs[place % 2], (place // 2) * rows
+            target[
+                start + degree * degree * plan.atoms : start + (degree + 1) * (degree + 1) * plan.atoms, :
+            ] = piece.reshape((2 * degree + 1) * plan.atoms, channels).astype(target.dtype)
 
 
 def rotate_kernel(plan, lay, *refs):
@@ -261,7 +264,8 @@
         self.share = share
         self.half_rows = -(-(-(-share // 2)) // 16) * 16
         tiles = self.half_rows // 16
-        self.sizes = [16 * ((tiles + STREAMS - 1 - k) // STREAMS) for k in range(STREAMS)]
+        middle = tiles * MIDDLE // 43
+        self.sizes = [16 * x for x in ((tiles - middle + 1) // 2, middle, (tiles - middle) // 2)]
         self.parts = plan.parts // 2
         self.rows = self.parts * share
 
@@ -317,15 +321,32 @@
             target[top * (parts // 2) + (index // (2 * lo)) * lo + index % lo] = total.astype(target.dtype)
 
 
-def add_kernel(lo, kept_ref, came_ref, *outs):
-    outs = outs[-2:] if lo is not None else outs[-1:]
-    for block in range(kept_ref.shape[0]):
-        total = kept_ref[block] + came_ref[block].astype(jnp.float32)
+def block_at(ref, block, size):
+    return ref.at[block] if len(ref.shape) == 3 else ref.at[block * size : (block + 1) * size]
+
+
+def add_kernel(lo, extra, kept_ref, came_ref, *refs):
+    count, size = kept_ref.shape[0], kept_ref.shape[1]
+    outs = refs[-2:] if lo is not None else refs[-1:]
+    for block in range(count):
+        total = kept_ref[block] + block_at(came_ref, block, size)[...].astype(jnp.float32)
         if lo is None:
             outs[0][...] = total
             continue
         target = outs[(block // lo) % 2]
-        target[(block // (2 * lo)) * lo + block % lo] = total.astype(target.dtype)
+        block_at(target, (block // (2 * lo)) * lo + block % lo, size)[...] = total.astype(target.dtype)
+    if extra:
+        outs[1][count // 2 * size :, :] = refs[0][...]
+
+
+def fold_kernel(start, rows, kept_ref, came_ref, *outs):
+    count = kept_ref.shape[0] // rows
+    for place in range(count):
+        total = kept_ref[place * rows : (place + 1) * rows, :] + came_ref[
+            start + place * rows : start + (place + 1) * rows, :
+        ].astype(jnp.float32)
+        target = outs[place % 2]
+        target[place // 2 * rows : (place // 2 + 1) * rows, :] = total.astype(target.dtype)
 
 
 def join_kernel(shift, sizes, *refs):
@@ -459,12 +480,10 @@
     second_half = whole_call(
         functools.partial(gram_kernel, plan, lay), halves, [*sides], [flat], flops=3 * 10**9
     )
-    partial_sums = list(whole_call(
+    node_size = coeffs * atoms
+    folded, away = whole_call(
         functools.partial(message_kernel, plan),
-        [
-            jax.ShapeDtypeStruct((coeffs * atoms, channels), f32 if place == 0 else bf16)
-            for place in range(plan.n_dst)
-        ],
+        [jax.ShapeDtypeStruct((plan.n_dst // 2 * node_size, channels), kind) for kind in (f32, bf16)],
         [rot, dst_slot, *sides[: MMAX + 1], w_zero, w_one, w_two],
         [
             ((deepest * plan.n_dst, slots), bf16),
@@ -473,7 +492,7 @@
             ((deepest * plan.n_dst, channels), f32),
         ],
         flops=8 * 10**9,
-    ))
+    )
     n_bits = parts.bit_length() - 1
     came = [[swap_cores(half[2 * k + 1]) for half in (first_half, second_half)] for k in range(STREAMS)]
     kept_part = [None] * STREAMS
@@ -486,7 +505,7 @@
         for k in (1, 2, 0):
             if stage == n_bits:
                 mine[k] = whole_call(
-                    functools.partial(add_kernel, None),
+                    functools.partial(add_kernel, None, False),
                     [jax.ShapeDtypeStruct((sizes[k], channels), f32)],
                     [kept_part[k], came[k]],
                 )[0]
@@ -504,20 +523,30 @@
                     functools.partial(join_halves_kernel, 1 << place, lay.parts),
                     outs,
                     [*both],
-                            )
+                )
             else:
+                extra = False
+                if extra:
+                    start = shape[0] * sizes[k]
+                    outs[1] = jax.ShapeDtypeStruct((start + away.shape[0], channels), bf16)
                 kept_part[k], sent = whole_call(
-                    functools.partial(add_kernel, 1 << place),
+                    functools.partial(add_kernel, 1 << place, extra),
                     outs,
-                    [kept_part[k], came[k]] + ([partial_sums[1]] if stage == 1 else []),
+                    [kept_part[k], came[k]] + ([away] if extra or stage == 1 else []),
                 )
             came[k] = swap(sent, 1 << bit)
-    total = partial_sums[0]
-    for place, flip in enumerate(flips(plan.dst_bits)):
-        if place > 0:
-            total = total + swap(partial_sums[place], flip).astype(f32)
-    aggregated = total.astype(bf16).reshape(coeffs, atoms, channels).transpose(1, 0, 2)
-
+    arrived, start = swap(away, 1), 0
+    for number in range(1, len(plan.dst_bits) + 1):
+        count = plan.n_dst >> (number + 1)
+        shapes = [(count * node_size, channels)] * 2 if count else [(node_size, channels)]
+        outs = [jax.ShapeDtypeStruct(x, kind) for x, kind in zip(shapes, (f32, bf16) if count else (bf16,))]
+        folded, *away = whole_call(
+            functools.partial(fold_kernel, start, node_size), outs, [folded, arrived]
+        )
+        start = 0
+        if count:
+            arrived = swap(away[0], 1 << plan.dst_bits[number])
+    aggregated = folded.reshape(coeffs, atoms, channels).transpose(1, 0, 2)
     theirs = [swap_cores(item) for item in mine]
     weight_grad = whole_call(
         functools.partial(join_kernel, share - lay.half_rows, sizes),

time: 80.8 us -> 78.6 us (0.973)
  starting transfers between devices: 37.3 us -> 33.4 us
  waiting for transfers between devices: 22.8 us -> 25 us
    ppermute x21 -> x20, starting transfers between devices: 35 us -> 31.5 us  [swap(): return lax.ppermute(value, 'graph', [(i, i ^ flip) for i in range(count)])]
    ppermute x21 -> x20, waiting for transfers between devices: 20.8 us -> 22.9 us  [swap(): return lax.ppermute(value, 'graph', [(i, i ^ flip) for i in range(count)])]
    pallas_call x22 -> x24, Pallas kernels: 14.8 us -> 15.5 us  [whole_call(): pl.pallas_call(kernel, out_shape=outs, in_specs=specs, out_specs=[pl.Bloc...]
  transfers between devices with their start and end apart: 30 -> 29, of which waited for: 12 -> 10; matrix products, arithmetic and copies ran while one was open for 1% -> 0% of each run, Pallas kernels for 10% -> 12%
where the time goes in v5:
time: 78.6 us; the launch traced here: 78.4 us
  starting transfers between devices  33.4 us (42%)
  waiting for transfers between devices  25 us (32%)
  Pallas kernels  15.5 us (20%)
  local copies, waits for them, and re-layouts  3.01 us (4%)
  between operations  0.81 us (1%)
    ppermute x20, starting transfers between devices, swap(): return lax.ppermute(value, 'graph', [(i, i ^ flip) for i in range(count)])  31.5 us
    ppermute x20, waiting for transfers between devices, swap(): return lax.ppermute(value, 'graph', [(i, i ^ flip) for i in range(count)])  22.9 us
    pallas_call x24, Pallas kernels, whole_call(): pl.pallas_call(kernel, out_shape=outs, in_specs=specs, out_specs=[pl.Bloc...  15.5 us
    unnamed x12, local copies, waits for them, and re-layouts  3.01 us
    ppermute x9, waiting for transfers between devices, swap_cores(): return lax.ppermute(value, 'dp', [(i, 1 - i) for i in range(2)])  2.08 us
    ppermute x9, starting transfers between devices, swap_cores(): return lax.ppermute(value, 'dp', [(i, 1 - i) for i in range(2)])  1.87 us
  transfers between devices with their start and end apart: 29, of which 10 were waited for; matrix products, arithmetic and copies ran while one was open for 0% of the time, Pallas kernels for 12%

profile of v5, /device:TPU:0, one launch (start us, length us, event | category | flops | bytes accessed | tf_op | source)
XLA Modules:
  0.0 78.4 jit_solution(4253842897093163746)
XLA Ops:
  1.3 0.9 %copy-done.1 = bf16[16,49,128]{2,0,1:T(8,128)(2,1)S(1)} copy-done((bf16[16,49,128]{2,0,1:T(8,128)(2,1)S(1)}, bf16[16,49,128]{2,0,1:T(8,128)(2,1)}, u32[]{:S(2)}) %copy-start.1) | copy-done | bytes 200728
  2.6 3.0 %collective-permute-start = (bf16[800,128]{1,0:T(8,128)(2,1)S(1)}, bf16[800,128]{1,0:T(8,128)(2,1)S(1)}, u32[]{:S(2)}, u32[]{:S(2)}) collective-permute-start(bf16[800,128]{1,0:T(8,128)(2,1)S(1)} %shard_map.114.refs_1_), channel_id=1, source_target_pairs={{0,2},{1,3},{2,0},{3,1},{4,6},{5,7},{6,4},{7,5},{8,10},{9,11},{10,... | collective-permute-start | bytes 614408 | tf_op jit(solution)/shard_map/ppermute | solution.py:388
  5.5 2.6 %collective-permute-start.1 = (bf16[800,128]{1,0:T(8,128)(2,1)S(1)}, bf16[800,128]{1,0:T(8,128)(2,1)S(1)}, u32[]{:S(2)}, u32[]{:S(2)}) collective-permute-start(bf16[800,128]{1,0:T(8,128)(2,1)S(1)} %shard_map.114.refs_1_), channel_id=1, source_target_pairs={{0,8},{1,9},{2,10},{3,11},{4,12},{5,13},{6,14},{7,15},{8,0},{9,1},... | collective-permute-start | bytes 614408 | tf_op jit(solution)/shard_map/ppermute | solution.py:388
  8.1 1.6 %collective-permute-start.2 = (bf16[784,128]{1,0:T(8,128)(2,1)}, bf16[784,128]{1,0:T(8,128)(2,1)S(1)}, u32[]{:S(2)}, u32[]{:S(2)}) collective-permute-start(bf16[784,128]{1,0:T(8,128)(2,1)} %bitcast.17), channel_id=1, source_target_pairs={{0,4},{1,5},{2,6},{3,7},{4,0},{5,1},{6,2},{7,3},{8,12},{9,13},{10,... | collective-permute-start | bytes 602120 | tf_op jit(solution)/shard_map/ppermute | solution.py:388
  9.7 1.5 %collective-permute-start.3 = (bf16[784,128]{1,0:T(8,128)(2,1)}, bf16[784,128]{1,0:T(8,128)(2,1)S(1)}, u32[]{:S(2)}, u32[]{:S(2)}) collective-permute-start(bf16[784,128]{1,0:T(8,128)(2,1)} %bitcast.18), channel_id=1, source_target_pairs={{0,1},{1,0},{2,3},{3,2},{4,5},{5,4},{6,7},{7,6},{8,9},{9,8},{10,11... | collective-permute-start | bytes 602120 | tf_op jit(solution)/shard_map/ppermute | solution.py:388
  11.2 1.1 %copy-done = bf16[256,29,49]{0,1,2:T(8,128)(2,1)S(1)} copy-done((bf16[256,29,49]{0,1,2:T(8,128)(2,1)S(1)}, bf16[256,29,49]{0,1,2:T(8,128)(2,1)}, u32[]{:S(2)}) %copy-start) | copy-done | bytes 727576
  12.3 0.9 %copy-done.2 = bf16[16,49,128]{2,0,1:T(8,128)(2,1)S(1)} copy-done((bf16[16,49,128]{2,0,1:T(8,128)(2,1)S(1)}, bf16[16,49,128]{2,0,1:T(8,128)(2,1)}, u32[]{:S(2)}) %copy-start.2) | copy-done | bytes 200728
  13.4 4.4 %collective-permute-done.2.refs_1_ = bf16[784,128]{1,0:T(8,128)(2,1)S(1)} collective-permute-done((bf16[784,128]{1,0:T(8,128)(2,1)}, bf16[784,128]{1,0:T(8,128)(2,1)S(1)}, u32[]{:S(2)}, u32[]{:S(2)}) %collective-permute-start.2) | collective-permute-done | bytes 200736 | tf_op jit(solution)/shard_map/ppermute | solution.py:388
  18.3 1.5 %collective-permute-start.5 = (bf16[784,128]{1,0:T(8,128)(2,1)S(1)}, bf16[784,128]{1,0:T(8,128)(2,1)S(1)}, u32[]{:S(2)}, u32[]{:S(2)}) collective-permute-start(bf16[784,128]{1,0:T(8,128)(2,1)S(1)} %get-tuple-element.59.refs_7_), channel_id=1, source_target_pairs={{0,1},{1,0},{2,3},{3,2},{4,5},{5,4},{6,7},{7,6},{8,9},{9,8},{10,11... | collective-permute-start | bytes 602120 | tf_op jit(solution)/shard_map/ppermute | solution.py:388
  19.9 4.2 %collective-permute-done.5.refs_8_ = bf16[784,128]{1,0:T(8,128)(2,1)S(1)} collective-permute-done((bf16[784,128]{1,0:T(8,128)(2,1)S(1)}, bf16[784,128]{1,0:T(8,128)(2,1)S(1)}, u32[]{:S(2)}, u32[]{:S(2)}) %collective-permute-start.5) | collective-permute-done | bytes 200736 | tf_op jit(solution)/shard_map/ppermute | solution.py:388
  24.0 5.1 %shard_map.116 = (f32[1568,256]{1,0:T(8,128)S(1)}, s32[8,256]{1,0:T(8,128)S(1)}, bf16[896,256]{1,0:T(8,128)(2,1)S(1)}, bf16[768,512]{1,0:T(8,128)(2,1)S(1)}, bf1...) custom-call(bf16[49,32,256]{2,1,0:T(8,128)(2,1)S(1)} %get-tuple-elem, ...), custom_call_target="tpu_custom_call" | custom-call | flops 5000000000 | bytes 100000 | tf_op jit(solution)/shard_map/pallas_call | solution.py:374
  29.8 2.2 %shard_map.120 = (f32[8,224,128]{2,1,0:T(8,128)S(1)}, bf16[8,224,128]{2,1,0:T(8,128)(2,1)S(1)}, f32[8,240,128]{2,1,0:T(8,128)S(1)}, bf16[8,240,128]{2,1,0:T(8,12...) custom-call(bf16[896,256]{1,0:T(8,128)(2,1)S(1)} %get-tuple-element.62.refs_2_.refs_0_, ...), custom_call_target="tpu_custom_call" | custom-call | flops 3000000000 | bytes 100000 | tf_op jit(solution)/shard_map/pallas_call | solution.py:374
  33.0 1.5 %collective-permute-done.9.refs_3_ = bf16[8,224,128]{2,1,0:T(8,128)(2,1)S(1)} collective-permute-done((bf16[8,224,128]{2,1,0:T(8,128)(2,1)S(1)}, bf16[8,224,128]{2,1,0:T(8,128)(2,1)S(1)}, u32[]{:S(2)}, u32[]{:S(2)}) %collective-permute-start.9) | collective-permute-done | bytes 458784 | tf_op jit(solution)/shard_map/ppermute | solution.py:392
  34.7 1.6 %collective-permute-start.10 = (bf16[8,224,128]{2,1,0:T(8,128)(2,1)S(1)}, bf16[8,224,128]{2,1,0:T(8,128)(2,1)S(1)}, u32[]{:S(2)}, u32[]{:S(2)}) collective-permute-start(bf16[8,224,128]{2,1,0:T(8,128)(2,1)S(1)} %get-tuple-element.79), channel_id=1, source_target_pairs={{0,1},{1,0},{2,3},{3,2},{4,5},{5,4},{6,7},{7,6},{8,9},{9,8},{10,11... | collective-permute-start | bytes 1376264 | tf_op jit(solution)/shard_map/ppermute | solution.py:388
  36.5 1.3 %collective-permute-start.22 = (bf16[8,224,128]{2,1,0:T(8,128)(2,1)S(1)}, bf16[8,224,128]{2,1,0:T(8,128)(2,1)S(1)}, u32[]{:S(2)}, u32[]{:S(2)}) collective-permute-start(bf16[8,224,128]{2,1,0:T(8,128)(2,1)S(1)} %get-tuple-element.103), channel_id=1, source_target_pairs={{0,4},{1,5},{2,6},{3,7},{4,0},{5,1},{6,2},{7,3},{8,12},{9,13},{10,... | collective-permute-start | bytes 1376264 | tf_op jit(solution)/shard_map/ppermute | solution.py:388
  38.0 1.6 %collective-permute-start.16 = (bf16[8,240,128]{2,1,0:T(8,128)(2,1)S(1)}, bf16[8,240,128]{2,1,0:T(8,128)(2,1)S(1)}, u32[]{:S(2)}, u32[]{:S(2)}) collective-permute-start(bf16[8,240,128]{2,1,0:T(8,128)(2,1)S(1)} %get-tuple-element.91), channel_id=1, source_target_pairs={{0,2},{1,3},{2,0},{3,1},{4,6},{5,7},{6,4},{7,5},{8,10},{9,11},{10,... | collective-permute-start | bytes 1474568 | tf_op jit(solution)/shard_map/ppermute | solution.py:388
  39.6 5.1 %shard_map.117 = (f32[1568,128]{1,0:T(8,128)S(1)}, bf16[1568,128]{1,0:T(8,128)(2,1)S(1)}) custom-call(f32[1568,256]{1,0:T(8,128)S(1)} %get-tuple-element.60.refs_0_, s32[8,256]{1,0:T(8,128)S(1)} %get-tuple-element.61.refs_1_, bf16[896,256]{1,0:T(8,128)(2,1)S(1)} %get-tuple-element.62.refs_2_.refs_0_, bf16[768,512]{1,0:T(8,128)(2,1)S(1)} %get-tuple-element.63.refs_3_.refs_1_, ...), custom_call_target="tpu_custom_call" | custom-call | flops 8000000000 | bytes 100000 | tf_op jit(solution)/shard_map/pallas_call | solution.py:374
  44.7 1.1 %collective-permute-start.6 = (bf16[1568,128]{1,0:T(8,128)(2,1)S(1)}, bf16[1568,128]{1,0:T(8,128)(2,1)S(1)}, u32[]{:S(2)}, u32[]{:S(2)}) collective-permute-start(bf16[1568,128]{1,0:T(8,128)(2,1)S(1)} %get-tuple-element.66.refs_0_), channel_id=1, source_target_pairs={{0,1},{1,0},{2,3},{3,2},{4,5},{5,4},{6,7},{7,6},{8,9},{9,8},{10,11... | collective-permute-start | bytes 1204232 | tf_op jit(solution)/shard_map/ppermute | solution.py:388
  45.8 5.0 %collective-permute-done.16.came_ref = bf16[8,240,128]{2,1,0:T(8,128)(2,1)S(1)} collective-permute-done((bf16[8,240,128]{2,1,0:T(8,128)(2,1)S(1)}, bf16[8,240,128]{2,1,0:T(8,128)(2,1)S(1)}, u32[]{:S(2)}, u32[]{:S(2)}) %collective-permute-start.16) | collective-permute-done | bytes 491552 | tf_op jit(solution)/shard_map/ppermute | solution.py:388
  50.8 0.9 %collective-permute-start.17 = (bf16[4,240,128]{2,1,0:T(8,128)(2,1)S(1)}, bf16[4,240,128]{2,1,0:T(8,128)(2,1)S(1)}, u32[]{:S(2)}, u32[]{:S(2)}) collective-permute-start(bf16[4,240,128]{2,1,0:T(8,128)(2,1)S(1)} %get-tuple-element.93), channel_id=1, source_target_pairs={{0,4},{1,5},{2,6},{3,7},{4,0},{5,1},{6,2},{7,3},{8,12},{9,13},{10,... | collective-permute-start | bytes 737288 | tf_op jit(solution)/shard_map/ppermute | solution.py:388
  51.8 1.6 %collective-permute-start.11 = (bf16[4,224,128]{2,1,0:T(8,128)(2,1)S(1)}, bf16[4,224,128]{2,1,0:T(8,128)(2,1)S(1)}, u32[]{:S(2)}, u32[]{:S(2)}) collective-permute-start(bf16[4,224,128]{2,1,0:T(8,128)(2,1)S(1)} %get-tuple-element.81), channel_id=1, source_target_pairs={{0,2},{1,3},{2,0},{3,1},{4,6},{5,7},{6,4},{7,5},{8,10},{9,11},{10,... | collective-permute-start | bytes 688136 | tf_op jit(solution)/shard_map/ppermute | solution.py:388
  53.4 1.4 %collective-permute-start.23 = (bf16[4,224,128]{2,1,0:T(8,128)(2,1)S(1)}, bf16[4,224,128]{2,1,0:T(8,128)(2,1)S(1)}, u32[]{:S(2)}, u32[]{:S(2)}) collective-permute-start(bf16[4,224,128]{2,1,0:T(8,128)(2,1)S(1)} %get-tuple-element.105), channel_id=1, source_target_pairs={{0,1},{1,0},{2,3},{3,2},{4,5},{5,4},{6,7},{7,6},{8,9},{9,8},{10,11... | collective-permute-start | bytes 688136 | tf_op jit(solution)/shard_map/ppermute | solution.py:388
  54.8 2.6 %collective-permute-done.17.came_ref = bf16[4,240,128]{2,1,0:T(8,128)(2,1)S(1)} collective-permute-done((bf16[4,240,128]{2,1,0:T(8,128)(2,1)S(1)}, bf16[4,240,128]{2,1,0:T(8,128)(2,1)S(1)}, u32[]{:S(2)}, u32[]{:S(2)}) %collective-permute-start.17) | collective-permute-done | bytes 245792 | tf_op jit(solution)/shard_map/ppermute | solution.py:388
  57.5 1.7 %collective-permute-start.18 = (bf16[2,240,128]{2,1,0:T(8,128)(2,1)S(1)}, bf16[2,240,128]{2,1,0:T(8,128)(2,1)S(1)}, u32[]{:S(2)}, u32[]{:S(2)}) collective-permute-start(bf16[2,240,128]{2,1,0:T(8,128)(2,1)S(1)} %get-tuple-element.95), channel_id=1, source_target_pairs={{0,1},{1,0},{2,3},{3,2},{4,5},{5,4},{6,7},{7,6},{8,9},{9,8},{10,11... | collective-permute-start | bytes 368648 | tf_op jit(solution)/shard_map/ppermute | solution.py:388
  60.1 2.0 %collective-permute-done.23.came_ref = bf16[4,224,128]{2,1,0:T(8,128)(2,1)S(1)} collective-permute-done((bf16[4,224,128]{2,1,0:T(8,128)(2,1)S(1)}, bf16[4,224,128]{2,1,0:T(8,128)(2,1)S(1)}, u32[]{:S(2)}, u32[]{:S(2)}) %collective-permute-start.23) | collective-permute-done | bytes 229408 | tf_op jit(solution)/shard_map/ppermute | solution.py:388
  62.1 1.1 %collective-permute-start.24 = (bf16[2,224,128]{2,1,0:T(8,128)(2,1)S(1)}, bf16[2,224,128]{2,1,0:T(8,128)(2,1)S(1)}, u32[]{:S(2)}, u32[]{:S(2)}) collective-permute-start(bf16[2,224,128]{2,1,0:T(8,128)(2,1)S(1)} %get-tuple-element.107), channel_id=1, source_target_pairs={{0,2},{1,3},{2,0},{3,1},{4,6},{5,7},{6,4},{7,5},{8,10},{9,11},{10,... | collective-permute-start | bytes 344072 | tf_op jit(solution)/shard_map/ppermute | solution.py:388
  63.3 1.3 %collective-permute-start.7 = (bf16[784,128]{1,0:T(8,128)(2,1)S(1)}, bf16[784,128]{1,0:T(8,128)(2,1)S(1)}, u32[]{:S(2)}, u32[]{:S(2)}) collective-permute-start(bf16[784,128]{1,0:T(8,128)(2,1)S(1)} %get-tuple-element.68), channel_id=1, source_target_pairs={{0,4},{1,5},{2,6},{3,7},{4,0},{5,1},{6,2},{7,3},{8,12},{9,13},{10,... | collective-permute-start | bytes 602120 | tf_op jit(solution)/shard_map/ppermute | solution.py:388
  64.6 3.3 %collective-permute-start.19 = (bf16[1,240,128]{2,1,0:T(8,128)(2,1)S(1)}, bf16[1,240,128]{2,1,0:T(8,128)(2,1)S(1)}, u32[]{:S(2)}, u32[]{:S(2)}) collective-permute-start(bf16[1,240,128]{2,1,0:T(8,128)(2,1)S(1)} %get-tuple-element.97), channel_id=1, source_target_pairs={{0,8},{1,9},{2,10},{3,11},{4,12},{5,13},{6,14},{7,15},{8,0},{9,1},... | collective-permute-start | bytes 184328 | tf_op jit(solution)/shard_map/ppermute | solution.py:388
  68.1 3.0 %collective-permute-start.25 = (bf16[1,224,128]{2,1,0:T(8,128)(2,1)S(1)}, bf16[1,224,128]{2,1,0:T(8,128)(2,1)S(1)}, u32[]{:S(2)}, u32[]{:S(2)}) collective-permute-start(bf16[1,224,128]{2,1,0:T(8,128)(2,1)S(1)} %get-tuple-element.109), channel_id=1, source_target_pairs={{0,8},{1,9},{2,10},{3,11},{4,12},{5,13},{6,14},{7,15},{8,0},{9,1},... | collective-permute-start | bytes 172040 | tf_op jit(solution)/shard_map/ppermute | solution.py:388
  71.0 1.1 %collective-permute-done.19.came_ref = bf16[1,240,128]{2,1,0:T(8,128)(2,1)S(1)} collective-permute-done((bf16[1,240,128]{2,1,0:T(8,128)(2,1)S(1)}, bf16[1,240,128]{2,1,0:T(8,128)(2,1)S(1)}, u32[]{:S(2)}, u32[]{:S(2)}) %collective-permute-start.19) | collective-permute-done | bytes 61472 | tf_op jit(solution)/shard_map/ppermute | solution.py:388
  72.2 3.3 %collective-permute-done.13.came_ref = bf16[1,224,128]{2,1,0:T(8,128)(2,1)S(1)} collective-permute-done((bf16[1,224,128]{2,1,0:T(8,128)(2,1)S(1)}, bf16[1,224,128]{2,1,0:T(8,128)(2,1)S(1)}, u32[]{:S(2)}, u32[]{:S(2)}) %collective-permute-start.13) | collective-permute-done | bytes 57376 | tf_op jit(solution)/shard_map/ppermute | solution.py:388
  77.5 0.9 %shard_map.136 = f32[1368,128]{1,0:T(8,128)} custom-call(f32[224,128]{1,0:T(8,128)S(1)} %shard_map.125.refs_0_, f32[240,128]{1,0:T(8,128)S(1)} %shard_map.130.refs_1_, f32[224,128]{1,0:T(8,128)S(1)} %shard_map.135.refs_2_, f32[224,128]{1,0:T(8,128)S(1)} %collective-permute-done.26.refs_3_, f32[240,128]{1,0:T(8,128)S(1)} %collective-permute-done.27.refs_4_, ...), custom_call_target="tpu_custom_call" | custom-call | flops 1000000 | bytes 100000 | tf_op jit(solution)/shard_map/pallas_call | solution.py:374
  (63 shorter events, 7.4 us)
Async XLA Ops:
  2.6 15.2 %collective-permute-start = (bf16[800,128]{1,0:T(8,128)(2,1)S(1)}, bf16[800,128]{1,0:T(8,128)(2,1)S(1)}, u32[]{:S(2)}, u32[]{:S(2)}) collective-permute-start(bf16[800,128]{1,0:T(8,128)(2,1)S(1)} %shard_map.114.refs_1_), channel_id=1, source_target_pairs={{0,2},{1,3},{2,0},{3,1},{4,6},{5,7},{6,4},{7,5},{8,10},{9,11},{10,... | collective-permute-start | bytes 614408 | tf_op jit(solution)/shard_map/ppermute | solution.py:388
  5.5 12.3 %collective-permute-start.1 = (bf16[800,128]{1,0:T(8,128)(2,1)S(1)}, bf16[800,128]{1,0:T(8,128)(2,1)S(1)}, u32[]{:S(2)}, u32[]{:S(2)}) collective-permute-start(bf16[800,128]{1,0:T(8,128)(2,1)S(1)} %shard_map.114.refs_1_), channel_id=1, source_target_pairs={{0,8},{1,9},{2,10},{3,11},{4,12},{5,13},{6,14},{7,15},{8,0},{9,1},... | collective-permute-start | bytes 614408 | tf_op jit(solution)/shard_map/ppermute | solution.py:388
  8.1 9.7 %collective-permute-start.2 = (bf16[784,128]{1,0:T(8,128)(2,1)}, bf16[784,128]{1,0:T(8,128)(2,1)S(1)}, u32[]{:S(2)}, u32[]{:S(2)}) collective-permute-start(bf16[784,128]{1,0:T(8,128)(2,1)} %bitcast.17), channel_id=1, source_target_pairs={{0,4},{1,5},{2,6},{3,7},{4,0},{5,1},{6,2},{7,3},{8,12},{9,13},{10,... | collective-permute-start | bytes 602120 | tf_op jit(solution)/shard_map/ppermute | solution.py:388
  9.7 8.1 %collective-permute-start.3 = (bf16[784,128]{1,0:T(8,128)(2,1)}, bf16[784,128]{1,0:T(8,128)(2,1)S(1)}, u32[]{:S(2)}, u32[]{:S(2)}) collective-permute-start(bf16[784,128]{1,0:T(8,128)(2,1)} %bitcast.18), channel_id=1, source_target_pairs={{0,1},{1,0},{2,3},{3,2},{4,5},{5,4},{6,7},{7,6},{8,9},{9,8},{10,11... | collective-permute-start | bytes 602120 | tf_op jit(solution)/shard_map/ppermute | solution.py:388
  17.8 6.2 %collective-permute-start.4 = (bf16[800,128]{1,0:T(8,128)(2,1)S(1)}, bf16[800,128]{1,0:T(8,128)(2,1)S(1)}, u32[]{:S(2)}, u32[]{:S(2)}) collective-permute-start(bf16[800,128]{1,0:T(8,128)(2,1)S(1)} %get-tuple-element.58.refs_3_), channel_id=1, source_target_pairs={{0,2},{1,3},{2,0},{3,1},{4,6},{5,7},{6,4},{7,5},{8,10},{9,11},{10,... | collective-permute-start | bytes 614408 | tf_op jit(solution)/shard_map/ppermute | solution.py:388
  18.3 5.7 %collective-permute-start.5 = (bf16[784,128]{1,0:T(8,128)(2,1)S(1)}, bf16[784,128]{1,0:T(8,128)(2,1)S(1)}, u32[]{:S(2)}, u32[]{:S(2)}) collective-permute-start(bf16[784,128]{1,0:T(8,128)(2,1)S(1)} %get-tuple-element.59.refs_7_), channel_id=1, source_target_pairs={{0,1},{1,0},{2,3},{3,2},{4,5},{5,4},{6,7},{7,6},{8,9},{9,8},{10,11... | collective-permute-start | bytes 602120 | tf_op jit(solution)/shard_map/ppermute | solution.py:388
  29.2 3.4 %collective-permute-start.8 = (bf16[8,224,128]{2,1,0:T(8,128)(2,1)S(1)}, bf16[8,224,128]{2,1,0:T(8,128)(2,1)S(1)}, u32[]{:S(2)}, u32[]{:S(2)}) collective-permute-start(bf16[8,224,128]{2,1,0:T(8,128)(2,1)S(1)} %get-tuple-element.70), channel_id=1, source_target_pairs={{0,16},{16,0},{1,17},{17,1},{2,18},{18,2},{3,19},{19,3},{4,20},{20... | collective-permute-start | bytes 1376264 | tf_op jit(solution)/shard_map/ppermute | solution.py:392
  29.3 8.5 %collective-permute-start.14 = (bf16[8,240,128]{2,1,0:T(8,128)(2,1)S(1)}, bf16[8,240,128]{2,1,0:T(8,128)(2,1)S(1)}, u32[]{:S(2)}, u32[]{:S(2)}) collective-permute-start(bf16[8,240,128]{2,1,0:T(8,128)(2,1)S(1)} %get-tuple-element.87), channel_id=1, source_target_pairs={{0,16},{16,0},{1,17},{17,1},{2,18},{18,2},{3,19},{19,3},{4,20},{20... | collective-permute-start | bytes 1474568 | tf_op jit(solution)/shard_map/ppermute | solution.py:392
  31.9 5.9 %collective-permute-start.15 = (bf16[8,240,128]{2,1,0:T(8,128)(2,1)S(1)}, bf16[8,240,128]{2,1,0:T(8,128)(2,1)S(1)}, u32[]{:S(2)}, u32[]{:S(2)}) collective-permute-start(bf16[8,240,128]{2,1,0:T(8,128)(2,1)S(1)} %get-tuple-element.89), channel_id=1, source_target_pairs={{0,16},{16,0},{1,17},{17,1},{2,18},{18,2},{3,19},{19,3},{4,20},{20... | collective-permute-start | bytes 1474568 | tf_op jit(solution)/shard_map/ppermute | solution.py:392
  32.1 2.4 %collective-permute-start.9 = (bf16[8,224,128]{2,1,0:T(8,128)(2,1)S(1)}, bf16[8,224,128]{2,1,0:T(8,128)(2,1)S(1)}, u32[]{:S(2)}, u32[]{:S(2)}) collective-permute-start(bf16[8,224,128]{2,1,0:T(8,128)(2,1)S(1)} %get-tuple-element.77), channel_id=1, source_target_pairs={{0,16},{16,0},{1,17},{17,1},{2,18},{18,2},{3,19},{19,3},{4,20},{20... | collective-permute-start | bytes 1376264 | tf_op jit(solution)/shard_map/ppermute | solution.py:392
  32.5 3.8 %collective-permute-start.20 = (bf16[8,224,128]{2,1,0:T(8,128)(2,1)S(1)}, bf16[8,224,128]{2,1,0:T(8,128)(2,1)S(1)}, u32[]{:S(2)}, u32[]{:S(2)}) collective-permute-start(bf16[8,224,128]{2,1,0:T(8,128)(2,1)S(1)} %get-tuple-element.99), channel_id=1, source_target_pairs={{0,16},{16,0},{1,17},{17,1},{2,18},{18,2},{3,19},{19,3},{4,20},{20... | collective-permute-start | bytes 1376264 | tf_op jit(solution)/shard_map/ppermute | solution.py:392
  32.6 3.7 %collective-permute-start.21 = (bf16[8,224,128]{2,1,0:T(8,128)(2,1)S(1)}, bf16[8,224,128]{2,1,0:T(8,128)(2,1)S(1)}, u32[]{:S(2)}, u32[]{:S(2)}) collective-permute-start(bf16[8,224,128]{2,1,0:T(8,128)(2,1)S(1)} %get-tuple-element.101), channel_id=1, source_target_pairs={{0,16},{16,0},{1,17},{17,1},{2,18},{18,2},{3,19},{19,3},{4,20},{20... | collective-permute-start | bytes 1376264 | tf_op jit(solution)/shard_map/ppermute | solution.py:392
  34.7 17.0 %collective-permute-start.10 = (bf16[8,224,128]{2,1,0:T(8,128)(2,1)S(1)}, bf16[8,224,128]{2,1,0:T(8,128)(2,1)S(1)}, u32[]{:S(2)}, u32[]{:S(2)}) collective-permute-start(bf16[8,224,128]{2,1,0:T(8,128)(2,1)S(1)} %get-tuple-element.79), channel_id=1, source_target_pairs={{0,1},{1,0},{2,3},{3,2},{4,5},{5,4},{6,7},{7,6},{8,9},{9,8},{10,11... | collective-permute-start | bytes 1376264 | tf_op jit(solution)/shard_map/ppermute | solution.py:388
  36.3 3.2 %copy-start.4 = (bf16[2,640,640]{2,1,0:T(8,128)(2,1)S(1)}, bf16[2,640,640]{2,1,0:T(8,128)(2,1)}, u32[]{:S(2)}) copy-start(bf16[2,640,640]{2,1,0:T(8,128)(2,1)} %refs_7_.1) | copy-start | bytes 4915204
  36.3 3.2 %copy-start.5 = (bf16[896,896]{1,0:T(8,128)(2,1)S(1)}, bf16[896,896]{1,0:T(8,128)(2,1)}, u32[]{:S(2)}) copy-start(bf16[896,896]{1,0:T(8,128)(2,1)} %refs_5_.1) | copy-start | bytes 4816900
  36.5 3.1 %copy-start.3 = (bf16[2,768,768]{2,1,0:T(8,128)(2,1)S(1)}, bf16[2,768,768]{2,1,0:T(8,128)(2,1)}, u32[]{:S(2)}) copy-start(bf16[2,768,768]{2,1,0:T(8,128)(2,1)} %refs_6_.1) | copy-start | bytes 7077892
  36.5 16.8 %collective-permute-start.22 = (bf16[8,224,128]{2,1,0:T(8,128)(2,1)S(1)}, bf16[8,224,128]{2,1,0:T(8,128)(2,1)S(1)}, u32[]{:S(2)}, u32[]{:S(2)}) collective-permute-start(bf16[8,224,128]{2,1,0:T(8,128)(2,1)S(1)} %get-tuple-element.103), channel_id=1, source_target_pairs={{0,4},{1,5},{2,6},{3,7},{4,0},{5,1},{6,2},{7,3},{8,12},{9,13},{10,... | collective-permute-start | bytes 1376264 | tf_op jit(solution)/shard_map/ppermute | solution.py:388
  38.0 12.8 %collective-permute-start.16 = (bf16[8,240,128]{2,1,0:T(8,128)(2,1)S(1)}, bf16[8,240,128]{2,1,0:T(8,128)(2,1)S(1)}, u32[]{:S(2)}, u32[]{:S(2)}) collective-permute-start(bf16[8,240,128]{2,1,0:T(8,128)(2,1)S(1)} %get-tuple-element.91), channel_id=1, source_target_pairs={{0,2},{1,3},{2,0},{3,1},{4,6},{5,7},{6,4},{7,5},{8,10},{9,11},{10,... | collective-permute-start | bytes 1474568 | tf_op jit(solution)/shard_map/ppermute | solution.py:388
  44.7 18.5 %collective-permute-start.6 = (bf16[1568,128]{1,0:T(8,128)(2,1)S(1)}, bf16[1568,128]{1,0:T(8,128)(2,1)S(1)}, u32[]{:S(2)}, u32[]{:S(2)}) collective-permute-start(bf16[1568,128]{1,0:T(8,128)(2,1)S(1)} %get-tuple-element.66.refs_0_), channel_id=1, source_target_pairs={{0,1},{1,0},{2,3},{3,2},{4,5},{5,4},{6,7},{7,6},{8,9},{9,8},{10,11... | collective-permute-start | bytes 1204232 | tf_op jit(solution)/shard_map/ppermute | solution.py:388
  50.8 6.6 %collective-permute-start.17 = (bf16[4,240,128]{2,1,0:T(8,128)(2,1)S(1)}, bf16[4,240,128]{2,1,0:T(8,128)(2,1)S(1)}, u32[]{:S(2)}, u32[]{:S(2)}) collective-permute-start(bf16[4,240,128]{2,1,0:T(8,128)(2,1)S(1)} %get-tuple-element.93), channel_id=1, source_target_pairs={{0,4},{1,5},{2,6},{3,7},{4,0},{5,1},{6,2},{7,3},{8,12},{9,13},{10,... | collective-permute-start | bytes 737288 | tf_op jit(solution)/shard_map/ppermute | solution.py:388
  51.8 7.4 %collective-permute-start.11 = (bf16[4,224,128]{2,1,0:T(8,128)(2,1)S(1)}, bf16[4,224,128]{2,1,0:T(8,128)(2,1)S(1)}, u32[]{:S(2)}, u32[]{:S(2)}) collective-permute-start(bf16[4,224,128]{2,1,0:T(8,128)(2,1)S(1)} %get-tuple-element.81), channel_id=1, source_target_pairs={{0,2},{1,3},{2,0},{3,1},{4,6},{5,7},{6,4},{7,5},{8,10},{9,11},{10,... | collective-permute-start | bytes 688136 | tf_op jit(solution)/shard_map/ppermute | solution.py:388
  53.4 8.6 %collective-permute-start.23 = (bf16[4,224,128]{2,1,0:T(8,128)(2,1)S(1)}, bf16[4,224,128]{2,1,0:T(8,128)(2,1)S(1)}, u32[]{:S(2)}, u32[]{:S(2)}) collective-permute-start(bf16[4,224,128]{2,1,0:T(8,128)(2,1)S(1)} %get-tuple-element.105), channel_id=1, source_target_pairs={{0,1},{1,0},{2,3},{3,2},{4,5},{5,4},{6,7},{7,6},{8,9},{9,8},{10,11... | collective-permute-start | bytes 688136 | tf_op jit(solution)/shard_map/ppermute | solution.py:388
  57.5 7.1 %collective-permute-start.18 = (bf16[2,240,128]{2,1,0:T(8,128)(2,1)S(1)}, bf16[2,240,128]{2,1,0:T(8,128)(2,1)S(1)}, u32[]{:S(2)}, u32[]{:S(2)}) collective-permute-start(bf16[2,240,128]{2,1,0:T(8,128)(2,1)S(1)} %get-tuple-element.95), channel_id=1, source_target_pairs={{0,1},{1,0},{2,3},{3,2},{4,5},{5,4},{6,7},{7,6},{8,9},{9,8},{10,11... | collective-permute-start | bytes 368648 | tf_op jit(solution)/shard_map/ppermute | solution.py:388
  59.2 8.7 %collective-permute-start.12 = (bf16[2,224,128]{2,1,0:T(8,128)(2,1)S(1)}, bf16[2,224,128]{2,1,0:T(8,128)(2,1)S(1)}, u32[]{:S(2)}, u32[]{:S(2)}) collective-permute-start(bf16[2,224,128]{2,1,0:T(8,128)(2,1)S(1)} %get-tuple-element.83), channel_id=1, source_target_pairs={{0,4},{1,5},{2,6},{3,7},{4,0},{5,1},{6,2},{7,3},{8,12},{9,13},{10,... | collective-permute-start | bytes 344072 | tf_op jit(solution)/shard_map/ppermute | solution.py:388
  62.1 5.9 %collective-permute-start.24 = (bf16[2,224,128]{2,1,0:T(8,128)(2,1)S(1)}, bf16[2,224,128]{2,1,0:T(8,128)(2,1)S(1)}, u32[]{:S(2)}, u32[]{:S(2)}) collective-permute-start(bf16[2,224,128]{2,1,0:T(8,128)(2,1)S(1)} %get-tuple-element.107), channel_id=1, source_target_pairs={{0,2},{1,3},{2,0},{3,1},{4,6},{5,7},{6,4},{7,5},{8,10},{9,11},{10,... | collective-permute-start | bytes 344072 | tf_op jit(solution)/shard_map/ppermute | solution.py:388
  63.3 12.9 %collective-permute-start.7 = (bf16[784,128]{1,0:T(8,128)(2,1)S(1)}, bf16[784,128]{1,0:T(8,128)(2,1)S(1)}, u32[]{:S(2)}, u32[]{:S(2)}) collective-permute-start(bf16[784,128]{1,0:T(8,128)(2,1)S(1)} %get-tuple-element.68), channel_id=1, source_target_pairs={{0,4},{1,5},{2,6},{3,7},{4,0},{5,1},{6,2},{7,3},{8,12},{9,13},{10,... | collective-permute-start | bytes 602120 | tf_op jit(solution)/shard_map/ppermute | solution.py:388
  64.6 7.5 %collective-permute-start.19 = (bf16[1,240,128]{2,1,0:T(8,128)(2,1)S(1)}, bf16[1,240,128]{2,1,0:T(8,128)(2,1)S(1)}, u32[]{:S(2)}, u32[]{:S(2)}) collective-permute-start(bf16[1,240,128]{2,1,0:T(8,128)(2,1)S(1)} %get-tuple-element.97), channel_id=1, source_target_pairs={{0,8},{1,9},{2,10},{3,11},{4,12},{5,13},{6,14},{7,15},{8,0},{9,1},... | collective-permute-start | bytes 184328 | tf_op jit(solution)/shard_map/ppermute | solution.py:388
  67.9 7.5 %collective-permute-start.13 = (bf16[1,224,128]{2,1,0:T(8,128)(2,1)S(1)}, bf16[1,224,128]{2,1,0:T(8,128)(2,1)S(1)}, u32[]{:S(2)}, u32[]{:S(2)}) collective-permute-start(bf16[1,224,128]{2,1,0:T(8,128)(2,1)S(1)} %get-tuple-element.85), channel_id=1, source_target_pairs={{0,8},{1,9},{2,10},{3,11},{4,12},{5,13},{6,14},{7,15},{8,0},{9,1},... | collective-permute-start | bytes 172040 | tf_op jit(solution)/shard_map/ppermute | solution.py:388
  68.1 8.0 %collective-permute-start.25 = (bf16[1,224,128]{2,1,0:T(8,128)(2,1)S(1)}, bf16[1,224,128]{2,1,0:T(8,128)(2,1)S(1)}, u32[]{:S(2)}, u32[]{:S(2)}) collective-permute-start(bf16[1,224,128]{2,1,0:T(8,128)(2,1)S(1)} %get-tuple-element.109), channel_id=1, source_target_pairs={{0,8},{1,9},{2,10},{3,11},{4,12},{5,13},{6,14},{7,15},{8,0},{9,1},... | collective-permute-start | bytes 172040 | tf_op jit(solution)/shard_map/ppermute | solution.py:388
  72.1 5.4 %collective-permute-start.27 = (f32[240,128]{1,0:T(8,128)S(1)}, f32[240,128]{1,0:T(8,128)S(1)}, u32[]{:S(2)}, u32[]{:S(2)}) collective-permute-start(f32[240,128]{1,0:T(8,128)S(1)} %shard_map.130.refs_1_), channel_id=1, source_target_pairs={{0,16},{16,0},{1,17},{17,1},{2,18},{18,2},{3,19},{19,3},{4,20},{20... | collective-permute-start | bytes 368648 | tf_op jit(solution)/shard_map/ppermute | solution.py:392
  75.5 1.4 %collective-permute-start.26 = (f32[224,128]{1,0:T(8,128)S(1)}, f32[224,128]{1,0:T(8,128)S(1)}, u32[]{:S(2)}, u32[]{:S(2)}) collective-permute-start(f32[224,128]{1,0:T(8,128)S(1)} %shard_map.125.refs_0_), channel_id=1, source_target_pairs={{0,16},{16,0},{1,17},{17,1},{2,18},{18,2},{3,19},{19,3},{4,20},{20... | collective-permute-start | bytes 344072 | tf_op jit(solution)/shard_map/ppermute | solution.py:392
  76.1 1.4 %collective-permute-start.28 = (f32[224,128]{1,0:T(8,128)S(1)}, f32[224,128]{1,0:T(8,128)S(1)}, u32[]{:S(2)}, u32[]{:S(2)}) collective-permute-start(f32[224,128]{1,0:T(8,128)S(1)} %shard_map.135.refs_2_), channel_id=1, source_target_pairs={{0,16},{16,0},{1,17},{17,1},{2,18},{18,2},{3,19},{19,3},{4,20},{20... | collective-permute-start | bytes 344072 | tf_op jit(solution)/shard_map/ppermute | solution.py:392
  (3 other events, 3.0 us)

commit v6 on v5

--- a/solution.py
+++ b/solution.py
@@ -367,7 +367,7 @@
     return int(np.prod(shape[:-2], initial=1)) * rows * lanes * jnp.dtype(dtype).itemsize
 
 
-def whole_call(kernel, outs, args, scratch=(), flops=10**6, passed=0):
+def whole_call(kernel, outs, args, scratch=(), flops=10**9, passed=0):
     specs = [pl.BlockSpec(memory_space=pltpu.VMEM)] * len(args)
     held = sum(padded_bytes(x.shape, x.dtype) for x in [*args, *outs])
     held = held + sum(padded_bytes(*item) for item in scratch)

time: 78.6 us -> 77.7 us (0.989)
  local copies, waits for them, and re-layouts: 3.01 us -> 0.95 us
  starting transfers between devices: 33.4 us -> 34.6 us
    unnamed x12, local copies, waits for them, and re-layouts: 3.01 us -> 0.95 us
    ppermute x9, waiting for transfers between devices: 2.08 us -> 0.67 us  [swap_cores(): return lax.ppermute(value, 'dp', [(i, 1 - i) for i in range(2)])]
    ppermute x20, waiting for transfers between devices: 22.9 us -> 24 us  [swap(): return lax.ppermute(value, 'graph', [(i, i ^ flip) for i in range(count)])]
    ppermute x20, starting transfers between devices: 31.5 us -> 32.3 us  [swap(): return lax.ppermute(value, 'graph', [(i, i ^ flip) for i in range(count)])]
  transfers between devices with their start and end apart: 29 -> 29, of which waited for: 10 -> 11; matrix products, arithmetic and copies ran while one was open for 0% -> 0% of each run, Pallas kernels for 12% -> 12%
where the time goes in v6:
time: 77.7 us; the launch traced here: 77.6 us
  starting transfers between devices  34.6 us (45%)
  waiting for transfers between devices  24.7 us (32%)
  Pallas kernels  15.8 us (20%)
  local copies, waits for them, and re-layouts  0.95 us (1%)
  between operations  0.8 us (1%)
    ppermute x20, starting transfers between devices, swap(): return lax.ppermute(value, 'graph', [(i, i ^ flip) for i in range(count)])  32.3 us
    ppermute x20, waiting for transfers between devices, swap(): return lax.ppermute(value, 'graph', [(i, i ^ flip) for i in range(count)])  24 us
    pallas_call x24, Pallas kernels, whole_call(): pl.pallas_call(kernel, out_shape=outs, in_specs=specs, out_specs=[pl.Bloc...  15.8 us
    ppermute x9, starting transfers between devices, swap_cores(): return lax.ppermute(value, 'dp', [(i, 1 - i) for i in range(2)])  2.34 us
  transfers between devices with their start and end apart: 29, of which 11 were waited for; matrix products, arithmetic and copies ran while one was open for 0% of the time, Pallas kernels for 12%

profile of v6, /device:TPU:0, one launch (start us, length us, event | category | flops | bytes accessed | tf_op | source)
XLA Modules:
  0.0 77.6 jit_solution(1320478830808103927)
XLA Ops:
  1.3 0.9 %copy-done.4 = bf16[16,49,128]{2,0,1:T(8,128)(2,1)S(1)} copy-done((bf16[16,49,128]{2,0,1:T(8,128)(2,1)S(1)}, bf16[16,49,128]{2,0,1:T(8,128)(2,1)}, u32[]{:S(2)}) %copy-start.4) | copy-done | bytes 200728
  2.6 3.0 %collective-permute-start = (bf16[800,128]{1,0:T(8,128)(2,1)S(1)}, bf16[800,128]{1,0:T(8,128)(2,1)S(1)}, u32[]{:S(2)}, u32[]{:S(2)}) collective-permute-start(bf16[800,128]{1,0:T(8,128)(2,1)S(1)} %shard_map.114.refs_1_), channel_id=1, source_target_pairs={{0,2},{1,3},{2,0},{3,1},{4,6},{5,7},{6,4},{7,5},{8,10},{9,11},{10,... | collective-permute-start | bytes 614408 | tf_op jit(solution)/shard_map/ppermute | solution.py:388
  5.5 2.6 %collective-permute-start.1 = (bf16[800,128]{1,0:T(8,128)(2,1)S(1)}, bf16[800,128]{1,0:T(8,128)(2,1)S(1)}, u32[]{:S(2)}, u32[]{:S(2)}) collective-permute-start(bf16[800,128]{1,0:T(8,128)(2,1)S(1)} %shard_map.114.refs_1_), channel_id=1, source_target_pairs={{0,8},{1,9},{2,10},{3,11},{4,12},{5,13},{6,14},{7,15},{8,0},{9,1},... | collective-permute-start | bytes 614408 | tf_op jit(solution)/shard_map/ppermute | solution.py:388
  8.1 1.6 %collective-permute-start.2 = (bf16[784,128]{1,0:T(8,128)(2,1)S(1)}, bf16[784,128]{1,0:T(8,128)(2,1)S(1)}, u32[]{:S(2)}, u32[]{:S(2)}) collective-permute-start(bf16[784,128]{1,0:T(8,128)(2,1)S(1)} %bitcast.17), channel_id=1, source_target_pairs={{0,4},{1,5},{2,6},{3,7},{4,0},{5,1},{6,2},{7,3},{8,12},{9,13},{10,... | collective-permute-start | bytes 602120 | tf_op jit(solution)/shard_map/ppermute | solution.py:388
  9.7 1.5 %collective-permute-start.3 = (bf16[784,128]{1,0:T(8,128)(2,1)S(1)}, bf16[784,128]{1,0:T(8,128)(2,1)S(1)}, u32[]{:S(2)}, u32[]{:S(2)}) collective-permute-start(bf16[784,128]{1,0:T(8,128)(2,1)S(1)} %bitcast.18), channel_id=1, source_target_pairs={{0,1},{1,0},{2,3},{3,2},{4,5},{5,4},{6,7},{7,6},{8,9},{9,8},{10,11... | collective-permute-start | bytes 602120 | tf_op jit(solution)/shard_map/ppermute | solution.py:388
  11.3 6.2 %collective-permute-done.2.refs_1_ = bf16[784,128]{1,0:T(8,128)(2,1)S(1)} collective-permute-done((bf16[784,128]{1,0:T(8,128)(2,1)S(1)}, bf16[784,128]{1,0:T(8,128)(2,1)S(1)}, u32[]{:S(2)}, u32[]{:S(2)}) %collective-permute-start.2) | collective-permute-done | bytes 200736 | tf_op jit(solution)/shard_map/ppermute | solution.py:388
  18.1 1.5 %collective-permute-start.5 = (bf16[784,128]{1,0:T(8,128)(2,1)S(1)}, bf16[784,128]{1,0:T(8,128)(2,1)S(1)}, u32[]{:S(2)}, u32[]{:S(2)}) collective-permute-start(bf16[784,128]{1,0:T(8,128)(2,1)S(1)} %get-tuple-element.59.refs_7_), channel_id=1, source_target_pairs={{0,1},{1,0},{2,3},{3,2},{4,5},{5,4},{6,7},{7,6},{8,9},{9,8},{10,11... | collective-permute-start | bytes 602120 | tf_op jit(solution)/shard_map/ppermute | solution.py:388
  19.7 4.2 %collective-permute-done.5.refs_8_ = bf16[784,128]{1,0:T(8,128)(2,1)S(1)} collective-permute-done((bf16[784,128]{1,0:T(8,128)(2,1)S(1)}, bf16[784,128]{1,0:T(8,128)(2,1)S(1)}, u32[]{:S(2)}, u32[]{:S(2)}) %collective-permute-start.5) | collective-permute-done | bytes 200736 | tf_op jit(solution)/shard_map/ppermute | solution.py:388
  23.8 5.2 %shard_map.116 = (f32[1568,256]{1,0:T(8,128)S(1)}, s32[8,256]{1,0:T(8,128)S(1)}, bf16[896,256]{1,0:T(8,128)(2,1)S(1)}, bf16[768,512]{1,0:T(8,128)(2,1)S(1)}, bf1...) custom-call(bf16[49,32,256]{2,1,0:T(8,128)(2,1)S(1)} %get-tuple-elem, ...), custom_call_target="tpu_custom_call" | custom-call | flops 5000000000 | bytes 100000 | tf_op jit(solution)/shard_map/pallas_call | solution.py:374
  29.1 2.2 %shard_map.120 = (f32[8,224,128]{2,1,0:T(8,128)S(1)}, bf16[8,224,128]{2,1,0:T(8,128)(2,1)S(1)}, f32[8,240,128]{2,1,0:T(8,128)S(1)}, bf16[8,240,128]{2,1,0:T(8,12...) custom-call(bf16[896,256]{1,0:T(8,128)(2,1)S(1)} %get-tuple-element.62.refs_2_.refs_0_, ...), custom_call_target="tpu_custom_call" | custom-call | flops 3000000000 | bytes 100000 | tf_op jit(solution)/shard_map/pallas_call | solution.py:374
  33.4 1.6 %collective-permute-start.10 = (bf16[8,224,128]{2,1,0:T(8,128)(2,1)S(1)}, bf16[8,224,128]{2,1,0:T(8,128)(2,1)S(1)}, u32[]{:S(2)}, u32[]{:S(2)}) collective-permute-start(bf16[8,224,128]{2,1,0:T(8,128)(2,1)S(1)} %get-tuple-element.79), channel_id=1, source_target_pairs={{0,1},{1,0},{2,3},{3,2},{4,5},{5,4},{6,7},{7,6},{8,9},{9,8},{10,11... | collective-permute-start | bytes 1376264 | tf_op jit(solution)/shard_map/ppermute | solution.py:388
  35.3 1.5 %collective-permute-start.22 = (bf16[8,224,128]{2,1,0:T(8,128)(2,1)S(1)}, bf16[8,224,128]{2,1,0:T(8,128)(2,1)S(1)}, u32[]{:S(2)}, u32[]{:S(2)}) collective-permute-start(bf16[8,224,128]{2,1,0:T(8,128)(2,1)S(1)} %get-tuple-element.103), channel_id=1, source_target_pairs={{0,4},{1,5},{2,6},{3,7},{4,0},{5,1},{6,2},{7,3},{8,12},{9,13},{10,... | collective-permute-start | bytes 1376264 | tf_op jit(solution)/shard_map/ppermute | solution.py:388
  37.0 1.6 %collective-permute-start.16 = (bf16[8,240,128]{2,1,0:T(8,128)(2,1)S(1)}, bf16[8,240,128]{2,1,0:T(8,128)(2,1)S(1)}, u32[]{:S(2)}, u32[]{:S(2)}) collective-permute-start(bf16[8,240,128]{2,1,0:T(8,128)(2,1)S(1)} %get-tuple-element.91), channel_id=1, source_target_pairs={{0,2},{1,3},{2,0},{3,1},{4,6},{5,7},{6,4},{7,5},{8,10},{9,11},{10,... | collective-permute-start | bytes 1474568 | tf_op jit(solution)/shard_map/ppermute | solution.py:388
  38.6 5.2 %shard_map.117 = (f32[1568,128]{1,0:T(8,128)S(1)}, bf16[1568,128]{1,0:T(8,128)(2,1)S(1)}) custom-call(f32[1568,256]{1,0:T(8,128)S(1)} %get-tuple-element.60.refs_0_, s32[8,256]{1,0:T(8,128)S(1)} %get-tuple-element.61.refs_1_, bf16[896,256]{1,0:T(8,128)(2,1)S(1)} %get-tuple-element.62.refs_2_.refs_0_, bf16[768,512]{1,0:T(8,128)(2,1)S(1)} %get-tuple-element.63.refs_3_.refs_1_, ...), custom_call_target="tpu_custom_call" | custom-call | flops 8000000000 | bytes 100000 | tf_op jit(solution)/shard_map/pallas_call | solution.py:374
  43.8 1.2 %collective-permute-start.6 = (bf16[1568,128]{1,0:T(8,128)(2,1)S(1)}, bf16[1568,128]{1,0:T(8,128)(2,1)S(1)}, u32[]{:S(2)}, u32[]{:S(2)}) collective-permute-start(bf16[1568,128]{1,0:T(8,128)(2,1)S(1)} %get-tuple-element.66.refs_0_), channel_id=1, source_target_pairs={{0,1},{1,0},{2,3},{3,2},{4,5},{5,4},{6,7},{7,6},{8,9},{9,8},{10,11... | collective-permute-start | bytes 1204232 | tf_op jit(solution)/shard_map/ppermute | solution.py:388
  45.0 1.3 %collective-permute-done.10.came_ref = bf16[8,224,128]{2,1,0:T(8,128)(2,1)S(1)} collective-permute-done((bf16[8,224,128]{2,1,0:T(8,128)(2,1)S(1)}, bf16[8,224,128]{2,1,0:T(8,128)(2,1)S(1)}, u32[]{:S(2)}, u32[]{:S(2)}) %collective-permute-start.10) | collective-permute-done | bytes 458784 | tf_op jit(solution)/shard_map/ppermute | solution.py:388
  46.4 1.6 %collective-permute-start.11 = (bf16[4,224,128]{2,1,0:T(8,128)(2,1)S(1)}, bf16[4,224,128]{2,1,0:T(8,128)(2,1)S(1)}, u32[]{:S(2)}, u32[]{:S(2)}) collective-permute-start(bf16[4,224,128]{2,1,0:T(8,128)(2,1)S(1)} %get-tuple-element.81), channel_id=1, source_target_pairs={{0,2},{1,3},{2,0},{3,1},{4,6},{5,7},{6,4},{7,5},{8,10},{9,11},{10,... | collective-permute-start | bytes 688136 | tf_op jit(solution)/shard_map/ppermute | solution.py:388
  48.1 1.7 %collective-permute-start.23 = (bf16[4,224,128]{2,1,0:T(8,128)(2,1)S(1)}, bf16[4,224,128]{2,1,0:T(8,128)(2,1)S(1)}, u32[]{:S(2)}, u32[]{:S(2)}) collective-permute-start(bf16[4,224,128]{2,1,0:T(8,128)(2,1)S(1)} %get-tuple-element.105), channel_id=1, source_target_pairs={{0,1},{1,0},{2,3},{3,2},{4,5},{5,4},{6,7},{7,6},{8,9},{9,8},{10,11... | collective-permute-start | bytes 688136 | tf_op jit(solution)/shard_map/ppermute | solution.py:388
  49.8 1.4 %collective-permute-done.16.came_ref = bf16[8,240,128]{2,1,0:T(8,128)(2,1)S(1)} collective-permute-done((bf16[8,240,128]{2,1,0:T(8,128)(2,1)S(1)}, bf16[8,240,128]{2,1,0:T(8,128)(2,1)S(1)}, u32[]{:S(2)}, u32[]{:S(2)}) %collective-permute-start.16) | collective-permute-done | bytes 491552 | tf_op jit(solution)/shard_map/ppermute | solution.py:388
  52.0 4.1 %collective-permute-done.6.came_ref = bf16[1568,128]{1,0:T(8,128)(2,1)S(1)} collective-permute-done((bf16[1568,128]{1,0:T(8,128)(2,1)S(1)}, bf16[1568,128]{1,0:T(8,128)(2,1)S(1)}, u32[]{:S(2)}, u32[]{:S(2)}) %collective-permute-start.6) | collective-permute-done | bytes 401440 | tf_op jit(solution)/shard_map/ppermute | solution.py:388
  56.2 0.8 %collective-permute-start.7 = (bf16[784,128]{1,0:T(8,128)(2,1)S(1)}, bf16[784,128]{1,0:T(8,128)(2,1)S(1)}, u32[]{:S(2)}, u32[]{:S(2)}) collective-permute-start(bf16[784,128]{1,0:T(8,128)(2,1)S(1)} %get-tuple-element.68), channel_id=1, source_target_pairs={{0,4},{1,5},{2,6},{3,7},{4,0},{5,1},{6,2},{7,3},{8,12},{9,13},{10,... | collective-permute-start | bytes 602120 | tf_op jit(solution)/shard_map/ppermute | solution.py:388
  57.0 1.4 %collective-permute-start.12 = (bf16[2,224,128]{2,1,0:T(8,128)(2,1)S(1)}, bf16[2,224,128]{2,1,0:T(8,128)(2,1)S(1)}, u32[]{:S(2)}, u32[]{:S(2)}) collective-permute-start(bf16[2,224,128]{2,1,0:T(8,128)(2,1)S(1)} %get-tuple-element.83), channel_id=1, source_target_pairs={{0,4},{1,5},{2,6},{3,7},{4,0},{5,1},{6,2},{7,3},{8,12},{9,13},{10,... | collective-permute-start | bytes 344072 | tf_op jit(solution)/shard_map/ppermute | solution.py:388
  58.4 1.4 %collective-permute-done.23.came_ref = bf16[4,224,128]{2,1,0:T(8,128)(2,1)S(1)} collective-permute-done((bf16[4,224,128]{2,1,0:T(8,128)(2,1)S(1)}, bf16[4,224,128]{2,1,0:T(8,128)(2,1)S(1)}, u32[]{:S(2)}, u32[]{:S(2)}) %collective-permute-start.23) | collective-permute-done | bytes 229408 | tf_op jit(solution)/shard_map/ppermute | solution.py:388
  59.9 1.6 %collective-permute-start.24 = (bf16[2,224,128]{2,1,0:T(8,128)(2,1)S(1)}, bf16[2,224,128]{2,1,0:T(8,128)(2,1)S(1)}, u32[]{:S(2)}, u32[]{:S(2)}) collective-permute-start(bf16[2,224,128]{2,1,0:T(8,128)(2,1)S(1)} %get-tuple-element.107), channel_id=1, source_target_pairs={{0,2},{1,3},{2,0},{3,1},{4,6},{5,7},{6,4},{7,5},{8,10},{9,11},{10,... | collective-permute-start | bytes 344072 | tf_op jit(solution)/shard_map/ppermute | solution.py:388
  61.6 1.6 %collective-permute-start.18 = (bf16[2,240,128]{2,1,0:T(8,128)(2,1)S(1)}, bf16[2,240,128]{2,1,0:T(8,128)(2,1)S(1)}, u32[]{:S(2)}, u32[]{:S(2)}) collective-permute-start(bf16[2,240,128]{2,1,0:T(8,128)(2,1)S(1)} %get-tuple-element.95), channel_id=1, source_target_pairs={{0,1},{1,0},{2,3},{3,2},{4,5},{5,4},{6,7},{7,6},{8,9},{9,8},{10,11... | collective-permute-start | bytes 368648 | tf_op jit(solution)/shard_map/ppermute | solution.py:388
  63.1 1.2 %collective-permute-done.12.came_ref = bf16[2,224,128]{2,1,0:T(8,128)(2,1)S(1)} collective-permute-done((bf16[2,224,128]{2,1,0:T(8,128)(2,1)S(1)}, bf16[2,224,128]{2,1,0:T(8,128)(2,1)S(1)}, u32[]{:S(2)}, u32[]{:S(2)}) %collective-permute-start.12) | collective-permute-done | bytes 114720 | tf_op jit(solution)/shard_map/ppermute | solution.py:388
  64.3 3.3 %collective-permute-start.13 = (bf16[1,224,128]{2,1,0:T(8,128)(2,1)S(1)}, bf16[1,224,128]{2,1,0:T(8,128)(2,1)S(1)}, u32[]{:S(2)}, u32[]{:S(2)}) collective-permute-start(bf16[1,224,128]{2,1,0:T(8,128)(2,1)S(1)} %get-tuple-element.85), channel_id=1, source_target_pairs={{0,8},{1,9},{2,10},{3,11},{4,12},{5,13},{6,14},{7,15},{8,0},{9,1},... | collective-permute-start | bytes 172040 | tf_op jit(solution)/shard_map/ppermute | solution.py:388
  68.0 2.8 %collective-permute-start.19 = (bf16[1,240,128]{2,1,0:T(8,128)(2,1)S(1)}, bf16[1,240,128]{2,1,0:T(8,128)(2,1)S(1)}, u32[]{:S(2)}, u32[]{:S(2)}) collective-permute-start(bf16[1,240,128]{2,1,0:T(8,128)(2,1)S(1)} %get-tuple-element.97), channel_id=1, source_target_pairs={{0,8},{1,9},{2,10},{3,11},{4,12},{5,13},{6,14},{7,15},{8,0},{9,1},... | collective-permute-start | bytes 184328 | tf_op jit(solution)/shard_map/ppermute | solution.py:388
  70.7 1.5 %collective-permute-done.13.came_ref = bf16[1,224,128]{2,1,0:T(8,128)(2,1)S(1)} collective-permute-done((bf16[1,224,128]{2,1,0:T(8,128)(2,1)S(1)}, bf16[1,224,128]{2,1,0:T(8,128)(2,1)S(1)}, u32[]{:S(2)}, u32[]{:S(2)}) %collective-permute-start.13) | collective-permute-done | bytes 57376 | tf_op jit(solution)/shard_map/ppermute | solution.py:388
  72.3 2.7 %collective-permute-done.19.came_ref = bf16[1,240,128]{2,1,0:T(8,128)(2,1)S(1)} collective-permute-done((bf16[1,240,128]{2,1,0:T(8,128)(2,1)S(1)}, bf16[1,240,128]{2,1,0:T(8,128)(2,1)S(1)}, u32[]{:S(2)}, u32[]{:S(2)}) %collective-permute-start.19) | collective-permute-done | bytes 61472 | tf_op jit(solution)/shard_map/ppermute | solution.py:388
  75.7 0.7 shard_map.119
  76.6 0.9 %shard_map.136 = f32[1368,128]{1,0:T(8,128)} custom-call(f32[224,128]{1,0:T(8,128)S(1)} %shard_map.125.refs_0_, f32[240,128]{1,0:T(8,128)S(1)} %shard_map.130.refs_1_, f32[224,128]{1,0:T(8,128)S(1)} %shard_map.135.refs_2_, f32[224,128]{1,0:T(8,128)S(1)} %collective-permute-done.26.refs_3_, f32[240,128]{1,0:T(8,128)S(1)} %collective-permute-done.27.refs_4_, ...), custom_call_target="tpu_custom_call" | custom-call | flops 1000000000 | bytes 100000 | tf_op jit(solution)/shard_map/pallas_call | solution.py:374
  (63 shorter events, 6.8 us)
Async XLA Ops:
  2.3 5.9 %copy-start.5 = (bf16[16,49,128]{2,0,1:T(8,128)(2,1)S(1)}, bf16[16,49,128]{2,0,1:T(8,128)(2,1)}, u32[]{:S(2)}) copy-start(bf16[16,49,128]{2,0,1:T(8,128)(2,1)} %param.11) | copy-start | bytes 602116
  2.3 8.9 %copy-start.3 = (bf16[256,29,49]{0,1,2:T(8,128)(2,1)S(1)}, bf16[256,29,49]{0,1,2:T(8,128)(2,1)}, u32[]{:S(2)}) copy-start(bf16[256,29,49]{0,1,2:T(8,128)(2,1)} %param.12) | copy-start | bytes 2182660
  2.6 15.0 %collective-permute-start = (bf16[800,128]{1,0:T(8,128)(2,1)S(1)}, bf16[800,128]{1,0:T(8,128)(2,1)S(1)}, u32[]{:S(2)}, u32[]{:S(2)}) collective-permute-start(bf16[800,128]{1,0:T(8,128)(2,1)S(1)} %shard_map.114.refs_1_), channel_id=1, source_target_pairs={{0,2},{1,3},{2,0},{3,1},{4,6},{5,7},{6,4},{7,5},{8,10},{9,11},{10,... | collective-permute-start | bytes 614408 | tf_op jit(solution)/shard_map/ppermute | solution.py:388
  5.5 12.0 %collective-permute-start.1 = (bf16[800,128]{1,0:T(8,128)(2,1)S(1)}, bf16[800,128]{1,0:T(8,128)(2,1)S(1)}, u32[]{:S(2)}, u32[]{:S(2)}) collective-permute-start(bf16[800,128]{1,0:T(8,128)(2,1)S(1)} %shard_map.114.refs_1_), channel_id=1, source_target_pairs={{0,8},{1,9},{2,10},{3,11},{4,12},{5,13},{6,14},{7,15},{8,0},{9,1},... | collective-permute-start | bytes 614408 | tf_op jit(solution)/shard_map/ppermute | solution.py:388
  8.1 9.4 %collective-permute-start.2 = (bf16[784,128]{1,0:T(8,128)(2,1)S(1)}, bf16[784,128]{1,0:T(8,128)(2,1)S(1)}, u32[]{:S(2)}, u32[]{:S(2)}) collective-permute-start(bf16[784,128]{1,0:T(8,128)(2,1)S(1)} %bitcast.17), channel_id=1, source_target_pairs={{0,4},{1,5},{2,6},{3,7},{4,0},{5,1},{6,2},{7,3},{8,12},{9,13},{10,... | collective-permute-start | bytes 602120 | tf_op jit(solution)/shard_map/ppermute | solution.py:388
  9.7 7.9 %collective-permute-start.3 = (bf16[784,128]{1,0:T(8,128)(2,1)S(1)}, bf16[784,128]{1,0:T(8,128)(2,1)S(1)}, u32[]{:S(2)}, u32[]{:S(2)}) collective-permute-start(bf16[784,128]{1,0:T(8,128)(2,1)S(1)} %bitcast.18), channel_id=1, source_target_pairs={{0,1},{1,0},{2,3},{3,2},{4,5},{5,4},{6,7},{7,6},{8,9},{9,8},{10,11... | collective-permute-start | bytes 602120 | tf_op jit(solution)/shard_map/ppermute | solution.py:388
  17.6 6.2 %collective-permute-start.4 = (bf16[800,128]{1,0:T(8,128)(2,1)S(1)}, bf16[800,128]{1,0:T(8,128)(2,1)S(1)}, u32[]{:S(2)}, u32[]{:S(2)}) collective-permute-start(bf16[800,128]{1,0:T(8,128)(2,1)S(1)} %get-tuple-element.58.refs_3_), channel_id=1, source_target_pairs={{0,2},{1,3},{2,0},{3,1},{4,6},{5,7},{6,4},{7,5},{8,10},{9,11},{10,... | collective-permute-start | bytes 614408 | tf_op jit(solution)/shard_map/ppermute | solution.py:388
  18.1 5.7 %collective-permute-start.5 = (bf16[784,128]{1,0:T(8,128)(2,1)S(1)}, bf16[784,128]{1,0:T(8,128)(2,1)S(1)}, u32[]{:S(2)}, u32[]{:S(2)}) collective-permute-start(bf16[784,128]{1,0:T(8,128)(2,1)S(1)} %get-tuple-element.59.refs_7_), channel_id=1, source_target_pairs={{0,1},{1,0},{2,3},{3,2},{4,5},{5,4},{6,7},{7,6},{8,9},{9,8},{10,11... | collective-permute-start | bytes 602120 | tf_op jit(solution)/shard_map/ppermute | solution.py:388
  29.0 3.5 %collective-permute-start.8 = (bf16[8,224,128]{2,1,0:T(8,128)(2,1)S(1)}, bf16[8,224,128]{2,1,0:T(8,128)(2,1)S(1)}, u32[]{:S(2)}, u32[]{:S(2)}) collective-permute-start(bf16[8,224,128]{2,1,0:T(8,128)(2,1)S(1)} %get-tuple-element.70), channel_id=1, source_target_pairs={{0,16},{16,0},{1,17},{17,1},{2,18},{18,2},{3,19},{19,3},{4,20},{20... | collective-permute-start | bytes 1376264 | tf_op jit(solution)/shard_map/ppermute | solution.py:392
  31.3 2.0 %collective-permute-start.9 = (bf16[8,224,128]{2,1,0:T(8,128)(2,1)S(1)}, bf16[8,224,128]{2,1,0:T(8,128)(2,1)S(1)}, u32[]{:S(2)}, u32[]{:S(2)}) collective-permute-start(bf16[8,224,128]{2,1,0:T(8,128)(2,1)S(1)} %get-tuple-element.77), channel_id=1, source_target_pairs={{0,16},{16,0},{1,17},{17,1},{2,18},{18,2},{3,19},{19,3},{4,20},{20... | collective-permute-start | bytes 1376264 | tf_op jit(solution)/shard_map/ppermute | solution.py:392
  31.9 3.2 %collective-permute-start.20 = (bf16[8,224,128]{2,1,0:T(8,128)(2,1)S(1)}, bf16[8,224,128]{2,1,0:T(8,128)(2,1)S(1)}, u32[]{:S(2)}, u32[]{:S(2)}) collective-permute-start(bf16[8,224,128]{2,1,0:T(8,128)(2,1)S(1)} %get-tuple-element.99), channel_id=1, source_target_pairs={{0,16},{16,0},{1,17},{17,1},{2,18},{18,2},{3,19},{19,3},{4,20},{20... | collective-permute-start | bytes 1376264 | tf_op jit(solution)/shard_map/ppermute | solution.py:392
  31.9 3.1 %collective-permute-start.21 = (bf16[8,224,128]{2,1,0:T(8,128)(2,1)S(1)}, bf16[8,224,128]{2,1,0:T(8,128)(2,1)S(1)}, u32[]{:S(2)}, u32[]{:S(2)}) collective-permute-start(bf16[8,224,128]{2,1,0:T(8,128)(2,1)S(1)} %get-tuple-element.101), channel_id=1, source_target_pairs={{0,16},{16,0},{1,17},{17,1},{2,18},{18,2},{3,19},{19,3},{4,20},{20... | collective-permute-start | bytes 1376264 | tf_op jit(solution)/shard_map/ppermute | solution.py:392
  32.4 4.5 %collective-permute-start.14 = (bf16[8,240,128]{2,1,0:T(8,128)(2,1)S(1)}, bf16[8,240,128]{2,1,0:T(8,128)(2,1)S(1)}, u32[]{:S(2)}, u32[]{:S(2)}) collective-permute-start(bf16[8,240,128]{2,1,0:T(8,128)(2,1)S(1)} %get-tuple-element.87), channel_id=1, source_target_pairs={{0,16},{16,0},{1,17},{17,1},{2,18},{18,2},{3,19},{19,3},{4,20},{20... | collective-permute-start | bytes 1474568 | tf_op jit(solution)/shard_map/ppermute | solution.py:392
  32.4 4.4 %collective-permute-start.15 = (bf16[8,240,128]{2,1,0:T(8,128)(2,1)S(1)}, bf16[8,240,128]{2,1,0:T(8,128)(2,1)S(1)}, u32[]{:S(2)}, u32[]{:S(2)}) collective-permute-start(bf16[8,240,128]{2,1,0:T(8,128)(2,1)S(1)} %get-tuple-element.89), channel_id=1, source_target_pairs={{0,16},{16,0},{1,17},{17,1},{2,18},{18,2},{3,19},{19,3},{4,20},{20... | collective-permute-start | bytes 1474568 | tf_op jit(solution)/shard_map/ppermute | solution.py:392
  33.4 12.9 %collective-permute-start.10 = (bf16[8,224,128]{2,1,0:T(8,128)(2,1)S(1)}, bf16[8,224,128]{2,1,0:T(8,128)(2,1)S(1)}, u32[]{:S(2)}, u32[]{:S(2)}) collective-permute-start(bf16[8,224,128]{2,1,0:T(8,128)(2,1)S(1)} %get-tuple-element.79), channel_id=1, source_target_pairs={{0,1},{1,0},{2,3},{3,2},{4,5},{5,4},{6,7},{7,6},{8,9},{9,8},{10,11... | collective-permute-start | bytes 1376264 | tf_op jit(solution)/shard_map/ppermute | solution.py:388
  35.1 3.5 %copy-start.1 = (bf16[2,640,640]{2,1,0:T(8,128)(2,1)S(1)}, bf16[2,640,640]{2,1,0:T(8,128)(2,1)}, u32[]{:S(2)}) copy-start(bf16[2,640,640]{2,1,0:T(8,128)(2,1)} %refs_7_.1) | copy-start | bytes 4915204
  35.3 12.7 %collective-permute-start.22 = (bf16[8,224,128]{2,1,0:T(8,128)(2,1)S(1)}, bf16[8,224,128]{2,1,0:T(8,128)(2,1)S(1)}, u32[]{:S(2)}, u32[]{:S(2)}) collective-permute-start(bf16[8,224,128]{2,1,0:T(8,128)(2,1)S(1)} %get-tuple-element.103), channel_id=1, source_target_pairs={{0,4},{1,5},{2,6},{3,7},{4,0},{5,1},{6,2},{7,3},{8,12},{9,13},{10,... | collective-permute-start | bytes 1376264 | tf_op jit(solution)/shard_map/ppermute | solution.py:388
  37.0 14.2 %collective-permute-start.16 = (bf16[8,240,128]{2,1,0:T(8,128)(2,1)S(1)}, bf16[8,240,128]{2,1,0:T(8,128)(2,1)S(1)}, u32[]{:S(2)}, u32[]{:S(2)}) collective-permute-start(bf16[8,240,128]{2,1,0:T(8,128)(2,1)S(1)} %get-tuple-element.91), channel_id=1, source_target_pairs={{0,2},{1,3},{2,0},{3,1},{4,6},{5,7},{6,4},{7,5},{8,10},{9,11},{10,... | collective-permute-start | bytes 1474568 | tf_op jit(solution)/shard_map/ppermute | solution.py:388
  43.8 12.2 %collective-permute-start.6 = (bf16[1568,128]{1,0:T(8,128)(2,1)S(1)}, bf16[1568,128]{1,0:T(8,128)(2,1)S(1)}, u32[]{:S(2)}, u32[]{:S(2)}) collective-permute-start(bf16[1568,128]{1,0:T(8,128)(2,1)S(1)} %get-tuple-element.66.refs_0_), channel_id=1, source_target_pairs={{0,1},{1,0},{2,3},{3,2},{4,5},{5,4},{6,7},{7,6},{8,9},{9,8},{10,11... | collective-permute-start | bytes 1204232 | tf_op jit(solution)/shard_map/ppermute | solution.py:388
  46.4 10.6 %collective-permute-start.11 = (bf16[4,224,128]{2,1,0:T(8,128)(2,1)S(1)}, bf16[4,224,128]{2,1,0:T(8,128)(2,1)S(1)}, u32[]{:S(2)}, u32[]{:S(2)}) collective-permute-start(bf16[4,224,128]{2,1,0:T(8,128)(2,1)S(1)} %get-tuple-element.81), channel_id=1, source_target_pairs={{0,2},{1,3},{2,0},{3,1},{4,6},{5,7},{6,4},{7,5},{8,10},{9,11},{10,... | collective-permute-start | bytes 688136 | tf_op jit(solution)/shard_map/ppermute | solution.py:388
  48.1 11.7 %collective-permute-start.23 = (bf16[4,224,128]{2,1,0:T(8,128)(2,1)S(1)}, bf16[4,224,128]{2,1,0:T(8,128)(2,1)S(1)}, u32[]{:S(2)}, u32[]{:S(2)}) collective-permute-start(bf16[4,224,128]{2,1,0:T(8,128)(2,1)S(1)} %get-tuple-element.105), channel_id=1, source_target_pairs={{0,1},{1,0},{2,3},{3,2},{4,5},{5,4},{6,7},{7,6},{8,9},{9,8},{10,11... | collective-permute-start | bytes 688136 | tf_op jit(solution)/shard_map/ppermute | solution.py:388
  51.3 10.2 %collective-permute-start.17 = (bf16[4,240,128]{2,1,0:T(8,128)(2,1)S(1)}, bf16[4,240,128]{2,1,0:T(8,128)(2,1)S(1)}, u32[]{:S(2)}, u32[]{:S(2)}) collective-permute-start(bf16[4,240,128]{2,1,0:T(8,128)(2,1)S(1)} %get-tuple-element.93), channel_id=1, source_target_pairs={{0,4},{1,5},{2,6},{3,7},{4,0},{5,1},{6,2},{7,3},{8,12},{9,13},{10,... | collective-permute-start | bytes 737288 | tf_op jit(solution)/shard_map/ppermute | solution.py:388
  56.2 19.5 %collective-permute-start.7 = (bf16[784,128]{1,0:T(8,128)(2,1)S(1)}, bf16[784,128]{1,0:T(8,128)(2,1)S(1)}, u32[]{:S(2)}, u32[]{:S(2)}) collective-permute-start(bf16[784,128]{1,0:T(8,128)(2,1)S(1)} %get-tuple-element.68), channel_id=1, source_target_pairs={{0,4},{1,5},{2,6},{3,7},{4,0},{5,1},{6,2},{7,3},{8,12},{9,13},{10,... | collective-permute-start | bytes 602120 | tf_op jit(solution)/shard_map/ppermute | solution.py:388
  57.0 7.3 %collective-permute-start.12 = (bf16[2,224,128]{2,1,0:T(8,128)(2,1)S(1)}, bf16[2,224,128]{2,1,0:T(8,128)(2,1)S(1)}, u32[]{:S(2)}, u32[]{:S(2)}) collective-permute-start(bf16[2,224,128]{2,1,0:T(8,128)(2,1)S(1)} %get-tuple-element.83), channel_id=1, source_target_pairs={{0,4},{1,5},{2,6},{3,7},{4,0},{5,1},{6,2},{7,3},{8,12},{9,13},{10,... | collective-permute-start | bytes 344072 | tf_op jit(solution)/shard_map/ppermute | solution.py:388
  59.9 7.8 %collective-permute-start.24 = (bf16[2,224,128]{2,1,0:T(8,128)(2,1)S(1)}, bf16[2,224,128]{2,1,0:T(8,128)(2,1)S(1)}, u32[]{:S(2)}, u32[]{:S(2)}) collective-permute-start(bf16[2,224,128]{2,1,0:T(8,128)(2,1)S(1)} %get-tuple-element.107), channel_id=1, source_target_pairs={{0,2},{1,3},{2,0},{3,1},{4,6},{5,7},{6,4},{7,5},{8,10},{9,11},{10,... | collective-permute-start | bytes 344072 | tf_op jit(solution)/shard_map/ppermute | solution.py:388
  61.6 6.4 %collective-permute-start.18 = (bf16[2,240,128]{2,1,0:T(8,128)(2,1)S(1)}, bf16[2,240,128]{2,1,0:T(8,128)(2,1)S(1)}, u32[]{:S(2)}, u32[]{:S(2)}) collective-permute-start(bf16[2,240,128]{2,1,0:T(8,128)(2,1)S(1)} %get-tuple-element.95), channel_id=1, source_target_pairs={{0,1},{1,0},{2,3},{3,2},{4,5},{5,4},{6,7},{7,6},{8,9},{9,8},{10,11... | collective-permute-start | bytes 368648 | tf_op jit(solution)/shard_map/ppermute | solution.py:388
  64.3 7.9 %collective-permute-start.13 = (bf16[1,224,128]{2,1,0:T(8,128)(2,1)S(1)}, bf16[1,224,128]{2,1,0:T(8,128)(2,1)S(1)}, u32[]{:S(2)}, u32[]{:S(2)}) collective-permute-start(bf16[1,224,128]{2,1,0:T(8,128)(2,1)S(1)} %get-tuple-element.85), channel_id=1, source_target_pairs={{0,8},{1,9},{2,10},{3,11},{4,12},{5,13},{6,14},{7,15},{8,0},{9,1},... | collective-permute-start | bytes 172040 | tf_op jit(solution)/shard_map/ppermute | solution.py:388
  67.7 7.4 %collective-permute-start.25 = (bf16[1,224,128]{2,1,0:T(8,128)(2,1)S(1)}, bf16[1,224,128]{2,1,0:T(8,128)(2,1)S(1)}, u32[]{:S(2)}, u32[]{:S(2)}) collective-permute-start(bf16[1,224,128]{2,1,0:T(8,128)(2,1)S(1)} %get-tuple-element.109), channel_id=1, source_target_pairs={{0,8},{1,9},{2,10},{3,11},{4,12},{5,13},{6,14},{7,15},{8,0},{9,1},... | collective-permute-start | bytes 172040 | tf_op jit(solution)/shard_map/ppermute | solution.py:388
  68.0 7.0 %collective-permute-start.19 = (bf16[1,240,128]{2,1,0:T(8,128)(2,1)S(1)}, bf16[1,240,128]{2,1,0:T(8,128)(2,1)S(1)}, u32[]{:S(2)}, u32[]{:S(2)}) collective-permute-start(bf16[1,240,128]{2,1,0:T(8,128)(2,1)S(1)} %get-tuple-element.97), channel_id=1, source_target_pairs={{0,8},{1,9},{2,10},{3,11},{4,12},{5,13},{6,14},{7,15},{8,0},{9,1},... | collective-permute-start | bytes 184328 | tf_op jit(solution)/shard_map/ppermute | solution.py:388
  72.2 4.2 %collective-permute-start.26 = (f32[224,128]{1,0:T(8,128)S(1)}, f32[224,128]{1,0:T(8,128)S(1)}, u32[]{:S(2)}, u32[]{:S(2)}) collective-permute-start(f32[224,128]{1,0:T(8,128)S(1)} %shard_map.125.refs_0_), channel_id=1, source_target_pairs={{0,16},{16,0},{1,17},{17,1},{2,18},{18,2},{3,19},{19,3},{4,20},{20... | collective-permute-start | bytes 344072 | tf_op jit(solution)/shard_map/ppermute | solution.py:392
  75.0 1.6 %collective-permute-start.27 = (f32[240,128]{1,0:T(8,128)S(1)}, f32[240,128]{1,0:T(8,128)S(1)}, u32[]{:S(2)}, u32[]{:S(2)}) collective-permute-start(f32[240,128]{1,0:T(8,128)S(1)} %shard_map.130.refs_1_), channel_id=1, source_target_pairs={{0,16},{16,0},{1,17},{17,1},{2,18},{18,2},{3,19},{19,3},{4,20},{20... | collective-permute-start | bytes 368648 | tf_op jit(solution)/shard_map/ppermute | solution.py:392
  75.1 1.5 %collective-permute-start.28 = (f32[224,128]{1,0:T(8,128)S(1)}, f32[224,128]{1,0:T(8,128)S(1)}, u32[]{:S(2)}, u32[]{:S(2)}) collective-permute-start(f32[224,128]{1,0:T(8,128)S(1)} %shard_map.135.refs_2_), channel_id=1, source_target_pairs={{0,16},{16,0},{1,17},{17,1},{2,18},{18,2},{3,19},{19,3},{4,20},{20... | collective-permute-start | bytes 344072 | tf_op jit(solution)/shard_map/ppermute | solution.py:392
  (3 other events, 6.2 us)

commit v7 on v6

--- a/solution.py
+++ b/solution.py
@@ -339,7 +339,7 @@
         outs[1][count // 2 * size :, :] = refs[0][...]
 
 
-def fold_kernel(start, rows, kept_ref, came_ref, *outs):
+def fold_kernel(start, rows, kept_ref, came_ref, after_ref, *outs):
     count = kept_ref.shape[0] // rows
     for place in range(count):
         total = kept_ref[place * rows : (place + 1) * rows, :] + came_ref[
@@ -535,13 +535,15 @@
                     [kept_part[k], came[k]] + ([away] if extra or stage == 1 else []),
                 )
             came[k] = swap(sent, 1 << bit)
+            if (k, stage) == (0, 2):
+                after = sent
     arrived, start = swap(away, 1), 0
     for number in range(1, len(plan.dst_bits) + 1):
         count = plan.n_dst >> (number + 1)
         shapes = [(count * node_size, channels)] * 2 if count else [(node_size, channels)]
         outs = [jax.ShapeDtypeStruct(x, kind) for x, kind in zip(shapes, (f32, bf16) if count else (bf16,))]
         folded, *away = whole_call(
-            functools.partial(fold_kernel, start, node_size), outs, [folded, arrived]
+            functools.partial(fold_kernel, start, node_size), outs, [folded, arrived, after]
         )
         start = 0
         if count:

time: 77.7 us -> 76.4 us (0.983)
  starting transfers between devices: 34.6 us -> 27.2 us
  waiting for transfers between devices: 24.7 us -> 30.7 us
    ppermute x20, starting transfers between devices: 32.3 us -> 25.2 us  [swap(): return lax.ppermute(value, 'graph', [(i, i ^ flip) for i in range(count)])]
    ppermute x20, waiting for transfers between devices: 24 us -> 28 us  [swap(): return lax.ppermute(value, 'graph', [(i, i ^ flip) for i in range(count)])]
    ppermute x9, waiting for transfers between devices: 0.67 us -> 2.71 us  [swap_cores(): return lax.ppermute(value, 'dp', [(i, 1 - i) for i in range(2)])]
  transfers between devices with their start and end apart: 29 -> 29, of which waited for: 11 -> 15; matrix products, arithmetic and copies ran while one was open for 0% -> 0% of each run, Pallas kernels for 12% -> 10%
where the time goes in v7:
time: 76.4 us; the launch traced here: 76.2 us
  waiting for transfers between devices  30.7 us (40%)
  starting transfers between devices  27.2 us (36%)
  Pallas kernels  15.8 us (21%)
  local copies, waits for them, and re-layouts  0.96 us (1%)
  between operations  0.78 us (1%)
    ppermute x20, waiting for transfers between devices, swap(): return lax.ppermute(value, 'graph', [(i, i ^ flip) for i in range(count)])  28 us
    ppermute x20, starting transfers between devices, swap(): return lax.ppermute(value, 'graph', [(i, i ^ flip) for i in range(count)])  25.2 us
    pallas_call x24, Pallas kernels, whole_call(): pl.pallas_call(kernel, out_shape=outs, in_specs=specs, out_specs=[pl.Bloc...  15.8 us
    ppermute x9, waiting for transfers between devices, swap_cores(): return lax.ppermute(value, 'dp', [(i, 1 - i) for i in range(2)])  2.71 us
    ppermute x9, starting transfers between devices, swap_cores(): return lax.ppermute(value, 'dp', [(i, 1 - i) for i in range(2)])  1.98 us
  transfers between devices with their start and end apart: 29, of which 15 were waited for; matrix products, arithmetic and copies ran while one was open for 0% of the time, Pallas kernels for 10%

profile of v7, /device:TPU:0, one launch (start us, length us, event | category | flops | bytes accessed | tf_op | source)
XLA Modules:
  0.0 76.2 jit_solution(3849636881629685957)
XLA Ops:
  0.6 0.7 pad_add_fusion.edge_ref
  1.3 0.9 %copy-done.4 = bf16[16,49,128]{2,0,1:T(8,128)(2,1)S(1)} copy-done((bf16[16,49,128]{2,0,1:T(8,128)(2,1)S(1)}, bf16[16,49,128]{2,0,1:T(8,128)(2,1)}, u32[]{:S(2)}) %copy-start.4) | copy-done | bytes 200728
  2.6 4.1 %collective-permute-start.1 = (bf16[800,128]{1,0:T(8,128)(2,1)S(1)}, bf16[800,128]{1,0:T(8,128)(2,1)S(1)}, u32[]{:S(2)}, u32[]{:S(2)}) collective-permute-start(bf16[800,128]{1,0:T(8,128)(2,1)S(1)} %shard_map.114.refs_1_), channel_id=1, source_target_pairs={{0,8},{1,9},{2,10},{3,11},{4,12},{5,13},{6,14},{7,15},{8,0},{9,1},... | collective-permute-start | bytes 614408 | tf_op jit(solution)/shard_map/ppermute | solution.py:388
  6.6 1.5 %collective-permute-start = (bf16[800,128]{1,0:T(8,128)(2,1)S(1)}, bf16[800,128]{1,0:T(8,128)(2,1)S(1)}, u32[]{:S(2)}, u32[]{:S(2)}) collective-permute-start(bf16[800,128]{1,0:T(8,128)(2,1)S(1)} %shard_map.114.refs_1_), channel_id=1, source_target_pairs={{0,2},{1,3},{2,0},{3,1},{4,6},{5,7},{6,4},{7,5},{8,10},{9,11},{10,... | collective-permute-start | bytes 614408 | tf_op jit(solution)/shard_map/ppermute | solution.py:388
  8.1 1.5 %collective-permute-start.3 = (bf16[784,128]{1,0:T(8,128)(2,1)S(1)}, bf16[784,128]{1,0:T(8,128)(2,1)S(1)}, u32[]{:S(2)}, u32[]{:S(2)}) collective-permute-start(bf16[784,128]{1,0:T(8,128)(2,1)S(1)} %bitcast.17), channel_id=1, source_target_pairs={{0,1},{1,0},{2,3},{3,2},{4,5},{5,4},{6,7},{7,6},{8,9},{9,8},{10,11... | collective-permute-start | bytes 602120 | tf_op jit(solution)/shard_map/ppermute | solution.py:388
  9.6 1.6 %collective-permute-start.2 = (bf16[784,128]{1,0:T(8,128)(2,1)S(1)}, bf16[784,128]{1,0:T(8,128)(2,1)S(1)}, u32[]{:S(2)}, u32[]{:S(2)}) collective-permute-start(bf16[784,128]{1,0:T(8,128)(2,1)S(1)} %bitcast.18), channel_id=1, source_target_pairs={{0,4},{1,5},{2,6},{3,7},{4,0},{5,1},{6,2},{7,3},{8,12},{9,13},{10,... | collective-permute-start | bytes 602120 | tf_op jit(solution)/shard_map/ppermute | solution.py:388
  11.3 3.0 %collective-permute-done.3.refs_3_.refs_6_ = bf16[784,128]{1,0:T(8,128)(2,1)S(1)} collective-permute-done((bf16[784,128]{1,0:T(8,128)(2,1)S(1)}, bf16[784,128]{1,0:T(8,128)(2,1)S(1)}, u32[]{:S(2)}, u32[]{:S(2)}) %collective-permute-start.3) | collective-permute-done | bytes 200736 | tf_op jit(solution)/shard_map/ppermute | solution.py:388
  14.3 4.4 %collective-permute-done.2.refs_1_ = bf16[784,128]{1,0:T(8,128)(2,1)S(1)} collective-permute-done((bf16[784,128]{1,0:T(8,128)(2,1)S(1)}, bf16[784,128]{1,0:T(8,128)(2,1)S(1)}, u32[]{:S(2)}, u32[]{:S(2)}) %collective-permute-start.2) | collective-permute-done | bytes 200736 | tf_op jit(solution)/shard_map/ppermute | solution.py:388
  19.9 5.2 %collective-permute-done.5.refs_8_ = bf16[784,128]{1,0:T(8,128)(2,1)S(1)} collective-permute-done((bf16[784,128]{1,0:T(8,128)(2,1)S(1)}, bf16[784,128]{1,0:T(8,128)(2,1)S(1)}, u32[]{:S(2)}, u32[]{:S(2)}) %collective-permute-start.5) | collective-permute-done | bytes 200736 | tf_op jit(solution)/shard_map/ppermute | solution.py:388
  25.1 5.2 %shard_map.116 = (f32[1568,256]{1,0:T(8,128)S(1)}, s32[8,256]{1,0:T(8,128)S(1)}, bf16[896,256]{1,0:T(8,128)(2,1)S(1)}, bf16[768,512]{1,0:T(8,128)(2,1)S(1)}, bf1...) custom-call(bf16[49,32,256]{2,1,0:T(8,128)(2,1)S(1)} %get-tuple-elem, ...), custom_call_target="tpu_custom_call" | custom-call | flops 5000000000 | bytes 100000 | tf_op jit(solution)/shard_map/pallas_call | solution.py:374
  30.3 2.2 %shard_map.118 = (f32[8,224,128]{2,1,0:T(8,128)S(1)}, bf16[8,224,128]{2,1,0:T(8,128)(2,1)S(1)}, f32[8,240,128]{2,1,0:T(8,128)S(1)}, bf16[8,240,128]{2,1,0:T(8,12...) custom-call(bf16[896,256]{1,0:T(8,128)(2,1)S(1)} %get-tuple-element.62.refs_2_.refs_0_, ...), custom_call_target="tpu_custom_call" | custom-call | flops 3000000000 | bytes 100000 | tf_op jit(solution)/shard_map/pallas_call | solution.py:374
  33.6 0.7 collective-permute-done.8.refs_3_
  37.0 0.7 collective-permute-done.14.refs_1_
  38.0 1.5 %collective-permute-start.16 = (bf16[8,240,128]{2,1,0:T(8,128)(2,1)S(1)}, bf16[8,240,128]{2,1,0:T(8,128)(2,1)S(1)}, u32[]{:S(2)}, u32[]{:S(2)}) collective-permute-start(bf16[8,240,128]{2,1,0:T(8,128)(2,1)S(1)} %get-tuple-element.91), channel_id=1, source_target_pairs={{0,2},{1,3},{2,0},{3,1},{4,6},{5,7},{6,4},{7,5},{8,10},{9,11},{10,... | collective-permute-start | bytes 1474568 | tf_op jit(solution)/shard_map/ppermute | solution.py:388
  39.5 5.2 %shard_map.117 = (f32[1568,128]{1,0:T(8,128)S(1)}, bf16[1568,128]{1,0:T(8,128)(2,1)S(1)}) custom-call(f32[1568,256]{1,0:T(8,128)S(1)} %get-tuple-element.60.refs_0_, s32[8,256]{1,0:T(8,128)S(1)} %get-tuple-element.61.refs_1_, bf16[896,256]{1,0:T(8,128)(2,1)S(1)} %get-tuple-element.62.refs_2_.refs_0_, bf16[768,512]{1,0:T(8,128)(2,1)S(1)} %get-tuple-element.63.refs_3_.refs_1_, ...), custom_call_target="tpu_custom_call" | custom-call | flops 8000000000 | bytes 100000 | tf_op jit(solution)/shard_map/pallas_call | solution.py:374
  44.8 0.7 collective-permute-start.6
  45.5 2.5 %collective-permute-done.9.came_ref = bf16[8,224,128]{2,1,0:T(8,128)(2,1)S(1)} collective-permute-done((bf16[8,224,128]{2,1,0:T(8,128)(2,1)S(1)}, bf16[8,224,128]{2,1,0:T(8,128)(2,1)S(1)}, u32[]{:S(2)}, u32[]{:S(2)}) %collective-permute-start.9) | collective-permute-done | bytes 458784 | tf_op jit(solution)/shard_map/ppermute | solution.py:388
  48.1 1.5 %collective-permute-start.10 = (bf16[4,224,128]{2,1,0:T(8,128)(2,1)S(1)}, bf16[4,224,128]{2,1,0:T(8,128)(2,1)S(1)}, u32[]{:S(2)}, u32[]{:S(2)}) collective-permute-start(bf16[4,224,128]{2,1,0:T(8,128)(2,1)S(1)} %get-tuple-element.79), channel_id=1, source_target_pairs={{0,2},{1,3},{2,0},{3,1},{4,6},{5,7},{6,4},{7,5},{8,10},{9,11},{10,... | collective-permute-start | bytes 688136 | tf_op jit(solution)/shard_map/ppermute | solution.py:388
  50.3 1.8 %collective-permute-done.16.came_ref = bf16[8,240,128]{2,1,0:T(8,128)(2,1)S(1)} collective-permute-done((bf16[8,240,128]{2,1,0:T(8,128)(2,1)S(1)}, bf16[8,240,128]{2,1,0:T(8,128)(2,1)S(1)}, u32[]{:S(2)}, u32[]{:S(2)}) %collective-permute-start.16) | collective-permute-done | bytes 491552 | tf_op jit(solution)/shard_map/ppermute | solution.py:388
  52.2 1.0 %collective-permute-start.17 = (bf16[4,240,128]{2,1,0:T(8,128)(2,1)S(1)}, bf16[4,240,128]{2,1,0:T(8,128)(2,1)S(1)}, u32[]{:S(2)}, u32[]{:S(2)}) collective-permute-start(bf16[4,240,128]{2,1,0:T(8,128)(2,1)S(1)} %get-tuple-element.93), channel_id=1, source_target_pairs={{0,4},{1,5},{2,6},{3,7},{4,0},{5,1},{6,2},{7,3},{8,12},{9,13},{10,... | collective-permute-start | bytes 737288 | tf_op jit(solution)/shard_map/ppermute | solution.py:388
  53.2 3.0 %collective-permute-done.10.came_ref = bf16[4,224,128]{2,1,0:T(8,128)(2,1)S(1)} collective-permute-done((bf16[4,224,128]{2,1,0:T(8,128)(2,1)S(1)}, bf16[4,224,128]{2,1,0:T(8,128)(2,1)S(1)}, u32[]{:S(2)}, u32[]{:S(2)}) %collective-permute-start.10) | collective-permute-done | bytes 229408 | tf_op jit(solution)/shard_map/ppermute | solution.py:388
  57.1 1.5 %collective-permute-start.11 = (bf16[784,128]{1,0:T(8,128)(2,1)S(1)}, bf16[784,128]{1,0:T(8,128)(2,1)S(1)}, u32[]{:S(2)}, u32[]{:S(2)}) collective-permute-start(bf16[784,128]{1,0:T(8,128)(2,1)S(1)} %get-tuple-element.82), channel_id=1, source_target_pairs={{0,4},{1,5},{2,6},{3,7},{4,0},{5,1},{6,2},{7,3},{8,12},{9,13},{10,... | collective-permute-start | bytes 602120 | tf_op jit(solution)/shard_map/ppermute | solution.py:388
  58.5 2.8 %collective-permute-done.23.came_ref = bf16[4,224,128]{2,1,0:T(8,128)(2,1)S(1)} collective-permute-done((bf16[4,224,128]{2,1,0:T(8,128)(2,1)S(1)}, bf16[4,224,128]{2,1,0:T(8,128)(2,1)S(1)}, u32[]{:S(2)}, u32[]{:S(2)}) %collective-permute-start.23) | collective-permute-done | bytes 229408 | tf_op jit(solution)/shard_map/ppermute | solution.py:388
  61.4 1.5 %collective-permute-start.24 = (bf16[2,224,128]{2,1,0:T(8,128)(2,1)S(1)}, bf16[2,224,128]{2,1,0:T(8,128)(2,1)S(1)}, u32[]{:S(2)}, u32[]{:S(2)}) collective-permute-start(bf16[2,224,128]{2,1,0:T(8,128)(2,1)S(1)} %get-tuple-element.107), channel_id=1, source_target_pairs={{0,2},{1,3},{2,0},{3,1},{4,6},{5,7},{6,4},{7,5},{8,10},{9,11},{10,... | collective-permute-start | bytes 344072 | tf_op jit(solution)/shard_map/ppermute | solution.py:388
  63.6 1.5 %collective-permute-start.13 = (bf16[1,224,128]{2,1,0:T(8,128)(2,1)S(1)}, bf16[1,224,128]{2,1,0:T(8,128)(2,1)S(1)}, u32[]{:S(2)}, u32[]{:S(2)}) collective-permute-start(bf16[1,224,128]{2,1,0:T(8,128)(2,1)S(1)} %get-tuple-element.85), channel_id=1, source_target_pairs={{0,8},{1,9},{2,10},{3,11},{4,12},{5,13},{6,14},{7,15},{8,0},{9,1},... | collective-permute-start | bytes 172040 | tf_op jit(solution)/shard_map/ppermute | solution.py:388
  65.1 1.1 %collective-permute-done.24.came_ref = bf16[2,224,128]{2,1,0:T(8,128)(2,1)S(1)} collective-permute-done((bf16[2,224,128]{2,1,0:T(8,128)(2,1)S(1)}, bf16[2,224,128]{2,1,0:T(8,128)(2,1)S(1)}, u32[]{:S(2)}, u32[]{:S(2)}) %collective-permute-start.24) | collective-permute-done | bytes 114720 | tf_op jit(solution)/shard_map/ppermute | solution.py:388
  66.3 1.7 %collective-permute-start.25 = (bf16[1,224,128]{2,1,0:T(8,128)(2,1)S(1)}, bf16[1,224,128]{2,1,0:T(8,128)(2,1)S(1)}, u32[]{:S(2)}, u32[]{:S(2)}) collective-permute-start(bf16[1,224,128]{2,1,0:T(8,128)(2,1)S(1)} %get-tuple-element.109), channel_id=1, source_target_pairs={{0,8},{1,9},{2,10},{3,11},{4,12},{5,13},{6,14},{7,15},{8,0},{9,1},... | collective-permute-start | bytes 172040 | tf_op jit(solution)/shard_map/ppermute | solution.py:388
  68.0 1.4 %collective-permute-start.19 = (bf16[1,240,128]{2,1,0:T(8,128)(2,1)S(1)}, bf16[1,240,128]{2,1,0:T(8,128)(2,1)S(1)}, u32[]{:S(2)}, u32[]{:S(2)}) collective-permute-start(bf16[1,240,128]{2,1,0:T(8,128)(2,1)S(1)} %get-tuple-element.97), channel_id=1, source_target_pairs={{0,8},{1,9},{2,10},{3,11},{4,12},{5,13},{6,14},{7,15},{8,0},{9,1},... | collective-permute-start | bytes 184328 | tf_op jit(solution)/shard_map/ppermute | solution.py:388
  69.4 1.0 %collective-permute-done.13.came_ref = bf16[1,224,128]{2,1,0:T(8,128)(2,1)S(1)} collective-permute-done((bf16[1,224,128]{2,1,0:T(8,128)(2,1)S(1)}, bf16[1,224,128]{2,1,0:T(8,128)(2,1)S(1)}, u32[]{:S(2)}, u32[]{:S(2)}) %collective-permute-start.13) | collective-permute-done | bytes 57376 | tf_op jit(solution)/shard_map/ppermute | solution.py:388
  70.5 3.1 %collective-permute-done.19.came_ref = bf16[1,240,128]{2,1,0:T(8,128)(2,1)S(1)} collective-permute-done((bf16[1,240,128]{2,1,0:T(8,128)(2,1)S(1)}, bf16[1,240,128]{2,1,0:T(8,128)(2,1)S(1)}, u32[]{:S(2)}, u32[]{:S(2)}) %collective-permute-start.19) | collective-permute-done | bytes 61472 | tf_op jit(solution)/shard_map/ppermute | solution.py:388
  74.3 0.7 shard_map.123
  75.3 0.9 %shard_map.136 = f32[1368,128]{1,0:T(8,128)} custom-call(f32[224,128]{1,0:T(8,128)S(1)} %shard_map.125.refs_0_, f32[240,128]{1,0:T(8,128)S(1)} %shard_map.130.refs_1_, f32[224,128]{1,0:T(8,128)S(1)} %shard_map.135.refs_2_, f32[224,128]{1,0:T(8,128)S(1)} %collective-permute-done.26.refs_3_, f32[240,128]{1,0:T(8,128)S(1)} %collective-permute-done.27.refs_4_, ...), custom_call_target="tpu_custom_call" | custom-call | flops 1000000000 | bytes 100000 | tf_op jit(solution)/shard_map/pallas_call | solution.py:374
  (63 shorter events, 9.2 us)
Async XLA Ops:
  2.3 5.9 %copy-start.5 = (bf16[16,49,128]{2,0,1:T(8,128)(2,1)S(1)}, bf16[16,49,128]{2,0,1:T(8,128)(2,1)}, u32[]{:S(2)}) copy-start(bf16[16,49,128]{2,0,1:T(8,128)(2,1)} %param.11) | copy-start | bytes 602116
  2.3 8.9 %copy-start.3 = (bf16[256,29,49]{0,1,2:T(8,128)(2,1)S(1)}, bf16[256,29,49]{0,1,2:T(8,128)(2,1)}, u32[]{:S(2)}) copy-start(bf16[256,29,49]{0,1,2:T(8,128)(2,1)} %param.12) | copy-start | bytes 2182660
  2.6 16.2 %collective-permute-start.1 = (bf16[800,128]{1,0:T(8,128)(2,1)S(1)}, bf16[800,128]{1,0:T(8,128)(2,1)S(1)}, u32[]{:S(2)}, u32[]{:S(2)}) collective-permute-start(bf16[800,128]{1,0:T(8,128)(2,1)S(1)} %shard_map.114.refs_1_), channel_id=1, source_target_pairs={{0,8},{1,9},{2,10},{3,11},{4,12},{5,13},{6,14},{7,15},{8,0},{9,1},... | collective-permute-start | bytes 614408 | tf_op jit(solution)/shard_map/ppermute | solution.py:388
  6.6 12.1 %collective-permute-start = (bf16[800,128]{1,0:T(8,128)(2,1)S(1)}, bf16[800,128]{1,0:T(8,128)(2,1)S(1)}, u32[]{:S(2)}, u32[]{:S(2)}) collective-permute-start(bf16[800,128]{1,0:T(8,128)(2,1)S(1)} %shard_map.114.refs_1_), channel_id=1, source_target_pairs={{0,2},{1,3},{2,0},{3,1},{4,6},{5,7},{6,4},{7,5},{8,10},{9,11},{10,... | collective-permute-start | bytes 614408 | tf_op jit(solution)/shard_map/ppermute | solution.py:388
  8.1 6.2 %collective-permute-start.3 = (bf16[784,128]{1,0:T(8,128)(2,1)S(1)}, bf16[784,128]{1,0:T(8,128)(2,1)S(1)}, u32[]{:S(2)}, u32[]{:S(2)}) collective-permute-start(bf16[784,128]{1,0:T(8,128)(2,1)S(1)} %bitcast.17), channel_id=1, source_target_pairs={{0,1},{1,0},{2,3},{3,2},{4,5},{5,4},{6,7},{7,6},{8,9},{9,8},{10,11... | collective-permute-start | bytes 602120 | tf_op jit(solution)/shard_map/ppermute | solution.py:388
  9.6 9.1 %collective-permute-start.2 = (bf16[784,128]{1,0:T(8,128)(2,1)S(1)}, bf16[784,128]{1,0:T(8,128)(2,1)S(1)}, u32[]{:S(2)}, u32[]{:S(2)}) collective-permute-start(bf16[784,128]{1,0:T(8,128)(2,1)S(1)} %bitcast.18), channel_id=1, source_target_pairs={{0,4},{1,5},{2,6},{3,7},{4,0},{5,1},{6,2},{7,3},{8,12},{9,13},{10,... | collective-permute-start | bytes 602120 | tf_op jit(solution)/shard_map/ppermute | solution.py:388
  18.7 6.3 %collective-permute-start.4 = (bf16[800,128]{1,0:T(8,128)(2,1)S(1)}, bf16[800,128]{1,0:T(8,128)(2,1)S(1)}, u32[]{:S(2)}, u32[]{:S(2)}) collective-permute-start(bf16[800,128]{1,0:T(8,128)(2,1)S(1)} %get-tuple-element.58.refs_3_), channel_id=1, source_target_pairs={{0,2},{1,3},{2,0},{3,1},{4,6},{5,7},{6,4},{7,5},{8,10},{9,11},{10,... | collective-permute-start | bytes 614408 | tf_op jit(solution)/shard_map/ppermute | solution.py:388
  19.4 5.7 %collective-permute-start.5 = (bf16[784,128]{1,0:T(8,128)(2,1)S(1)}, bf16[784,128]{1,0:T(8,128)(2,1)S(1)}, u32[]{:S(2)}, u32[]{:S(2)}) collective-permute-start(bf16[784,128]{1,0:T(8,128)(2,1)S(1)} %get-tuple-element.59.refs_7_), channel_id=1, source_target_pairs={{0,1},{1,0},{2,3},{3,2},{4,5},{5,4},{6,7},{7,6},{8,9},{9,8},{10,11... | collective-permute-start | bytes 602120 | tf_op jit(solution)/shard_map/ppermute | solution.py:388
  32.5 1.9 %collective-permute-start.8 = (bf16[8,224,128]{2,1,0:T(8,128)(2,1)S(1)}, bf16[8,224,128]{2,1,0:T(8,128)(2,1)S(1)}, u32[]{:S(2)}, u32[]{:S(2)}) collective-permute-start(bf16[8,224,128]{2,1,0:T(8,128)(2,1)S(1)} %get-tuple-element.75), channel_id=1, source_target_pairs={{0,16},{16,0},{1,17},{17,1},{2,18},{18,2},{3,19},{19,3},{4,20},{20... | collective-permute-start | bytes 1376264 | tf_op jit(solution)/shard_map/ppermute | solution.py:392
  32.6 2.5 %collective-permute-start.7 = (bf16[8,224,128]{2,1,0:T(8,128)(2,1)S(1)}, bf16[8,224,128]{2,1,0:T(8,128)(2,1)S(1)}, u32[]{:S(2)}, u32[]{:S(2)}) collective-permute-start(bf16[8,224,128]{2,1,0:T(8,128)(2,1)S(1)} %get-tuple-element.68), channel_id=1, source_target_pairs={{0,16},{16,0},{1,17},{17,1},{2,18},{18,2},{3,19},{19,3},{4,20},{20... | collective-permute-start | bytes 1376264 | tf_op jit(solution)/shard_map/ppermute | solution.py:392
  33.0 2.7 %collective-permute-start.21 = (bf16[8,224,128]{2,1,0:T(8,128)(2,1)S(1)}, bf16[8,224,128]{2,1,0:T(8,128)(2,1)S(1)}, u32[]{:S(2)}, u32[]{:S(2)}) collective-permute-start(bf16[8,224,128]{2,1,0:T(8,128)(2,1)S(1)} %get-tuple-element.101), channel_id=1, source_target_pairs={{0,16},{16,0},{1,17},{17,1},{2,18},{18,2},{3,19},{19,3},{4,20},{20... | collective-permute-start | bytes 1376264 | tf_op jit(solution)/shard_map/ppermute | solution.py:392
  33.1 3.2 %collective-permute-start.20 = (bf16[8,224,128]{2,1,0:T(8,128)(2,1)S(1)}, bf16[8,224,128]{2,1,0:T(8,128)(2,1)S(1)}, u32[]{:S(2)}, u32[]{:S(2)}) collective-permute-start(bf16[8,224,128]{2,1,0:T(8,128)(2,1)S(1)} %get-tuple-element.99), channel_id=1, source_target_pairs={{0,16},{16,0},{1,17},{17,1},{2,18},{18,2},{3,19},{19,3},{4,20},{20... | collective-permute-start | bytes 1376264 | tf_op jit(solution)/shard_map/ppermute | solution.py:392
  33.6 3.5 %collective-permute-start.15 = (bf16[8,240,128]{2,1,0:T(8,128)(2,1)S(1)}, bf16[8,240,128]{2,1,0:T(8,128)(2,1)S(1)}, u32[]{:S(2)}, u32[]{:S(2)}) collective-permute-start(bf16[8,240,128]{2,1,0:T(8,128)(2,1)S(1)} %get-tuple-element.89), channel_id=1, source_target_pairs={{0,16},{16,0},{1,17},{17,1},{2,18},{18,2},{3,19},{19,3},{4,20},{20... | collective-permute-start | bytes 1474568 | tf_op jit(solution)/shard_map/ppermute | solution.py:392
  34.4 3.4 %collective-permute-start.14 = (bf16[8,240,128]{2,1,0:T(8,128)(2,1)S(1)}, bf16[8,240,128]{2,1,0:T(8,128)(2,1)S(1)}, u32[]{:S(2)}, u32[]{:S(2)}) collective-permute-start(bf16[8,240,128]{2,1,0:T(8,128)(2,1)S(1)} %get-tuple-element.87), channel_id=1, source_target_pairs={{0,16},{16,0},{1,17},{17,1},{2,18},{18,2},{3,19},{19,3},{4,20},{20... | collective-permute-start | bytes 1474568 | tf_op jit(solution)/shard_map/ppermute | solution.py:392
  35.2 12.8 %collective-permute-start.9 = (bf16[8,224,128]{2,1,0:T(8,128)(2,1)S(1)}, bf16[8,224,128]{2,1,0:T(8,128)(2,1)S(1)}, u32[]{:S(2)}, u32[]{:S(2)}) collective-permute-start(bf16[8,224,128]{2,1,0:T(8,128)(2,1)S(1)} %get-tuple-element.77), channel_id=1, source_target_pairs={{0,1},{1,0},{2,3},{3,2},{4,5},{5,4},{6,7},{7,6},{8,9},{9,8},{10,11... | collective-permute-start | bytes 1376264 | tf_op jit(solution)/shard_map/ppermute | solution.py:388
  36.3 3.2 %copy-start.2 = (bf16[896,896]{1,0:T(8,128)(2,1)S(1)}, bf16[896,896]{1,0:T(8,128)(2,1)}, u32[]{:S(2)}) copy-start(bf16[896,896]{1,0:T(8,128)(2,1)} %refs_5_.1) | copy-start | bytes 4816900
  36.5 13.1 %collective-permute-start.22 = (bf16[8,224,128]{2,1,0:T(8,128)(2,1)S(1)}, bf16[8,224,128]{2,1,0:T(8,128)(2,1)S(1)}, u32[]{:S(2)}, u32[]{:S(2)}) collective-permute-start(bf16[8,224,128]{2,1,0:T(8,128)(2,1)S(1)} %get-tuple-element.103), channel_id=1, source_target_pairs={{0,4},{1,5},{2,6},{3,7},{4,0},{5,1},{6,2},{7,3},{8,12},{9,13},{10,... | collective-permute-start | bytes 1376264 | tf_op jit(solution)/shard_map/ppermute | solution.py:388
  38.0 14.1 %collective-permute-start.16 = (bf16[8,240,128]{2,1,0:T(8,128)(2,1)S(1)}, bf16[8,240,128]{2,1,0:T(8,128)(2,1)S(1)}, u32[]{:S(2)}, u32[]{:S(2)}) collective-permute-start(bf16[8,240,128]{2,1,0:T(8,128)(2,1)S(1)} %get-tuple-element.91), channel_id=1, source_target_pairs={{0,2},{1,3},{2,0},{3,1},{4,6},{5,7},{6,4},{7,5},{8,10},{9,11},{10,... | collective-permute-start | bytes 1474568 | tf_op jit(solution)/shard_map/ppermute | solution.py:388
  44.8 12.2 %collective-permute-start.6 = (bf16[1568,128]{1,0:T(8,128)(2,1)S(1)}, bf16[1568,128]{1,0:T(8,128)(2,1)S(1)}, u32[]{:S(2)}, u32[]{:S(2)}) collective-permute-start(bf16[1568,128]{1,0:T(8,128)(2,1)S(1)} %get-tuple-element.66.refs_0_), channel_id=1, source_target_pairs={{0,1},{1,0},{2,3},{3,2},{4,5},{5,4},{6,7},{7,6},{8,9},{9,8},{10,11... | collective-permute-start | bytes 1204232 | tf_op jit(solution)/shard_map/ppermute | solution.py:388
  48.1 8.1 %collective-permute-start.10 = (bf16[4,224,128]{2,1,0:T(8,128)(2,1)S(1)}, bf16[4,224,128]{2,1,0:T(8,128)(2,1)S(1)}, u32[]{:S(2)}, u32[]{:S(2)}) collective-permute-start(bf16[4,224,128]{2,1,0:T(8,128)(2,1)S(1)} %get-tuple-element.79), channel_id=1, source_target_pairs={{0,2},{1,3},{2,0},{3,1},{4,6},{5,7},{6,4},{7,5},{8,10},{9,11},{10,... | collective-permute-start | bytes 688136 | tf_op jit(solution)/shard_map/ppermute | solution.py:388
  49.7 11.6 %collective-permute-start.23 = (bf16[4,224,128]{2,1,0:T(8,128)(2,1)S(1)}, bf16[4,224,128]{2,1,0:T(8,128)(2,1)S(1)}, u32[]{:S(2)}, u32[]{:S(2)}) collective-permute-start(bf16[4,224,128]{2,1,0:T(8,128)(2,1)S(1)} %get-tuple-element.105), channel_id=1, source_target_pairs={{0,1},{1,0},{2,3},{3,2},{4,5},{5,4},{6,7},{7,6},{8,9},{9,8},{10,11... | collective-permute-start | bytes 688136 | tf_op jit(solution)/shard_map/ppermute | solution.py:388
  52.2 10.7 %collective-permute-start.17 = (bf16[4,240,128]{2,1,0:T(8,128)(2,1)S(1)}, bf16[4,240,128]{2,1,0:T(8,128)(2,1)S(1)}, u32[]{:S(2)}, u32[]{:S(2)}) collective-permute-start(bf16[4,240,128]{2,1,0:T(8,128)(2,1)S(1)} %get-tuple-element.93), channel_id=1, source_target_pairs={{0,4},{1,5},{2,6},{3,7},{4,0},{5,1},{6,2},{7,3},{8,12},{9,13},{10,... | collective-permute-start | bytes 737288 | tf_op jit(solution)/shard_map/ppermute | solution.py:388
  56.3 7.4 %collective-permute-start.12 = (bf16[2,224,128]{2,1,0:T(8,128)(2,1)S(1)}, bf16[2,224,128]{2,1,0:T(8,128)(2,1)S(1)}, u32[]{:S(2)}, u32[]{:S(2)}) collective-permute-start(bf16[2,224,128]{2,1,0:T(8,128)(2,1)S(1)} %get-tuple-element.80.after_ref), channel_id=1, source_target_pairs={{0,4},{1,5},{2,6},{3,7},{4,0},{5,1},{6,2},{7,3},{8,12},{9,13},{10,... | collective-permute-start | bytes 344072 | tf_op jit(solution)/shard_map/ppermute | solution.py:388
  57.1 17.2 %collective-permute-start.11 = (bf16[784,128]{1,0:T(8,128)(2,1)S(1)}, bf16[784,128]{1,0:T(8,128)(2,1)S(1)}, u32[]{:S(2)}, u32[]{:S(2)}) collective-permute-start(bf16[784,128]{1,0:T(8,128)(2,1)S(1)} %get-tuple-element.82), channel_id=1, source_target_pairs={{0,4},{1,5},{2,6},{3,7},{4,0},{5,1},{6,2},{7,3},{8,12},{9,13},{10,... | collective-permute-start | bytes 602120 | tf_op jit(solution)/shard_map/ppermute | solution.py:388
  61.4 4.9 %collective-permute-start.24 = (bf16[2,224,128]{2,1,0:T(8,128)(2,1)S(1)}, bf16[2,224,128]{2,1,0:T(8,128)(2,1)S(1)}, u32[]{:S(2)}, u32[]{:S(2)}) collective-permute-start(bf16[2,224,128]{2,1,0:T(8,128)(2,1)S(1)} %get-tuple-element.107), channel_id=1, source_target_pairs={{0,2},{1,3},{2,0},{3,1},{4,6},{5,7},{6,4},{7,5},{8,10},{9,11},{10,... | collective-permute-start | bytes 344072 | tf_op jit(solution)/shard_map/ppermute | solution.py:388
  63.0 5.0 %collective-permute-start.18 = (bf16[2,240,128]{2,1,0:T(8,128)(2,1)S(1)}, bf16[2,240,128]{2,1,0:T(8,128)(2,1)S(1)}, u32[]{:S(2)}, u32[]{:S(2)}) collective-permute-start(bf16[2,240,128]{2,1,0:T(8,128)(2,1)S(1)} %get-tuple-element.95), channel_id=1, source_target_pairs={{0,1},{1,0},{2,3},{3,2},{4,5},{5,4},{6,7},{7,6},{8,9},{9,8},{10,11... | collective-permute-start | bytes 368648 | tf_op jit(solution)/shard_map/ppermute | solution.py:388
  63.6 6.7 %collective-permute-start.13 = (bf16[1,224,128]{2,1,0:T(8,128)(2,1)S(1)}, bf16[1,224,128]{2,1,0:T(8,128)(2,1)S(1)}, u32[]{:S(2)}, u32[]{:S(2)}) collective-permute-start(bf16[1,224,128]{2,1,0:T(8,128)(2,1)S(1)} %get-tuple-element.85), channel_id=1, source_target_pairs={{0,8},{1,9},{2,10},{3,11},{4,12},{5,13},{6,14},{7,15},{8,0},{9,1},... | collective-permute-start | bytes 172040 | tf_op jit(solution)/shard_map/ppermute | solution.py:388
  66.3 7.4 %collective-permute-start.25 = (bf16[1,224,128]{2,1,0:T(8,128)(2,1)S(1)}, bf16[1,224,128]{2,1,0:T(8,128)(2,1)S(1)}, u32[]{:S(2)}, u32[]{:S(2)}) collective-permute-start(bf16[1,224,128]{2,1,0:T(8,128)(2,1)S(1)} %get-tuple-element.109), channel_id=1, source_target_pairs={{0,8},{1,9},{2,10},{3,11},{4,12},{5,13},{6,14},{7,15},{8,0},{9,1},... | collective-permute-start | bytes 172040 | tf_op jit(solution)/shard_map/ppermute | solution.py:388
  68.0 5.6 %collective-permute-start.19 = (bf16[1,240,128]{2,1,0:T(8,128)(2,1)S(1)}, bf16[1,240,128]{2,1,0:T(8,128)(2,1)S(1)}, u32[]{:S(2)}, u32[]{:S(2)}) collective-permute-start(bf16[1,240,128]{2,1,0:T(8,128)(2,1)S(1)} %get-tuple-element.97), channel_id=1, source_target_pairs={{0,8},{1,9},{2,10},{3,11},{4,12},{5,13},{6,14},{7,15},{8,0},{9,1},... | collective-permute-start | bytes 184328 | tf_op jit(solution)/shard_map/ppermute | solution.py:388
  70.4 4.6 %collective-permute-start.26 = (f32[224,128]{1,0:T(8,128)S(1)}, f32[224,128]{1,0:T(8,128)S(1)}, u32[]{:S(2)}, u32[]{:S(2)}) collective-permute-start(f32[224,128]{1,0:T(8,128)S(1)} %shard_map.125.refs_0_), channel_id=1, source_target_pairs={{0,16},{16,0},{1,17},{17,1},{2,18},{18,2},{3,19},{19,3},{4,20},{20... | collective-permute-start | bytes 344072 | tf_op jit(solution)/shard_map/ppermute | solution.py:392
  73.6 1.6 %collective-permute-start.27 = (f32[240,128]{1,0:T(8,128)S(1)}, f32[240,128]{1,0:T(8,128)S(1)}, u32[]{:S(2)}, u32[]{:S(2)}) collective-permute-start(f32[240,128]{1,0:T(8,128)S(1)} %shard_map.130.refs_1_), channel_id=1, source_target_pairs={{0,16},{16,0},{1,17},{17,1},{2,18},{18,2},{3,19},{19,3},{4,20},{20... | collective-permute-start | bytes 368648 | tf_op jit(solution)/shard_map/ppermute | solution.py:392
  73.7 1.5 %collective-permute-start.28 = (f32[224,128]{1,0:T(8,128)S(1)}, f32[224,128]{1,0:T(8,128)S(1)}, u32[]{:S(2)}, u32[]{:S(2)}) collective-permute-start(f32[224,128]{1,0:T(8,128)S(1)} %shard_map.135.refs_2_), channel_id=1, source_target_pairs={{0,16},{16,0},{1,17},{17,1},{2,18},{18,2},{3,19},{19,3},{4,20},{20... | collective-permute-start | bytes 344072 | tf_op jit(solution)/shard_map/ppermute | solution.py:392
  (3 other events, 5.9 us)

commit v8 on v7

--- a/solution.py
+++ b/solution.py
@@ -11,6 +11,7 @@
 LMAX = 6
 MMAX = 2
 TABLE_ROWS = 32
+USED_ROWS = 16
 MIB = 1024 * 1024
 STREAMS = 3
 MIDDLE = 15
@@ -110,17 +111,22 @@
 
 
 def fill_rotation(rot_ref, wide_ref, angle):
-    coeffs, rows, angles = wide_ref.shape
+    coeffs, _, angles = wide_ref.shape
     angle_hot = hot(iota((angles, angle.shape[1]), 0) == angle).astype(jnp.bfloat16)
-    rot_ref[...] = nn(wide_ref[...].reshape(coeffs * rows, angles), angle_hot)
+    lines = coeffs * USED_ROWS
+    rot_ref[0:lines, :] = nn(wide_ref[:, 0:USED_ROWS, :].reshape(lines, angles), angle_hot)
 
 
 def widen_kernel(wigner_ref, own_ref, wide_ref, copy_ref):
-    kept = wigner_ref.shape[1]
-    wide_ref[:, kept:, :] = jnp.zeros(
-        (wide_ref.shape[0], wide_ref.shape[1] - kept, wide_ref.shape[2]), wide_ref.dtype
-    )
-    wide_ref[:, 0:kept, :] = wigner_ref[...]
+    for degree in range(LMAX + 1):
+        rows = rows_of_degree(degree)
+        for coeff in range(degree * degree, (degree + 1) * (degree + 1)):
+            block = wigner_ref[coeff].astype(jnp.float32)
+            rest = jnp.zeros((USED_ROWS - len(rows), block.shape[1]), jnp.float32)
+            picked = [block[row : row + 1, :] for row in rows]
+            wide_ref[coeff, 0:USED_ROWS, :] = jnp.concatenate([*picked, rest], axis=0).astype(
+                jnp.bfloat16
+            )
     copy_ref[...] = own_ref[...]
 
 
@@ -132,7 +138,7 @@
     atoms, slots = atom_hot.shape
     layers = atom_hot.reshape(atoms // 16, 16, slots)
     for order in range(2 * degree + 1):
-        line = (degree * degree + order) * TABLE_ROWS + row
+        line = (degree * degree + order) * USED_ROWS + rows_of_degree(degree).index(row)
         entry = jnp.broadcast_to(rot_ref[line : line + 1, :], (16, slots)).astype(jnp.bfloat16)
         spread_ref[order * atoms : (order + 1) * atoms, :] = (layers * entry[None]).reshape(
             atoms, slots

time: 76.4 us -> 76.2 us (level)
  no operation moved by 1% of the time
where the time goes in v8:
time: 76.2 us; the launch traced here: 76 us
  waiting for transfers between devices  30.7 us (40%)
  starting transfers between devices  27.1 us (36%)
  Pallas kernels  15.7 us (21%)
  local copies, waits for them, and re-layouts  0.96 us (1%)
  between operations  0.78 us (1%)
    ppermute x20, waiting for transfers between devices, swap(): return lax.ppermute(value, 'graph', [(i, i ^ flip) for i in range(count)])  28 us
    ppermute x20, starting transfers between devices, swap(): return lax.ppermute(value, 'graph', [(i, i ^ flip) for i in range(count)])  25.2 us
    pallas_call x24, Pallas kernels, whole_call(): pl.pallas_call(kernel, out_shape=outs, in_specs=specs, out_specs=[pl.Bloc...  15.7 us
    ppermute x9, waiting for transfers between devices, swap_cores(): return lax.ppermute(value, 'dp', [(i, 1 - i) for i in range(2)])  2.7 us
    ppermute x9, starting transfers between devices, swap_cores(): return lax.ppermute(value, 'dp', [(i, 1 - i) for i in range(2)])  1.98 us
  transfers between devices with their start and end apart: 29, of which 15 were waited for; matrix products, arithmetic and copies ran while one was open for 0% of the time, Pallas kernels for 10%

profile of v8, /device:TPU:0, one launch (start us, length us, event | category | flops | bytes accessed | tf_op | source)
XLA Modules:
  0.0 76.0 jit_solution(2565587758198372505)
XLA Ops:
  0.6 0.7 pad_add_fusion.edge_ref
  1.3 0.9 %copy-done.4 = bf16[16,49,128]{2,0,1:T(8,128)(2,1)S(1)} copy-done((bf16[16,49,128]{2,0,1:T(8,128)(2,1)S(1)}, bf16[16,49,128]{2,0,1:T(8,128)(2,1)}, u32[]{:S(2)}) %copy-start.4) | copy-done | bytes 200728
  2.6 4.1 %collective-permute-start.1 = (bf16[800,128]{1,0:T(8,128)(2,1)S(1)}, bf16[800,128]{1,0:T(8,128)(2,1)S(1)}, u32[]{:S(2)}, u32[]{:S(2)}) collective-permute-start(bf16[800,128]{1,0:T(8,128)(2,1)S(1)} %shard_map.114.refs_1_), channel_id=1, source_target_pairs={{0,8},{1,9},{2,10},{3,11},{4,12},{5,13},{6,14},{7,15},{8,0},{9,1},... | collective-permute-start | bytes 614408 | tf_op jit(solution)/shard_map/ppermute | solution.py:394
  6.6 1.5 %collective-permute-start = (bf16[800,128]{1,0:T(8,128)(2,1)S(1)}, bf16[800,128]{1,0:T(8,128)(2,1)S(1)}, u32[]{:S(2)}, u32[]{:S(2)}) collective-permute-start(bf16[800,128]{1,0:T(8,128)(2,1)S(1)} %shard_map.114.refs_1_), channel_id=1, source_target_pairs={{0,2},{1,3},{2,0},{3,1},{4,6},{5,7},{6,4},{7,5},{8,10},{9,11},{10,... | collective-permute-start | bytes 614408 | tf_op jit(solution)/shard_map/ppermute | solution.py:394
  8.1 1.5 %collective-permute-start.3 = (bf16[784,128]{1,0:T(8,128)(2,1)S(1)}, bf16[784,128]{1,0:T(8,128)(2,1)S(1)}, u32[]{:S(2)}, u32[]{:S(2)}) collective-permute-start(bf16[784,128]{1,0:T(8,128)(2,1)S(1)} %bitcast.17), channel_id=1, source_target_pairs={{0,1},{1,0},{2,3},{3,2},{4,5},{5,4},{6,7},{7,6},{8,9},{9,8},{10,11... | collective-permute-start | bytes 602120 | tf_op jit(solution)/shard_map/ppermute | solution.py:394
  9.6 1.6 %collective-permute-start.2 = (bf16[784,128]{1,0:T(8,128)(2,1)S(1)}, bf16[784,128]{1,0:T(8,128)(2,1)S(1)}, u32[]{:S(2)}, u32[]{:S(2)}) collective-permute-start(bf16[784,128]{1,0:T(8,128)(2,1)S(1)} %bitcast.18), channel_id=1, source_target_pairs={{0,4},{1,5},{2,6},{3,7},{4,0},{5,1},{6,2},{7,3},{8,12},{9,13},{10,... | collective-permute-start | bytes 602120 | tf_op jit(solution)/shard_map/ppermute | solution.py:394
  11.4 2.9 %collective-permute-done.3.refs_3_.refs_6_ = bf16[784,128]{1,0:T(8,128)(2,1)S(1)} collective-permute-done((bf16[784,128]{1,0:T(8,128)(2,1)S(1)}, bf16[784,128]{1,0:T(8,128)(2,1)S(1)}, u32[]{:S(2)}, u32[]{:S(2)}) %collective-permute-start.3) | collective-permute-done | bytes 200736 | tf_op jit(solution)/shard_map/ppermute | solution.py:394
  14.3 4.4 %collective-permute-done.2.refs_1_ = bf16[784,128]{1,0:T(8,128)(2,1)S(1)} collective-permute-done((bf16[784,128]{1,0:T(8,128)(2,1)S(1)}, bf16[784,128]{1,0:T(8,128)(2,1)S(1)}, u32[]{:S(2)}, u32[]{:S(2)}) %collective-permute-start.2) | collective-permute-done | bytes 200736 | tf_op jit(solution)/shard_map/ppermute | solution.py:394
  19.9 5.2 %collective-permute-done.5.refs_8_ = bf16[784,128]{1,0:T(8,128)(2,1)S(1)} collective-permute-done((bf16[784,128]{1,0:T(8,128)(2,1)S(1)}, bf16[784,128]{1,0:T(8,128)(2,1)S(1)}, u32[]{:S(2)}, u32[]{:S(2)}) %collective-permute-start.5) | collective-permute-done | bytes 200736 | tf_op jit(solution)/shard_map/ppermute | solution.py:394
  25.1 5.0 %shard_map.116 = (f32[1568,256]{1,0:T(8,128)S(1)}, s32[8,256]{1,0:T(8,128)S(1)}, bf16[896,256]{1,0:T(8,128)(2,1)S(1)}, bf16[768,512]{1,0:T(8,128)(2,1)S(1)}, bf1...) custom-call(bf16[49,32,256]{2,1,0:T(8,128)(2,1)S(1)} %get-tuple-elem, ...), custom_call_target="tpu_custom_call" | custom-call | flops 5000000000 | bytes 100000 | tf_op jit(solution)/shard_map/pallas_call | solution.py:380
  30.1 2.2 %shard_map.118 = (f32[8,224,128]{2,1,0:T(8,128)S(1)}, bf16[8,224,128]{2,1,0:T(8,128)(2,1)S(1)}, f32[8,240,128]{2,1,0:T(8,128)S(1)}, bf16[8,240,128]{2,1,0:T(8,12...) custom-call(bf16[896,256]{1,0:T(8,128)(2,1)S(1)} %get-tuple-element.62.refs_2_.refs_0_, ...), custom_call_target="tpu_custom_call" | custom-call | flops 3000000000 | bytes 100000 | tf_op jit(solution)/shard_map/pallas_call | solution.py:380
  33.5 0.7 collective-permute-done.8.refs_3_
  36.9 0.7 collective-permute-done.14.refs_1_
  37.8 1.5 %collective-permute-start.16 = (bf16[8,240,128]{2,1,0:T(8,128)(2,1)S(1)}, bf16[8,240,128]{2,1,0:T(8,128)(2,1)S(1)}, u32[]{:S(2)}, u32[]{:S(2)}) collective-permute-start(bf16[8,240,128]{2,1,0:T(8,128)(2,1)S(1)} %get-tuple-element.91), channel_id=1, source_target_pairs={{0,2},{1,3},{2,0},{3,1},{4,6},{5,7},{6,4},{7,5},{8,10},{9,11},{10,... | collective-permute-start | bytes 1474568 | tf_op jit(solution)/shard_map/ppermute | solution.py:394
  39.4 5.2 %shard_map.117 = (f32[1568,128]{1,0:T(8,128)S(1)}, bf16[1568,128]{1,0:T(8,128)(2,1)S(1)}) custom-call(f32[1568,256]{1,0:T(8,128)S(1)} %get-tuple-element.60.refs_0_, s32[8,256]{1,0:T(8,128)S(1)} %get-tuple-element.61.refs_1_, bf16[896,256]{1,0:T(8,128)(2,1)S(1)} %get-tuple-element.62.refs_2_.refs_0_, bf16[768,512]{1,0:T(8,128)(2,1)S(1)} %get-tuple-element.63.refs_3_.refs_1_, ...), custom_call_target="tpu_custom_call" | custom-call | flops 8000000000 | bytes 100000 | tf_op jit(solution)/shard_map/pallas_call | solution.py:380
  44.6 0.7 collective-permute-start.6
  45.3 2.5 %collective-permute-done.9.came_ref = bf16[8,224,128]{2,1,0:T(8,128)(2,1)S(1)} collective-permute-done((bf16[8,224,128]{2,1,0:T(8,128)(2,1)S(1)}, bf16[8,224,128]{2,1,0:T(8,128)(2,1)S(1)}, u32[]{:S(2)}, u32[]{:S(2)}) %collective-permute-start.9) | collective-permute-done | bytes 458784 | tf_op jit(solution)/shard_map/ppermute | solution.py:394
  47.9 1.5 %collective-permute-start.10 = (bf16[4,224,128]{2,1,0:T(8,128)(2,1)S(1)}, bf16[4,224,128]{2,1,0:T(8,128)(2,1)S(1)}, u32[]{:S(2)}, u32[]{:S(2)}) collective-permute-start(bf16[4,224,128]{2,1,0:T(8,128)(2,1)S(1)} %get-tuple-element.79), channel_id=1, source_target_pairs={{0,2},{1,3},{2,0},{3,1},{4,6},{5,7},{6,4},{7,5},{8,10},{9,11},{10,... | collective-permute-start | bytes 688136 | tf_op jit(solution)/shard_map/ppermute | solution.py:394
  50.2 1.8 %collective-permute-done.16.came_ref = bf16[8,240,128]{2,1,0:T(8,128)(2,1)S(1)} collective-permute-done((bf16[8,240,128]{2,1,0:T(8,128)(2,1)S(1)}, bf16[8,240,128]{2,1,0:T(8,128)(2,1)S(1)}, u32[]{:S(2)}, u32[]{:S(2)}) %collective-permute-start.16) | collective-permute-done | bytes 491552 | tf_op jit(solution)/shard_map/ppermute | solution.py:394
  52.0 1.0 %collective-permute-start.17 = (bf16[4,240,128]{2,1,0:T(8,128)(2,1)S(1)}, bf16[4,240,128]{2,1,0:T(8,128)(2,1)S(1)}, u32[]{:S(2)}, u32[]{:S(2)}) collective-permute-start(bf16[4,240,128]{2,1,0:T(8,128)(2,1)S(1)} %get-tuple-element.93), channel_id=1, source_target_pairs={{0,4},{1,5},{2,6},{3,7},{4,0},{5,1},{6,2},{7,3},{8,12},{9,13},{10,... | collective-permute-start | bytes 737288 | tf_op jit(solution)/shard_map/ppermute | solution.py:394
  53.0 3.0 %collective-permute-done.10.came_ref = bf16[4,224,128]{2,1,0:T(8,128)(2,1)S(1)} collective-permute-done((bf16[4,224,128]{2,1,0:T(8,128)(2,1)S(1)}, bf16[4,224,128]{2,1,0:T(8,128)(2,1)S(1)}, u32[]{:S(2)}, u32[]{:S(2)}) %collective-permute-start.10) | collective-permute-done | bytes 229408 | tf_op jit(solution)/shard_map/ppermute | solution.py:394
  56.9 1.4 %collective-permute-start.11 = (bf16[784,128]{1,0:T(8,128)(2,1)S(1)}, bf16[784,128]{1,0:T(8,128)(2,1)S(1)}, u32[]{:S(2)}, u32[]{:S(2)}) collective-permute-start(bf16[784,128]{1,0:T(8,128)(2,1)S(1)} %get-tuple-element.82), channel_id=1, source_target_pairs={{0,4},{1,5},{2,6},{3,7},{4,0},{5,1},{6,2},{7,3},{8,12},{9,13},{10,... | collective-permute-start | bytes 602120 | tf_op jit(solution)/shard_map/ppermute | solution.py:394
  58.4 2.8 %collective-permute-done.23.came_ref = bf16[4,224,128]{2,1,0:T(8,128)(2,1)S(1)} collective-permute-done((bf16[4,224,128]{2,1,0:T(8,128)(2,1)S(1)}, bf16[4,224,128]{2,1,0:T(8,128)(2,1)S(1)}, u32[]{:S(2)}, u32[]{:S(2)}) %collective-permute-start.23) | collective-permute-done | bytes 229408 | tf_op jit(solution)/shard_map/ppermute | solution.py:394
  61.2 1.5 %collective-permute-start.24 = (bf16[2,224,128]{2,1,0:T(8,128)(2,1)S(1)}, bf16[2,224,128]{2,1,0:T(8,128)(2,1)S(1)}, u32[]{:S(2)}, u32[]{:S(2)}) collective-permute-start(bf16[2,224,128]{2,1,0:T(8,128)(2,1)S(1)} %get-tuple-element.107), channel_id=1, source_target_pairs={{0,2},{1,3},{2,0},{3,1},{4,6},{5,7},{6,4},{7,5},{8,10},{9,11},{10,... | collective-permute-start | bytes 344072 | tf_op jit(solution)/shard_map/ppermute | solution.py:394
  63.5 1.5 %collective-permute-start.13 = (bf16[1,224,128]{2,1,0:T(8,128)(2,1)S(1)}, bf16[1,224,128]{2,1,0:T(8,128)(2,1)S(1)}, u32[]{:S(2)}, u32[]{:S(2)}) collective-permute-start(bf16[1,224,128]{2,1,0:T(8,128)(2,1)S(1)} %get-tuple-element.85), channel_id=1, source_target_pairs={{0,8},{1,9},{2,10},{3,11},{4,12},{5,13},{6,14},{7,15},{8,0},{9,1},... | collective-permute-start | bytes 172040 | tf_op jit(solution)/shard_map/ppermute | solution.py:394
  65.0 1.1 %collective-permute-done.24.came_ref = bf16[2,224,128]{2,1,0:T(8,128)(2,1)S(1)} collective-permute-done((bf16[2,224,128]{2,1,0:T(8,128)(2,1)S(1)}, bf16[2,224,128]{2,1,0:T(8,128)(2,1)S(1)}, u32[]{:S(2)}, u32[]{:S(2)}) %collective-permute-start.24) | collective-permute-done | bytes 114720 | tf_op jit(solution)/shard_map/ppermute | solution.py:394
  66.1 1.7 %collective-permute-start.25 = (bf16[1,224,128]{2,1,0:T(8,128)(2,1)S(1)}, bf16[1,224,128]{2,1,0:T(8,128)(2,1)S(1)}, u32[]{:S(2)}, u32[]{:S(2)}) collective-permute-start(bf16[1,224,128]{2,1,0:T(8,128)(2,1)S(1)} %get-tuple-element.109), channel_id=1, source_target_pairs={{0,8},{1,9},{2,10},{3,11},{4,12},{5,13},{6,14},{7,15},{8,0},{9,1},... | collective-permute-start | bytes 172040 | tf_op jit(solution)/shard_map/ppermute | solution.py:394
  67.8 1.4 %collective-permute-start.19 = (bf16[1,240,128]{2,1,0:T(8,128)(2,1)S(1)}, bf16[1,240,128]{2,1,0:T(8,128)(2,1)S(1)}, u32[]{:S(2)}, u32[]{:S(2)}) collective-permute-start(bf16[1,240,128]{2,1,0:T(8,128)(2,1)S(1)} %get-tuple-element.97), channel_id=1, source_target_pairs={{0,8},{1,9},{2,10},{3,11},{4,12},{5,13},{6,14},{7,15},{8,0},{9,1},... | collective-permute-start | bytes 184328 | tf_op jit(solution)/shard_map/ppermute | solution.py:394
  69.2 1.0 %collective-permute-done.13.came_ref = bf16[1,224,128]{2,1,0:T(8,128)(2,1)S(1)} collective-permute-done((bf16[1,224,128]{2,1,0:T(8,128)(2,1)S(1)}, bf16[1,224,128]{2,1,0:T(8,128)(2,1)S(1)}, u32[]{:S(2)}, u32[]{:S(2)}) %collective-permute-start.13) | collective-permute-done | bytes 57376 | tf_op jit(solution)/shard_map/ppermute | solution.py:394
  70.3 3.1 %collective-permute-done.19.came_ref = bf16[1,240,128]{2,1,0:T(8,128)(2,1)S(1)} collective-permute-done((bf16[1,240,128]{2,1,0:T(8,128)(2,1)S(1)}, bf16[1,240,128]{2,1,0:T(8,128)(2,1)S(1)}, u32[]{:S(2)}, u32[]{:S(2)}) %collective-permute-start.19) | collective-permute-done | bytes 61472 | tf_op jit(solution)/shard_map/ppermute | solution.py:394
  74.1 0.7 shard_map.123
  75.1 0.9 %shard_map.136 = f32[1368,128]{1,0:T(8,128)} custom-call(f32[224,128]{1,0:T(8,128)S(1)} %shard_map.125.refs_0_, f32[240,128]{1,0:T(8,128)S(1)} %shard_map.130.refs_1_, f32[224,128]{1,0:T(8,128)S(1)} %shard_map.135.refs_2_, f32[224,128]{1,0:T(8,128)S(1)} %collective-permute-done.26.refs_3_, f32[240,128]{1,0:T(8,128)S(1)} %collective-permute-done.27.refs_4_, ...), custom_call_target="tpu_custom_call" | custom-call | flops 1000000000 | bytes 100000 | tf_op jit(solution)/shard_map/pallas_call | solution.py:380
  (63 shorter events, 9.2 us)
Async XLA Ops:
  2.3 5.9 %copy-start.5 = (bf16[16,49,128]{2,0,1:T(8,128)(2,1)S(1)}, bf16[16,49,128]{2,0,1:T(8,128)(2,1)}, u32[]{:S(2)}) copy-start(bf16[16,49,128]{2,0,1:T(8,128)(2,1)} %param.11) | copy-start | bytes 602116
  2.3 8.9 %copy-start.3 = (bf16[256,29,49]{0,1,2:T(8,128)(2,1)S(1)}, bf16[256,29,49]{0,1,2:T(8,128)(2,1)}, u32[]{:S(2)}) copy-start(bf16[256,29,49]{0,1,2:T(8,128)(2,1)} %param.12) | copy-start | bytes 2182660
  2.6 16.2 %collective-permute-start.1 = (bf16[800,128]{1,0:T(8,128)(2,1)S(1)}, bf16[800,128]{1,0:T(8,128)(2,1)S(1)}, u32[]{:S(2)}, u32[]{:S(2)}) collective-permute-start(bf16[800,128]{1,0:T(8,128)(2,1)S(1)} %shard_map.114.refs_1_), channel_id=1, source_target_pairs={{0,8},{1,9},{2,10},{3,11},{4,12},{5,13},{6,14},{7,15},{8,0},{9,1},... | collective-permute-start | bytes 614408 | tf_op jit(solution)/shard_map/ppermute | solution.py:394
  6.6 12.1 %collective-permute-start = (bf16[800,128]{1,0:T(8,128)(2,1)S(1)}, bf16[800,128]{1,0:T(8,128)(2,1)S(1)}, u32[]{:S(2)}, u32[]{:S(2)}) collective-permute-start(bf16[800,128]{1,0:T(8,128)(2,1)S(1)} %shard_map.114.refs_1_), channel_id=1, source_target_pairs={{0,2},{1,3},{2,0},{3,1},{4,6},{5,7},{6,4},{7,5},{8,10},{9,11},{10,... | collective-permute-start | bytes 614408 | tf_op jit(solution)/shard_map/ppermute | solution.py:394
  8.1 6.2 %collective-permute-start.3 = (bf16[784,128]{1,0:T(8,128)(2,1)S(1)}, bf16[784,128]{1,0:T(8,128)(2,1)S(1)}, u32[]{:S(2)}, u32[]{:S(2)}) collective-permute-start(bf16[784,128]{1,0:T(8,128)(2,1)S(1)} %bitcast.17), channel_id=1, source_target_pairs={{0,1},{1,0},{2,3},{3,2},{4,5},{5,4},{6,7},{7,6},{8,9},{9,8},{10,11... | collective-permute-start | bytes 602120 | tf_op jit(solution)/shard_map/ppermute | solution.py:394
  9.6 9.1 %collective-permute-start.2 = (bf16[784,128]{1,0:T(8,128)(2,1)S(1)}, bf16[784,128]{1,0:T(8,128)(2,1)S(1)}, u32[]{:S(2)}, u32[]{:S(2)}) collective-permute-start(bf16[784,128]{1,0:T(8,128)(2,1)S(1)} %bitcast.18), channel_id=1, source_target_pairs={{0,4},{1,5},{2,6},{3,7},{4,0},{5,1},{6,2},{7,3},{8,12},{9,13},{10,... | collective-permute-start | bytes 602120 | tf_op jit(solution)/shard_map/ppermute | solution.py:394
  18.7 6.3 %collective-permute-start.4 = (bf16[800,128]{1,0:T(8,128)(2,1)S(1)}, bf16[800,128]{1,0:T(8,128)(2,1)S(1)}, u32[]{:S(2)}, u32[]{:S(2)}) collective-permute-start(bf16[800,128]{1,0:T(8,128)(2,1)S(1)} %get-tuple-element.58.refs_3_), channel_id=1, source_target_pairs={{0,2},{1,3},{2,0},{3,1},{4,6},{5,7},{6,4},{7,5},{8,10},{9,11},{10,... | collective-permute-start | bytes 614408 | tf_op jit(solution)/shard_map/ppermute | solution.py:394
  19.4 5.7 %collective-permute-start.5 = (bf16[784,128]{1,0:T(8,128)(2,1)S(1)}, bf16[784,128]{1,0:T(8,128)(2,1)S(1)}, u32[]{:S(2)}, u32[]{:S(2)}) collective-permute-start(bf16[784,128]{1,0:T(8,128)(2,1)S(1)} %get-tuple-element.59.refs_7_), channel_id=1, source_target_pairs={{0,1},{1,0},{2,3},{3,2},{4,5},{5,4},{6,7},{7,6},{8,9},{9,8},{10,11... | collective-permute-start | bytes 602120 | tf_op jit(solution)/shard_map/ppermute | solution.py:394
  32.3 1.9 %collective-permute-start.8 = (bf16[8,224,128]{2,1,0:T(8,128)(2,1)S(1)}, bf16[8,224,128]{2,1,0:T(8,128)(2,1)S(1)}, u32[]{:S(2)}, u32[]{:S(2)}) collective-permute-start(bf16[8,224,128]{2,1,0:T(8,128)(2,1)S(1)} %get-tuple-element.75), channel_id=1, source_target_pairs={{0,16},{16,0},{1,17},{17,1},{2,18},{18,2},{3,19},{19,3},{4,20},{20... | collective-permute-start | bytes 1376264 | tf_op jit(solution)/shard_map/ppermute | solution.py:398
  32.4 2.5 %collective-permute-start.7 = (bf16[8,224,128]{2,1,0:T(8,128)(2,1)S(1)}, bf16[8,224,128]{2,1,0:T(8,128)(2,1)S(1)}, u32[]{:S(2)}, u32[]{:S(2)}) collective-permute-start(bf16[8,224,128]{2,1,0:T(8,128)(2,1)S(1)} %get-tuple-element.68), channel_id=1, source_target_pairs={{0,16},{16,0},{1,17},{17,1},{2,18},{18,2},{3,19},{19,3},{4,20},{20... | collective-permute-start | bytes 1376264 | tf_op jit(solution)/shard_map/ppermute | solution.py:398
  32.9 2.8 %collective-permute-start.21 = (bf16[8,224,128]{2,1,0:T(8,128)(2,1)S(1)}, bf16[8,224,128]{2,1,0:T(8,128)(2,1)S(1)}, u32[]{:S(2)}, u32[]{:S(2)}) collective-permute-start(bf16[8,224,128]{2,1,0:T(8,128)(2,1)S(1)} %get-tuple-element.101), channel_id=1, source_target_pairs={{0,16},{16,0},{1,17},{17,1},{2,18},{18,2},{3,19},{19,3},{4,20},{20... | collective-permute-start | bytes 1376264 | tf_op jit(solution)/shard_map/ppermute | solution.py:398
  33.0 3.2 %collective-permute-start.20 = (bf16[8,224,128]{2,1,0:T(8,128)(2,1)S(1)}, bf16[8,224,128]{2,1,0:T(8,128)(2,1)S(1)}, u32[]{:S(2)}, u32[]{:S(2)}) collective-permute-start(bf16[8,224,128]{2,1,0:T(8,128)(2,1)S(1)} %get-tuple-element.99), channel_id=1, source_target_pairs={{0,16},{16,0},{1,17},{17,1},{2,18},{18,2},{3,19},{19,3},{4,20},{20... | collective-permute-start | bytes 1376264 | tf_op jit(solution)/shard_map/ppermute | solution.py:398
  33.4 3.5 %collective-permute-start.15 = (bf16[8,240,128]{2,1,0:T(8,128)(2,1)S(1)}, bf16[8,240,128]{2,1,0:T(8,128)(2,1)S(1)}, u32[]{:S(2)}, u32[]{:S(2)}) collective-permute-start(bf16[8,240,128]{2,1,0:T(8,128)(2,1)S(1)} %get-tuple-element.89), channel_id=1, source_target_pairs={{0,16},{16,0},{1,17},{17,1},{2,18},{18,2},{3,19},{19,3},{4,20},{20... | collective-permute-start | bytes 1474568 | tf_op jit(solution)/shard_map/ppermute | solution.py:398
  34.2 3.4 %collective-permute-start.14 = (bf16[8,240,128]{2,1,0:T(8,128)(2,1)S(1)}, bf16[8,240,128]{2,1,0:T(8,128)(2,1)S(1)}, u32[]{:S(2)}, u32[]{:S(2)}) collective-permute-start(bf16[8,240,128]{2,1,0:T(8,128)(2,1)S(1)} %get-tuple-element.87), channel_id=1, source_target_pairs={{0,16},{16,0},{1,17},{17,1},{2,18},{18,2},{3,19},{19,3},{4,20},{20... | collective-permute-start | bytes 1474568 | tf_op jit(solution)/shard_map/ppermute | solution.py:398
  35.0 12.8 %collective-permute-start.9 = (bf16[8,224,128]{2,1,0:T(8,128)(2,1)S(1)}, bf16[8,224,128]{2,1,0:T(8,128)(2,1)S(1)}, u32[]{:S(2)}, u32[]{:S(2)}) collective-permute-start(bf16[8,224,128]{2,1,0:T(8,128)(2,1)S(1)} %get-tuple-element.77), channel_id=1, source_target_pairs={{0,1},{1,0},{2,3},{3,2},{4,5},{5,4},{6,7},{7,6},{8,9},{9,8},{10,11... | collective-permute-start | bytes 1376264 | tf_op jit(solution)/shard_map/ppermute | solution.py:394
  36.2 3.2 %copy-start.2 = (bf16[896,896]{1,0:T(8,128)(2,1)S(1)}, bf16[896,896]{1,0:T(8,128)(2,1)}, u32[]{:S(2)}) copy-start(bf16[896,896]{1,0:T(8,128)(2,1)} %refs_5_.1) | copy-start | bytes 4816900
  36.4 13.1 %collective-permute-start.22 = (bf16[8,224,128]{2,1,0:T(8,128)(2,1)S(1)}, bf16[8,224,128]{2,1,0:T(8,128)(2,1)S(1)}, u32[]{:S(2)}, u32[]{:S(2)}) collective-permute-start(bf16[8,224,128]{2,1,0:T(8,128)(2,1)S(1)} %get-tuple-element.103), channel_id=1, source_target_pairs={{0,4},{1,5},{2,6},{3,7},{4,0},{5,1},{6,2},{7,3},{8,12},{9,13},{10,... | collective-permute-start | bytes 1376264 | tf_op jit(solution)/shard_map/ppermute | solution.py:394
  37.8 14.1 %collective-permute-start.16 = (bf16[8,240,128]{2,1,0:T(8,128)(2,1)S(1)}, bf16[8,240,128]{2,1,0:T(8,128)(2,1)S(1)}, u32[]{:S(2)}, u32[]{:S(2)}) collective-permute-start(bf16[8,240,128]{2,1,0:T(8,128)(2,1)S(1)} %get-tuple-element.91), channel_id=1, source_target_pairs={{0,2},{1,3},{2,0},{3,1},{4,6},{5,7},{6,4},{7,5},{8,10},{9,11},{10,... | collective-permute-start | bytes 1474568 | tf_op jit(solution)/shard_map/ppermute | solution.py:394
  44.6 12.2 %collective-permute-start.6 = (bf16[1568,128]{1,0:T(8,128)(2,1)S(1)}, bf16[1568,128]{1,0:T(8,128)(2,1)S(1)}, u32[]{:S(2)}, u32[]{:S(2)}) collective-permute-start(bf16[1568,128]{1,0:T(8,128)(2,1)S(1)} %get-tuple-element.66.refs_0_), channel_id=1, source_target_pairs={{0,1},{1,0},{2,3},{3,2},{4,5},{5,4},{6,7},{7,6},{8,9},{9,8},{10,11... | collective-permute-start | bytes 1204232 | tf_op jit(solution)/shard_map/ppermute | solution.py:394
  47.9 8.1 %collective-permute-start.10 = (bf16[4,224,128]{2,1,0:T(8,128)(2,1)S(1)}, bf16[4,224,128]{2,1,0:T(8,128)(2,1)S(1)}, u32[]{:S(2)}, u32[]{:S(2)}) collective-permute-start(bf16[4,224,128]{2,1,0:T(8,128)(2,1)S(1)} %get-tuple-element.79), channel_id=1, source_target_pairs={{0,2},{1,3},{2,0},{3,1},{4,6},{5,7},{6,4},{7,5},{8,10},{9,11},{10,... | collective-permute-start | bytes 688136 | tf_op jit(solution)/shard_map/ppermute | solution.py:394
  49.5 11.6 %collective-permute-start.23 = (bf16[4,224,128]{2,1,0:T(8,128)(2,1)S(1)}, bf16[4,224,128]{2,1,0:T(8,128)(2,1)S(1)}, u32[]{:S(2)}, u32[]{:S(2)}) collective-permute-start(bf16[4,224,128]{2,1,0:T(8,128)(2,1)S(1)} %get-tuple-element.105), channel_id=1, source_target_pairs={{0,1},{1,0},{2,3},{3,2},{4,5},{5,4},{6,7},{7,6},{8,9},{9,8},{10,11... | collective-permute-start | bytes 688136 | tf_op jit(solution)/shard_map/ppermute | solution.py:394
  52.0 10.7 %collective-permute-start.17 = (bf16[4,240,128]{2,1,0:T(8,128)(2,1)S(1)}, bf16[4,240,128]{2,1,0:T(8,128)(2,1)S(1)}, u32[]{:S(2)}, u32[]{:S(2)}) collective-permute-start(bf16[4,240,128]{2,1,0:T(8,128)(2,1)S(1)} %get-tuple-element.93), channel_id=1, source_target_pairs={{0,4},{1,5},{2,6},{3,7},{4,0},{5,1},{6,2},{7,3},{8,12},{9,13},{10,... | collective-permute-start | bytes 737288 | tf_op jit(solution)/shard_map/ppermute | solution.py:394
  56.1 7.4 %collective-permute-start.12 = (bf16[2,224,128]{2,1,0:T(8,128)(2,1)S(1)}, bf16[2,224,128]{2,1,0:T(8,128)(2,1)S(1)}, u32[]{:S(2)}, u32[]{:S(2)}) collective-permute-start(bf16[2,224,128]{2,1,0:T(8,128)(2,1)S(1)} %get-tuple-element.80.after_ref), channel_id=1, source_target_pairs={{0,4},{1,5},{2,6},{3,7},{4,0},{5,1},{6,2},{7,3},{8,12},{9,13},{10,... | collective-permute-start | bytes 344072 | tf_op jit(solution)/shard_map/ppermute | solution.py:394
  56.9 17.2 %collective-permute-start.11 = (bf16[784,128]{1,0:T(8,128)(2,1)S(1)}, bf16[784,128]{1,0:T(8,128)(2,1)S(1)}, u32[]{:S(2)}, u32[]{:S(2)}) collective-permute-start(bf16[784,128]{1,0:T(8,128)(2,1)S(1)} %get-tuple-element.82), channel_id=1, source_target_pairs={{0,4},{1,5},{2,6},{3,7},{4,0},{5,1},{6,2},{7,3},{8,12},{9,13},{10,... | collective-permute-start | bytes 602120 | tf_op jit(solution)/shard_map/ppermute | solution.py:394
  61.2 4.9 %collective-permute-start.24 = (bf16[2,224,128]{2,1,0:T(8,128)(2,1)S(1)}, bf16[2,224,128]{2,1,0:T(8,128)(2,1)S(1)}, u32[]{:S(2)}, u32[]{:S(2)}) collective-permute-start(bf16[2,224,128]{2,1,0:T(8,128)(2,1)S(1)} %get-tuple-element.107), channel_id=1, source_target_pairs={{0,2},{1,3},{2,0},{3,1},{4,6},{5,7},{6,4},{7,5},{8,10},{9,11},{10,... | collective-permute-start | bytes 344072 | tf_op jit(solution)/shard_map/ppermute | solution.py:394
  62.8 5.0 %collective-permute-start.18 = (bf16[2,240,128]{2,1,0:T(8,128)(2,1)S(1)}, bf16[2,240,128]{2,1,0:T(8,128)(2,1)S(1)}, u32[]{:S(2)}, u32[]{:S(2)}) collective-permute-start(bf16[2,240,128]{2,1,0:T(8,128)(2,1)S(1)} %get-tuple-element.95), channel_id=1, source_target_pairs={{0,1},{1,0},{2,3},{3,2},{4,5},{5,4},{6,7},{7,6},{8,9},{9,8},{10,11... | collective-permute-start | bytes 368648 | tf_op jit(solution)/shard_map/ppermute | solution.py:394
  63.5 6.7 %collective-permute-start.13 = (bf16[1,224,128]{2,1,0:T(8,128)(2,1)S(1)}, bf16[1,224,128]{2,1,0:T(8,128)(2,1)S(1)}, u32[]{:S(2)}, u32[]{:S(2)}) collective-permute-start(bf16[1,224,128]{2,1,0:T(8,128)(2,1)S(1)} %get-tuple-element.85), channel_id=1, source_target_pairs={{0,8},{1,9},{2,10},{3,11},{4,12},{5,13},{6,14},{7,15},{8,0},{9,1},... | collective-permute-start | bytes 172040 | tf_op jit(solution)/shard_map/ppermute | solution.py:394
  66.1 7.4 %collective-permute-start.25 = (bf16[1,224,128]{2,1,0:T(8,128)(2,1)S(1)}, bf16[1,224,128]{2,1,0:T(8,128)(2,1)S(1)}, u32[]{:S(2)}, u32[]{:S(2)}) collective-permute-start(bf16[1,224,128]{2,1,0:T(8,128)(2,1)S(1)} %get-tuple-element.109), channel_id=1, source_target_pairs={{0,8},{1,9},{2,10},{3,11},{4,12},{5,13},{6,14},{7,15},{8,0},{9,1},... | collective-permute-start | bytes 172040 | tf_op jit(solution)/shard_map/ppermute | solution.py:394
  67.8 5.6 %collective-permute-start.19 = (bf16[1,240,128]{2,1,0:T(8,128)(2,1)S(1)}, bf16[1,240,128]{2,1,0:T(8,128)(2,1)S(1)}, u32[]{:S(2)}, u32[]{:S(2)}) collective-permute-start(bf16[1,240,128]{2,1,0:T(8,128)(2,1)S(1)} %get-tuple-element.97), channel_id=1, source_target_pairs={{0,8},{1,9},{2,10},{3,11},{4,12},{5,13},{6,14},{7,15},{8,0},{9,1},... | collective-permute-start | bytes 184328 | tf_op jit(solution)/shard_map/ppermute | solution.py:394
  70.2 4.6 %collective-permute-start.26 = (f32[224,128]{1,0:T(8,128)S(1)}, f32[224,128]{1,0:T(8,128)S(1)}, u32[]{:S(2)}, u32[]{:S(2)}) collective-permute-start(f32[224,128]{1,0:T(8,128)S(1)} %shard_map.125.refs_0_), channel_id=1, source_target_pairs={{0,16},{16,0},{1,17},{17,1},{2,18},{18,2},{3,19},{19,3},{4,20},{20... | collective-permute-start | bytes 344072 | tf_op jit(solution)/shard_map/ppermute | solution.py:398
  73.5 1.6 %collective-permute-start.27 = (f32[240,128]{1,0:T(8,128)S(1)}, f32[240,128]{1,0:T(8,128)S(1)}, u32[]{:S(2)}, u32[]{:S(2)}) collective-permute-start(f32[240,128]{1,0:T(8,128)S(1)} %shard_map.130.refs_1_), channel_id=1, source_target_pairs={{0,16},{16,0},{1,17},{17,1},{2,18},{18,2},{3,19},{19,3},{4,20},{20... | collective-permute-start | bytes 368648 | tf_op jit(solution)/shard_map/ppermute | solution.py:398
  73.6 1.5 %collective-permute-start.28 = (f32[224,128]{1,0:T(8,128)S(1)}, f32[224,128]{1,0:T(8,128)S(1)}, u32[]{:S(2)}, u32[]{:S(2)}) collective-permute-start(f32[224,128]{1,0:T(8,128)S(1)} %shard_map.135.refs_2_), channel_id=1, source_target_pairs={{0,16},{16,0},{1,17},{17,1},{2,18},{18,2},{3,19},{19,3},{4,20},{20... | collective-permute-start | bytes 344072 | tf_op jit(solution)/shard_map/ppermute | solution.py:398
  (3 other events, 5.9 us)

commit v9 on v8

--- a/solution.py
+++ b/solution.py
@@ -287,8 +287,8 @@
             begin = max(0, (low - base) // length // 16 * 16)
             if begin < top:
                 left = left_refs[azimuth][begin:top, :]
-                for first in range(0, length, 2):
-                    width = min(2, length - first)
+                for first in range(0, length, 4):
+                    width = min(4, length - first)
                     block = nt(left, right[first * channels : (first + width) * channels, :])
                     for step in range(width):
                         start = base - low + lay.margin + begin * length + first + step

time: 76.2 us -> 76.2 us (level)
  no operation moved by 1% of the time
where the time goes in v9:
time: 76.2 us; the launch traced here: 76 us
  waiting for transfers between devices  30.7 us (40%)
  starting transfers between devices  27.1 us (36%)
  Pallas kernels  15.7 us (21%)
  local copies, waits for them, and re-layouts  0.96 us (1%)
  between operations  0.78 us (1%)
    ppermute x20, waiting for transfers between devices, swap(): return lax.ppermute(value, 'graph', [(i, i ^ flip) for i in range(count)])  28 us
    ppermute x20, starting transfers between devices, swap(): return lax.ppermute(value, 'graph', [(i, i ^ flip) for i in range(count)])  25.2 us
    pallas_call x24, Pallas kernels, whole_call(): pl.pallas_call(kernel, out_shape=outs, in_specs=specs, out_specs=[pl.Bloc...  15.7 us
    ppermute x9, waiting for transfers between devices, swap_cores(): return lax.ppermute(value, 'dp', [(i, 1 - i) for i in range(2)])  2.7 us
    ppermute x9, starting transfers between devices, swap_cores(): return lax.ppermute(value, 'dp', [(i, 1 - i) for i in range(2)])  1.98 us
  transfers between devices with their start and end apart: 29, of which 15 were waited for; matrix products, arithmetic and copies ran while one was open for 0% of the time, Pallas kernels for 10%

profile of v9, /device:TPU:0, one launch (start us, length us, event | category | flops | bytes accessed | tf_op | source)
XLA Modules:
  0.0 76.0 jit_solution(2565587758198372505)
XLA Ops:
  0.6 0.7 pad_add_fusion.edge_ref
  1.3 0.9 %copy-done.4 = bf16[16,49,128]{2,0,1:T(8,128)(2,1)S(1)} copy-done((bf16[16,49,128]{2,0,1:T(8,128)(2,1)S(1)}, bf16[16,49,128]{2,0,1:T(8,128)(2,1)}, u32[]{:S(2)}) %copy-start.4) | copy-done | bytes 200728
  2.6 4.1 %collective-permute-start.1 = (bf16[800,128]{1,0:T(8,128)(2,1)S(1)}, bf16[800,128]{1,0:T(8,128)(2,1)S(1)}, u32[]{:S(2)}, u32[]{:S(2)}) collective-permute-start(bf16[800,128]{1,0:T(8,128)(2,1)S(1)} %shard_map.114.refs_1_), channel_id=1, source_target_pairs={{0,8},{1,9},{2,10},{3,11},{4,12},{5,13},{6,14},{7,15},{8,0},{9,1},... | collective-permute-start | bytes 614408 | tf_op jit(solution)/shard_map/ppermute | solution.py:394
  6.6 1.5 %collective-permute-start = (bf16[800,128]{1,0:T(8,128)(2,1)S(1)}, bf16[800,128]{1,0:T(8,128)(2,1)S(1)}, u32[]{:S(2)}, u32[]{:S(2)}) collective-permute-start(bf16[800,128]{1,0:T(8,128)(2,1)S(1)} %shard_map.114.refs_1_), channel_id=1, source_target_pairs={{0,2},{1,3},{2,0},{3,1},{4,6},{5,7},{6,4},{7,5},{8,10},{9,11},{10,... | collective-permute-start | bytes 614408 | tf_op jit(solution)/shard_map/ppermute | solution.py:394
  8.1 1.5 %collective-permute-start.3 = (bf16[784,128]{1,0:T(8,128)(2,1)S(1)}, bf16[784,128]{1,0:T(8,128)(2,1)S(1)}, u32[]{:S(2)}, u32[]{:S(2)}) collective-permute-start(bf16[784,128]{1,0:T(8,128)(2,1)S(1)} %bitcast.17), channel_id=1, source_target_pairs={{0,1},{1,0},{2,3},{3,2},{4,5},{5,4},{6,7},{7,6},{8,9},{9,8},{10,11... | collective-permute-start | bytes 602120 | tf_op jit(solution)/shard_map/ppermute | solution.py:394
  9.6 1.6 %collective-permute-start.2 = (bf16[784,128]{1,0:T(8,128)(2,1)S(1)}, bf16[784,128]{1,0:T(8,128)(2,1)S(1)}, u32[]{:S(2)}, u32[]{:S(2)}) collective-permute-start(bf16[784,128]{1,0:T(8,128)(2,1)S(1)} %bitcast.18), channel_id=1, source_target_pairs={{0,4},{1,5},{2,6},{3,7},{4,0},{5,1},{6,2},{7,3},{8,12},{9,13},{10,... | collective-permute-start | bytes 602120 | tf_op jit(solution)/shard_map/ppermute | solution.py:394
  11.4 2.9 %collective-permute-done.3.refs_3_.refs_6_ = bf16[784,128]{1,0:T(8,128)(2,1)S(1)} collective-permute-done((bf16[784,128]{1,0:T(8,128)(2,1)S(1)}, bf16[784,128]{1,0:T(8,128)(2,1)S(1)}, u32[]{:S(2)}, u32[]{:S(2)}) %collective-permute-start.3) | collective-permute-done | bytes 200736 | tf_op jit(solution)/shard_map/ppermute | solution.py:394
  14.3 4.4 %collective-permute-done.2.refs_1_ = bf16[784,128]{1,0:T(8,128)(2,1)S(1)} collective-permute-done((bf16[784,128]{1,0:T(8,128)(2,1)S(1)}, bf16[784,128]{1,0:T(8,128)(2,1)S(1)}, u32[]{:S(2)}, u32[]{:S(2)}) %collective-permute-start.2) | collective-permute-done | bytes 200736 | tf_op jit(solution)/shard_map/ppermute | solution.py:394
  19.9 5.2 %collective-permute-done.5.refs_8_ = bf16[784,128]{1,0:T(8,128)(2,1)S(1)} collective-permute-done((bf16[784,128]{1,0:T(8,128)(2,1)S(1)}, bf16[784,128]{1,0:T(8,128)(2,1)S(1)}, u32[]{:S(2)}, u32[]{:S(2)}) %collective-permute-start.5) | collective-permute-done | bytes 200736 | tf_op jit(solution)/shard_map/ppermute | solution.py:394
  25.1 5.0 %shard_map.116 = (f32[1568,256]{1,0:T(8,128)S(1)}, s32[8,256]{1,0:T(8,128)S(1)}, bf16[896,256]{1,0:T(8,128)(2,1)S(1)}, bf16[768,512]{1,0:T(8,128)(2,1)S(1)}, bf1...) custom-call(bf16[49,32,256]{2,1,0:T(8,128)(2,1)S(1)} %get-tuple-elem, ...), custom_call_target="tpu_custom_call" | custom-call | flops 5000000000 | bytes 100000 | tf_op jit(solution)/shard_map/pallas_call | solution.py:380
  30.1 2.2 %shard_map.118 = (f32[8,224,128]{2,1,0:T(8,128)S(1)}, bf16[8,224,128]{2,1,0:T(8,128)(2,1)S(1)}, f32[8,240,128]{2,1,0:T(8,128)S(1)}, bf16[8,240,128]{2,1,0:T(8,12...) custom-call(bf16[896,256]{1,0:T(8,128)(2,1)S(1)} %get-tuple-element.62.refs_2_.refs_0_, ...), custom_call_target="tpu_custom_call" | custom-call | flops 3000000000 | bytes 100000 | tf_op jit(solution)/shard_map/pallas_call | solution.py:380
  33.5 0.7 collective-permute-done.8.refs_3_
  36.9 0.7 collective-permute-done.14.refs_1_
  37.8 1.5 %collective-permute-start.16 = (bf16[8,240,128]{2,1,0:T(8,128)(2,1)S(1)}, bf16[8,240,128]{2,1,0:T(8,128)(2,1)S(1)}, u32[]{:S(2)}, u32[]{:S(2)}) collective-permute-start(bf16[8,240,128]{2,1,0:T(8,128)(2,1)S(1)} %get-tuple-element.91), channel_id=1, source_target_pairs={{0,2},{1,3},{2,0},{3,1},{4,6},{5,7},{6,4},{7,5},{8,10},{9,11},{10,... | collective-permute-start | bytes 1474568 | tf_op jit(solution)/shard_map/ppermute | solution.py:394
  39.4 5.2 %shard_map.117 = (f32[1568,128]{1,0:T(8,128)S(1)}, bf16[1568,128]{1,0:T(8,128)(2,1)S(1)}) custom-call(f32[1568,256]{1,0:T(8,128)S(1)} %get-tuple-element.60.refs_0_, s32[8,256]{1,0:T(8,128)S(1)} %get-tuple-element.61.refs_1_, bf16[896,256]{1,0:T(8,128)(2,1)S(1)} %get-tuple-element.62.refs_2_.refs_0_, bf16[768,512]{1,0:T(8,128)(2,1)S(1)} %get-tuple-element.63.refs_3_.refs_1_, ...), custom_call_target="tpu_custom_call" | custom-call | flops 8000000000 | bytes 100000 | tf_op jit(solution)/shard_map/pallas_call | solution.py:380
  44.6 0.7 collective-permute-start.6
  45.3 2.5 %collective-permute-done.9.came_ref = bf16[8,224,128]{2,1,0:T(8,128)(2,1)S(1)} collective-permute-done((bf16[8,224,128]{2,1,0:T(8,128)(2,1)S(1)}, bf16[8,224,128]{2,1,0:T(8,128)(2,1)S(1)}, u32[]{:S(2)}, u32[]{:S(2)}) %collective-permute-start.9) | collective-permute-done | bytes 458784 | tf_op jit(solution)/shard_map/ppermute | solution.py:394
  47.9 1.5 %collective-permute-start.10 = (bf16[4,224,128]{2,1,0:T(8,128)(2,1)S(1)}, bf16[4,224,128]{2,1,0:T(8,128)(2,1)S(1)}, u32[]{:S(2)}, u32[]{:S(2)}) collective-permute-start(bf16[4,224,128]{2,1,0:T(8,128)(2,1)S(1)} %get-tuple-element.79), channel_id=1, source_target_pairs={{0,2},{1,3},{2,0},{3,1},{4,6},{5,7},{6,4},{7,5},{8,10},{9,11},{10,... | collective-permute-start | bytes 688136 | tf_op jit(solution)/shard_map/ppermute | solution.py:394
  50.2 1.8 %collective-permute-done.16.came_ref = bf16[8,240,128]{2,1,0:T(8,128)(2,1)S(1)} collective-permute-done((bf16[8,240,128]{2,1,0:T(8,128)(2,1)S(1)}, bf16[8,240,128]{2,1,0:T(8,128)(2,1)S(1)}, u32[]{:S(2)}, u32[]{:S(2)}) %collective-permute-start.16) | collective-permute-done | bytes 491552 | tf_op jit(solution)/shard_map/ppermute | solution.py:394
  52.0 1.0 %collective-permute-start.17 = (bf16[4,240,128]{2,1,0:T(8,128)(2,1)S(1)}, bf16[4,240,128]{2,1,0:T(8,128)(2,1)S(1)}, u32[]{:S(2)}, u32[]{:S(2)}) collective-permute-start(bf16[4,240,128]{2,1,0:T(8,128)(2,1)S(1)} %get-tuple-element.93), channel_id=1, source_target_pairs={{0,4},{1,5},{2,6},{3,7},{4,0},{5,1},{6,2},{7,3},{8,12},{9,13},{10,... | collective-permute-start | bytes 737288 | tf_op jit(solution)/shard_map/ppermute | solution.py:394
  53.0 3.0 %collective-permute-done.10.came_ref = bf16[4,224,128]{2,1,0:T(8,128)(2,1)S(1)} collective-permute-done((bf16[4,224,128]{2,1,0:T(8,128)(2,1)S(1)}, bf16[4,224,128]{2,1,0:T(8,128)(2,1)S(1)}, u32[]{:S(2)}, u32[]{:S(2)}) %collective-permute-start.10) | collective-permute-done | bytes 229408 | tf_op jit(solution)/shard_map/ppermute | solution.py:394
  56.9 1.4 %collective-permute-start.11 = (bf16[784,128]{1,0:T(8,128)(2,1)S(1)}, bf16[784,128]{1,0:T(8,128)(2,1)S(1)}, u32[]{:S(2)}, u32[]{:S(2)}) collective-permute-start(bf16[784,128]{1,0:T(8,128)(2,1)S(1)} %get-tuple-element.82), channel_id=1, source_target_pairs={{0,4},{1,5},{2,6},{3,7},{4,0},{5,1},{6,2},{7,3},{8,12},{9,13},{10,... | collective-permute-start | bytes 602120 | tf_op jit(solution)/shard_map/ppermute | solution.py:394
  58.4 2.8 %collective-permute-done.23.came_ref = bf16[4,224,128]{2,1,0:T(8,128)(2,1)S(1)} collective-permute-done((bf16[4,224,128]{2,1,0:T(8,128)(2,1)S(1)}, bf16[4,224,128]{2,1,0:T(8,128)(2,1)S(1)}, u32[]{:S(2)}, u32[]{:S(2)}) %collective-permute-start.23) | collective-permute-done | bytes 229408 | tf_op jit(solution)/shard_map/ppermute | solution.py:394
  61.2 1.5 %collective-permute-start.24 = (bf16[2,224,128]{2,1,0:T(8,128)(2,1)S(1)}, bf16[2,224,128]{2,1,0:T(8,128)(2,1)S(1)}, u32[]{:S(2)}, u32[]{:S(2)}) collective-permute-start(bf16[2,224,128]{2,1,0:T(8,128)(2,1)S(1)} %get-tuple-element.107), channel_id=1, source_target_pairs={{0,2},{1,3},{2,0},{3,1},{4,6},{5,7},{6,4},{7,5},{8,10},{9,11},{10,... | collective-permute-start | bytes 344072 | tf_op jit(solution)/shard_map/ppermute | solution.py:394
  63.5 1.5 %collective-permute-start.13 = (bf16[1,224,128]{2,1,0:T(8,128)(2,1)S(1)}, bf16[1,224,128]{2,1,0:T(8,128)(2,1)S(1)}, u32[]{:S(2)}, u32[]{:S(2)}) collective-permute-start(bf16[1,224,128]{2,1,0:T(8,128)(2,1)S(1)} %get-tuple-element.85), channel_id=1, source_target_pairs={{0,8},{1,9},{2,10},{3,11},{4,12},{5,13},{6,14},{7,15},{8,0},{9,1},... | collective-permute-start | bytes 172040 | tf_op jit(solution)/shard_map/ppermute | solution.py:394
  65.0 1.1 %collective-permute-done.24.came_ref = bf16[2,224,128]{2,1,0:T(8,128)(2,1)S(1)} collective-permute-done((bf16[2,224,128]{2,1,0:T(8,128)(2,1)S(1)}, bf16[2,224,128]{2,1,0:T(8,128)(2,1)S(1)}, u32[]{:S(2)}, u32[]{:S(2)}) %collective-permute-start.24) | collective-permute-done | bytes 114720 | tf_op jit(solution)/shard_map/ppermute | solution.py:394
  66.1 1.7 %collective-permute-start.25 = (bf16[1,224,128]{2,1,0:T(8,128)(2,1)S(1)}, bf16[1,224,128]{2,1,0:T(8,128)(2,1)S(1)}, u32[]{:S(2)}, u32[]{:S(2)}) collective-permute-start(bf16[1,224,128]{2,1,0:T(8,128)(2,1)S(1)} %get-tuple-element.109), channel_id=1, source_target_pairs={{0,8},{1,9},{2,10},{3,11},{4,12},{5,13},{6,14},{7,15},{8,0},{9,1},... | collective-permute-start | bytes 172040 | tf_op jit(solution)/shard_map/ppermute | solution.py:394
  67.8 1.4 %collective-permute-start.19 = (bf16[1,240,128]{2,1,0:T(8,128)(2,1)S(1)}, bf16[1,240,128]{2,1,0:T(8,128)(2,1)S(1)}, u32[]{:S(2)}, u32[]{:S(2)}) collective-permute-start(bf16[1,240,128]{2,1,0:T(8,128)(2,1)S(1)} %get-tuple-element.97), channel_id=1, source_target_pairs={{0,8},{1,9},{2,10},{3,11},{4,12},{5,13},{6,14},{7,15},{8,0},{9,1},... | collective-permute-start | bytes 184328 | tf_op jit(solution)/shard_map/ppermute | solution.py:394
  69.2 1.0 %collective-permute-done.13.came_ref = bf16[1,224,128]{2,1,0:T(8,128)(2,1)S(1)} collective-permute-done((bf16[1,224,128]{2,1,0:T(8,128)(2,1)S(1)}, bf16[1,224,128]{2,1,0:T(8,128)(2,1)S(1)}, u32[]{:S(2)}, u32[]{:S(2)}) %collective-permute-start.13) | collective-permute-done | bytes 57376 | tf_op jit(solution)/shard_map/ppermute | solution.py:394
  70.3 3.1 %collective-permute-done.19.came_ref = bf16[1,240,128]{2,1,0:T(8,128)(2,1)S(1)} collective-permute-done((bf16[1,240,128]{2,1,0:T(8,128)(2,1)S(1)}, bf16[1,240,128]{2,1,0:T(8,128)(2,1)S(1)}, u32[]{:S(2)}, u32[]{:S(2)}) %collective-permute-start.19) | collective-permute-done | bytes 61472 | tf_op jit(solution)/shard_map/ppermute | solution.py:394
  74.1 0.7 shard_map.123
  75.1 0.9 %shard_map.136 = f32[1368,128]{1,0:T(8,128)} custom-call(f32[224,128]{1,0:T(8,128)S(1)} %shard_map.125.refs_0_, f32[240,128]{1,0:T(8,128)S(1)} %shard_map.130.refs_1_, f32[224,128]{1,0:T(8,128)S(1)} %shard_map.135.refs_2_, f32[224,128]{1,0:T(8,128)S(1)} %collective-permute-done.26.refs_3_, f32[240,128]{1,0:T(8,128)S(1)} %collective-permute-done.27.refs_4_, ...), custom_call_target="tpu_custom_call" | custom-call | flops 1000000000 | bytes 100000 | tf_op jit(solution)/shard_map/pallas_call | solution.py:380
  (63 shorter events, 9.2 us)
Async XLA Ops:
  2.3 5.9 %copy-start.5 = (bf16[16,49,128]{2,0,1:T(8,128)(2,1)S(1)}, bf16[16,49,128]{2,0,1:T(8,128)(2,1)}, u32[]{:S(2)}) copy-start(bf16[16,49,128]{2,0,1:T(8,128)(2,1)} %param.11) | copy-start | bytes 602116
  2.3 8.9 %copy-start.3 = (bf16[256,29,49]{0,1,2:T(8,128)(2,1)S(1)}, bf16[256,29,49]{0,1,2:T(8,128)(2,1)}, u32[]{:S(2)}) copy-start(bf16[256,29,49]{0,1,2:T(8,128)(2,1)} %param.12) | copy-start | bytes 2182660
  2.6 16.2 %collective-permute-start.1 = (bf16[800,128]{1,0:T(8,128)(2,1)S(1)}, bf16[800,128]{1,0:T(8,128)(2,1)S(1)}, u32[]{:S(2)}, u32[]{:S(2)}) collective-permute-start(bf16[800,128]{1,0:T(8,128)(2,1)S(1)} %shard_map.114.refs_1_), channel_id=1, source_target_pairs={{0,8},{1,9},{2,10},{3,11},{4,12},{5,13},{6,14},{7,15},{8,0},{9,1},... | collective-permute-start | bytes 614408 | tf_op jit(solution)/shard_map/ppermute | solution.py:394
  6.6 12.1 %collective-permute-start = (bf16[800,128]{1,0:T(8,128)(2,1)S(1)}, bf16[800,128]{1,0:T(8,128)(2,1)S(1)}, u32[]{:S(2)}, u32[]{:S(2)}) collective-permute-start(bf16[800,128]{1,0:T(8,128)(2,1)S(1)} %shard_map.114.refs_1_), channel_id=1, source_target_pairs={{0,2},{1,3},{2,0},{3,1},{4,6},{5,7},{6,4},{7,5},{8,10},{9,11},{10,... | collective-permute-start | bytes 614408 | tf_op jit(solution)/shard_map/ppermute | solution.py:394
  8.1 6.2 %collective-permute-start.3 = (bf16[784,128]{1,0:T(8,128)(2,1)S(1)}, bf16[784,128]{1,0:T(8,128)(2,1)S(1)}, u32[]{:S(2)}, u32[]{:S(2)}) collective-permute-start(bf16[784,128]{1,0:T(8,128)(2,1)S(1)} %bitcast.17), channel_id=1, source_target_pairs={{0,1},{1,0},{2,3},{3,2},{4,5},{5,4},{6,7},{7,6},{8,9},{9,8},{10,11... | collective-permute-start | bytes 602120 | tf_op jit(solution)/shard_map/ppermute | solution.py:394
  9.6 9.1 %collective-permute-start.2 = (bf16[784,128]{1,0:T(8,128)(2,1)S(1)}, bf16[784,128]{1,0:T(8,128)(2,1)S(1)}, u32[]{:S(2)}, u32[]{:S(2)}) collective-permute-start(bf16[784,128]{1,0:T(8,128)(2,1)S(1)} %bitcast.18), channel_id=1, source_target_pairs={{0,4},{1,5},{2,6},{3,7},{4,0},{5,1},{6,2},{7,3},{8,12},{9,13},{10,... | collective-permute-start | bytes 602120 | tf_op jit(solution)/shard_map/ppermute | solution.py:394
  18.7 6.3 %collective-permute-start.4 = (bf16[800,128]{1,0:T(8,128)(2,1)S(1)}, bf16[800,128]{1,0:T(8,128)(2,1)S(1)}, u32[]{:S(2)}, u32[]{:S(2)}) collective-permute-start(bf16[800,128]{1,0:T(8,128)(2,1)S(1)} %get-tuple-element.58.refs_3_), channel_id=1, source_target_pairs={{0,2},{1,3},{2,0},{3,1},{4,6},{5,7},{6,4},{7,5},{8,10},{9,11},{10,... | collective-permute-start | bytes 614408 | tf_op jit(solution)/shard_map/ppermute | solution.py:394
  19.4 5.7 %collective-permute-start.5 = (bf16[784,128]{1,0:T(8,128)(2,1)S(1)}, bf16[784,128]{1,0:T(8,128)(2,1)S(1)}, u32[]{:S(2)}, u32[]{:S(2)}) collective-permute-start(bf16[784,128]{1,0:T(8,128)(2,1)S(1)} %get-tuple-element.59.refs_7_), channel_id=1, source_target_pairs={{0,1},{1,0},{2,3},{3,2},{4,5},{5,4},{6,7},{7,6},{8,9},{9,8},{10,11... | collective-permute-start | bytes 602120 | tf_op jit(solution)/shard_map/ppermute | solution.py:394
  32.3 1.9 %collective-permute-start.8 = (bf16[8,224,128]{2,1,0:T(8,128)(2,1)S(1)}, bf16[8,224,128]{2,1,0:T(8,128)(2,1)S(1)}, u32[]{:S(2)}, u32[]{:S(2)}) collective-permute-start(bf16[8,224,128]{2,1,0:T(8,128)(2,1)S(1)} %get-tuple-element.75), channel_id=1, source_target_pairs={{0,16},{16,0},{1,17},{17,1},{2,18},{18,2},{3,19},{19,3},{4,20},{20... | collective-permute-start | bytes 1376264 | tf_op jit(solution)/shard_map/ppermute | solution.py:398
  32.4 2.5 %collective-permute-start.7 = (bf16[8,224,128]{2,1,0:T(8,128)(2,1)S(1)}, bf16[8,224,128]{2,1,0:T(8,128)(2,1)S(1)}, u32[]{:S(2)}, u32[]{:S(2)}) collective-permute-start(bf16[8,224,128]{2,1,0:T(8,128)(2,1)S(1)} %get-tuple-element.68), channel_id=1, source_target_pairs={{0,16},{16,0},{1,17},{17,1},{2,18},{18,2},{3,19},{19,3},{4,20},{20... | collective-permute-start | bytes 1376264 | tf_op jit(solution)/shard_map/ppermute | solution.py:398
  32.9 2.8 %collective-permute-start.21 = (bf16[8,224,128]{2,1,0:T(8,128)(2,1)S(1)}, bf16[8,224,128]{2,1,0:T(8,128)(2,1)S(1)}, u32[]{:S(2)}, u32[]{:S(2)}) collective-permute-start(bf16[8,224,128]{2,1,0:T(8,128)(2,1)S(1)} %get-tuple-element.101), channel_id=1, source_target_pairs={{0,16},{16,0},{1,17},{17,1},{2,18},{18,2},{3,19},{19,3},{4,20},{20... | collective-permute-start | bytes 1376264 | tf_op jit(solution)/shard_map/ppermute | solution.py:398
  33.0 3.2 %collective-permute-start.20 = (bf16[8,224,128]{2,1,0:T(8,128)(2,1)S(1)}, bf16[8,224,128]{2,1,0:T(8,128)(2,1)S(1)}, u32[]{:S(2)}, u32[]{:S(2)}) collective-permute-start(bf16[8,224,128]{2,1,0:T(8,128)(2,1)S(1)} %get-tuple-element.99), channel_id=1, source_target_pairs={{0,16},{16,0},{1,17},{17,1},{2,18},{18,2},{3,19},{19,3},{4,20},{20... | collective-permute-start | bytes 1376264 | tf_op jit(solution)/shard_map/ppermute | solution.py:398
  33.4 3.5 %collective-permute-start.15 = (bf16[8,240,128]{2,1,0:T(8,128)(2,1)S(1)}, bf16[8,240,128]{2,1,0:T(8,128)(2,1)S(1)}, u32[]{:S(2)}, u32[]{:S(2)}) collective-permute-start(bf16[8,240,128]{2,1,0:T(8,128)(2,1)S(1)} %get-tuple-element.89), channel_id=1, source_target_pairs={{0,16},{16,0},{1,17},{17,1},{2,18},{18,2},{3,19},{19,3},{4,20},{20... | collective-permute-start | bytes 1474568 | tf_op jit(solution)/shard_map/ppermute | solution.py:398
  34.2 3.4 %collective-permute-start.14 = (bf16[8,240,128]{2,1,0:T(8,128)(2,1)S(1)}, bf16[8,240,128]{2,1,0:T(8,128)(2,1)S(1)}, u32[]{:S(2)}, u32[]{:S(2)}) collective-permute-start(bf16[8,240,128]{2,1,0:T(8,128)(2,1)S(1)} %get-tuple-element.87), channel_id=1, source_target_pairs={{0,16},{16,0},{1,17},{17,1},{2,18},{18,2},{3,19},{19,3},{4,20},{20... | collective-permute-start | bytes 1474568 | tf_op jit(solution)/shard_map/ppermute | solution.py:398
  35.0 12.8 %collective-permute-start.9 = (bf16[8,224,128]{2,1,0:T(8,128)(2,1)S(1)}, bf16[8,224,128]{2,1,0:T(8,128)(2,1)S(1)}, u32[]{:S(2)}, u32[]{:S(2)}) collective-permute-start(bf16[8,224,128]{2,1,0:T(8,128)(2,1)S(1)} %get-tuple-element.77), channel_id=1, source_target_pairs={{0,1},{1,0},{2,3},{3,2},{4,5},{5,4},{6,7},{7,6},{8,9},{9,8},{10,11... | collective-permute-start | bytes 1376264 | tf_op jit(solution)/shard_map/ppermute | solution.py:394
  36.2 3.2 %copy-start.2 = (bf16[896,896]{1,0:T(8,128)(2,1)S(1)}, bf16[896,896]{1,0:T(8,128)(2,1)}, u32[]{:S(2)}) copy-start(bf16[896,896]{1,0:T(8,128)(2,1)} %refs_5_.1) | copy-start | bytes 4816900
  36.4 13.1 %collective-permute-start.22 = (bf16[8,224,128]{2,1,0:T(8,128)(2,1)S(1)}, bf16[8,224,128]{2,1,0:T(8,128)(2,1)S(1)}, u32[]{:S(2)}, u32[]{:S(2)}) collective-permute-start(bf16[8,224,128]{2,1,0:T(8,128)(2,1)S(1)} %get-tuple-element.103), channel_id=1, source_target_pairs={{0,4},{1,5},{2,6},{3,7},{4,0},{5,1},{6,2},{7,3},{8,12},{9,13},{10,... | collective-permute-start | bytes 1376264 | tf_op jit(solution)/shard_map/ppermute | solution.py:394
  37.8 14.1 %collective-permute-start.16 = (bf16[8,240,128]{2,1,0:T(8,128)(2,1)S(1)}, bf16[8,240,128]{2,1,0:T(8,128)(2,1)S(1)}, u32[]{:S(2)}, u32[]{:S(2)}) collective-permute-start(bf16[8,240,128]{2,1,0:T(8,128)(2,1)S(1)} %get-tuple-element.91), channel_id=1, source_target_pairs={{0,2},{1,3},{2,0},{3,1},{4,6},{5,7},{6,4},{7,5},{8,10},{9,11},{10,... | collective-permute-start | bytes 1474568 | tf_op jit(solution)/shard_map/ppermute | solution.py:394
  44.6 12.2 %collective-permute-start.6 = (bf16[1568,128]{1,0:T(8,128)(2,1)S(1)}, bf16[1568,128]{1,0:T(8,128)(2,1)S(1)}, u32[]{:S(2)}, u32[]{:S(2)}) collective-permute-start(bf16[1568,128]{1,0:T(8,128)(2,1)S(1)} %get-tuple-element.66.refs_0_), channel_id=1, source_target_pairs={{0,1},{1,0},{2,3},{3,2},{4,5},{5,4},{6,7},{7,6},{8,9},{9,8},{10,11... | collective-permute-start | bytes 1204232 | tf_op jit(solution)/shard_map/ppermute | solution.py:394
  47.9 8.1 %collective-permute-start.10 = (bf16[4,224,128]{2,1,0:T(8,128)(2,1)S(1)}, bf16[4,224,128]{2,1,0:T(8,128)(2,1)S(1)}, u32[]{:S(2)}, u32[]{:S(2)}) collective-permute-start(bf16[4,224,128]{2,1,0:T(8,128)(2,1)S(1)} %get-tuple-element.79), channel_id=1, source_target_pairs={{0,2},{1,3},{2,0},{3,1},{4,6},{5,7},{6,4},{7,5},{8,10},{9,11},{10,... | collective-permute-start | bytes 688136 | tf_op jit(solution)/shard_map/ppermute | solution.py:394
  49.5 11.6 %collective-permute-start.23 = (bf16[4,224,128]{2,1,0:T(8,128)(2,1)S(1)}, bf16[4,224,128]{2,1,0:T(8,128)(2,1)S(1)}, u32[]{:S(2)}, u32[]{:S(2)}) collective-permute-start(bf16[4,224,128]{2,1,0:T(8,128)(2,1)S(1)} %get-tuple-element.105), channel_id=1, source_target_pairs={{0,1},{1,0},{2,3},{3,2},{4,5},{5,4},{6,7},{7,6},{8,9},{9,8},{10,11... | collective-permute-start | bytes 688136 | tf_op jit(solution)/shard_map/ppermute | solution.py:394
  52.0 10.7 %collective-permute-start.17 = (bf16[4,240,128]{2,1,0:T(8,128)(2,1)S(1)}, bf16[4,240,128]{2,1,0:T(8,128)(2,1)S(1)}, u32[]{:S(2)}, u32[]{:S(2)}) collective-permute-start(bf16[4,240,128]{2,1,0:T(8,128)(2,1)S(1)} %get-tuple-element.93), channel_id=1, source_target_pairs={{0,4},{1,5},{2,6},{3,7},{4,0},{5,1},{6,2},{7,3},{8,12},{9,13},{10,... | collective-permute-start | bytes 737288 | tf_op jit(solution)/shard_map/ppermute | solution.py:394
  56.1 7.4 %collective-permute-start.12 = (bf16[2,224,128]{2,1,0:T(8,128)(2,1)S(1)}, bf16[2,224,128]{2,1,0:T(8,128)(2,1)S(1)}, u32[]{:S(2)}, u32[]{:S(2)}) collective-permute-start(bf16[2,224,128]{2,1,0:T(8,128)(2,1)S(1)} %get-tuple-element.80.after_ref), channel_id=1, source_target_pairs={{0,4},{1,5},{2,6},{3,7},{4,0},{5,1},{6,2},{7,3},{8,12},{9,13},{10,... | collective-permute-start | bytes 344072 | tf_op jit(solution)/shard_map/ppermute | solution.py:394
  56.9 17.2 %collective-permute-start.11 = (bf16[784,128]{1,0:T(8,128)(2,1)S(1)}, bf16[784,128]{1,0:T(8,128)(2,1)S(1)}, u32[]{:S(2)}, u32[]{:S(2)}) collective-permute-start(bf16[784,128]{1,0:T(8,128)(2,1)S(1)} %get-tuple-element.82), channel_id=1, source_target_pairs={{0,4},{1,5},{2,6},{3,7},{4,0},{5,1},{6,2},{7,3},{8,12},{9,13},{10,... | collective-permute-start | bytes 602120 | tf_op jit(solution)/shard_map/ppermute | solution.py:394
  61.2 4.9 %collective-permute-start.24 = (bf16[2,224,128]{2,1,0:T(8,128)(2,1)S(1)}, bf16[2,224,128]{2,1,0:T(8,128)(2,1)S(1)}, u32[]{:S(2)}, u32[]{:S(2)}) collective-permute-start(bf16[2,224,128]{2,1,0:T(8,128)(2,1)S(1)} %get-tuple-element.107), channel_id=1, source_target_pairs={{0,2},{1,3},{2,0},{3,1},{4,6},{5,7},{6,4},{7,5},{8,10},{9,11},{10,... | collective-permute-start | bytes 344072 | tf_op jit(solution)/shard_map/ppermute | solution.py:394
  62.8 5.0 %collective-permute-start.18 = (bf16[2,240,128]{2,1,0:T(8,128)(2,1)S(1)}, bf16[2,240,128]{2,1,0:T(8,128)(2,1)S(1)}, u32[]{:S(2)}, u32[]{:S(2)}) collective-permute-start(bf16[2,240,128]{2,1,0:T(8,128)(2,1)S(1)} %get-tuple-element.95), channel_id=1, source_target_pairs={{0,1},{1,0},{2,3},{3,2},{4,5},{5,4},{6,7},{7,6},{8,9},{9,8},{10,11... | collective-permute-start | bytes 368648 | tf_op jit(solution)/shard_map/ppermute | solution.py:394
  63.5 6.7 %collective-permute-start.13 = (bf16[1,224,128]{2,1,0:T(8,128)(2,1)S(1)}, bf16[1,224,128]{2,1,0:T(8,128)(2,1)S(1)}, u32[]{:S(2)}, u32[]{:S(2)}) collective-permute-start(bf16[1,224,128]{2,1,0:T(8,128)(2,1)S(1)} %get-tuple-element.85), channel_id=1, source_target_pairs={{0,8},{1,9},{2,10},{3,11},{4,12},{5,13},{6,14},{7,15},{8,0},{9,1},... | collective-permute-start | bytes 172040 | tf_op jit(solution)/shard_map/ppermute | solution.py:394
  66.1 7.4 %collective-permute-start.25 = (bf16[1,224,128]{2,1,0:T(8,128)(2,1)S(1)}, bf16[1,224,128]{2,1,0:T(8,128)(2,1)S(1)}, u32[]{:S(2)}, u32[]{:S(2)}) collective-permute-start(bf16[1,224,128]{2,1,0:T(8,128)(2,1)S(1)} %get-tuple-element.109), channel_id=1, source_target_pairs={{0,8},{1,9},{2,10},{3,11},{4,12},{5,13},{6,14},{7,15},{8,0},{9,1},... | collective-permute-start | bytes 172040 | tf_op jit(solution)/shard_map/ppermute | solution.py:394
  67.8 5.6 %collective-permute-start.19 = (bf16[1,240,128]{2,1,0:T(8,128)(2,1)S(1)}, bf16[1,240,128]{2,1,0:T(8,128)(2,1)S(1)}, u32[]{:S(2)}, u32[]{:S(2)}) collective-permute-start(bf16[1,240,128]{2,1,0:T(8,128)(2,1)S(1)} %get-tuple-element.97), channel_id=1, source_target_pairs={{0,8},{1,9},{2,10},{3,11},{4,12},{5,13},{6,14},{7,15},{8,0},{9,1},... | collective-permute-start | bytes 184328 | tf_op jit(solution)/shard_map/ppermute | solution.py:394
  70.2 4.6 %collective-permute-start.26 = (f32[224,128]{1,0:T(8,128)S(1)}, f32[224,128]{1,0:T(8,128)S(1)}, u32[]{:S(2)}, u32[]{:S(2)}) collective-permute-start(f32[224,128]{1,0:T(8,128)S(1)} %shard_map.125.refs_0_), channel_id=1, source_target_pairs={{0,16},{16,0},{1,17},{17,1},{2,18},{18,2},{3,19},{19,3},{4,20},{20... | collective-permute-start | bytes 344072 | tf_op jit(solution)/shard_map/ppermute | solution.py:398
  73.5 1.6 %collective-permute-start.27 = (f32[240,128]{1,0:T(8,128)S(1)}, f32[240,128]{1,0:T(8,128)S(1)}, u32[]{:S(2)}, u32[]{:S(2)}) collective-permute-start(f32[240,128]{1,0:T(8,128)S(1)} %shard_map.130.refs_1_), channel_id=1, source_target_pairs={{0,16},{16,0},{1,17},{17,1},{2,18},{18,2},{3,19},{19,3},{4,20},{20... | collective-permute-start | bytes 368648 | tf_op jit(solution)/shard_map/ppermute | solution.py:398
  73.6 1.5 %collective-permute-start.28 = (f32[224,128]{1,0:T(8,128)S(1)}, f32[224,128]{1,0:T(8,128)S(1)}, u32[]{:S(2)}, u32[]{:S(2)}) collective-permute-start(f32[224,128]{1,0:T(8,128)S(1)} %shard_map.135.refs_2_), channel_id=1, source_target_pairs={{0,16},{16,0},{1,17},{17,1},{2,18},{18,2},{3,19},{19,3},{4,20},{20... | collective-permute-start | bytes 344072 | tf_op jit(solution)/shard_map/ppermute | solution.py:398
  (3 other events, 5.9 us)
